TPU v7x, 32 devices: a whole 2x2x4 slice. The times are simulated.
32 devices in a mesh: dp: 8 (over z, core), mp: 4 (over y, x).
Axes of the slice: x: 2, y: 2, z: 4, core: 2. Of those that a mesh axis runs over, the one named last changes fastest.
Arguments:
- tokens: bfloat16 [16, 1024, 1600], P('dp', 'mp'), may hold values from -6 to 6
- cotangent: bfloat16 [16, 1024, 1600], P('dp', 'mp'), may hold values from -6 to 6
- block_order: int32 [8], replicated, may hold values from 0 to 7, each once
- qkv_weight: bfloat16 [2, 1600, 4800], P(None, 'dp'), may hold values from -0.15625 to 0.15625
- proj_weight: bfloat16 [2, 1600, 1600], P(None, 'dp'), may hold values from -3 to 3
- fc_weight: bfloat16 [2, 1600, 6400], P(None, 'dp', 'mp'), may hold values from -0.15625 to 0.15625
- fc2_weight: bfloat16 [2, 6400, 1600], P(None, 'mp', 'dp'), may hold values from -0.078125 to 0.078125
- fc_bias: bfloat16 [2, 6400], P(None, ('mp', 'dp')), may hold values from -1.5 to 1.5
- norm_gain: bfloat16 [2, 2, 1600], P(None, None, 'dp'), may hold values from 0.5 to 1.5
- norm_shift: bfloat16 [2, 2, 1600], P(None, None, 'dp'), may hold values from -1.5 to 1.5
- attn_bias: bfloat16 [2, 2, 1600], P(None, None, 'dp'), may hold values from -1.5 to 1.5
- out_bias: bfloat16 [2, 2, 1600], P(None, None, 'dp'), may hold values from -1.5 to 1.5
Outputs:
- outputs: float32 [16, 1024, 1600], P('dp', 'mp')
- input_grad: float32 [16, 1024, 1600], P('dp', 'mp')
- qkv_weight_grad: float32 [2, 1600, 4800], P(None, 'dp', 'mp')
- proj_weight_grad: float32 [2, 1600, 1600], P(None, 'dp', 'mp')
- fc_weight_grad: float32 [2, 1600, 6400], P(None, 'dp', 'mp')
- fc2_weight_grad: float32 [2, 6400, 1600], P(None, 'mp', 'dp')
- fc_bias_grad: float32 [2, 6400], P(None, ('mp', 'dp'))
- norm_gain_grad: float32 [2, 2, 1600], P(None, None, 'dp')
- norm_shift_grad: float32 [2, 2, 1600], P(None, None, 'dp')
- attn_bias_grad: float32 [2, 2, 1600], P(None, None, 'dp')
- out_bias_grad: float32 [2, 2, 1600], P(None, None, 'dp')
Inputs may be any that keep to these rules, and one draw needn't show every extreme that they name: A permutation: block slot 2r and 2r + 1 of a sequence, held by index r of mp, hold the blocks numbered block_order[2r] and block_order[2r + 1] of 128 tokens.
All inputs are finite; a program needn't handle non-finite values.
Results may differ from a plain program's by a relative error of at most 0.015.
Values may be sent and summed in bfloat16 or wider, within the bound.
A program may use at most 448 MiB of HBM per device.

v0:
```python
import jax
import jax.numpy as jnp
from jax import lax
from jax.sharding import PartitionSpec as P

HD = 64
LAYERS = 2


eps = 1e-05


def layer_norm(value, gain, shift):
    mean = jnp.mean(value, axis=-1, keepdims=True)
    centred = value - mean
    spread = jnp.mean(centred * centred, axis=-1, keepdims=True)
    return centred * lax.rsqrt(spread + eps) * gain + shift


def fetch_params(weights, layer):
    pieces = tuple((w[layer] for w in weights))
    return (
        lax.all_gather(pieces[0], "dp", axis=0, tiled=True),
        lax.all_gather(pieces[1], "dp", axis=0, tiled=True),
        lax.all_gather(pieces[2], "dp", axis=0, tiled=True),
        lax.all_gather(pieces[3], "dp", axis=1, tiled=True),
        lax.all_gather(pieces[4], "dp", axis=0, tiled=True),
        lax.all_gather(pieces[5], "dp", axis=1, tiled=True),
        lax.all_gather(pieces[6], "dp", axis=1, tiled=True),
        lax.all_gather(pieces[7], "dp", axis=1, tiled=True),
        lax.all_gather(pieces[8], "dp", axis=1, tiled=True),
    )


def fetch_again(weights, layer):
    pieces = tuple((w[layer] for w in weights))
    return (
        lax.all_gather(pieces[0], "dp", axis=0, tiled=True),
        lax.all_gather(pieces[1], "dp", axis=0, tiled=True),
        lax.all_gather(pieces[2], "dp", axis=0, tiled=True),
        lax.all_gather(pieces[3], "dp", axis=1, tiled=True),
        lax.all_gather(pieces[4], "dp", axis=0, tiled=True),
        lax.all_gather(pieces[5], "dp", axis=1, tiled=True),
        lax.all_gather(pieces[6], "dp", axis=1, tiled=True),
        lax.all_gather(pieces[7], "dp", axis=1, tiled=True),
        lax.all_gather(pieces[8], "dp", axis=1, tiled=True),
    )


def scores_of(query_heads, key_heads, visible, scale):
    scores = (
        jnp.einsum("qhd,khd->hqk", query_heads, key_heads, preferred_element_type=jnp.float32)
        * scale
    )
    return jnp.where(visible, scores, -1e30)


def body(
    tokens,
    cotangent,
    block_order,
    qkv_weight,
    proj_weight,
    fc_weight,
    fc2_weight,
    fc_bias,
    norm_gain,
    norm_shift,
    attn_bias,
    out_bias,
):
    weights = (
        qkv_weight,
        proj_weight,
        fc_weight,
        fc2_weight,
        fc_bias,
        norm_gain,
        norm_shift,
        attn_bias,
        out_bias,
    )
    seqs, local, width = tokens.shape
    heads = width // HD
    scale = HD ** (-0.5)
    model_size = lax.axis_size("mp")
    data_size = lax.axis_size("dp")
    length = local * model_size
    half = local // 2
    rank = lax.axis_index("mp")
    owned = lax.dynamic_slice_in_dim(block_order, 2 * rank, 2)
    offsets = jnp.arange(local, dtype=jnp.int32)
    query_place = jnp.where(offsets < half, owned[0], owned[1]) * half + offsets % half
    every = jnp.arange(length, dtype=jnp.int32)
    key_place = jnp.repeat(block_order, half) * half + every % half
    visible = key_place[None, :] <= query_place[:, None]
    count = seqs * local

    def attend_one(pack):
        query_heads, key_heads, value_heads = pack
        scores = scores_of(query_heads, key_heads, visible, scale)
        top = jnp.max(scores, axis=-1, keepdims=True)
        expo = jnp.exp(scores - top)
        total = jnp.sum(expo, axis=-1, keepdims=True)
        probs = (expo / total).astype(jnp.bfloat16)
        logsum = top + jnp.log(total)
        attended = jnp.einsum(
            "hqk,khd->qhd", probs, value_heads, preferred_element_type=jnp.float32
        )
        return (attended.reshape(local, width).astype(jnp.bfloat16), logsum)

    def attend_back(pack):
        query_heads, key_heads, value_heads, grad_heads, logsum = pack
        scores = scores_of(query_heads, key_heads, visible, scale)
        probs = jnp.exp(scores - logsum)
        prob_grad = jnp.einsum(
            "qhd,khd->hqk", grad_heads, value_heads, preferred_element_type=jnp.float32
        )
        value_grad = jnp.einsum(
            "hqk,qhd->khd",
            probs.astype(jnp.bfloat16),
            grad_heads,
            preferred_element_type=jnp.float32,
        )
        score_grad = (
            probs * (prob_grad - jnp.sum(probs * prob_grad, axis=-1, keepdims=True))
        ).astype(jnp.bfloat16)
        query_grad = (
            jnp.einsum("hqk,khd->qhd", score_grad, key_heads, preferred_element_type=jnp.float32)
            * scale
        )
        key_grad = (
            jnp.einsum("hqk,qhd->khd", score_grad, query_heads, preferred_element_type=jnp.float32)
            * scale
        )
        return (
            query_grad.reshape(local, width),
            key_grad.reshape(length, width),
            value_grad.reshape(length, width),
        )

    hidden = tokens.reshape(count, width).astype(jnp.float32)
    saved = []
    for layer in range(LAYERS):
        params = fetch_params(weights, layer)
        qkv_full, proj_full, fc_full, fc2_full, fc_b = (
            params[0],
            params[1],
            params[2],
            params[3],
            params[4],
        )
        gains = params[5].astype(jnp.float32)
        shifts = params[6].astype(jnp.float32)
        bias_in = params[7].astype(jnp.float32)
        bias_out = params[8].astype(jnp.float32)
        normed = layer_norm(hidden, gains[0], shifts[0]).astype(jnp.bfloat16)
        mixed = jnp.dot(normed, qkv_full, preferred_element_type=jnp.float32)
        query = (mixed[:, :width] + bias_in[0]).astype(jnp.bfloat16)
        key = mixed[:, width : 2 * width].astype(jnp.bfloat16)
        value = (mixed[:, 2 * width :] + bias_in[1]).astype(jnp.bfloat16)
        keys, values = (
            lax.all_gather(key.reshape(seqs, local, width), "mp", axis=1, tiled=True),
            lax.all_gather(value.reshape(seqs, local, width), "mp", axis=1, tiled=True),
        )
        query_heads = query.reshape(seqs, local, heads, HD)
        key_heads = keys.reshape(seqs, length, heads, HD)
        value_heads = values.reshape(seqs, length, heads, HD)
        attended, logsum = lax.map(attend_one, (query_heads, key_heads, value_heads))
        attended = attended.reshape(count, width)
        middle = (
            hidden + jnp.dot(attended, proj_full, preferred_element_type=jnp.float32) + bias_out[0]
        )
        normed_two = layer_norm(middle, gains[1], shifts[1]).astype(jnp.bfloat16)
        group_rows = lax.all_gather(normed_two, "mp", axis=0, tiled=True)
        inner = jnp.dot(group_rows, fc_full, preferred_element_type=jnp.float32) + fc_b.astype(
            jnp.float32
        )
        active = jax.nn.gelu(inner, approximate=True).astype(jnp.bfloat16)

        def down_rows(start, rows, active=active, fc2_full=fc2_full):
            return jnp.dot(active, fc2_full, preferred_element_type=jnp.float32)

        reduced = lax.psum_scatter(
            down_rows(jnp.int32(0), lax.axis_size("mp") * count).astype(jnp.bfloat16),
            "mp",
            scatter_dimension=0,
            tiled=True,
        ).astype(jnp.float32)
        output = middle + reduced + bias_out[1]
        kept_params = None
        kept_pairs = None
        saved.append(
            (
                hidden,
                normed,
                query,
                key,
                value,
                logsum,
                attended,
                middle,
                group_rows,
                inner,
                kept_params,
                kept_pairs,
            )
        )
        hidden = output
    outputs = hidden.reshape(seqs, local, width)
    grad = cotangent.reshape(count, width).astype(jnp.float32)
    collected = []
    for layer in reversed(range(LAYERS)):
        (
            hidden_in,
            normed,
            query,
            key,
            value,
            logsum,
            attended,
            middle,
            group_rows,
            inner,
            kept_params,
            kept_pairs,
        ) = saved[layer]
        params = fetch_again(weights, layer)
        keys, values = (
            lax.all_gather(key.reshape(seqs, local, width), "mp", axis=1, tiled=True),
            lax.all_gather(value.reshape(seqs, local, width), "mp", axis=1, tiled=True),
        )
        qkv_full, proj_full, fc_full, fc2_full = (params[0], params[1], params[2], params[3])
        gains = params[5].astype(jnp.float32)
        shifts = params[6].astype(jnp.float32)
        out_grad = grad.astype(jnp.bfloat16)
        mlp_bias_grad = jnp.sum(out_grad.astype(jnp.float32), axis=0)
        group_grad = lax.all_gather(out_grad, "mp", axis=0, tiled=True)
        active = jax.nn.gelu(inner, approximate=True).astype(jnp.bfloat16)
        fc2_grad = jnp.einsum("nf,nd->fd", active, group_grad, preferred_element_type=jnp.float32)
        active_grad = jnp.einsum(
            "nd,fd->nf", group_grad, fc2_full, preferred_element_type=jnp.float32
        )
        _, gelu_back = jax.vjp(lambda v: jax.nn.gelu(v, approximate=True), inner)
        inner_grad = gelu_back(active_grad)[0].astype(jnp.bfloat16)
        fc_bias_grad = jnp.sum(inner_grad.astype(jnp.float32), axis=0)
        fc_grad = jnp.einsum(
            "nd,nf->df", group_rows, inner_grad, preferred_element_type=jnp.float32
        )

        def back_rows(start, rows, inner_grad=inner_grad, fc_full=fc_full):
            return jnp.einsum("nf,df->nd", inner_grad, fc_full, preferred_element_type=jnp.float32)

        normed_two_grad = lax.psum_scatter(
            back_rows(jnp.int32(0), lax.axis_size("mp") * count).astype(jnp.bfloat16),
            "mp",
            scatter_dimension=0,
            tiled=True,
        ).astype(jnp.float32)
        _, norm_two_back = jax.vjp(layer_norm, middle, gains[1], shifts[1])
        middle_part, gain_two, shift_two = norm_two_back(normed_two_grad)
        middle_grad = grad + middle_part
        branch_grad = middle_grad.astype(jnp.bfloat16)
        attn_out_bias_grad = jnp.sum(branch_grad.astype(jnp.float32), axis=0)
        proj_grad = jnp.einsum(
            "nd,ne->de", attended, branch_grad, preferred_element_type=jnp.float32
        )
        attended_grad = jnp.einsum(
            "ne,de->nd", branch_grad, proj_full, preferred_element_type=jnp.float32
        ).astype(jnp.bfloat16)
        grad_heads = attended_grad.reshape(seqs, local, heads, HD)
        query_heads = query.reshape(seqs, local, heads, HD)
        key_heads = keys.reshape(seqs, length, heads, HD)
        value_heads = values.reshape(seqs, length, heads, HD)
        query_grad, key_grad, value_grad = lax.map(
            attend_back, (query_heads, key_heads, value_heads, grad_heads, logsum)
        )
        key_part, value_part = (
            lax.psum_scatter(
                key_grad.astype(jnp.bfloat16), "mp", scatter_dimension=1, tiled=True
            ).astype(jnp.float32),
            lax.psum_scatter(
                value_grad.astype(jnp.bfloat16), "mp", scatter_dimension=1, tiled=True
            ).astype(jnp.float32),
        )
        query_round = query_grad.reshape(count, width).astype(jnp.bfloat16)
        key_round = key_part.reshape(count, width).astype(jnp.bfloat16)
        value_round = value_part.reshape(count, width).astype(jnp.bfloat16)
        mixed_grad = jnp.concatenate([query_round, key_round, value_round], axis=1)
        bias_in_grad = jnp.stack(
            [
                jnp.sum(query_round.astype(jnp.float32), axis=0),
                jnp.sum(value_round.astype(jnp.float32), axis=0),
            ]
        )
        qkv_grad = jnp.einsum("nd,ne->de", normed, mixed_grad, preferred_element_type=jnp.float32)
        normed_grad = jnp.einsum(
            "ne,de->nd", mixed_grad, qkv_full, preferred_element_type=jnp.float32
        )
        _, norm_one_back = jax.vjp(layer_norm, hidden_in, gains[0], shifts[0])
        hidden_part, gain_one, shift_one = norm_one_back(normed_grad)
        grad = middle_grad + hidden_part
        gain_grad = jnp.stack([gain_one, gain_two])
        shift_grad = jnp.stack([shift_one, shift_two])
        bias_out_grad = jnp.stack([attn_out_bias_grad, mlp_bias_grad])
        shards = (
            lax.psum_scatter(
                qkv_grad.astype(jnp.bfloat16), "dp", scatter_dimension=0, tiled=True
            ).astype(jnp.float32),
            lax.psum_scatter(
                proj_grad.astype(jnp.bfloat16), "dp", scatter_dimension=0, tiled=True
            ).astype(jnp.float32),
            lax.psum_scatter(
                fc_grad.astype(jnp.bfloat16), "dp", scatter_dimension=0, tiled=True
            ).astype(jnp.float32),
            lax.psum_scatter(
                fc2_grad.astype(jnp.bfloat16), "dp", scatter_dimension=1, tiled=True
            ).astype(jnp.float32),
            lax.psum_scatter(
                fc_bias_grad.astype(jnp.bfloat16), "dp", scatter_dimension=0, tiled=True
            ).astype(jnp.float32),
            lax.psum_scatter(
                gain_grad.astype(jnp.bfloat16), "dp", scatter_dimension=1, tiled=True
            ).astype(jnp.float32),
            lax.psum_scatter(
                shift_grad.astype(jnp.bfloat16), "dp", scatter_dimension=1, tiled=True
            ).astype(jnp.float32),
            lax.psum_scatter(
                bias_in_grad.astype(jnp.bfloat16), "dp", scatter_dimension=1, tiled=True
            ).astype(jnp.float32),
            lax.psum_scatter(
                bias_out_grad.astype(jnp.bfloat16), "dp", scatter_dimension=1, tiled=True
            ).astype(jnp.float32),
        )
        projections = (
            lax.psum_scatter(
                shards[0].astype(jnp.bfloat16), "mp", scatter_dimension=1, tiled=True
            ).astype(jnp.float32),
            lax.psum_scatter(
                shards[1].astype(jnp.bfloat16), "mp", scatter_dimension=1, tiled=True
            ).astype(jnp.float32),
        )
        smaller = lax.psum((shards[5], shards[6], shards[7], shards[8]), "mp")
        factor = 1.0 / data_size
        collected.append(
            (
                projections[0] * factor,
                projections[1] * factor,
                shards[2] * factor,
                shards[3] * factor,
                shards[4] * factor,
                smaller[0] * factor,
                smaller[1] * factor,
                smaller[2] * factor,
                smaller[3] * factor,
            )
        )
    collected = collected[::-1]
    stacked = tuple((jnp.stack([entry[index] for entry in collected]) for index in range(9)))
    input_grad = grad.reshape(seqs, local, width)
    return (
        outputs,
        input_grad,
        stacked[0],
        stacked[1],
        stacked[2],
        stacked[3],
        stacked[4],
        stacked[5],
        stacked[6],
        stacked[7],
        stacked[8],
    )


def solution(mesh):
    return jax.shard_map(
        body,
        mesh=mesh,
        in_specs=(
            P("dp", "mp", None),
            P("dp", "mp", None),
            P(),
            P(None, "dp", None),
            P(None, "dp", None),
            P(None, "dp", "mp"),
            P(None, "mp", "dp"),
            P(None, ("mp", "dp")),
            P(None, None, "dp"),
            P(None, None, "dp"),
            P(None, None, "dp"),
            P(None, None, "dp"),
        ),
        out_specs=(
            P("dp", "mp", None),
            P("dp", "mp", None),
            P(None, "dp", "mp"),
            P(None, "dp", "mp"),
            P(None, "dp", "mp"),
            P(None, "mp", "dp"),
            P(None, ("mp", "dp")),
            P(None, None, "dp"),
            P(None, None, "dp"),
            P(None, None, "dp"),
            P(None, None, "dp"),
        ),
        check_vma=False,
    )
```

profile of v0, /device:TPU:1, one launch (start us, length us, event | category | flops | bytes accessed | tf_op | source)
XLA Modules:
  0.0 3291.9 jit_solution(6843973450623480767)
XLA Ops:
  14.0 18.9 all-gather
  33.8 26.0 all-gather.1
  61.4 26.8 slice_reduce_fusion.10
  88.2 27.3 slice_reduce_fusion.9
  115.4 48.0 %all-gather.51.cloned.1.call-done = bf16[1,1600,4800]{2,1,0:T(8,128)(2,1)} async-done(((bf16[1,200,4800]{2,1,0:T(8,128)(2,1)}), bf16[1,1600,4800]{2,1,0:T(8,128)(2,1)}) %all-gather.51.cloned.1.call-update) | async-done | bytes 15360016 | tf_op jit(solution)/shard_map/all_gather | solution.py:23
  205.1 25.8 slice_reduce_fusion.12
  258.8 26.8 slice_reduce_fusion.8
  287.7 22.4 all-gather.37.cloned.1.call-done
  317.7 119.6 %all-gather.35.cloned.1.call-done = bf16[2,1024,1600]{1,0,2:T(2,128)(2,1)} async-done(((bf16[2,256,1600]{1,0,2:T(2,128)(2,1)}), bf16[2,1024,1600]{1,0,2:T(2,128)(2,1)}) %all-gather.35.cloned.1.call-update) | async-done | bytes 6553616 | tf_op jit(solution)/shard_map/all_gather | solution.py:164
  446.2 82.6 %while.56 = (s32[]{:T(128)}, bf16[2,256,1600]{1,2,0:T(8,128)(2,1)}, f32[2,25,256,1]{2,1,3,0:T(8,128)S(1)}, bf16[2,1024,25,64]{1,3,2,0:T(8,128)(2,1)}, bf16[2,256...) while((s32[]{:T(128)}, bf16[2,256,1600]{1,2,0:T(8,128)(2,1)}, ...), condition=%wide.region_5.6_spmd.clone, body=%wide.region_2.5_spmd.clone.sunk | while | flops 1757030144 | bytes 89754736 | solution.py:169
  562.2 64.1 %all-gather.39.cloned.1.call-done = bf16[2048,1600]{0,1:T(8,128)(2,1)} async-done(((bf16[512,1600]{0,1:T(8,128)(2,1)}), bf16[2048,1600]{0,1:T(8,128)(2,1)}) %all-gather.39.cloned.1.call-update) | async-done | bytes 6553616 | tf_op jit(solution)/shard_map/all_gather | solution.py:175
  626.3 18.5 fusion.134
  644.9 40.8 %all-gather.57.cloned.1.call-done = bf16[1,1600,1600]{1,2,0:T(8,128)(2,1)} async-done(((bf16[1,1600,200]{1,2,0:T(8,128)(2,1)}), bf16[1,1600,1600]{1,2,0:T(8,128)(2,1)}) %all-gather.57.cloned.1.call-update) | async-done | bytes 5120016 | tf_op jit(solution)/shard_map/all_gather | solution.py:26
  685.7 19.7 convolution_convert_fusion.7
  707.2 16.6 all-gather.9
  742.0 26.8 slice_reduce_fusion.2
  768.8 27.0 slice_reduce_fusion.1
  799.8 120.4 %all-gather.59.cloned.1.call-done = bf16[1,1600,4800]{2,1,0:T(8,128)(2,1)} async-done(((bf16[1,200,4800]{2,1,0:T(8,128)(2,1)}), bf16[1,1600,4800]{2,1,0:T(8,128)(2,1)}) %all-gather.59.cloned.1.call-update) | async-done | bytes 15360016 | tf_op jit(solution)/shard_map/all_gather | solution.py:23
  958.3 25.8 slice_reduce_fusion.4
  1007.8 26.8 slice_reduce_fusion
  1036.5 26.6 all-gather.43.cloned.1.call-done
  1070.7 119.6 %all-gather.41.cloned.1.call-done = bf16[2,1024,1600]{1,0,2:T(2,128)(2,1)} async-done(((bf16[2,256,1600]{1,0,2:T(2,128)(2,1)}), bf16[2,1024,1600]{1,0,2:T(2,128)(2,1)}) %all-gather.41.cloned.1.call-update) | async-done | bytes 6553616 | tf_op jit(solution)/shard_map/all_gather | solution.py:164
  1197.9 85.9 %while.57 = (s32[]{:T(128)}, bf16[2,256,1600]{1,2,0:T(8,128)(2,1)S(1)}, f32[2,25,256,1]{2,1,3,0:T(8,128)S(1)}, bf16[2,1024,25,64]{1,3,2,0:T(8,128)(2,1)}, bf16[2...) while((s32[]{:T(128)}, ...), condition=%wide.region_14.15_spmd.clone, body=%wide.region_11.14_spmd.clone.sunk | while | flops 1757030144 | bytes 89754736 | solution.py:169
  1306.6 72.3 %all-gather.45.cloned.1.call-done = bf16[2048,1600]{0,1:T(8,128)(2,1)} async-done(((bf16[512,1600]{0,1:T(8,128)(2,1)}), bf16[2048,1600]{0,1:T(8,128)(2,1)}) %all-gather.45.cloned.1.call-update) | async-done | bytes 6553616 | tf_op jit(solution)/shard_map/all_gather | solution.py:175
  1378.9 18.7 fusion.122
  1397.6 40.0 %all-gather.65.cloned.1.call-done = bf16[1,1600,1600]{1,2,0:T(8,128)(2,1)} async-done(((bf16[1,1600,200]{1,2,0:T(8,128)(2,1)}), bf16[1,1600,1600]{1,2,0:T(8,128)(2,1)}) %all-gather.65.cloned.1.call-update) | async-done | bytes 5120016 | tf_op jit(solution)/shard_map/all_gather | solution.py:26
  1437.6 72.3 %all-gather.47.cloned.1.call-done = bf16[2048,1600]{0,1:T(8,128)(2,1)} async-done(((bf16[512,1600]{0,1:T(8,128)(2,1)}), bf16[2048,1600]{0,1:T(8,128)(2,1)}) %all-gather.47.cloned.1.call-update) | async-done | bytes 6553616 | tf_op jit(solution)/shard_map/all_gather | solution.py:238
  1509.8 28.9 fusion.208
  1538.7 17.8 convolution_convert_fusion.5
  1556.6 19.4 convolution_convert_fusion.6
  1576.5 52.6 %reduce-scatter.53.cloned.1.call-done = bf16[512,1600]{0,1:T(8,128)(2,1)} async-done(((bf16[2048,1600]{0,1:T(8,128)(2,1)}), bf16[512,1600]{0,1:T(8,128)(2,1)}) %reduce-scatter.53.cloned.1.call-update) | async-done | bytes 1638416 | tf_op jit(solution)/shard_map/reduce_scatter | solution.py:254
  1631.2 73.2 %reduce-scatter.51.cloned.1.call-done = bf16[512,1600]{0,1:T(8,128)(2,1)} async-done(((bf16[2048,1600]{0,1:T(8,128)(2,1)}), bf16[512,1600]{0,1:T(8,128)(2,1)}) %reduce-scatter.51.cloned.1.call-update) | async-done | bytes 1638416 | tf_op jit(solution)/shard_map/reduce_scatter | solution.py:184
  1729.2 175.6 %while.58 = (s32[]{:T(128)}, bf16[2,256,1600]{1,2,0:T(8,128)(2,1)}, bf16[2,1024,1600]{1,2,0:T(8,128)(2,1)}, bf16[2,1024,1600]{1,2,0:T(8,128)(2,1)}, bf16[2,1024,...) while((s32[]{:T(128)}, bf16[2,256,1600]{1,2,0:T(8,128)(2,1)}, ...), condition=%wide.region_23.24_spmd.clone, body=%wide.region_21.23_spmd.clone.sunk | while | flops 4257638144 | bytes 284929280 | solution.py:275
  1742.4 20.8 multiply_reduce_fusion.11
  1763.2 21.8 multiply_convert_fusion.10
  1830.0 20.8 multiply_reduce_fusion.11
  1850.8 21.8 multiply_convert_fusion.10
  1908.6 68.7 %reduce-scatter.57.cloned.1.call-done = bf16[2,256,1600]{1,2,0:T(8,128)(2,1)} async-done(((bf16[2,1024,1600]{1,2,0:T(8,128)(2,1)}), bf16[2,256,1600]{1,2,0:T(8,128)(2,1)}) %reduce-scatter.57.cloned.1.call-update) | async-done | bytes 1638416 | tf_op jit(solution)/shard_map/reduce_scatter | solution.py:282
  1980.9 71.7 %reduce-scatter.55.cloned.1.call-done = bf16[2,256,1600]{1,2,0:T(8,128)(2,1)} async-done(((bf16[2,1024,1600]{1,2,0:T(8,128)(2,1)}), bf16[2,256,1600]{1,2,0:T(8,128)(2,1)}) %reduce-scatter.55.cloned.1.call-update) | async-done | bytes 1638416 | tf_op jit(solution)/shard_map/reduce_scatter | solution.py:279
  2089.4 72.3 %all-gather.49.cloned.1.call-done = bf16[2048,1600]{0,1:T(8,128)(2,1)} async-done(((bf16[512,1600]{0,1:T(8,128)(2,1)}), bf16[2048,1600]{0,1:T(8,128)(2,1)}) %all-gather.49.cloned.1.call-update) | async-done | bytes 6553616 | tf_op jit(solution)/shard_map/all_gather | solution.py:238
  2161.6 29.2 fusion.209
  2190.8 17.7 convolution_convert_fusion.4
  2217.9 63.2 %reduce-scatter.59.cloned.1.call-done = bf16[512,1600]{0,1:T(8,128)(2,1)} async-done(((bf16[2048,1600]{0,1:T(8,128)(2,1)}), bf16[512,1600]{0,1:T(8,128)(2,1)}) %reduce-scatter.59.cloned.1.call-update) | async-done | bytes 1638416 | tf_op jit(solution)/shard_map/reduce_scatter | solution.py:254
  2328.8 188.9 %while.59 = (s32[]{:T(128)}, bf16[2,256,1600]{1,2,0:T(8,128)(2,1)}, bf16[2,1024,1600]{1,2,0:T(8,128)(2,1)}, bf16[2,1024,1600]{1,2,0:T(8,128)(2,1)}, bf16[2,1024,...) while((s32[]{:T(128)}, bf16[2,256,1600]{1,2,0:T(8,128)(2,1)}, ...), condition=%wide.region_33.34_spmd.clone, body=%wide.region_31.33_spmd.clone.sunk | while | flops 4257638144 | bytes 275098848 | solution.py:275
  2344.3 22.8 multiply_reduce_fusion.12
  2367.1 22.4 multiply_convert_fusion.11
  2439.0 22.8 multiply_reduce_fusion.12
  2461.9 22.4 multiply_convert_fusion.11
  2518.4 17.5 convolution_convert_fusion.10
  2536.6 21.7 convolution_convert_fusion.8
  2560.7 21.9 convolution_convert_fusion.9
  2582.7 17.3 convolution_convert_fusion.11
  2609.6 30.3 reduce-scatter.63.cloned.1.call-done
  2643.4 72.1 %reduce-scatter.61.cloned.1.call-done = bf16[2,256,1600]{1,2,0:T(8,128)(2,1)} async-done(((bf16[2,1024,1600]{1,2,0:T(8,128)(2,1)}), bf16[2,256,1600]{1,2,0:T(8,128)(2,1)}) %reduce-scatter.61.cloned.1.call-update) | async-done | bytes 1638416 | tf_op jit(solution)/shard_map/reduce_scatter | solution.py:279
  2745.0 31.9 reduce-scatter.83.cloned.1.call-done
  2779.2 60.3 %reduce-scatter.87.cloned.1.call-done = bf16[1600,200]{0,1:T(8,128)(2,1)} async-done(((bf16[1600,1600]{0,1:T(8,128)(2,1)}), bf16[1600,200]{0,1:T(8,128)(2,1)}) %reduce-scatter.87.cloned.1.call-update) | async-done | bytes 640016
  2847.4 23.1 reduce-scatter.75.cloned.1.call-done
  2874.3 57.7 %reduce-scatter.85.cloned.1.call-done = bf16[1600,200]{0,1:T(8,128)(2,1)} async-done(((bf16[1600,1600]{0,1:T(8,128)(2,1)}), bf16[1600,200]{0,1:T(8,128)(2,1)}) %reduce-scatter.85.cloned.1.call-update) | async-done | bytes 640016
  2936.2 58.4 %reduce-scatter.81.cloned.1.call-done = bf16[200,1600]{1,0:T(8,128)(2,1)} async-done(((bf16[1600,1600]{1,0:T(8,128)(2,1)}), bf16[200,1600]{1,0:T(8,128)(2,1)}) %reduce-scatter.81.cloned.1.call-update) | async-done | bytes 640016
  3000.7 24.4 reduce-scatter.73.cloned.1.call-done
  3028.1 38.6 %reduce-scatter.71.cloned.1.call-done = bf16[1200,200]{1,0:T(8,128)(2,1)} async-done(((bf16[4800,200]{1,0:T(8,128)(2,1)}), bf16[1200,200]{1,0:T(8,128)(2,1)}) %reduce-scatter.71.cloned.1.call-update) | async-done | bytes 480016
  3070.9 17.0 fusion.188
  3089.6 135.0 %reduce-scatter.65.cloned.1.call-done = bf16[200,4800]{1,0:T(8,128)(2,1)} async-done(((bf16[1600,4800]{1,0:T(8,128)(2,1)}), bf16[200,4800]{1,0:T(8,128)(2,1)}) %reduce-scatter.65.cloned.1.call-update) | async-done | bytes 1920016 | tf_op jit(solution)/shard_map/reduce_scatter | solution.py:307
  3241.6 25.3 all-reduce.19
  (601 shorter events, 852.8 us)
Async XLA Ops:
  7.2 156.3 %all-gather.51.cloned.1.call-start = ((), (), s32[]{:S(2)}) async-start(), calls=%async_computation.38 | async-start | bytes 17510400 | tf_op jit(solution)/shard_map/all_gather | solution.py:23
  11.7 298.4 %all-gather.37.cloned.1.call-start = ((), (), s32[]{:S(2)}) async-start(), calls=%async_computation.21 | async-start | bytes 8192000 | tf_op jit(solution)/shard_map/all_gather | solution.py:163
  12.0 151.5 %copy-start.69 = (f32[1,2,2,128]{3,1,2,0:T(2,128)}, f32[1,2,2,128]{3,1,2,0:T(2,128)S(1)}, u32[]{:S(2)}) copy-start(f32[1,2,2,128]{3,1,2,0:T(2,128)S(1)} %copy.155) | copy-start | bytes 6148
  12.5 151.0 %copy-start.72 = (f32[512]{0:T(512)}, f32[512]{0:T(512)S(1)}, u32[]{:S(2)}) copy-start(f32[512]{0:T(512)S(1)} %rsqrt.44) | copy-start | bytes 6148
  61.4 117.6 %copy-start.15 = (f32[2,200,8,256]{3,2,0,1:T(8,128)}, f32[2,200,8,256]{3,2,0,1:T(8,128)S(1)}, u32[]{:S(2)}) copy-start(f32[2,200,8,256]{3,2,0,1:T(8,128)S(1)} %copy.153) | copy-start | bytes 9830404
  88.2 90.8 %copy-start.50 = (f32[1600]{0:T(1024)}, f32[1600]{0:T(1024)S(1)}, u32[]{:S(2)}) copy-start(f32[1600]{0:T(1024)S(1)} %get-tuple-element.516) | copy-start | bytes 19204
  186.9 250.3 %all-gather.35.cloned.1.call-start = ((), (), s32[]{:S(2)}) async-start(), calls=%async_computation.20 | async-start | bytes 8192000 | tf_op jit(solution)/shard_map/all_gather | solution.py:164
  235.7 297.4 %all-gather.53.cloned.1.call-start = ((), (), s32[]{:S(2)}) async-start(), calls=%async_computation.39 | async-start | bytes 5990400 | tf_op jit(solution)/shard_map/all_gather | solution.py:24
  238.3 323.9 %all-gather.55.cloned.1.call-start = ((), (), s32[]{:S(2)}) async-start(), calls=%async_computation.40 | async-start | bytes 5990400 | tf_op jit(solution)/shard_map/all_gather | solution.py:25
  239.6 386.7 %all-gather.39.cloned.1.call-start = ((), (), s32[]{:S(2)}) async-start(), calls=%async_computation.22 | async-start | bytes 8192000 | tf_op jit(solution)/shard_map/all_gather | solution.py:175
  540.5 255.2 %copy-start.2 = (f32[512,1600]{0,1:T(8,128)}, f32[512,1600]{0,1:T(8,128)S(1)}, u32[]{:S(2)}) copy-start(f32[512,1600]{0,1:T(8,128)S(1)} %get-tuple-element.670) | copy-start | bytes 9830404
  543.2 142.5 %all-gather.57.cloned.1.call-start = ((), (), s32[]{:S(2)}) async-start(), calls=%async_computation.41 | async-start | bytes 5990400 | tf_op jit(solution)/shard_map/all_gather | solution.py:26
  545.7 250.0 %reduce-scatter.49.cloned.1.call-start = ((), (), s32[]{:S(2)}) async-start(), calls=%async_computation.23 | async-start | bytes 8192000 | tf_op jit(solution)/shard_map/reduce_scatter | solution.py:184
  562.2 123.5 %copy-start.101 = (f32[1600]{0:T(1024)}, f32[1600]{0:T(1024)S(1)}, u32[]{:S(2)}) copy-start(f32[1600]{0:T(1024)S(1)} %convert_element_type.446) | copy-start | bytes 19204
  705.4 214.8 %all-gather.59.cloned.1.call-start = ((), (), s32[]{:S(2)}) async-start(), calls=%async_computation.42 | async-start | bytes 17510400 | tf_op jit(solution)/shard_map/all_gather | solution.py:23
  706.2 356.9 %all-gather.43.cloned.1.call-start = ((), (), s32[]{:S(2)}) async-start(), calls=%async_computation.25 | async-start | bytes 8192000 | tf_op jit(solution)/shard_map/all_gather | solution.py:163
  724.7 71.1 %copy-start.63 = (f32[1600]{0:T(1024)S(1)}, f32[1600]{0:T(1024)}, u32[]{:S(2)}) copy-start(f32[1600]{0:T(1024)} %get-tuple-element.513) | copy-start | bytes 19204
  768.8 151.4 %copy-start.52 = (f32[1600]{0:T(1024)}, f32[1600]{0:T(1024)S(1)}, u32[]{:S(2)}) copy-start(f32[1600]{0:T(1024)S(1)} %get-tuple-element.508) | copy-start | bytes 19204
  795.7 124.5 %copy-start.97 = (f32[1600]{0:T(1024)}, f32[1600]{0:T(1024)S(1)}, u32[]{:S(2)}) copy-start(f32[1600]{0:T(1024)S(1)} %get-tuple-element.510) | copy-start | bytes 19204
  797.7 139.1 %copy-start.61 = (f32[512]{0:T(512)}, f32[512]{0:T(512)S(1)}, u32[]{:S(2)}) copy-start(f32[512]{0:T(512)S(1)} %broadcast_multiply_fusion.3) | copy-start | bytes 6148
  799.8 137.0 %copy-start.81 = (f32[512]{0:T(512)}, f32[512]{0:T(512)S(1)}, u32[]{:S(2)}) copy-start(f32[512]{0:T(512)S(1)} %multiply_reduce_fusion.7) | copy-start | bytes 6148
  799.8 137.0 %copy-start.75 = (f32[512]{0:T(512)}, f32[512]{0:T(512)S(1)}, u32[]{:S(2)}) copy-start(f32[512]{0:T(512)S(1)} %fusion.171) | copy-start | bytes 6148
  940.3 249.9 %all-gather.41.cloned.1.call-start = ((), (), s32[]{:S(2)}) async-start(), calls=%async_computation.24 | async-start | bytes 8192000 | tf_op jit(solution)/shard_map/all_gather | solution.py:164
  988.9 297.6 %all-gather.61.cloned.1.call-start = ((), (), s32[]{:S(2)}) async-start(), calls=%async_computation.43 | async-start | bytes 5990400 | tf_op jit(solution)/shard_map/all_gather | solution.py:24
  989.5 317.1 %all-gather.63.cloned.1.call-start = ((), (), s32[]{:S(2)}) async-start(), calls=%async_computation.44 | async-start | bytes 5990400 | tf_op jit(solution)/shard_map/all_gather | solution.py:25
  990.3 388.7 %all-gather.45.cloned.1.call-start = ((), (), s32[]{:S(2)}) async-start(), calls=%async_computation.26 | async-start | bytes 8192000 | tf_op jit(solution)/shard_map/all_gather | solution.py:175
  1294.0 416.8 %copy-start.7 = (f32[512,1600]{0,1:T(8,128)}, f32[512,1600]{0,1:T(8,128)S(1)}, u32[]{:S(2)}) copy-start(f32[512,1600]{0,1:T(8,128)S(1)} %get-tuple-element.672) | copy-start | bytes 9830404
  1294.0 416.8 %copy-start.48 = (f32[512]{0:T(512)}, f32[512]{0:T(512)S(1)}, u32[]{:S(2)}) copy-start(f32[512]{0:T(512)S(1)} %broadcast_multiply_fusion.2) | copy-start | bytes 6148
  1294.4 416.4 %copy-start.57 = (f32[512]{0:T(512)}, f32[512]{0:T(512)S(1)}, u32[]{:S(2)}) copy-start(f32[512]{0:T(512)S(1)} %fusion.172) | copy-start | bytes 6148
  1296.7 140.9 %all-gather.65.cloned.1.call-start = ((), (), s32[]{:S(2)}) async-start(), calls=%async_computation.45 | async-start | bytes 5990400 | tf_op jit(solution)/shard_map/all_gather | solution.py:26
  1297.3 212.6 %all-gather.47.cloned.1.call-start = ((), (), s32[]{:S(2)}) async-start(), calls=%async_computation.28 | async-start | bytes 8192000 | tf_op jit(solution)/shard_map/all_gather | solution.py:238
  1300.1 329.0 %reduce-scatter.53.cloned.1.call-start = ((), (), s32[]{:S(2)}) async-start(), calls=%async_computation.29 | async-start | bytes 8192000 | tf_op jit(solution)/shard_map/reduce_scatter | solution.py:254
  1300.2 256.4 %copy-start.104 = (f32[1600]{0:T(1024)}, f32[1600]{0:T(1024)S(1)}, u32[]{:S(2)}) copy-start(f32[1600]{0:T(1024)S(1)} %convert_element_type.447) | copy-start | bytes 19204
  1556.5 147.9 %reduce-scatter.51.cloned.1.call-start = ((), (), s32[]{:S(2)}) async-start(), calls=%async_computation.27 | async-start | bytes 8192000 | tf_op jit(solution)/shard_map/reduce_scatter | solution.py:184
  1576.0 128.4 %copy-start.64 = (f32[1600]{0:T(1024)S(1)}, f32[1600]{0:T(1024)}, u32[]{:S(2)}) copy-start(f32[1600]{0:T(1024)} %get-tuple-element.505) | copy-start | bytes 19204
  1576.0 401.3 %reduce-scatter.57.cloned.1.call-start = ((), (), s32[]{:S(2)}) async-start(), calls=%async_computation.31 | async-start | bytes 8192000 | tf_op jit(solution)/shard_map/reduce_scatter | solution.py:282
  1631.1 79.7 %copy-start.67 = (f32[512]{0:T(512)}, f32[512]{0:T(512)S(1)}, u32[]{:S(2)}) copy-start(f32[512]{0:T(512)S(1)} %multiply_multiply_fusion.7) | copy-start | bytes 6148
  1904.8 147.8 %reduce-scatter.55.cloned.1.call-start = ((), (), s32[]{:S(2)}) async-start(), calls=%async_computation.30 | async-start | bytes 8192000 | tf_op jit(solution)/shard_map/reduce_scatter | solution.py:279
  1905.4 256.3 %all-gather.49.cloned.1.call-start = ((), (), s32[]{:S(2)}) async-start(), calls=%async_computation.32 | async-start | bytes 8192000 | tf_op jit(solution)/shard_map/all_gather | solution.py:238
  2084.5 77.2 %copy-start.102 = (f32[1600]{0:T(1024)S(1)}, f32[1600]{0:T(1024)}, u32[]{:S(2)}) copy-start(f32[1600]{0:T(1024)} %copy-done.101) | copy-start | bytes 19204
  2089.3 191.8 %reduce-scatter.59.cloned.1.call-start = ((), (), s32[]{:S(2)}) async-start(), calls=%async_computation.33 | async-start | bytes 8192000 | tf_op jit(solution)/shard_map/reduce_scatter | solution.py:254
  2208.6 349.8 %reduce-scatter.79.cloned.1.call-start = ((), (), s32[]{:S(2)}) async-start(), calls=%async_computation.51 | async-start | bytes 5990400
  2217.6 65.7 %copy-start.55 = (f32[512]{0:T(512)S(1)}, f32[512]{0:T(512)}, u32[]{:S(2)}) copy-start(f32[512]{0:T(512)} %copy-done.54) | copy-start | bytes 6148
  2217.6 382.5 %reduce-scatter.77.cloned.1.call-start = ((), (), s32[]{:S(2)}) async-start(), calls=%async_computation.50 | async-start | bytes 5990400
  2295.2 307.3 %reduce-scatter.67.cloned.1.call-start = ((), (), s32[]{:S(2)}) async-start(), calls=%async_computation.37 | async-start | bytes 17510400 | tf_op jit(solution)/shard_map/reduce_scatter | solution.py:307
  2311.1 328.7 %reduce-scatter.63.cloned.1.call-start = ((), (), s32[]{:S(2)}) async-start(), calls=%async_computation.35 | async-start | bytes 8192000 | tf_op jit(solution)/shard_map/reduce_scatter | solution.py:282
  2517.7 197.7 %reduce-scatter.61.cloned.1.call-start = ((), (), s32[]{:S(2)}) async-start(), calls=%async_computation.34 | async-start | bytes 8192000 | tf_op jit(solution)/shard_map/reduce_scatter | solution.py:279
  2518.3 258.6 %reduce-scatter.83.cloned.1.call-start = ((), (), s32[]{:S(2)}) async-start(), calls=%async_computation.53 | async-start | bytes 5990400
  2535.9 303.5 %reduce-scatter.87.cloned.1.call-start = ((), (), s32[]{:S(2)}) async-start(), calls=%async_computation.55 | async-start | bytes 5990400
  2558.3 312.2 %reduce-scatter.75.cloned.1.call-start = ((), (), s32[]{:S(2)}) async-start(), calls=%async_computation.49 | async-start | bytes 1024000
  2560.7 371.4 %reduce-scatter.85.cloned.1.call-start = ((), (), s32[]{:S(2)}) async-start(), calls=%async_computation.54 | async-start | bytes 5990400
  2582.6 412.0 %reduce-scatter.81.cloned.1.call-start = ((), (), s32[]{:S(2)}) async-start(), calls=%async_computation.52 | async-start | bytes 5990400
  2600.0 425.0 %reduce-scatter.73.cloned.1.call-start = ((), (), s32[]{:S(2)}) async-start(), calls=%async_computation.48 | async-start | bytes 1024000
  2602.4 464.3 %reduce-scatter.71.cloned.1.call-start = ((), (), s32[]{:S(2)}) async-start(), calls=%async_computation.47 | async-start | bytes 3072000
  2606.7 617.9 %reduce-scatter.65.cloned.1.call-start = ((), (), s32[]{:S(2)}) async-start(), calls=%async_computation.36 | async-start | bytes 17510400 | tf_op jit(solution)/shard_map/reduce_scatter | solution.py:307
  2742.6 99.1 %copy-start.88 = (bf16[1600]{0:T(1024)(128)(2,1)S(1)}, bf16[1600]{0:T(1024)(128)(2,1)}, u32[]{:S(2)}) copy-start(bf16[1600]{0:T(1024)(128)(2,1)} %get-tuple-element.499) | copy-start | bytes 9604
  2742.6 99.1 %copy-start.87 = (bf16[1600]{0:T(1024)(128)(2,1)S(1)}, bf16[1600]{0:T(1024)(128)(2,1)}, u32[]{:S(2)}) copy-start(bf16[1600]{0:T(1024)(128)(2,1)} %get-tuple-element.624) | copy-start | bytes 9604
  2742.6 539.8 %reduce-scatter.69.cloned.1.call-start = ((), (), s32[]{:S(2)}) async-start(), calls=%async_computation.46 | async-start | bytes 3072000
  3089.6 139.2 %copy-start.4 = (f32[512,1600]{0,1:T(8,128)S(1)}, f32[512,1600]{0,1:T(8,128)}, u32[]{:S(2)}) copy-start(f32[512,1600]{0,1:T(8,128)} %copy-done.2) | copy-start | bytes 9830404
  3089.6 139.2 %copy-start.42 = (f32[1600]{0:T(1024)S(1)}, f32[1600]{0:T(1024)}, u32[]{:S(2)}) copy-start(f32[1600]{0:T(1024)} %get-tuple-element.515) | copy-start | bytes 19204
  3089.6 139.2 %copy-start.47 = (f32[512]{0:T(512)S(1)}, f32[512]{0:T(512)}, u32[]{:S(2)}) copy-start(f32[512]{0:T(512)} %copy-done.45) | copy-start | bytes 6148
  3089.6 139.2 %copy-start.56 = (f32[512]{0:T(512)S(1)}, f32[512]{0:T(512)}, u32[]{:S(2)}) copy-start(f32[512]{0:T(512)} %copy-done.54) | copy-start | bytes 6148
  3089.6 139.2 %copy-start.66 = (f32[512]{0:T(512)S(1)}, f32[512]{0:T(512)}, u32[]{:S(2)}) copy-start(f32[512]{0:T(512)} %copy-done.65) | copy-start | bytes 6148
  3089.6 139.2 %copy-start.86 = (f32[512]{0:T(512)S(1)}, f32[512]{0:T(512)}, u32[]{:S(2)}) copy-start(f32[512]{0:T(512)} %copy-done.85) | copy-start | bytes 6148
  (102 other events, 1169.1 us)
Sparse Core Ops, SparseCore 0:
  11.8 151.6 all-gather.50
  187.1 122.9 all-gather.36
  312.4 124.7 all-gather.34
  439.3 57.1 all-gather.52
  498.0 55.4 all-gather.54
  555.8 70.5 all-gather.38
  628.6 57.1 all-gather.56
  705.6 70.7 reduce-scatter.48
  778.6 141.5 all-gather.58
  940.5 122.5 all-gather.42
  1065.4 124.7 all-gather.40
  1192.3 57.1 all-gather.60
  1251.1 55.4 all-gather.62
  1308.3 70.5 all-gather.44
  1380.4 57.1 all-gather.64
  1439.3 70.5 all-gather.46
  1556.6 72.3 reduce-scatter.52
  1632.0 72.3 reduce-scatter.50
  1904.9 72.3 reduce-scatter.56
  1980.2 72.3 reduce-scatter.54
  2089.4 72.1 all-gather.48
  2208.7 72.3 reduce-scatter.58
  2283.4 58.9 reduce-scatter.78
  2344.6 60.1 reduce-scatter.76
  2407.2 156.4 reduce-scatter.66
  2566.9 72.8 reduce-scatter.62
  2643.0 72.3 reduce-scatter.60
  2717.8 59.0 reduce-scatter.82
  2779.3 60.0 reduce-scatter.86
  2843.0 27.4 reduce-scatter.74
  2872.9 59.0 reduce-scatter.84
  2934.5 60.1 reduce-scatter.80
  2997.6 27.3 reduce-scatter.72
  3028.4 38.2 reduce-scatter.70
  3069.2 155.4 reduce-scatter.64
  3228.9 38.6 reduce-scatter.68
where the time goes:
time: 3310 us; the launch traced here: 3290 us
  waiting for transfers between devices  1690 us (51%)
  matrix products  751 us (23%)
  local copies, waits for them, and re-layouts  401 us (12%)
  other arithmetic  233 us (7%)
  blocking collectives  195 us (6%)
    unnamed x46, waiting for transfers between devices  298 us
    all_gather x2, waiting for transfers between devices, body(): lax.all_gather(value.reshape(seqs, local, width), 'mp', axis=1, tiled=True)  239 us
    all_gather x2, waiting for transfers between devices, fetch_params(): lax.all_gather(pieces[0], 'dp', axis=0, tiled=True)  168 us
    dot_general x8, matrix products, scores_of(): jnp.einsum('qhd,khd->hqk', query_heads, key_heads, preferred_element_type...  145 us
    all_gather x2, waiting for transfers between devices, body(): group_grad = lax.all_gather(out_grad, 'mp', axis=0, tiled=True)  145 us
    reduce_scatter x2, waiting for transfers between devices, body(): lax.psum_scatter(key_grad.astype(jnp.bfloat16), 'mp', scatter_dimension=1...  144 us
    all_gather x2, waiting for transfers between devices, body(): group_rows = lax.all_gather(normed_two, 'mp', axis=0, tiled=True)  136 us
    reduce_scatter x2, waiting for transfers between devices, body(): lax.psum_scatter(qkv_grad.astype(jnp.bfloat16), 'dp', scatter_dimension=0...  135 us
  transfers between devices with their start and end apart: 36, of which 28 were waited for; matrix products, arithmetic and copies ran while one was open for 29% of the time, Pallas kernels for 0%

commit v1 on v0

--- a/solution.py
+++ b/solution.py
@@ -1,6 +1,10 @@
+import functools
+
 import jax
 import jax.numpy as jnp
 from jax import lax
+from jax.experimental import pallas as pl
+from jax.experimental.pallas import tpu as pltpu
 from jax.sharding import PartitionSpec as P
 
 HD = 64
@@ -55,7 +59,7 @@
     return jnp.where(visible, scores, -1e30)
 
 
-def body(
+def general_body(
     tokens,
     cotangent,
     block_order,
@@ -373,7 +377,493 @@
     )
 
 
+def grid_index(mesh):
+    shape = dict(mesh.shape)
+    return shape["dp"] // 2, shape["mp"]
+
+
+def spots(planes):
+    return [(z, c, y, x) for z in range(planes) for c in range(2) for y in range(2) for x in range(2)]
+
+
+def flat(z, c, y, x):
+    return (z * 2 + c) * 4 + y * 2 + x
+
+
+def pairs_of(planes, move):
+    both = [(flat(*spot), flat(*move(*spot))) for spot in spots(planes)]
+    return [pair for pair in both if pair[0] != pair[1]]
+
+
+AXES = ("dp", "mp")
+LANES = 128
+
+
+def nt(a, b):
+    return lax.dot_general(a, b, (((1,), (1,)), ((), ())), preferred_element_type=jnp.float32)
+
+
+def tn(a, b):
+    return lax.dot_general(a, b, (((0,), (0,)), ((), ())), preferred_element_type=jnp.float32)
+
+
+def nn(a, b):
+    return jnp.dot(a, b, preferred_element_type=jnp.float32)
+
+
+def sort_keys(slot_ref, blocks, ok, own_ref, other_ref, cat, put):
+    half = blocks * LANES // 2
+    cat[:half] = jnp.where(ok, own_ref[...], 0)
+    cat[half:] = jnp.where(ok, other_ref[...], 0)
+    for j in range(blocks):
+        start = pl.multiple_of(slot_ref[j] * LANES, LANES)
+        put(j, cat[pl.ds(start, LANES), :])
+
+
+def two_heads(rows, first):
+    zero = jnp.zeros_like(rows)
+    return jnp.concatenate([jnp.where(first, rows, zero), jnp.where(first, zero, rows)], axis=0)
+
+
+def attend_kernel(width, blocks, qblocks, place_ref, slot_ref, q_ref, ko_ref, ks_ref, vo_ref, vs_ref,
+                  o_ref, lse_ref, cat, ksort, vturn):
+    lane = lax.broadcasted_iota(jnp.int32, (1, LANES), 1)
+    ok = lane + pl.program_id(0) * LANES < width
+    first = lane < HD
+
+    def put_k(j, rows):
+        ksort[j * LANES:(j + 1) * LANES, :] = rows
+
+    def put_v(j, rows):
+        vturn[:, j * LANES:(j + 1) * LANES] = rows.astype(jnp.float32).T.astype(jnp.bfloat16)
+
+    sort_keys(slot_ref, blocks, ok, ko_ref, ks_ref, cat, put_k)
+    sort_keys(slot_ref, blocks, ok, vo_ref, vs_ref, cat, put_v)
+
+    def one(b, carry):
+        place = place_ref[b]
+        here = pl.ds(pl.multiple_of(b * LANES, LANES), LANES)
+        rows = (jnp.where(ok, q_ref[here, :], 0) * (HD ** -0.5)).astype(jnp.bfloat16)
+        q2 = two_heads(rows, first)
+        for n in range(1, blocks // 2 + 1):
+            @pl.when(place // 2 == n - 1)
+            def _(n=n):
+                keys = 2 * LANES * n
+                s = nt(ksort[:keys, :], q2)
+                row = lax.broadcasted_iota(jnp.int32, (2 * LANES, 2 * LANES), 0) + (keys - 2 * LANES)
+                col = lax.broadcasted_iota(jnp.int32, (2 * LANES, 2 * LANES), 1) % LANES + place * LANES
+                tail = jnp.where(row <= col, s[keys - 2 * LANES:], -1e30)
+                s = tail if n == 1 else jnp.concatenate([s[:keys - 2 * LANES], tail], axis=0)
+                top = jnp.max(s, axis=0, keepdims=True)
+                e = jnp.exp(s - top)
+                total = jnp.sum(e, axis=0, keepdims=True)
+                turned = nn(vturn[:, :keys], e.astype(jnp.bfloat16)) / total
+                joined = jnp.concatenate([turned[:HD, :LANES], turned[HD:, LANES:]], axis=0)
+                o_ref[here, :] = joined.T.astype(jnp.bfloat16)
+                lse = top + jnp.log(total)
+                lse_ref[0, 0:1, here] = lse[:, :LANES]
+                lse_ref[0, 1:2, here] = lse[:, LANES:]
+        return carry
+
+    lax.fori_loop(0, qblocks, one, 0)
+
+
+def attend_back_kernel(width, blocks, qblocks, place_ref, slot_ref, q_ref, ko_ref, ks_ref, vo_ref, vs_ref,
+                       do_ref, o_ref, lse_ref, dq_ref, dko_ref, dks_ref, dvo_ref, dvs_ref,
+                       cat, ksort, kturn, vsort, dk, dv, loose):
+    lane = lax.broadcasted_iota(jnp.int32, (1, LANES), 1)
+    ok = lane + pl.program_id(0) * LANES < width
+    first = lane < HD
+
+    def put_k(j, rows):
+        ksort[j * LANES:(j + 1) * LANES, :] = rows
+        kturn[:, j * LANES:(j + 1) * LANES] = rows.astype(jnp.float32).T.astype(jnp.bfloat16)
+
+    def put_v(j, rows):
+        vsort[j * LANES:(j + 1) * LANES, :] = rows
+
+    sort_keys(slot_ref, blocks, ok, ko_ref, ks_ref, cat, put_k)
+    sort_keys(slot_ref, blocks, ok, vo_ref, vs_ref, cat, put_v)
+    dk[...] = jnp.zeros_like(dk)
+    dv[...] = jnp.zeros_like(dv)
+
+    def one(b, carry):
+        place = place_ref[b]
+        here = pl.ds(pl.multiple_of(b * LANES, LANES), LANES)
+        rows = (jnp.where(ok, q_ref[here, :], 0) * (HD ** -0.5)).astype(jnp.bfloat16)
+        q2 = two_heads(rows, first)
+        do = jnp.where(ok, do_ref[here, :], 0)
+        do2 = two_heads(do, first)
+        both = (do.astype(jnp.float32) * jnp.where(ok, o_ref[here, :], 0).astype(jnp.float32)).T
+        delta = jnp.concatenate(
+            [jnp.sum(both[:HD], axis=0, keepdims=True), jnp.sum(both[HD:], axis=0, keepdims=True)], axis=1
+        )
+        lse = jnp.concatenate([lse_ref[0, 0:1, here], lse_ref[0, 1:2, here]], axis=1)
+        for n in range(1, blocks // 2 + 1):
+            @pl.when(place // 2 == n - 1)
+            def _(n=n):
+                keys = 2 * LANES * n
+                s = nt(ksort[:keys, :], q2)
+                row = lax.broadcasted_iota(jnp.int32, (2 * LANES, 2 * LANES), 0) + (keys - 2 * LANES)
+                col = lax.broadcasted_iota(jnp.int32, (2 * LANES, 2 * LANES), 1) % LANES + place * LANES
+                tail = jnp.where(row <= col, s[keys - 2 * LANES:], -1e30)
+                s = tail if n == 1 else jnp.concatenate([s[:keys - 2 * LANES], tail], axis=0)
+                p = jnp.exp(s - lse)
+                dp = nt(vsort[:keys, :], do2)
+                ds = (p * (dp - delta)).astype(jnp.bfloat16)
+                dv[:keys, :] += nn(p.astype(jnp.bfloat16), do2)
+                dk[:keys, :] += nn(ds, q2)
+                turned = nn(kturn[:, :keys], ds) * (HD ** -0.5)
+                joined = jnp.concatenate([turned[:HD, :LANES], turned[HD:, LANES:]], axis=0)
+                dq_ref[here, :] = joined.T.astype(jnp.bfloat16)
+        return carry
+
+    lax.fori_loop(0, qblocks, one, 0)
+    half = blocks * LANES // 2
+    for source, mine, theirs in ((dk, dko_ref, dks_ref), (dv, dvo_ref, dvs_ref)):
+        for j in range(blocks):
+            start = pl.multiple_of(slot_ref[j] * LANES, LANES)
+            loose[pl.ds(start, LANES), :] = source[j * LANES:(j + 1) * LANES, :]
+        mine[...] = loose[:half]
+        theirs[...] = loose[half:].astype(jnp.bfloat16)
+
+
+def attention_specs(rows):
+    tall = pl.BlockSpec((rows, LANES), lambda i, *_: (0, i))
+    stat = pl.BlockSpec((1, 2, rows), lambda i, *_: (i, 0, 0))
+    return tall, stat
+
+
+def attention(place, slot, q, ko, ks, vo, vs):
+    rows, width = q.shape
+    steps = -(-width // LANES)
+    blocks, keys = slot.shape[0], slot.shape[0] * LANES
+    tall, stat = attention_specs(rows)
+    elems = rows * keys * steps * 2
+    return pl.pallas_call(
+        functools.partial(attend_kernel, width, blocks, place.shape[0]),
+        grid_spec=pltpu.PrefetchScalarGridSpec(
+            num_scalar_prefetch=2,
+            grid=(steps,),
+            in_specs=[tall] * 5,
+            out_specs=[tall, stat],
+            scratch_shapes=[
+                pltpu.VMEM((keys, LANES), jnp.bfloat16),
+                pltpu.VMEM((keys, LANES), jnp.bfloat16),
+                pltpu.VMEM((LANES, keys), jnp.bfloat16),
+            ],
+        ),
+        out_shape=[
+            jax.ShapeDtypeStruct((rows, width), jnp.bfloat16),
+            jax.ShapeDtypeStruct((steps, 2, rows), jnp.float32),
+        ],
+        cost_estimate=pl.CostEstimate(flops=elems * HD * 8, bytes_accessed=rows * width * 12, transcendentals=elems),
+        compiler_params=pltpu.CompilerParams(vmem_limit_bytes=40 * 2 ** 20),
+        name="attention",
+    )(place, slot, q, ko, ks, vo, vs)
+
+
+def attention_back(place, slot, q, ko, ks, vo, vs, do, o, lse):
+    rows, width = q.shape
+    steps = -(-width // LANES)
+    blocks, keys = slot.shape[0], slot.shape[0] * LANES
+    tall, stat = attention_specs(rows)
+    elems = rows * keys * steps * 2
+    wide = jax.ShapeDtypeStruct((rows, width), jnp.float32)
+    thin = jax.ShapeDtypeStruct((rows, width), jnp.bfloat16)
+    return pl.pallas_call(
+        functools.partial(attend_back_kernel, width, blocks, place.shape[0]),
+        grid_spec=pltpu.PrefetchScalarGridSpec(
+            num_scalar_prefetch=2,
+            grid=(steps,),
+            in_specs=[tall] * 7 + [stat],
+            out_specs=[tall] * 5,
+            scratch_shapes=[
+                pltpu.VMEM((keys, LANES), jnp.bfloat16),
+                pltpu.VMEM((keys, LANES), jnp.bfloat16),
+                pltpu.VMEM((LANES, keys), jnp.bfloat16),
+                pltpu.VMEM((keys, LANES), jnp.bfloat16),
+                pltpu.VMEM((keys, LANES), jnp.float32),
+                pltpu.VMEM((keys, LANES), jnp.float32),
+                pltpu.VMEM((keys, LANES), jnp.float32),
+            ],
+        ),
+        out_shape=[thin, wide, thin, wide, thin],
+        cost_estimate=pl.CostEstimate(flops=elems * HD * 20, bytes_accessed=rows * width * 30, transcendentals=elems),
+        compiler_params=pltpu.CompilerParams(vmem_limit_bytes=40 * 2 ** 20),
+        name="attention_back",
+    )(place, slot, q, ko, ks, vo, vs, do, o, lse)
+
+
+def bf(value):
+    return value.astype(jnp.bfloat16)
+
+
+def f32(value):
+    return value.astype(jnp.float32)
+
+
+def norm_parts(value):
+    mean = jnp.mean(value, axis=-1, keepdims=True)
+    centred = value - mean
+    spread = jnp.mean(centred * centred, axis=-1, keepdims=True)
+    return centred, lax.rsqrt(spread + eps)
+
+
+def norm_back(grad, value, gain):
+    centred, rate = norm_parts(value)
+    hat = centred * rate
+    scaled = grad * gain
+    inner = scaled - jnp.mean(scaled, axis=-1, keepdims=True) - hat * jnp.mean(scaled * hat, axis=-1, keepdims=True)
+    return inner * rate, jnp.sum(grad * hat, axis=0), jnp.sum(grad, axis=0)
+
+
+def quick_body(
+    planes,
+    tokens,
+    cotangent,
+    block_order,
+    qkv_weight,
+    proj_weight,
+    fc_weight,
+    fc2_weight,
+    fc_bias,
+    norm_gain,
+    norm_shift,
+    attn_bias,
+    out_bias,
+):
+    seqs, local, width = tokens.shape
+    slots = local // LANES
+    dp_rank = lax.axis_index("dp")
+    mp_rank = lax.axis_index("mp")
+    core, row, col = dp_rank % 2, mp_rank // 2, mp_rank % 2
+    over_x = pairs_of(planes, lambda z, c, y, x: (z, c, y, 1 - x))
+    over_y = pairs_of(planes, lambda z, c, y, x: (z, c, 1 - y, x))
+    over_c = pairs_of(planes, lambda z, c, y, x: (z, 1 - c, y, x))
+    swap_yc = pairs_of(planes, lambda z, c, y, x: (z, y, c, x))
+    swap_xc = pairs_of(planes, lambda z, c, y, x: (z, x, y, c))
+
+    along_z = [
+        [flat(z, c, y, x) for z in range(planes)] for c in range(2) for y in range(2) for x in range(2)
+    ]
+
+    def go(value, pairs):
+        return lax.ppermute(value, AXES, pairs)
+
+    def turn_yc(value):
+        return jnp.where(row == core, value, go(value, swap_yc))
+
+    def turn_xc(value):
+        return jnp.where(col == core, value, go(value, swap_xc))
+
+    def sum_z(value):
+        return lax.psum_scatter(value, AXES, axis_index_groups=along_z, scatter_dimension=0, tiled=True)
+
+    def spread_in(value):
+        mine = lax.dynamic_index_in_dim(value, col, 0, keepdims=False)
+        theirs = lax.dynamic_index_in_dim(value, 1 - col, 0, keepdims=False)
+        return jnp.concatenate([turn_yc(mine), turn_yc(go(theirs, over_x))], axis=0)
+
+    def spread_out(value):
+        mine = turn_yc(value[:local])
+        theirs = go(turn_yc(value[local:]), over_x)
+        front = jnp.where(col == 0, mine, theirs)
+        back = jnp.where(col == 0, theirs, mine)
+        return f32(jnp.stack([front, back]))
+
+    ranks = jnp.stack([2 * core + col, 2 * core + 1 - col])
+    others = jnp.stack([2 * (1 - core) + col, 2 * (1 - core) + 1 - col])
+
+    def places(which):
+        return block_order.reshape(-1, slots)[which].reshape(-1)
+
+    place = places(ranks)
+    keyed = jnp.concatenate([place, places(others)])
+    blocks = keyed.shape[0]
+    order = jnp.arange(blocks, dtype=jnp.int32)
+    slot = jnp.sum(jnp.where(keyed[None, :] == order[:, None], order[None, :], 0), axis=1).astype(jnp.int32)
+
+    def add_pair(a, b):
+        return bf(f32(a) + f32(b))
+
+    def core_columns(value, which):
+        parts = value.reshape(value.shape[0], planes, 2, -1)
+        return lax.dynamic_index_in_dim(parts, which, 2, keepdims=False).reshape(value.shape[0], -1)
+
+    def gather_dp(piece):
+        return lax.all_gather(piece, "dp", axis=0, tiled=True)
+
+    def group(value):
+        beside = go(value, over_c)
+        across = go(value, over_y)
+        return jnp.concatenate([value, beside, across, go(across, over_c)], axis=0)
+
+    def ungroup(multiply, rows):
+        far = multiply(rows // 2, rows // 2)
+        near = multiply(0, rows // 2)
+        quarter = rows // 4
+        sent = far[:quarter] + f32(go(bf(far[quarter:]), over_c))
+        back = go(bf(sent), over_y)
+        return near[:quarter] + f32(go(bf(near[quarter:]), over_c)) + f32(back)
+
+    small = jnp.concatenate(
+        [norm_gain, norm_shift, attn_bias, out_bias, fc_bias[:, None, :]], axis=1
+    )
+    small = lax.all_gather(small, "dp", axis=0)
+    small = jnp.transpose(small, (1, 2, 0, 3)).reshape(LAYERS, 9, width)
+    units_bias = turn_xc(small[:, 8])
+    small = f32(small)
+
+    fetched = []
+    for layer in range(LAYERS):
+        qkv = qkv_weight[layer]
+        fetched.append(
+            dict(
+                k=gather_dp(qkv[:, width:2 * width]),
+                v=gather_dp(qkv[:, 2 * width:]),
+                q=gather_dp(qkv[:, :width]),
+                proj=gather_dp(proj_weight[layer]),
+                fc=turn_xc(gather_dp(fc_weight[layer])),
+                fc2=turn_xc(gather_dp(fc2_weight[layer].T)),
+                gain=small[layer, 0:2],
+                shift=small[layer, 2:4],
+                bias_in=small[layer, 4:6],
+                bias_out=small[layer, 6:8],
+                fc_b=f32(units_bias[layer]),
+            )
+        )
+
+    hidden = f32(spread_in(tokens))
+    grad_in = spread_in(cotangent)
+    saved = []
+    for layer in range(LAYERS):
+        w = fetched[layer]
+        centred, rate = norm_parts(hidden)
+        normed = bf(centred * rate * w["gain"][0] + w["shift"][0])
+        key = bf(nn(normed, w["k"]))
+        key_other = go(key, over_c)
+        value = bf(nn(normed, w["v"]) + w["bias_in"][1])
+        value_other = go(value, over_c)
+        query = bf(nn(normed, w["q"]) + w["bias_in"][0])
+        attended, lse = attention(place, slot, query, key, key_other, value, value_other)
+        middle = hidden + nn(attended, w["proj"]) + w["bias_out"][0]
+        centred, rate = norm_parts(middle)
+        normed_two = bf(centred * rate * w["gain"][1] + w["shift"][1])
+        rows_in = group(normed_two)
+        inner = nn(rows_in, w["fc"]) + w["fc_b"]
+        active = bf(jax.nn.gelu(inner, approximate=True))
+
+        def down(start, rows, active=active, w=w):
+            return nt(active[start:start + rows], w["fc2"])
+
+        output = middle + ungroup(down, rows_in.shape[0]) + w["bias_out"][1]
+        saved.append((hidden, normed, query, key, key_other, value, value_other, attended, lse, middle, rows_in, inner, active))
+        hidden = output
+    outputs = spread_out(bf(hidden))
+
+    grad = f32(grad_in)
+    factor = 1.0 / lax.axis_size("dp")
+    third, fourth = 3 * width // 4, width // 4
+    results = [None] * LAYERS
+    for layer in reversed(range(LAYERS)):
+        w = fetched[layer]
+        (hidden, normed, query, key, key_other, value, value_other, attended, lse, middle, rows_in, inner, active) = saved[layer]
+        out_grad = bf(grad)
+        mlp_bias_grad = jnp.sum(f32(out_grad), axis=0)
+        rows_grad = group(out_grad)
+        _, gelu_back = jax.vjp(lambda v: jax.nn.gelu(v, approximate=True), inner)
+        inner_grad = bf(gelu_back(nn(rows_grad, w["fc2"]))[0])
+
+        def up(start, rows, inner_grad=inner_grad, w=w):
+            return nt(inner_grad[start:start + rows], w["fc"])
+
+        normed_two_grad = ungroup(up, rows_in.shape[0])
+        fc2_grad = bf(tn(rows_grad, active))
+        fc_grad = bf(tn(rows_in, inner_grad))
+        units_grad = jnp.sum(f32(inner_grad), axis=0)
+        part, gain_two, shift_two = norm_back(normed_two_grad, middle, w["gain"][1])
+        middle_grad = grad + part
+        branch_grad = bf(middle_grad)
+        attn_out_grad = jnp.sum(f32(branch_grad), axis=0)
+        attended_grad = bf(nt(branch_grad, w["proj"]))
+        dq, dk_mine, dk_theirs, dv_mine, dv_theirs = attention_back(
+            place, slot, query, key, key_other, value, value_other, attended_grad, attended, lse
+        )
+        dk = bf(dk_mine + f32(go(dk_theirs, over_c)))
+        dv = bf(dv_mine + f32(go(dv_theirs, over_c)))
+        bias_in_grad = jnp.stack([jnp.sum(f32(dq), axis=0), jnp.sum(f32(dv), axis=0)])
+        normed_grad = nt(dq, w["q"]) + nt(dk, w["k"]) + nt(dv, w["v"])
+        part, gain_one, shift_one = norm_back(normed_grad, hidden, w["gain"][0])
+        grad = middle_grad + part
+
+        mixed = jnp.concatenate([dq, dk, dv], axis=1)
+        keep_cols = core_columns(normed, core), core_columns(attended, core)
+        send_cols = core_columns(normed, 1 - core), core_columns(attended, 1 - core)
+
+        def column(cols, near_y, near_x):
+            index = 2 * (row if near_y else 1 - row) + (col if near_x else 1 - col)
+            first = lax.dynamic_slice_in_dim(mixed, index * third, third, axis=1)
+            second = lax.dynamic_slice_in_dim(branch_grad, index * fourth, fourth, axis=1)
+            return bf(jnp.concatenate([tn(cols[0], first), tn(cols[1], second)], axis=1))
+
+        def chip_sum(near_y, near_x):
+            return add_pair(column(keep_cols, near_y, near_x), go(column(send_cols, near_y, near_x), over_c))
+
+        def row_sum(near_x):
+            return add_pair(chip_sum(True, near_x), go(chip_sum(False, near_x), over_y))
+
+        far_side = go(row_sum(False), over_x)
+        attn_part = sum_z(add_pair(row_sum(True), far_side))
+
+        def units_sum(value):
+            quarters = value.reshape(planes, 2, -1, width)
+            kept = lax.dynamic_index_in_dim(quarters, col, 1, keepdims=False)
+            sent = lax.dynamic_index_in_dim(quarters, 1 - col, 1, keepdims=False)
+            part = add_pair(kept, go(sent, over_x)).reshape(-1, width)
+            return turn_xc(sum_z(part))
+
+        fc2_part = units_sum(fc2_grad)
+        fc_part = units_sum(fc_grad)
+        sums = jnp.concatenate(
+            [
+                jnp.stack([gain_one, gain_two, shift_one, shift_two]),
+                bias_in_grad,
+                jnp.stack([attn_out_grad, mlp_bias_grad]),
+            ],
+            axis=0,
+        )
+        results[layer] = (attn_part, fc_part, fc2_part, sums, units_grad)
+
+    input_grad = spread_out(bf(grad))
+    sums = jnp.stack([entry[3] for entry in results])
+    sums = sums + go(sums, over_x)
+    sums = sums + go(sums, over_y)
+    units = turn_xc(jnp.stack([entry[4] for entry in results]))
+    sums = jnp.concatenate([sums, units[:, None, :]], axis=1)
+    sums = lax.psum_scatter(sums, "dp", scatter_dimension=2, tiled=True) * factor
+    attn_part = jnp.stack([f32(entry[0]) for entry in results]) * factor
+    return (
+        outputs,
+        input_grad,
+        attn_part[:, :, :third],
+        attn_part[:, :, third:],
+        jnp.stack([f32(entry[1]) for entry in results]) * factor,
+        jnp.stack([f32(entry[2]).T for entry in results]) * factor,
+        sums[:, 8],
+        sums[:, 0:2],
+        sums[:, 2:4],
+        sums[:, 4:6],
+        sums[:, 6:8],
+    )
+
+
 def solution(mesh):
+    planes = mesh.shape["dp"] // 2
+    if mesh.shape["mp"] == 4:
+        body = functools.partial(quick_body, planes)
+    else:
+        body = general_body
     return jax.shard_map(
         body,
         mesh=mesh,

time: 3310 us -> 1830 us (0.55)
  waiting for transfers between devices: 1690 us -> 655 us
  matrix products: 751 us -> 435 us
  local copies, waits for them, and re-layouts: 401 us -> 213 us
  blocking collectives: 195 us -> 15 us
  Pallas kernels: 0 us -> 176 us
  starting transfers between devices: 2.1 us -> 138 us
  other arithmetic: 233 us -> 173 us
    reduce_scatter x10 -> x0, waiting for transfers between devices: 567 us -> none  [the longest x2 144 us: body(): lax.psum_scatter(key_grad.astype(jnp.bfloat16), 'mp', scatter_dimension=1...]
    all_gather x16 -> x12, waiting for transfers between devices: 825 us -> 286 us  [gather_dp(): return lax.all_gather(piece, 'dp', axis=0, tiled=True)]
    ppermute x0 -> x74, waiting for transfers between devices: none -> 366 us  [go(): return lax.ppermute(value, AXES, pairs)]
    dot_general x52 -> x64, matrix products: 751 us -> 435 us  [the longest x36 160 us: tn(): lax.dot_general(a, b, (((0,), (0,)), ((), ())), preferred_element_type=jn...]
    unnamed x46 -> x26, waiting for transfers between devices: 298 us -> 2.88 us
    slice x20 -> x19, local copies, waits for them, and re-layouts: 232 us -> 19.2 us  [the longest x4 4.96 us: ungroup(): return near[:quarter] + f32(go(bf(near[quarter:]), over_c)) + f32(back)]
    pallas_call x0 -> x4, Pallas kernels: none -> 176 us  [the longest x2 97.5 us: attention_back(): pl.pallas_call(functools.partial(attend_back_kernel, width, blocks, place...]
    ppermute x0 -> x74, starting transfers between devices: none -> 137 us  [go(): return lax.ppermute(value, AXES, pairs)]
  transfers between devices with their start and end apart: 36 -> 93, of which waited for: 28 -> 29; matrix products, arithmetic and copies ran while one was open for 29% -> 39% of each run, Pallas kernels for 0% -> 10%
where the time goes in v1:
time: 1830 us; the launch traced here: 1820 us
  waiting for transfers between devices  655 us (36%)
  matrix products  435 us (24%)
  local copies, waits for them, and re-layouts  213 us (12%)
  Pallas kernels  176 us (10%)
  other arithmetic  173 us (9%)
  starting transfers between devices  138 us (8%)
    ppermute x74, waiting for transfers between devices, go(): return lax.ppermute(value, AXES, pairs)  366 us
    all_gather x12, waiting for transfers between devices, gather_dp(): return lax.all_gather(piece, 'dp', axis=0, tiled=True)  286 us
    dot_general x36, matrix products, tn(): lax.dot_general(a, b, (((0,), (0,)), ((), ())), preferred_element_type=jn...  160 us
    dot_general x12, matrix products, nn(): return jnp.dot(a, b, preferred_element_type=jnp.float32)  160 us
    ppermute x74, starting transfers between devices, go(): return lax.ppermute(value, AXES, pairs)  137 us
    dot_general x16, matrix products, nt(): lax.dot_general(a, b, (((1,), (1,)), ((), ())), preferred_element_type=jn...  114 us
    pallas_call x2, Pallas kernels, attention_back(): pl.pallas_call(functools.partial(attend_back_kernel, width, blocks, place...  97.5 us
    pallas_call x2, Pallas kernels, attention(): pl.pallas_call(functools.partial(attend_kernel, width, blocks, place.shap...  78.9 us
  transfers between devices with their start and end apart: 93, of which 29 were waited for; matrix products, arithmetic and copies ran while one was open for 39% of the time, Pallas kernels for 10%

profile of v1, /device:TPU:1, one launch (start us, length us, event | category | flops | bytes accessed | tf_op | source)
XLA Modules:
  0.0 1823.1 jit_solution(2437999751784408509)
XLA Ops:
  29.0 13.6 collective-permute-done.1
  47.4 15.0 all-gather
  71.5 7.3 convolution_convert_fusion.21
  79.0 50.2 %all-gather.22.cloned.1.call-done = bf16[1600,1600]{1,0:T(8,128)(2,1)} async-done(((bf16[200,1600]{1,0:T(8,128)(2,1)}), bf16[1600,1600]{1,0:T(8,128)(2,1)}) %all-gather.22.cloned.1.call-update) | async-done | bytes 5120016 | tf_op jit(solution)/shard_map/all_gather | solution.py:695
  129.3 6.3 add_convert_fusion.20.vo_ref
  142.6 43.8 %all-gather.36.cloned.1.call-done = bf16[1,1600,1600]{2,1,0:T(8,128)(2,1)} async-done(((bf16[1,200,1600]{2,1,0:T(8,128)(2,1)}), bf16[1,1600,1600]{2,1,0:T(8,128)(2,1)}) %all-gather.36.cloned.1.call-update) | async-done | bytes 5120016 | tf_op jit(solution)/shard_map/all_gather | solution.py:695
  189.7 53.8 %all-gather.24.cloned.1.call-done = bf16[1600,1600]{1,0:T(8,128)(2,1)} async-done(((bf16[200,1600]{1,0:T(8,128)(2,1)}), bf16[1600,1600]{1,0:T(8,128)(2,1)}) %all-gather.24.cloned.1.call-update) | async-done | bytes 5120016 | tf_op jit(solution)/shard_map/all_gather | solution.py:695
  247.2 53.8 %all-gather.18.cloned.1.call-done = bf16[1600,1600]{1,0:T(8,128)(2,1)} async-done(((bf16[200,1600]{1,0:T(8,128)(2,1)}), bf16[1600,1600]{1,0:T(8,128)(2,1)}) %all-gather.18.cloned.1.call-update) | async-done | bytes 5120016 | tf_op jit(solution)/shard_map/all_gather | solution.py:695
  301.1 8.0 add_convert_fusion.21.q_ref
  320.7 39.4 %attention.2 = (bf16[512,1600]{1,0:T(8,128)(2,1)S(1)}, f32[13,2,512]{2,1,0:T(2,128)S(1)}) custom-call(s32[4]{0:T(128)S(1)} %reshape.419.place_ref, s32[8]{0:T(128)S(1)} %select_reduce_fusion.slot_ref, bf16[512,1600]{1,0:T(8,128)(2,1)S(1)} %copy-done.26, bf16[512,1600]{1,0:T(8,128)(2,1)S(1)} %copy.189.ko_ref, bf16[512,1600]{1,0:T(8,128)(2,1)S(1)} %copy-done.4, ...), custom_call_target="tpu_custom_call" | custom-call | flops 6979321856 | bytes 9830400 | tf_op jit(solution)/shard_map/attention/pallas_call | solution.py:543
  361.3 6.9 fusion.176
  372.2 9.7 collective-permute-start.9
  385.6 16.7 collective-permute-done.6
  402.3 7.1 collective-permute-start.7
  414.9 7.0 broadcast_select_fusion.3
  421.9 24.3 %multiply_convert_fusion.1 = (bf16[2048,1600]{0,1:T(8,128)(2,1)}, f32[2048,1600]{0,1:T(8,128)}) fusion(f32[1600]{0:T(1024)S(1)} %get-tuple-element.72, bf16[1600,1600]{1,0:T(8,128)(2,1)} %broadcast_select_fusion.3, bf16[512,1600]{0,1:T(8,128)(2,1)} %collective-permute-done.7, bf16[512,1600]{0,1:T(8,128)(2,1)} %collective-permute-done.6, ...), kind=kOutput, calls=%fused_computation.23 | convolution fusion | flops 10544742400 | bytes 31340800 | tf_op jit(solution)/shard_map/dot_general | solution.py:411
  446.3 9.1 fusion.64
  465.2 9.4 fusion.69
  487.6 30.3 %collective-permute-done.13 = bf16[512,1600]{0,1:T(8,128)(2,1)S(1)} collective-permute-done((bf16[512,1600]{0,1:T(8,128)(2,1)S(1)}, bf16[512,1600]{0,1:T(8,128)(2,1)S(1)}, u32[]{:S(2)}, u32[]{:S(2)}) %collective-permute-start.13) | collective-permute-done | bytes 1638432 | tf_op jit(solution)/shard_map/ppermute | solution.py:652
  521.7 8.6 convolution_convert_fusion.20
  532.9 6.1 add_convert_fusion.18.vo_ref
  541.7 9.8 collective-permute-done.31
  559.8 27.5 %all-gather.26.cloned.1.call-done = bf16[1600,1600]{1,0:T(8,128)(2,1)} async-done(((bf16[200,1600]{1,0:T(8,128)(2,1)}), bf16[1600,1600]{1,0:T(8,128)(2,1)}) %all-gather.26.cloned.1.call-update) | async-done | bytes 5120016 | tf_op jit(solution)/shard_map/all_gather | solution.py:695
  587.3 7.1 add_convert_fusion.19.q_ref
  594.4 50.0 %all-gather.32.cloned.1.call-done = bf16[1600,1600]{1,0:T(8,128)(2,1)} async-done(((bf16[200,1600]{1,0:T(8,128)(2,1)}), bf16[1600,1600]{1,0:T(8,128)(2,1)}) %all-gather.32.cloned.1.call-update) | async-done | bytes 5120016 | tf_op jit(solution)/shard_map/all_gather | solution.py:695
  660.9 39.4 %attention.3 = (bf16[512,1600]{1,0:T(8,128)(2,1)S(1)}, f32[13,2,512]{2,1,0:T(2,128)S(1)}) custom-call(s32[4]{0:T(128)S(1)} %reshape.419.place_ref, s32[8]{0:T(128)S(1)} %select_reduce_fusion.slot_ref, bf16[512,1600]{1,0:T(8,128)(2,1)S(1)} %copy-done.24, bf16[512,1600]{1,0:T(8,128)(2,1)S(1)} %copy-done.12, bf16[512,1600]{1,0:T(8,128)(2,1)S(1)} %copy-done.14, ...), custom_call_target="tpu_custom_call" | custom-call | flops 6979321856 | bytes 9830400 | tf_op jit(solution)/shard_map/attention/pallas_call | solution.py:543
  701.5 7.0 fusion.177
  733.5 10.3 collective-permute-done.17
  749.7 7.0 broadcast_select_fusion.1
  762.1 18.9 %fusion.98 = f32[2048,1600]{0,1:T(8,128)} fusion(bf16[1600,1600]{1,0:T(8,128)(2,1)} %broadcast_select_fusion.1, bf16[512,1600]{0,1:T(8,128)(2,1)} %collective-permute-done.18, bf16[512,1600]{0,1:T(8,128)(2,1)} %collective-permute-done.17, bf16[512,1600]{0,1:T(8,128)(2,1)S(1)} %collective-permute-done.16, bf16[512,1600]{0,1:T(8,128)(2,1)} %add_convert_fusion.23), kind=kOutput, calls=%fused_computation.245 | convolution fusion | flops 10511974400 | bytes 24780800 | tf_op jit(solution)/shard_map/dot_general | solution.py:411
  781.0 30.5 %convert_reduce_fusion = (f32[1600]{0:T(1024)}, bf16[2048,1600]{0,1:T(8,128)(2,1)}, bf16[2048,1600]{0,1:T(8,128)(2,1)}) fusion(f32[2048,1600]{0,1:T(8,128)} %fusion.98, f32[1600]{0:T(1024)S(1)} %copy-done.160, bf16[2048,1600]{0,1:T(8,128)(2,1)} %constant_dynamic-update-slice_fusion, bf16[1600,1600]{1,0:T(8,128)(2,1)} %broadcast_select_fusion), kind=kOutput, calls=%fused_computation.20 | convolution fusion | flops 10567677952 | bytes 37900800 | tf_op jit(solution)/shard_map/dot_general | solution.py:411
  811.5 9.5 fusion.49
  821.1 10.2 fusion.52
  833.0 18.6 %convolution_convert_fusion = bf16[1600,1600]{1,0:T(8,128)(2,1)} fusion(bf16[2048,1600]{0,1:T(8,128)(2,1)} %constant_dynamic-update-slice_fusion, bf16[2048,1600]{0,1:T(8,128)(2,1)} %get-tuple-element.97), kind=kOutput, calls=%fused_computation.24 | convolution fusion | flops 10488320000 | bytes 18227200 | tf_op jit(solution)/shard_map/dot_general | solution.py:407
  851.6 8.1 fusion.55
  862.0 8.7 fusion.61
  877.7 17.8 convolution_convert_fusion.2
  900.3 11.4 collective-permute-done.35
  915.7 31.2 %collective-permute-done.23 = bf16[512,1600]{0,1:T(8,128)(2,1)} collective-permute-done((bf16[512,1600]{0,1:T(8,128)(2,1)}, bf16[512,1600]{0,1:T(8,128)(2,1)}, u32[]{:S(2)}, u32[]{:S(2)}) %collective-permute-start.23) | collective-permute-done | bytes 1638432 | tf_op jit(solution)/shard_map/ppermute | solution.py:652
  965.2 48.8 %attention_back.2 = (bf16[512,1600]{1,0:T(8,128)(2,1)S(1)}, f32[512,1600]{1,0:T(8,128)}, bf16[512,1600]{1,0:T(8,128)(2,1)S(1)}, f32[512,1600]{1,0:T(8,128)}, bf16[512,1600]{1,0:T(8,128)(2,1)S(1)}) custom-call(s32[4]{0:T(128)S(1)} %reshape.419.place_ref, s32[8]{0:T(128)S(1)} %select_reduce_fusion.slot_ref, bf16[512,1600]{1,0:T(8,128)(2,1)S(1)} %copy-done.25, ...), custom_call_target="tpu_custom_call" | custom-call | flops 17448304640 | bytes 24576000 | tf_op jit(solution)/shard_map/attention_back/pallas_call | solution.py:574
  1020.2 7.3 collective-permute-start.36
  1039.1 7.4 fusion.178
  1056.9 6.2 fusion.179
  1081.6 10.8 collective-permute-done.69
  1149.9 8.3 concatenate.169
  1161.3 29.4 %convert_reduce_fusion.1 = (f32[1600]{0:T(1024)}, bf16[2048,1600]{0,1:T(8,128)(2,1)}) fusion(f32[2048,1600]{0,1:T(8,128)} %get-tuple-element.141, f32[1600]{0:T(1024)S(1)} %copy-done.159, bf16[1600,1600]{1,0:T(8,128)(2,1)} %broadcast_select_fusion.2, bf16[512,1600]{0,1:T(8,128)(2,1)} %collective-permute-done.40, ...), kind=kOutput, calls=%fused_computation.21 | convolution fusion | flops 10587338752 | bytes 31347200 | tf_op jit(solution)/shard_map/dot_general | solution.py:411
  1190.7 8.3 fusion.43
  1205.5 6.4 fusion.46
  1230.5 22.9 %collective-permute-done.43 = bf16[512,1600]{0,1:T(8,128)(2,1)} collective-permute-done((bf16[512,1600]{0,1:T(8,128)(2,1)}, bf16[512,1600]{0,1:T(8,128)(2,1)}, u32[]{:S(2)}, u32[]{:S(2)}) %collective-permute-start.43) | collective-permute-done | bytes 1638432 | tf_op jit(solution)/shard_map/ppermute | solution.py:652
  1272.6 48.7 %attention_back.3 = (bf16[512,1600]{1,0:T(8,128)(2,1)S(1)}, f32[512,1600]{1,0:T(8,128)}, bf16[512,1600]{1,0:T(8,128)(2,1)S(1)}, f32[512,1600]{1,0:T(8,128)}, bf16[512,1600]{1,0:T(8,128)(2,1)S(1)}) custom-call(s32[4]{0:T(128)S(1)} %reshape.419.place_ref, s32[8]{0:T(128)S(1)} %select_reduce_fusion.slot_ref, bf16[512,1600]{1,0:T(8,128)(2,1)S(1)} %copy-done.27, ...), custom_call_target="tpu_custom_call" | custom-call | flops 17448304640 | bytes 24576000 | tf_op jit(solution)/shard_map/attention_back/pallas_call | solution.py:574
  1327.4 7.2 collective-permute-start.44
  1336.8 17.7 convolution_convert_fusion.3
  1358.6 7.4 fusion.180
  1378.5 6.2 fusion.181
  1392.2 36.6 %collective-permute-done.71 = f32[2,8,1600]{2,1,0:T(8,128)S(1)} collective-permute-done((f32[2,8,1600]{2,1,0:T(8,128)S(1)}, f32[2,8,1600]{2,1,0:T(8,128)S(1)}, u32[]{:S(2)}, u32[]{:S(2)}) %collective-permute-start.71) | collective-permute-done | bytes 102432 | tf_op jit(solution)/shard_map/ppermute | solution.py:652
  1443.9 17.9 convolution_convert_fusion.1
  1487.9 10.0 collective-permute-done.61
  1503.2 17.8 collective-permute-done.67
  1530.9 9.2 concatenate.160
  1614.4 37.2 %collective-permute-done.54 = bf16[800,1600]{1,0:T(8,128)(2,1)} collective-permute-done((bf16[800,1600]{1,0:T(8,128)(2,1)}, bf16[800,1600]{1,0:T(8,128)(2,1)}, u32[]{:S(2)}, u32[]{:S(2)}) %collective-permute-start.54) | collective-permute-done | bytes 2560032 | tf_op jit(solution)/shard_map/ppermute | solution.py:652
  1666.8 66.5 %collective-permute-done.26 = bf16[256,1600]{0,1:T(8,128)(2,1)} collective-permute-done((bf16[256,1600]{0,1:T(8,128)(2,1)}, bf16[256,1600]{0,1:T(8,128)(2,1)}, u32[]{:S(2)}, u32[]{:S(2)}) %collective-permute-start.26) | collective-permute-done | bytes 819232 | tf_op jit(solution)/shard_map/ppermute | solution.py:652
  1764.7 6.9 collective-permute-done.47
  1781.2 13.5 collective-permute-done.48
  1803.1 7.4 collective-permute-done.68
  (825 shorter events, 590.0 us)
Async XLA Ops:
  7.2 64.3 %all-gather.20.cloned.1.call-start = ((), (), s32[]{:S(2)}) async-start(), calls=%async_computation.7 | async-start | bytes 5990400 | tf_op jit(solution)/shard_map/all_gather | solution.py:695
  11.2 118.1 %all-gather.22.cloned.1.call-start = ((), (), s32[]{:S(2)}) async-start(), calls=%async_computation.8 | async-start | bytes 5990400 | tf_op jit(solution)/shard_map/all_gather | solution.py:695
  12.0 174.5 %all-gather.36.cloned.1.call-start = ((), (), s32[]{:S(2)}) async-start(), calls=%async_computation.15 | async-start | bytes 5990400 | tf_op jit(solution)/shard_map/all_gather | solution.py:695
  13.2 230.2 %all-gather.24.cloned.1.call-start = ((), (), s32[]{:S(2)}) async-start(), calls=%async_computation.9 | async-start | bytes 5990400 | tf_op jit(solution)/shard_map/all_gather | solution.py:695
  15.8 285.2 %all-gather.18.cloned.1.call-start = ((), (), s32[]{:S(2)}) async-start(), calls=%async_computation.6 | async-start | bytes 5990400 | tf_op jit(solution)/shard_map/all_gather | solution.py:695
  16.4 344.9 %all-gather.34.cloned.1.call-start = ((), (), s32[]{:S(2)}) async-start(), calls=%async_computation.14 | async-start | bytes 5990400 | tf_op jit(solution)/shard_map/all_gather | solution.py:695
  17.7 504.0 %all-gather.28.cloned.1.call-start = ((), (), s32[]{:S(2)}) async-start(), calls=%async_computation.11 | async-start | bytes 5990400 | tf_op jit(solution)/shard_map/all_gather | solution.py:695
  19.4 513.5 %all-gather.30.cloned.1.call-start = ((), (), s32[]{:S(2)}) async-start(), calls=%async_computation.12 | async-start | bytes 5990400 | tf_op jit(solution)/shard_map/all_gather | solution.py:695
  20.2 533.0 %all-gather.40.cloned.1.call-start = ((), (), s32[]{:S(2)}) async-start(), calls=%async_computation.17 | async-start | bytes 5990400 | tf_op jit(solution)/shard_map/all_gather | solution.py:695
  20.9 566.4 %all-gather.26.cloned.1.call-start = ((), (), s32[]{:S(2)}) async-start(), calls=%async_computation.10 | async-start | bytes 5990400 | tf_op jit(solution)/shard_map/all_gather | solution.py:695
  24.7 38.8 %collective-permute-start = (bf16[256,1600]{0,1:T(8,128)(2,1)S(1)}, bf16[256,1600]{0,1:T(8,128)(2,1)}, u32[]{:S(2)}, u32[]{:S(2)}) collective-permute-start(bf16[256,1600]{0,1:T(8,128)(2,1)S(1)} %get-tuple-element.126), channel_id=1, source_target_pairs={{2,4},{3,5},{4,2},{5,3},{10,12},{11,13},{12,10},{13,11},{18,20},{1... | collective-permute-start | bytes 2457608 | tf_op jit(solution)/shard_map/ppermute | solution.py:652
  29.0 615.5 %all-gather.32.cloned.1.call-start = ((), (), s32[]{:S(2)}) async-start(), calls=%async_computation.13 | async-start | bytes 5990400 | tf_op jit(solution)/shard_map/all_gather | solution.py:695
  78.8 230.2 %collective-permute-start.3 = (bf16[512,1600]{0,1:T(8,128)(2,1)}, bf16[512,1600]{0,1:T(8,128)(2,1)}, u32[]{:S(2)}, u32[]{:S(2)}) collective-permute-start(bf16[512,1600]{0,1:T(8,128)(2,1)} %convolution_convert_fusion.21), channel_id=1, source_target_pairs={{0,4},{1,5},{2,6},{3,7},{4,0},{5,1},{6,2},{7,3},{8,12},{9,13},{10,... | collective-permute-start | bytes 4915208 | tf_op jit(solution)/shard_map/ppermute | solution.py:652
  138.0 174.8 %collective-permute-start.4 = (bf16[512,1600]{0,1:T(8,128)(2,1)}, bf16[512,1600]{0,1:T(8,128)(2,1)}, u32[]{:S(2)}, u32[]{:S(2)}) collective-permute-start(bf16[512,1600]{0,1:T(8,128)(2,1)} %copy.188), channel_id=1, source_target_pairs={{0,4},{1,5},{2,6},{3,7},{4,0},{5,1},{6,2},{7,3},{8,12},{9,13},{10,... | collective-permute-start | bytes 4915208 | tf_op jit(solution)/shard_map/ppermute | solution.py:652
  186.5 228.5 %collective-permute-start.8 = (bf16[1600,1600]{1,0:T(8,128)(2,1)}, bf16[1600,1600]{1,0:T(8,128)(2,1)}, u32[]{:S(2)}, u32[]{:S(2)}) collective-permute-start(bf16[1600,1600]{1,0:T(8,128)(2,1)} %bitcast.237), channel_id=1, source_target_pairs={{1,4},{3,6},{4,1},{6,3},{9,12},{11,14},{12,9},{14,11},{17,20},{19,... | collective-permute-start | bytes 15360008 | tf_op jit(solution)/shard_map/ppermute | solution.py:652
  243.5 165.9 %collective-permute-start.10 = (bf16[1600,1600]{1,0:T(8,128)(2,1)}, bf16[1600,1600]{1,0:T(8,128)(2,1)}, u32[]{:S(2)}, u32[]{:S(2)}) collective-permute-start(bf16[1600,1600]{1,0:T(8,128)(2,1)} %all-gather.24.cloned.1.call-done), channel_id=1, source_target_pairs={{1,4},{3,6},{4,1},{6,3},{9,12},{11,14},{12,9},{14,11},{17,20},{19,... | collective-permute-start | bytes 15360008 | tf_op jit(solution)/shard_map/ppermute | solution.py:652
  372.1 329.4 %all-gather.38.cloned.1.call-start = ((), (), s32[]{:S(2)}) async-start(), calls=%async_computation.16 | async-start | bytes 5990400 | tf_op jit(solution)/shard_map/all_gather | solution.py:695
  384.5 78.5 %collective-permute-start.28 = (bf16[256,1600]{0,1:T(8,128)(2,1)}, bf16[256,1600]{0,1:T(8,128)(2,1)}, u32[]{:S(2)}, u32[]{:S(2)}) collective-permute-start(bf16[256,1600]{0,1:T(8,128)(2,1)} %get-tuple-element.122), channel_id=1, source_target_pairs={{0,1},{1,0},{2,3},{3,2},{4,5},{5,4},{6,7},{7,6},{8,9},{9,8},{10,11... | collective-permute-start | bytes 2457608 | tf_op jit(solution)/shard_map/ppermute | solution.py:652
  385.2 36.7 %collective-permute-start.5 = (bf16[512,1600]{0,1:T(8,128)(2,1)}, bf16[512,1600]{0,1:T(8,128)(2,1)}, u32[]{:S(2)}, u32[]{:S(2)}) collective-permute-start(bf16[512,1600]{0,1:T(8,128)(2,1)} %add_convert_fusion.25), channel_id=1, source_target_pairs={{0,4},{1,5},{2,6},{3,7},{4,0},{5,1},{6,2},{7,3},{8,12},{9,13},{10,... | collective-permute-start | bytes 4915208 | tf_op jit(solution)/shard_map/ppermute | solution.py:652
  463.0 1273.0 %reduce-scatter.26.cloned.1.call-start = ((), (), s32[]{:S(2)}) async-start(), calls=%async_computation.22 | async-start | bytes 3328000
  476.9 41.0 %collective-permute-start.13 = (bf16[512,1600]{0,1:T(8,128)(2,1)S(1)}, bf16[512,1600]{0,1:T(8,128)(2,1)S(1)}, u32[]{:S(2)}, u32[]{:S(2)}) collective-permute-start(bf16[512,1600]{0,1:T(8,128)(2,1)S(1)} %fusion.63), channel_id=1, source_target_pairs={{0,2},{1,3},{2,0},{3,1},{4,6},{5,7},{6,4},{7,5},{8,10},{9,11},{10,... | collective-permute-start | bytes 4915208 | tf_op jit(solution)/shard_map/ppermute | solution.py:652
  487.6 64.0 %collective-permute-start.31 = (bf16[512,1600]{0,1:T(8,128)(2,1)}, bf16[512,1600]{0,1:T(8,128)(2,1)}, u32[]{:S(2)}, u32[]{:S(2)}) collective-permute-start(bf16[512,1600]{0,1:T(8,128)(2,1)} %pad_maximum_fusion.12), channel_id=1, source_target_pairs={{0,2},{1,3},{2,0},{3,1},{4,6},{5,7},{6,4},{7,5},{8,10},{9,11},{10,... | collective-permute-start | bytes 4915208 | tf_op jit(solution)/shard_map/ppermute | solution.py:652
  530.3 114.2 %collective-permute-start.14 = (bf16[512,1600]{0,1:T(8,128)(2,1)}, bf16[512,1600]{0,1:T(8,128)(2,1)}, u32[]{:S(2)}, u32[]{:S(2)}) collective-permute-start(bf16[512,1600]{0,1:T(8,128)(2,1)} %convolution_convert_fusion.20), channel_id=1, source_target_pairs={{0,4},{1,5},{2,6},{3,7},{4,0},{5,1},{6,2},{7,3},{8,12},{9,13},{10,... | collective-permute-start | bytes 4915208 | tf_op jit(solution)/shard_map/ppermute | solution.py:652
  541.2 110.2 %collective-permute-start.15 = (bf16[512,1600]{0,1:T(8,128)(2,1)}, bf16[512,1600]{0,1:T(8,128)(2,1)}, u32[]{:S(2)}, u32[]{:S(2)}) collective-permute-start(bf16[512,1600]{0,1:T(8,128)(2,1)} %copy.195), channel_id=1, source_target_pairs={{0,4},{1,5},{2,6},{3,7},{4,0},{5,1},{6,2},{7,3},{8,12},{9,13},{10,... | collective-permute-start | bytes 4915208 | tf_op jit(solution)/shard_map/ppermute | solution.py:652
  541.3 173.4 %collective-permute-start.30 = (bf16[512,1600]{0,1:T(8,128)(2,1)}, bf16[512,1600]{0,1:T(8,128)(2,1)}, u32[]{:S(2)}, u32[]{:S(2)}) collective-permute-start(bf16[512,1600]{0,1:T(8,128)(2,1)} %pad_maximum_fusion.12), channel_id=1, source_target_pairs={{0,4},{1,5},{2,6},{3,7},{4,0},{5,1},{6,2},{7,3},{8,12},{9,13},{10,... | collective-permute-start | bytes 4915208 | tf_op jit(solution)/shard_map/ppermute | solution.py:652
  551.6 168.8 %collective-permute-start.32 = (bf16[512,1600]{0,1:T(8,128)(2,1)}, bf16[512,1600]{0,1:T(8,128)(2,1)}, u32[]{:S(2)}, u32[]{:S(2)}) collective-permute-start(bf16[512,1600]{0,1:T(8,128)(2,1)} %collective-permute-done.31), channel_id=1, source_target_pairs={{0,4},{1,5},{2,6},{3,7},{4,0},{5,1},{6,2},{7,3},{8,12},{9,13},{10,... | collective-permute-start | bytes 4915208 | tf_op jit(solution)/shard_map/ppermute | solution.py:652
  553.2 196.5 %collective-permute-start.19 = (bf16[1600,1600]{1,0:T(8,128)(2,1)}, bf16[1600,1600]{1,0:T(8,128)(2,1)}, u32[]{:S(2)}, u32[]{:S(2)}) collective-permute-start(bf16[1600,1600]{1,0:T(8,128)(2,1)} %bitcast.236), channel_id=1, source_target_pairs={{1,4},{3,6},{4,1},{6,3},{9,12},{11,14},{12,9},{14,11},{17,20},{19,... | collective-permute-start | bytes 15360008 | tf_op jit(solution)/shard_map/ppermute | solution.py:652
  644.5 112.2 %collective-permute-start.20 = (bf16[1600,1600]{1,0:T(8,128)(2,1)}, bf16[1600,1600]{1,0:T(8,128)(2,1)}, u32[]{:S(2)}, u32[]{:S(2)}) collective-permute-start(bf16[1600,1600]{1,0:T(8,128)(2,1)} %all-gather.32.cloned.1.call-done), channel_id=1, source_target_pairs={{1,4},{3,6},{4,1},{6,3},{9,12},{11,14},{12,9},{14,11},{17,20},{19,... | collective-permute-start | bytes 15360008 | tf_op jit(solution)/shard_map/ppermute | solution.py:652
  728.2 33.9 %collective-permute-start.16 = (bf16[512,1600]{0,1:T(8,128)(2,1)}, bf16[512,1600]{0,1:T(8,128)(2,1)S(1)}, u32[]{:S(2)}, u32[]{:S(2)}) collective-permute-start(bf16[512,1600]{0,1:T(8,128)(2,1)} %add_convert_fusion.23), channel_id=1, source_target_pairs={{0,4},{1,5},{2,6},{3,7},{4,0},{5,1},{6,2},{7,3},{8,12},{9,13},{10,... | collective-permute-start | bytes 4915208 | tf_op jit(solution)/shard_map/ppermute | solution.py:652
  833.0 39.4 %collective-permute-start.34 = (bf16[512,1600]{0,1:T(8,128)(2,1)}, bf16[512,1600]{0,1:T(8,128)(2,1)S(1)}, u32[]{:S(2)}, u32[]{:S(2)}) collective-permute-start(bf16[512,1600]{0,1:T(8,128)(2,1)} %slice.483), channel_id=1, source_target_pairs={{0,4},{1,5},{2,6},{3,7},{4,0},{5,1},{6,2},{7,3},{8,12},{9,13},{10,... | collective-permute-start | bytes 4915208 | tf_op jit(solution)/shard_map/ppermute | solution.py:652
  861.1 39.2 %collective-permute-start.33 = (bf16[512,1600]{0,1:T(8,128)(2,1)}, bf16[512,1600]{0,1:T(8,128)(2,1)S(1)}, u32[]{:S(2)}, u32[]{:S(2)}) collective-permute-start(bf16[512,1600]{0,1:T(8,128)(2,1)} %slice.484), channel_id=1, source_target_pairs={{0,4},{1,5},{2,6},{3,7},{4,0},{5,1},{6,2},{7,3},{8,12},{9,13},{10,... | collective-permute-start | bytes 4915208 | tf_op jit(solution)/shard_map/ppermute | solution.py:652
  872.3 43.3 %collective-permute-start.21 = (bf16[512,1600]{0,1:T(8,128)(2,1)}, bf16[512,1600]{0,1:T(8,128)(2,1)}, u32[]{:S(2)}, u32[]{:S(2)}) collective-permute-start(bf16[512,1600]{0,1:T(8,128)(2,1)} %slice.486), channel_id=1, source_target_pairs={{0,4},{1,5},{2,6},{3,7},{4,0},{5,1},{6,2},{7,3},{8,12},{9,13},{10,... | collective-permute-start | bytes 4915208 | tf_op jit(solution)/shard_map/ppermute | solution.py:652
  874.4 37.4 %collective-permute-start.35 = (bf16[512,1600]{0,1:T(8,128)(2,1)}, bf16[512,1600]{0,1:T(8,128)(2,1)S(1)}, u32[]{:S(2)}, u32[]{:S(2)}) collective-permute-start(bf16[512,1600]{0,1:T(8,128)(2,1)} %fusion.48), channel_id=1, source_target_pairs={{0,2},{1,3},{2,0},{3,1},{4,6},{5,7},{6,4},{7,5},{8,10},{9,11},{10,... | collective-permute-start | bytes 4915208 | tf_op jit(solution)/shard_map/ppermute | solution.py:652
  877.4 69.4 %collective-permute-start.23 = (bf16[512,1600]{0,1:T(8,128)(2,1)}, bf16[512,1600]{0,1:T(8,128)(2,1)}, u32[]{:S(2)}, u32[]{:S(2)}) collective-permute-start(bf16[512,1600]{0,1:T(8,128)(2,1)} %fusion.54), channel_id=1, source_target_pairs={{0,2},{1,3},{2,0},{3,1},{4,6},{5,7},{6,4},{7,5},{8,10},{9,11},{10,... | collective-permute-start | bytes 4915208 | tf_op jit(solution)/shard_map/ppermute | solution.py:652
  899.2 135.1 %collective-permute-start.65 = (bf16[4,200,1600]{2,1,0:T(8,128)(2,1)}, bf16[4,200,1600]{2,1,0:T(8,128)(2,1)}, u32[]{:S(2)}, u32[]{:S(2)}) collective-permute-start(bf16[4,200,1600]{2,1,0:T(8,128)(2,1)} %dynamic-slice_bitcast_fusion.2), channel_id=1, source_target_pairs={{0,1},{1,0},{2,3},{3,2},{4,5},{5,4},{6,7},{7,6},{8,9},{9,8},{10,11... | collective-permute-start | bytes 7680008 | tf_op jit(solution)/shard_map/ppermute | solution.py:652
  1033.2 59.1 %collective-permute-start.69 = (bf16[4,200,1600]{2,1,0:T(8,128)(2,1)}, bf16[4,200,1600]{2,1,0:T(8,128)(2,1)}, u32[]{:S(2)}, u32[]{:S(2)}) collective-permute-start(bf16[4,200,1600]{2,1,0:T(8,128)(2,1)} %dynamic-slice_bitcast_fusion), channel_id=1, source_target_pairs={{0,1},{1,0},{2,3},{3,2},{4,5},{5,4},{6,7},{7,6},{8,9},{9,8},{10,11... | collective-permute-start | bytes 7680008 | tf_op jit(solution)/shard_map/ppermute | solution.py:652
  1039.0 722.4 %reduce-scatter.30.cloned.1.call-start = ((), (), s32[]{:S(2)}) async-start(), calls=%async_computation.24 | async-start | bytes 3328000
  1073.8 36.9 %collective-permute-start.39 = (bf16[512,1600]{0,1:T(8,128)(2,1)}, bf16[512,1600]{0,1:T(8,128)(2,1)}, u32[]{:S(2)}, u32[]{:S(2)}) collective-permute-start(bf16[512,1600]{0,1:T(8,128)(2,1)} %get-tuple-element.74), channel_id=1, source_target_pairs={{0,2},{1,3},{2,0},{3,1},{4,6},{5,7},{6,4},{7,5},{8,10},{9,11},{10,... | collective-permute-start | bytes 4915208 | tf_op jit(solution)/shard_map/ppermute | solution.py:652
  1097.1 680.1 %all-reduce.9.cloned.1.call-start = ((), (), s32[]{:S(2)}) async-start(), calls=%async_computation.18 | async-start | bytes 425984
  1105.5 55.8 %collective-permute-start.38 = (bf16[512,1600]{0,1:T(8,128)(2,1)}, bf16[512,1600]{0,1:T(8,128)(2,1)}, u32[]{:S(2)}, u32[]{:S(2)}) collective-permute-start(bf16[512,1600]{0,1:T(8,128)(2,1)} %get-tuple-element.74), channel_id=1, source_target_pairs={{0,4},{1,5},{2,6},{3,7},{4,0},{5,1},{6,2},{7,3},{8,12},{9,13},{10,... | collective-permute-start | bytes 4915208 | tf_op jit(solution)/shard_map/ppermute | solution.py:652
  1110.7 50.6 %collective-permute-start.40 = (bf16[512,1600]{0,1:T(8,128)(2,1)}, bf16[512,1600]{0,1:T(8,128)(2,1)}, u32[]{:S(2)}, u32[]{:S(2)}) collective-permute-start(bf16[512,1600]{0,1:T(8,128)(2,1)} %collective-permute-done.39), channel_id=1, source_target_pairs={{0,4},{1,5},{2,6},{3,7},{4,0},{5,1},{6,2},{7,3},{8,12},{9,13},{10,... | collective-permute-start | bytes 4915208 | tf_op jit(solution)/shard_map/ppermute | solution.py:652
  1115.8 542.9 %collective-permute-start.25 = (bf16[256,1600]{0,1:T(8,128)(2,1)}, bf16[256,1600]{0,1:T(8,128)(2,1)}, u32[]{:S(2)}, u32[]{:S(2)}) collective-permute-start(bf16[256,1600]{0,1:T(8,128)(2,1)} %slice.366), channel_id=1, source_target_pairs={{2,4},{3,5},{4,2},{5,3},{10,12},{11,13},{12,10},{13,11},{18,20},{1... | collective-permute-start | bytes 2457608 | tf_op jit(solution)/shard_map/ppermute | solution.py:652
  1215.8 37.5 %collective-permute-start.43 = (bf16[512,1600]{0,1:T(8,128)(2,1)}, bf16[512,1600]{0,1:T(8,128)(2,1)}, u32[]{:S(2)}, u32[]{:S(2)}) collective-permute-start(bf16[512,1600]{0,1:T(8,128)(2,1)} %fusion.42), channel_id=1, source_target_pairs={{0,2},{1,3},{2,0},{3,1},{4,6},{5,7},{6,4},{7,5},{8,10},{9,11},{10,... | collective-permute-start | bytes 4915208 | tf_op jit(solution)/shard_map/ppermute | solution.py:652
  1218.5 268.5 %collective-permute-start.59 = (bf16[800,1600]{1,0:T(8,128)(2,1)}, bf16[800,1600]{1,0:T(8,128)(2,1)}, u32[]{:S(2)}, u32[]{:S(2)}) collective-permute-start(bf16[800,1600]{1,0:T(8,128)(2,1)} %pad_maximum_fusion.9), channel_id=1, source_target_pairs={{0,4},{1,5},{2,6},{3,7},{4,0},{5,1},{6,2},{7,3},{8,12},{9,13},{10,... | collective-permute-start | bytes 7680008 | tf_op jit(solution)/shard_map/ppermute | solution.py:652
  1227.8 250.5 %collective-permute-start.57 = (bf16[800,1600]{1,0:T(8,128)(2,1)}, bf16[800,1600]{1,0:T(8,128)(2,1)}, u32[]{:S(2)}, u32[]{:S(2)}) collective-permute-start(bf16[800,1600]{1,0:T(8,128)(2,1)} %pad_maximum_fusion.8), channel_id=1, source_target_pairs={{0,4},{1,5},{2,6},{3,7},{4,0},{5,1},{6,2},{7,3},{8,12},{9,13},{10,... | collective-permute-start | bytes 7680008 | tf_op jit(solution)/shard_map/ppermute | solution.py:652
  1327.4 40.1 %collective-permute-start.44 = (bf16[512,1600]{0,1:T(8,128)(2,1)}, bf16[512,1600]{0,1:T(8,128)(2,1)}, u32[]{:S(2)}, u32[]{:S(2)}) collective-permute-start(bf16[512,1600]{0,1:T(8,128)(2,1)} %copy.211), channel_id=1, source_target_pairs={{0,4},{1,5},{2,6},{3,7},{4,0},{5,1},{6,2},{7,3},{8,12},{9,13},{10,... | collective-permute-start | bytes 4915208 | tf_op jit(solution)/shard_map/ppermute | solution.py:652
  1367.5 71.5 %collective-permute-start.63 = (bf16[4,200,1600]{2,1,0:T(8,128)(2,1)}, bf16[4,200,1600]{2,1,0:T(8,128)(2,1)}, u32[]{:S(2)}, u32[]{:S(2)}) collective-permute-start(bf16[4,200,1600]{2,1,0:T(8,128)(2,1)} %dynamic-slice_bitcast_fusion.3), channel_id=1, source_target_pairs={{0,1},{1,0},{2,3},{3,2},{4,5},{5,4},{6,7},{7,6},{8,9},{9,8},{10,11... | collective-permute-start | bytes 7680008 | tf_op jit(solution)/shard_map/ppermute | solution.py:652
  1391.1 37.8 %collective-permute-start.71 = (f32[2,8,1600]{2,1,0:T(8,128)S(1)}, f32[2,8,1600]{2,1,0:T(8,128)S(1)}, u32[]{:S(2)}, u32[]{:S(2)}) collective-permute-start(f32[2,8,1600]{2,1,0:T(8,128)S(1)} %pad_maximum_fusion.22), channel_id=1, source_target_pairs={{0,1},{1,0},{2,3},{3,2},{4,5},{5,4},{6,7},{7,6},{8,9},{9,8},{10,11... | collective-permute-start | bytes 307208 | tf_op jit(solution)/shard_map/ppermute | solution.py:652
  1437.7 60.1 %collective-permute-start.61 = (bf16[800,1600]{1,0:T(8,128)(2,1)}, bf16[800,1600]{1,0:T(8,128)(2,1)}, u32[]{:S(2)}, u32[]{:S(2)}) collective-permute-start(bf16[800,1600]{1,0:T(8,128)(2,1)} %add_convert_fusion.2), channel_id=1, source_target_pairs={{0,2},{1,3},{2,0},{3,1},{4,6},{5,7},{6,4},{7,5},{8,10},{9,11},{10,... | collective-permute-start | bytes 7680008 | tf_op jit(solution)/shard_map/ppermute | solution.py:652
  1439.0 340.3 %reduce-scatter.24.cloned.1.call-start = ((), (), s32[]{:S(2)}) async-start(), calls=%async_computation.21 | async-start | bytes 3328000
  1443.8 354.4 %reduce-scatter.28.cloned.1.call-start = ((), (), s32[]{:S(2)}) async-start(), calls=%async_computation.23 | async-start | bytes 3328000
  1463.8 57.1 %collective-permute-start.67 = (bf16[4,200,1600]{2,1,0:T(8,128)(2,1)S(1)}, bf16[4,200,1600]{2,1,0:T(8,128)(2,1)S(1)}, u32[]{:S(2)}, u32[]{:S(2)}) collective-permute-start(bf16[4,200,1600]{2,1,0:T(8,128)(2,1)S(1)} %dynamic-slice_bitcast_fusion.1), channel_id=1, source_target_pairs={{0,1},{1,0},{2,3},{3,2},{4,5},{5,4},{6,7},{7,6},{8,9},{9,8},{10,11... | collective-permute-start | bytes 7680008 | tf_op jit(solution)/shard_map/ppermute | solution.py:652
  1478.3 113.1 %collective-permute-start.56 = (bf16[800,1600]{1,0:T(8,128)(2,1)}, bf16[800,1600]{1,0:T(8,128)(2,1)}, u32[]{:S(2)}, u32[]{:S(2)}) collective-permute-start(bf16[800,1600]{1,0:T(8,128)(2,1)} %pad_maximum_fusion.7), channel_id=1, source_target_pairs={{0,4},{1,5},{2,6},{3,7},{4,0},{5,1},{6,2},{7,3},{8,12},{9,13},{10,... | collective-permute-start | bytes 7680008 | tf_op jit(solution)/shard_map/ppermute | solution.py:652
  1487.0 105.0 %collective-permute-start.58 = (bf16[800,1600]{1,0:T(8,128)(2,1)}, bf16[800,1600]{1,0:T(8,128)(2,1)}, u32[]{:S(2)}, u32[]{:S(2)}) collective-permute-start(bf16[800,1600]{1,0:T(8,128)(2,1)} %add_convert_fusion.5), channel_id=1, source_target_pairs={{0,2},{1,3},{2,0},{3,1},{4,6},{5,7},{6,4},{7,5},{8,10},{9,11},{10,... | collective-permute-start | bytes 7680008 | tf_op jit(solution)/shard_map/ppermute | solution.py:652
  1503.1 89.9 %collective-permute-start.62 = (bf16[800,1600]{1,0:T(8,128)(2,1)}, bf16[800,1600]{1,0:T(8,128)(2,1)}, u32[]{:S(2)}, u32[]{:S(2)}) collective-permute-start(bf16[800,1600]{1,0:T(8,128)(2,1)} %add_convert_fusion.1), channel_id=1, source_target_pairs={{0,1},{1,0},{2,3},{3,2},{4,5},{5,4},{6,7},{7,6},{8,9},{9,8},{10,11... | collective-permute-start | bytes 7680008 | tf_op jit(solution)/shard_map/ppermute | solution.py:652
  1523.1 289.2 %reduce-scatter.22.cloned.1.call-start = ((), (), s32[]{:S(2)}) async-start(), calls=%async_computation.20 | async-start | bytes 3328000
  1545.2 41.7 %collective-permute-start.53 = (bf16[800,1600]{1,0:T(8,128)(2,1)}, bf16[800,1600]{1,0:T(8,128)(2,1)}, u32[]{:S(2)}, u32[]{:S(2)}) collective-permute-start(bf16[800,1600]{1,0:T(8,128)(2,1)} %pad_maximum_fusion.6), channel_id=1, source_target_pairs={{0,4},{1,5},{2,6},{3,7},{4,0},{5,1},{6,2},{7,3},{8,12},{9,13},{10,... | collective-permute-start | bytes 7680008 | tf_op jit(solution)/shard_map/ppermute | solution.py:652
  1592.0 59.6 %collective-permute-start.54 = (bf16[800,1600]{1,0:T(8,128)(2,1)}, bf16[800,1600]{1,0:T(8,128)(2,1)}, u32[]{:S(2)}, u32[]{:S(2)}) collective-permute-start(bf16[800,1600]{1,0:T(8,128)(2,1)} %add_convert_fusion.9), channel_id=1, source_target_pairs={{0,2},{1,3},{2,0},{3,1},{4,6},{5,7},{6,4},{7,5},{8,10},{9,11},{10,... | collective-permute-start | bytes 7680008 | tf_op jit(solution)/shard_map/ppermute | solution.py:652
  1598.9 213.3 %reduce-scatter.20.cloned.1.call-start = ((), (), s32[]{:S(2)}) async-start(), calls=%async_computation.19 | async-start | bytes 3328000
  1609.4 138.6 %collective-permute-start.49 = (bf16[800,1600]{1,0:T(8,128)(2,1)}, bf16[800,1600]{1,0:T(8,128)(2,1)}, u32[]{:S(2)}, u32[]{:S(2)}) collective-permute-start(bf16[800,1600]{1,0:T(8,128)(2,1)} %pad_maximum_fusion.3), channel_id=1, source_target_pairs={{0,4},{1,5},{2,6},{3,7},{4,0},{5,1},{6,2},{7,3},{8,12},{9,13},{10,... | collective-permute-start | bytes 7680008 | tf_op jit(solution)/shard_map/ppermute | solution.py:652
  1614.1 134.0 %collective-permute-start.51 = (bf16[800,1600]{1,0:T(8,128)(2,1)}, bf16[800,1600]{1,0:T(8,128)(2,1)}, u32[]{:S(2)}, u32[]{:S(2)}) collective-permute-start(bf16[800,1600]{1,0:T(8,128)(2,1)} %add_convert_fusion.12), channel_id=1, source_target_pairs={{0,2},{1,3},{2,0},{3,1},{4,6},{5,7},{6,4},{7,5},{8,10},{9,11},{10,... | collective-permute-start | bytes 7680008 | tf_op jit(solution)/shard_map/ppermute | solution.py:652
  1657.0 91.1 %collective-permute-start.55 = (bf16[800,1600]{1,0:T(8,128)(2,1)}, bf16[800,1600]{1,0:T(8,128)(2,1)}, u32[]{:S(2)}, u32[]{:S(2)}) collective-permute-start(bf16[800,1600]{1,0:T(8,128)(2,1)} %add_convert_fusion.8), channel_id=1, source_target_pairs={{0,1},{1,0},{2,3},{3,2},{4,5},{5,4},{6,7},{7,6},{8,9},{9,8},{10,11... | collective-permute-start | bytes 7680008 | tf_op jit(solution)/shard_map/ppermute | solution.py:652
  1661.2 72.2 %collective-permute-start.26 = (bf16[256,1600]{0,1:T(8,128)(2,1)}, bf16[256,1600]{0,1:T(8,128)(2,1)}, u32[]{:S(2)}, u32[]{:S(2)}) collective-permute-start(bf16[256,1600]{0,1:T(8,128)(2,1)} %get-tuple-element.125), channel_id=1, source_target_pairs={{0,1},{1,0},{2,3},{3,2},{4,5},{5,4},{6,7},{7,6},{8,9},{9,8},{10,11... | collective-permute-start | bytes 2457608 | tf_op jit(solution)/shard_map/ppermute | solution.py:652
  1661.2 72.1 %collective-permute-start.24 = (bf16[256,1600]{0,1:T(8,128)(2,1)}, bf16[256,1600]{0,1:T(8,128)(2,1)}, u32[]{:S(2)}, u32[]{:S(2)}) collective-permute-start(bf16[256,1600]{0,1:T(8,128)(2,1)} %get-tuple-element.124), channel_id=1, source_target_pairs={{2,4},{3,5},{4,2},{5,3},{10,12},{11,13},{12,10},{13,11},{18,20},{1... | collective-permute-start | bytes 2457608 | tf_op jit(solution)/shard_map/ppermute | solution.py:652
  (228 other events, 5673.3 us)
Sparse Core Ops, SparseCore 0:
  11.3 60.1 all-gather.19
  73.7 55.5 all-gather.21
  130.9 55.4 all-gather.35
  187.9 55.4 all-gather.23
  245.5 55.4 all-gather.17
  303.1 55.5 all-gather.33
  360.3 55.5 all-gather.27
  417.6 55.4 all-gather.29
  474.8 55.4 all-gather.39
  531.8 55.4 all-gather.25
  588.9 55.4 all-gather.31
  645.9 55.4 all-gather.37
  1039.1 50.6 reduce-scatter.25
  1097.2 51.6 reduce-scatter.29
  1439.1 53.9 all-reduce.8
  1495.4 53.4 reduce-scatter.23
  1551.1 52.6 reduce-scatter.27
  1606.1 52.5 reduce-scatter.21
  1753.8 50.1 reduce-scatter.19

commit v2 on v1

--- a/solution.py
+++ b/solution.py
@@ -595,6 +595,489 @@
     )(place, slot, q, ko, ks, vo, vs, do, o, lse)
 
 
+def gather_kernel(planes, piece_ref, small_ref, token_ref, cot_ref, out_ref, small_out, token_out, cot_out,
+                  send_sem, recv_sem, small_send, small_recv, swap_send, swap_recv, own_sem):
+    dp, mp = lax.axis_index("dp"), lax.axis_index("mp")
+    z, c = dp // 2, dp % 2
+    y, x = mp // 2, mp % 2
+    side = mp + 1 - 2 * x
+    across = mp + 2 - 4 * y
+    corner = 3 - mp
+    to_x, to_y, to_c = (dp, side), (dp, across), (dp + 1 - 2 * c, mp)
+    to_z = [(lax.rem(z + k, planes) * 2 + c, mp) for k in range(1, planes)]
+    same, turned = (z * 2 + y, c * 2 + x), (z * 2 + y, c * 2 + 1 - x)
+    barrier = pltpu.get_barrier_semaphore()
+    for peer in (to_x, to_y, to_c, *to_z, turned):
+        pl.semaphore_signal(barrier, inc=1, device_id=peer, device_id_type=pl.DeviceIdType.MESH)
+
+    @pl.when(y != c)
+    def _():
+        pl.semaphore_signal(barrier, inc=1, device_id=same, device_id_type=pl.DeviceIdType.MESH)
+
+    pl.semaphore_wait(barrier, 4 + len(to_z) + (y - c) * (y - c))
+
+    locals_ = [
+        pltpu.make_async_copy(piece_ref, out_ref.at[mp, dp], own_sem.at[0]),
+        pltpu.make_async_copy(small_ref, small_out.at[dp], own_sem.at[1]),
+    ]
+    for copy in locals_:
+        copy.start()
+    sent = []
+
+    def remote(source, target, sems, peer):
+        copy = pltpu.make_async_remote_copy(
+            src_ref=source,
+            dst_ref=target,
+            send_sem=sems[0],
+            recv_sem=sems[1],
+            device_id=peer,
+            device_id_type=pl.DeviceIdType.MESH,
+        )
+        copy.start()
+        return copy
+
+    def send(source, index, row, peer):
+        sent.append(remote(source, out_ref.at[index, row], (send_sem.at[len(sent)], recv_sem.at[index, row]), peer))
+
+    def arrived(index, row):
+        pltpu.make_async_copy(out_ref.at[index, row], out_ref.at[index, row], recv_sem.at[index, row]).wait()
+        return out_ref.at[index, row]
+
+    def swap(source, target, which):
+        moved = remote(source.at[1 - x], target.at[1], (swap_send.at[which, 1], swap_recv.at[which, 1]), turned)
+        kept = pltpu.make_async_copy(source.at[x], target.at[0], own_sem.at[2 + which])
+        pair = (source.at[x], target.at[0], (swap_send.at[which, 0], swap_recv.at[which, 0]), same)
+
+        @pl.when(y == c)
+        def _():
+            kept.start()
+
+        @pl.when(y != c)
+        def _():
+            remote(*pair)
+
+        def finish():
+            moved.wait()
+
+            @pl.when(y == c)
+            def _():
+                kept.wait()
+
+            @pl.when(y != c)
+            def _():
+                pltpu.make_async_remote_copy(
+                    src_ref=pair[0],
+                    dst_ref=pair[1],
+                    send_sem=pair[2][0],
+                    recv_sem=pair[2][1],
+                    device_id=same,
+                    device_id_type=pl.DeviceIdType.MESH,
+                ).wait()
+
+        return finish
+
+    rows = [lax.rem(z - k + planes, planes) * 2 + c for k in range(planes)]
+    little = []
+
+    def send_small(source, row, peer):
+        little.append(
+            remote(source, small_out.at[row], (small_send.at[len(little)], small_recv.at[row]), peer)
+        )
+
+    def small_arrived(row):
+        pltpu.make_async_copy(small_out.at[row], small_out.at[row], small_recv.at[row]).wait()
+        return small_out.at[row]
+
+    for peer in (*to_z, to_c):
+        send_small(small_ref, dp, peer)
+    for peer in to_z:
+        send(piece_ref, mp, dp, peer)
+    for peer in (to_x, to_y, to_c):
+        send(piece_ref, mp, dp, peer)
+    finishes = [swap(token_ref, token_out, 0)]
+    for k in range(planes):
+        if k > 0:
+            send_small(small_arrived(rows[k]), rows[k], to_c)
+            block = arrived(mp, rows[k])
+            for peer in (to_x, to_y, to_c):
+                send(block, mp, rows[k], peer)
+            send(arrived(corner, rows[k - 1]), corner, rows[k - 1], to_c)
+        block = arrived(side, rows[k])
+        if k % 2 == 0:
+            send(block, side, rows[k], to_y)
+        send(block, side, rows[k], to_c)
+        block = arrived(across, rows[k])
+        if k % 2 == 1:
+            send(block, across, rows[k], to_x)
+        send(block, across, rows[k], to_c)
+    finishes.append(swap(cot_ref, cot_out, 1))
+    send(arrived(corner, rows[-1]), corner, rows[-1], to_c)
+    for k in range(planes):
+        beside = rows[k] + 1 - 2 * c
+        small_arrived(beside)
+        for index in (mp, side, across, corner):
+            arrived(index, beside)
+    for copy in sent + little:
+        copy.wait_send()
+    for finish in finishes:
+        finish()
+    for copy in locals_:
+        copy.wait()
+
+
+def gather_four(planes, piece, small, tokens, cotangent):
+    count = (planes - 1) + 3 * planes + planes + 3 * planes
+    anywhere = pl.BlockSpec(memory_space=pl.ANY)
+    return pl.pallas_call(
+        functools.partial(gather_kernel, planes),
+        in_specs=[anywhere] * 4,
+        out_specs=[anywhere] * 4,
+        out_shape=[
+            jax.ShapeDtypeStruct((4, 2 * planes) + piece.shape, piece.dtype),
+            jax.ShapeDtypeStruct((2 * planes,) + small.shape, small.dtype),
+            jax.ShapeDtypeStruct(tokens.shape, tokens.dtype),
+            jax.ShapeDtypeStruct(cotangent.shape, cotangent.dtype),
+        ],
+        scratch_shapes=[
+            pltpu.SemaphoreType.DMA((count,)),
+            pltpu.SemaphoreType.DMA((4, 2 * planes)),
+            pltpu.SemaphoreType.DMA((2 * planes,)),
+            pltpu.SemaphoreType.DMA((2 * planes,)),
+            pltpu.SemaphoreType.DMA((2, 2)),
+            pltpu.SemaphoreType.DMA((2, 2)),
+            pltpu.SemaphoreType.DMA((4,)),
+        ],
+        cost_estimate=pl.CostEstimate(flops=0, bytes_accessed=300 * 2 ** 20, transcendentals=0),
+        compiler_params=pltpu.CompilerParams(collective_id=0, has_side_effects=True),
+        name="gather_four",
+    )(piece, small, tokens, cotangent)
+
+
+GROUPS, PARTS = 4, 2
+
+
+def tiles(width, body):
+    whole = width // 256
+
+    def step(j, carry):
+        body(pl.multiple_of(j * 256, 256), 256)
+        return carry
+
+    lax.fori_loop(0, whole, step, 0)
+    if width % 256:
+        body(whole * 256, width % 256)
+
+
+def units_kernel(back, *refs):
+    if back:
+        (x_ref, wa_ref, wb_ref, slope_ref, out_ref, rows_ref, left_ref, sums_ref, *scratch) = refs
+    else:
+        (x_ref, wa_ref, wb_ref, bias_ref, out_ref, rows_ref, left_ref, slope_ref, *scratch) = refs
+    (wa, wb, rows, own, far, beside, corner, got_c, got_f, give, got_y, left, slope,
+     in_sem, send_sem, recv_sem, out_sem) = scratch
+    width = wa.shape[1]
+    part = rows.shape[2]
+    dp, mp = lax.axis_index("dp"), lax.axis_index("mp")
+    to_c = (dp + 1 - 2 * (dp % 2), mp)
+    to_y = (dp, mp + 2 - 4 * (mp // 2))
+    loads = [
+        pltpu.make_async_copy(x_ref.at[pl.ds(h * part, part)], rows.at[0, h], in_sem.at[h]) for h in range(PARTS)
+    ]
+    loads += [pltpu.make_async_copy(wa_ref, wa, in_sem.at[2]), pltpu.make_async_copy(wb_ref, wb, in_sem.at[3])]
+    for load in loads:
+        load.start()
+    barrier = pltpu.get_barrier_semaphore()
+    for peer in (to_c, to_y):
+        pl.semaphore_signal(barrier, inc=1, device_id=peer, device_id_type=pl.DeviceIdType.MESH)
+    pl.semaphore_wait(barrier, 2)
+    sent = []
+
+    def send(source, target, slot, peer):
+        copy = pltpu.make_async_remote_copy(
+            src_ref=source,
+            dst_ref=target,
+            send_sem=send_sem.at[slot],
+            recv_sem=recv_sem.at[slot],
+            device_id=peer,
+            device_id_type=pl.DeviceIdType.MESH,
+        )
+        copy.start()
+        sent.append(copy)
+        return copy
+
+    kinds = {name: i for i, name in enumerate(("y", "c", "f", "beside", "corner", "give"))}
+
+    def slot_of(kind, h):
+        return kinds[kind] * PARTS + h
+
+    arrivals = {}
+    for h in range(PARTS):
+        loads[h].wait()
+        arrivals["y", h] = send(rows.at[0, h], rows.at[2, h], slot_of("y", h), to_y)
+        arrivals["c", h] = send(rows.at[0, h], rows.at[1, h], slot_of("c", h), to_c)
+    stores = []
+    busy = [[], []]
+    order = [(0, 0), (0, 1), (1, 0), (1, 1), (2, 0), (3, 0), (2, 1), (3, 1)]
+
+    def place(index):
+        group, h = order[index]
+        return pl.ds((group * PARTS + h) * part, part)
+
+    def fetch(index):
+        copy = pltpu.make_async_copy(slope_ref.at[place(index)], slope.at[index % 2], in_sem.at[4 + index % 2])
+        copy.start()
+        return copy
+
+    def store(source, target, index, kind):
+        copy = pltpu.make_async_copy(source, target, out_sem.at[kind, index])
+        copy.start()
+        return copy
+
+    fetched = {}
+    if back:
+        sums_ref[...] = jnp.zeros_like(sums_ref)
+        fetched[0] = fetch(0)
+    loads[2].wait()
+    loads[3].wait()
+
+    def work(index, target):
+        group, h = order[index]
+        side = index % 2
+        for copy in busy[side]:
+            copy.wait()
+        busy[side] = []
+        source = rows.at[group, h]
+        if back:
+            fetched[index].wait()
+            if index + 1 < len(order):
+                fetched[index + 1] = fetch(index + 1)
+
+        def first(at, size):
+            span = pl.ds(at, size)
+            value = nn(source[...], wa[:, span])
+            if back:
+                value = bf(value * f32(slope[side, :, span]))
+                left[side, :, span] = value
+                sums_ref[:, span] += jnp.sum(f32(value), axis=0, keepdims=True)
+            else:
+                value = value + bias_ref[:, span]
+                square = value * value
+                bend = jnp.tanh(0.7978845608028654 * value * (1.0 + 0.044715 * square))
+                half = 0.5 * (1.0 + bend)
+                left[side, :, span] = bf(value * half)
+                slope[side, :, span] = bf(
+                    half + 0.5 * value * (1.0 - bend * bend) * 0.7978845608028654 * (1.0 + 0.134145 * square)
+                )
+
+        tiles(width, first)
+        busy[side].append(store(left.at[side], left_ref.at[place(index)], index, 0))
+        if not back:
+            busy[side].append(store(slope.at[side], slope_ref.at[place(index)], index, 1))
+        stores.append(store(source, rows_ref.at[place(index)], index, 2))
+
+        def second(at, size):
+            span = pl.ds(at, size)
+            target[:, span] = nt(left[side], wb[span, :]).astype(target.dtype)
+
+        tiles(width, second)
+
+    def combine(h):
+        arrivals["corner", h].wait_recv()
+        give[h] = bf(far[h] + f32(got_f[h]))
+        arrivals["give", h] = send(give.at[h], got_y.at[h], slot_of("give", h), to_y)
+
+    work(0, own.at[0])
+    work(1, own.at[1])
+    for h in range(PARTS):
+        arrivals["c", h].wait_recv()
+        work(2 + h, beside.at[h])
+        arrivals["beside", h] = send(beside.at[h], got_c.at[h], slot_of("beside", h), to_c)
+    for h in range(PARTS):
+        arrivals["y", h].wait_recv()
+        arrivals["f", h] = send(rows.at[2, h], rows.at[3, h], slot_of("f", h), to_c)
+        work(4 + 2 * h, far.at[h])
+        arrivals["f", h].wait_recv()
+        work(5 + 2 * h, corner.at[h])
+        arrivals["corner", h] = send(corner.at[h], got_f.at[h], slot_of("corner", h), to_c)
+        combine(h)
+    for h in range(PARTS):
+        arrivals["beside", h].wait_recv()
+        arrivals["give", h].wait_recv()
+        out_ref[pl.ds(h * part, part), :] = own[h] + f32(got_c[h]) + f32(got_y[h])
+    for copy in sent:
+        copy.wait_send()
+    for copy in stores + busy[0] + busy[1]:
+        copy.wait()
+
+
+def units(back, x, wa, wb, extra):
+    rows, width = x.shape
+    part = rows // PARTS
+    half = jax.ShapeDtypeStruct((GROUPS * rows, width), jnp.bfloat16)
+    anywhere = pl.BlockSpec(memory_space=pl.ANY)
+    inside = pl.BlockSpec(memory_space=pltpu.VMEM)
+    thin, wide = pltpu.VMEM((PARTS, part, width), jnp.bfloat16), pltpu.VMEM((PARTS, part, width), jnp.float32)
+    count = 6 * PARTS
+    return pl.pallas_call(
+        functools.partial(units_kernel, back),
+        in_specs=[anywhere, anywhere, anywhere, anywhere if back else inside],
+        out_specs=[inside, anywhere, anywhere, inside if back else anywhere],
+        out_shape=[
+            jax.ShapeDtypeStruct((rows, width), jnp.float32),
+            half,
+            half,
+            jax.ShapeDtypeStruct((1, width), jnp.float32) if back else half,
+        ],
+        scratch_shapes=[
+            pltpu.VMEM(wa.shape, jnp.bfloat16),
+            pltpu.VMEM(wb.shape, jnp.bfloat16),
+            pltpu.VMEM((GROUPS, PARTS, part, width), jnp.bfloat16),
+            wide, wide, thin, thin, thin, thin, thin, thin, thin, thin,
+            pltpu.SemaphoreType.DMA((6,)),
+            pltpu.SemaphoreType.DMA((count,)),
+            pltpu.SemaphoreType.DMA((count,)),
+            pltpu.SemaphoreType.DMA((3, GROUPS * PARTS)),
+        ],
+        cost_estimate=pl.CostEstimate(
+            flops=60 * 10 ** 9, bytes_accessed=60 * 2 ** 20, transcendentals=0
+        ),
+        compiler_params=pltpu.CompilerParams(
+            collective_id=2 if back else 1, has_side_effects=True, vmem_limit_bytes=56 * 2 ** 20
+        ),
+        name="units_back" if back else "units",
+    )(x, wa, wb, extra)
+
+
+def settle_kernel(planes, keep_ref, send_ref, piece_ref, out_ref, pieces, outgo, income, total, from_y, from_x, to_give,
+                  final, from_z, load_sem, c_send, c_recv, xy_send, xy_recv, z_send, z_recv):
+    dp, mp = lax.axis_index("dp"), lax.axis_index("mp")
+    z, c = dp // 2, dp % 2
+    y, x = mp // 2, mp % 2
+    to_x, to_y = (dp, mp + 1 - 2 * x), (dp, mp + 2 - 4 * y)
+    to_c = (dp + 1 - 2 * c, mp)
+    others = [lax.rem(z + k, planes) for k in range(1, planes)]
+    barrier = pltpu.get_barrier_semaphore()
+    for peer in (to_x, to_y, to_c, *[(other * 2 + c, mp) for other in others]):
+        pl.semaphore_signal(barrier, inc=1, device_id=peer, device_id_type=pl.DeviceIdType.MESH)
+    loads = []
+    for k, (far_y, far_x) in enumerate(((1, 1), (1, 0), (0, 1), (0, 0))):
+        index = 2 * (1 - y if far_y else y) + (1 - x if far_x else x)
+        loads.append(pltpu.make_async_copy(piece_ref.at[index], pieces.at[k], load_sem.at[k]))
+        loads[-1].start()
+    pl.semaphore_wait(barrier, 3 + len(others))
+    width = pieces.shape[2]
+    tall = keep_ref.shape[0] // planes
+    half = planes // 2
+
+    def remote(source, target, sems, slot, peer):
+        copy = pltpu.make_async_remote_copy(
+            src_ref=source,
+            dst_ref=target,
+            send_sem=sems[0].at[slot],
+            recv_sem=sems[1].at[slot],
+            device_id=peer,
+            device_id_type=pl.DeviceIdType.MESH,
+        )
+        copy.start()
+        return copy
+
+    def product(left_ref, k, write):
+        def body(at, size):
+            span = pl.ds(at, size)
+            value = nn(left_ref[...], pieces[k, :, span])
+            for block in range(planes):
+                write(block, span, value[block * tall:(block + 1) * tall])
+
+        tiles(width, body)
+
+    crossing = []
+    for k in range(4):
+        loads[k].wait()
+
+        def put(block, span, value, k=k):
+            outgo[k, block, :, span] = bf(value)
+
+        product(send_ref, k, put)
+        crossing.append(remote(outgo.at[k], income.at[k], (c_send, c_recv), k, to_c))
+    first, second = pl.ds(0, half), pl.ds(half, half)
+    sent = []
+
+    def chip(k):
+        crossing[k].wait_recv()
+
+        def put(block, span, value, k=k):
+            total[k, block, :, span] = bf(value + f32(income[k, block, :, span]))
+
+        product(keep_ref, k, put)
+
+    def add(target, base, extras):
+        for block in range(half):
+            value = f32(base[block])
+            for extra in extras:
+                value = value + f32(extra[block])
+            target[block] = value.astype(target.dtype)
+
+    sems = (xy_send, xy_recv)
+    chip(0)
+    y0 = remote(total.at[0, first], from_y.at[0], sems, 0, to_y)
+    x0 = remote(total.at[0, second], from_x.at[0], sems, 1, to_x)
+    chip(1)
+    y1 = remote(total.at[1, first], from_y.at[1], sems, 2, to_y)
+    chip(2)
+    x1 = remote(total.at[2, second], from_x.at[1], sems, 3, to_x)
+    chip(3)
+    y0.wait_recv()
+    add(to_give.at[0], total.at[2, first], [from_y.at[0]])
+    x2 = remote(to_give.at[0], from_x.at[2], sems, 4, to_x)
+    x0.wait_recv()
+    add(to_give.at[1], total.at[1, second], [from_x.at[0]])
+    y2 = remote(to_give.at[1], from_y.at[2], sems, 5, to_y)
+    y1.wait_recv()
+    x2.wait_recv()
+    add(final.at[first], total.at[3, first], [from_y.at[1], from_x.at[2]])
+    x1.wait_recv()
+    y2.wait_recv()
+    add(final.at[second], total.at[3, second], [from_x.at[1], from_y.at[2]])
+    leaving = []
+    for k, other in enumerate(others):
+        leaving.append(remote(final.at[other], from_z.at[k], (z_send, z_recv), k, (other * 2 + c, mp)))
+    value = f32(final[z])
+    for k in range(len(others)):
+        leaving[k].wait_recv()
+        value = value + f32(from_z[k])
+    out_ref[...] = value * (1.0 / (2 * planes))
+    for copy in (*crossing, y0, x0, y1, x1, x2, y2, *leaving):
+        copy.wait_send()
+
+
+def settle_columns(planes, keep, send, pieces):
+    rows, width = keep.shape[0], pieces.shape[2]
+    tall = rows // planes
+    half = planes // 2
+    low = lambda *shape: pltpu.VMEM((*shape, tall, width), jnp.bfloat16)
+    inside = pl.BlockSpec(memory_space=pltpu.VMEM)
+    return pl.pallas_call(
+        functools.partial(settle_kernel, planes),
+        in_specs=[inside, inside, pl.BlockSpec(memory_space=pl.ANY)],
+        out_specs=inside,
+        out_shape=jax.ShapeDtypeStruct((tall, width), jnp.float32),
+        scratch_shapes=[
+            pltpu.VMEM(pieces.shape, jnp.bfloat16),
+            low(4, planes), low(4, planes), low(4, planes),
+            low(3, half), low(3, half), low(2, half), low(planes), low(planes - 1),
+            pltpu.SemaphoreType.DMA((4,)),
+            pltpu.SemaphoreType.DMA((4,)), pltpu.SemaphoreType.DMA((4,)),
+            pltpu.SemaphoreType.DMA((6,)), pltpu.SemaphoreType.DMA((6,)),
+            pltpu.SemaphoreType.DMA((planes - 1,)), pltpu.SemaphoreType.DMA((planes - 1,)),
+        ],
+        cost_estimate=pl.CostEstimate(flops=16 * 10 ** 9, bytes_accessed=60 * 2 ** 20, transcendentals=0),
+        compiler_params=pltpu.CompilerParams(
+            collective_id=3, has_side_effects=True, vmem_limit_bytes=58 * 2 ** 20
+        ),
+        name="settle_columns",
+    )(keep, send, pieces)
+
+
 def bf(value):
     return value.astype(jnp.bfloat16)
 
@@ -660,18 +1143,6 @@
     def sum_z(value):
         return lax.psum_scatter(value, AXES, axis_index_groups=along_z, scatter_dimension=0, tiled=True)
 
-    def spread_in(value):
-        mine = lax.dynamic_index_in_dim(value, col, 0, keepdims=False)
-        theirs = lax.dynamic_index_in_dim(value, 1 - col, 0, keepdims=False)
-        return jnp.concatenate([turn_yc(mine), turn_yc(go(theirs, over_x))], axis=0)
-
-    def spread_out(value):
-        mine = turn_yc(value[:local])
-        theirs = go(turn_yc(value[local:]), over_x)
-        front = jnp.where(col == 0, mine, theirs)
-        back = jnp.where(col == 0, theirs, mine)
-        return f32(jnp.stack([front, back]))
-
     ranks = jnp.stack([2 * core + col, 2 * core + 1 - col])
     others = jnp.stack([2 * (1 - core) + col, 2 * (1 - core) + 1 - col])
 
@@ -691,166 +1162,288 @@
         parts = value.reshape(value.shape[0], planes, 2, -1)
         return lax.dynamic_index_in_dim(parts, which, 2, keepdims=False).reshape(value.shape[0], -1)
 
+    def chip_sums(left, right):
+        keep, send = core_columns(left, core), core_columns(left, 1 - core)
+        size = right.shape[1] // 4
+
+        def one(near_y, near_x):
+            index = 2 * (row if near_y else 1 - row) + (col if near_x else 1 - col)
+            piece = lax.dynamic_slice_in_dim(right, index * size, size, axis=1)
+            return add_pair(tn(keep, piece), go(bf(tn(send, piece)), over_c))
+
+        return one(False, False), one(False, True), one(True, False), one(True, True)
+
     def gather_dp(piece):
         return lax.all_gather(piece, "dp", axis=0, tiled=True)
 
-    def group(value):
-        beside = go(value, over_c)
-        across = go(value, over_y)
-        return jnp.concatenate([value, beside, across, go(across, over_c)], axis=0)
-
-    def ungroup(multiply, rows):
-        far = multiply(rows // 2, rows // 2)
-        near = multiply(0, rows // 2)
-        quarter = rows // 4
-        sent = far[:quarter] + f32(go(bf(far[quarter:]), over_c))
-        back = go(bf(sent), over_y)
-        return near[:quarter] + f32(go(bf(near[quarter:]), over_c)) + f32(back)
-
-    small = jnp.concatenate(
-        [norm_gain, norm_shift, attn_bias, out_bias, fc_bias[:, None, :]], axis=1
-    )
-    small = lax.all_gather(small, "dp", axis=0)
-    small = jnp.transpose(small, (1, 2, 0, 3)).reshape(LAYERS, 9, width)
+    def after(values, *done):
+        return lax.optimization_barrier((values, done))[0]
+
+    def fence(*values):
+        return lax.optimization_barrier(values)
+
+    def stacked(layer):
+        qkv = qkv_weight[layer]
+        return jnp.stack([qkv[:, :width], qkv[:, width:2 * width], qkv[:, 2 * width:], proj_weight[layer]])
+
+    small = f32(jnp.concatenate([norm_gain, norm_shift, attn_bias, out_bias, fc_bias[:, None, :]], axis=1))
+    count = small.shape[0] * small.shape[1]
+    small = jnp.pad(small.reshape(count, -1), ((0, -count % 8), (0, 0)))
+    piece = lax.dynamic_index_in_dim(stacked(0), mp_rank, 0, keepdims=False)
+    full, small, token_rows, cot_rows = gather_four(planes, piece, small, tokens, cotangent)
+    first_four = full.reshape(4, width, width)
+    small = jnp.transpose(small[:, :count].reshape(-1, LAYERS, 9, width // (2 * planes)), (1, 2, 0, 3))
+    small = small.reshape(LAYERS, 9, width)
     units_bias = turn_xc(small[:, 8])
-    small = f32(small)
-
-    fetched = []
-    for layer in range(LAYERS):
-        qkv = qkv_weight[layer]
-        fetched.append(
-            dict(
-                k=gather_dp(qkv[:, width:2 * width]),
-                v=gather_dp(qkv[:, 2 * width:]),
-                q=gather_dp(qkv[:, :width]),
-                proj=gather_dp(proj_weight[layer]),
-                fc=turn_xc(gather_dp(fc_weight[layer])),
-                fc2=turn_xc(gather_dp(fc2_weight[layer].T)),
-                gain=small[layer, 0:2],
-                shift=small[layer, 2:4],
-                bias_in=small[layer, 4:6],
-                bias_out=small[layer, 6:8],
-                fc_b=f32(units_bias[layer]),
-            )
-        )
-
-    hidden = f32(spread_in(tokens))
-    grad_in = spread_in(cotangent)
-    saved = []
-    for layer in range(LAYERS):
-        w = fetched[layer]
-        centred, rate = norm_parts(hidden)
-        normed = bf(centred * rate * w["gain"][0] + w["shift"][0])
+
+    fc_slice = [None] * LAYERS
+    fc2_slice = [None] * LAYERS
+    fc_slice[0] = gather_dp(fc_weight[0])
+    fc2_slice[0] = gather_dp(fc2_weight[0].T)
+    qkv1 = qkv_weight[1]
+    pair_one = gather_dp(after(jnp.where(row == 0, qkv1[:, :width], qkv1[:, width:2 * width]), small))
+    pair_two = gather_dp(after(jnp.where(col == 0, qkv1[:, 2 * width:], proj_weight[1]), small))
+
+    def pair_send(whole, over):
+        tall = whole.shape[0] // 2
+        return go(lax.dynamic_slice_in_dim(whole, core * tall, tall, axis=0), over)
+
+    def pair_join(whole, got, beside, bit):
+        other = jnp.concatenate([jnp.where(core == 0, got, beside), jnp.where(core == 0, beside, got)], axis=0)
+        return jnp.where(bit == 0, whole, other), jnp.where(bit == 0, other, whole)
+
+    def turned_weight(slice_, moved):
+        return jnp.where(col == core, slice_, moved)
+
+    def normal(value, layer, which):
+        centred, rate = norm_parts(value)
+        return bf(centred * rate * small[layer, which] + small[layer, 2 + which])
+
+    def attend(layer, hidden, w):
+        normed = normal(hidden, layer, 0)
         key = bf(nn(normed, w["k"]))
         key_other = go(key, over_c)
-        value = bf(nn(normed, w["v"]) + w["bias_in"][1])
+        value = bf(nn(normed, w["v"]) + small[layer, 5])
         value_other = go(value, over_c)
-        query = bf(nn(normed, w["q"]) + w["bias_in"][0])
-        attended, lse = attention(place, slot, query, key, key_other, value, value_other)
-        middle = hidden + nn(attended, w["proj"]) + w["bias_out"][0]
-        centred, rate = norm_parts(middle)
-        normed_two = bf(centred * rate * w["gain"][1] + w["shift"][1])
-        rows_in = group(normed_two)
-        inner = nn(rows_in, w["fc"]) + w["fc_b"]
-        active = bf(jax.nn.gelu(inner, approximate=True))
-
-        def down(start, rows, active=active, w=w):
-            return nt(active[start:start + rows], w["fc2"])
-
-        output = middle + ungroup(down, rows_in.shape[0]) + w["bias_out"][1]
-        saved.append((hidden, normed, query, key, key_other, value, value_other, attended, lse, middle, rows_in, inner, active))
-        hidden = output
-    outputs = spread_out(bf(hidden))
-
-    grad = f32(grad_in)
+        query = bf(nn(normed, w["q"]) + small[layer, 4])
+        return normed, query, key, key_other, value, value_other
+
+    def project(layer, hidden, attended, w):
+        middle = hidden + nn(attended, w["proj"]) + small[layer, 6]
+        return middle, normal(middle, layer, 1)
+
+    saved = []
+    hidden = f32(token_rows.reshape(-1, width))
+    w = dict(q=first_four[0], k=first_four[1], v=first_four[2], proj=first_four[3])
+    parts = attend(0, hidden, w)
+    moved_fc = go(after(fc_slice[0], units_bias), swap_xc)
+    *parts, moved_fc, fc2_now, pair_one = fence(*parts, moved_fc, fc2_slice[0], pair_one)
+    normed, query, key, key_other, value, value_other = parts
+    fc_slice[1] = gather_dp(after(fc_weight[1], normed))
+    moved_fc2 = go(fc2_now, swap_xc)
+    got_one = pair_send(pair_one, over_y)
+    attended, lse = attention(place, slot, query, key, key_other, value, value_other)
+    attended, lse, moved_fc2, got_one = fence(attended, lse, moved_fc2, got_one)
+    fc2_slice[1] = gather_dp(after(fc2_weight[1].T, attended))
+    middle, normed_two = project(0, hidden, attended, w)
+    w["fc"] = turned_weight(fc_slice[0], moved_fc)
+    w["fc2"] = turned_weight(fc2_now, moved_fc2)
+    beside_one = go(got_one, over_c)
+    middle, normed_two, w["fc"], w["fc2"], beside_one, pair_two = fence(
+        middle, normed_two, w["fc"], w["fc2"], beside_one, pair_two
+    )
+    got_two = pair_send(pair_two, over_x)
+    ff_out, rows_in, active, slope = units(False, normed_two, w["fc"], w["fc2"], units_bias[0:1])
+    ff_out, rows_in, active, slope, got_two, fc_now = fence(ff_out, rows_in, active, slope, got_two, fc_slice[1])
+    saved.append((hidden, *parts, attended, lse, middle, rows_in, active, slope, w))
+    moved_fc = go(fc_now, swap_xc)
+    beside_two = go(got_two, over_c)
+    w = dict()
+    w["q"], w["k"] = pair_join(pair_one, got_one, beside_one, row)
+    w["v"], w["proj"] = pair_join(pair_two, got_two, beside_two, col)
+    hidden = middle + ff_out + small[0, 7]
+    *parts, moved_fc, fc2_now = fence(*attend(1, hidden, w), moved_fc, fc2_slice[1])
+    normed, query, key, key_other, value, value_other = parts
+    moved_fc2 = go(fc2_now, swap_xc)
+    attended, lse = attention(place, slot, query, key, key_other, value, value_other)
+    attended, lse, moved_fc2 = fence(attended, lse, moved_fc2)
+    middle, normed_two = project(1, hidden, attended, w)
+    w["fc"] = turned_weight(fc_now, moved_fc)
+    w["fc2"] = turned_weight(fc2_now, moved_fc2)
+    middle, normed_two, w["fc"], w["fc2"] = fence(middle, normed_two, w["fc"], w["fc2"])
+    ff_out, rows_in, active, slope = units(False, normed_two, w["fc"], w["fc2"], units_bias[1:2])
+    saved.append((hidden, *parts, attended, lse, middle, rows_in, active, slope, w))
+    final = bf(middle + ff_out + small[1, 7])
+
     factor = 1.0 / lax.axis_size("dp")
-    third, fourth = 3 * width // 4, width // 4
     results = [None] * LAYERS
-    for layer in reversed(range(LAYERS)):
-        w = fetched[layer]
-        (hidden, normed, query, key, key_other, value, value_other, attended, lse, middle, rows_in, inner, active) = saved[layer]
-        out_grad = bf(grad)
-        mlp_bias_grad = jnp.sum(f32(out_grad), axis=0)
-        rows_grad = group(out_grad)
-        _, gelu_back = jax.vjp(lambda v: jax.nn.gelu(v, approximate=True), inner)
-        inner_grad = bf(gelu_back(nn(rows_grad, w["fc2"]))[0])
-
-        def up(start, rows, inner_grad=inner_grad, w=w):
-            return nt(inner_grad[start:start + rows], w["fc"])
-
-        normed_two_grad = ungroup(up, rows_in.shape[0])
-        fc2_grad = bf(tn(rows_grad, active))
-        fc_grad = bf(tn(rows_in, inner_grad))
-        units_grad = jnp.sum(f32(inner_grad), axis=0)
-        part, gain_two, shift_two = norm_back(normed_two_grad, middle, w["gain"][1])
+
+    def units_split(value):
+        halves = value.reshape(2, -1, width)
+        kept = lax.dynamic_index_in_dim(halves, col, 0, keepdims=False)
+        return kept, lax.dynamic_index_in_dim(halves, 1 - col, 0, keepdims=False)
+
+    def mlp_back(layer, out_grad, *held):
+        (*_, active, slope, w) = saved[layer]
+        return units(True, out_grad, w["fc2"], w["fc"], slope)
+
+    def middle_back(layer, grad, da2):
+        middle, w = saved[layer][9], saved[layer][-1]
+        part, gain, shift = norm_back(da2, middle, small[layer, 1])
         middle_grad = grad + part
-        branch_grad = bf(middle_grad)
-        attn_out_grad = jnp.sum(f32(branch_grad), axis=0)
-        attended_grad = bf(nt(branch_grad, w["proj"]))
-        dq, dk_mine, dk_theirs, dv_mine, dv_theirs = attention_back(
-            place, slot, query, key, key_other, value, value_other, attended_grad, attended, lse
-        )
-        dk = bf(dk_mine + f32(go(dk_theirs, over_c)))
-        dv = bf(dv_mine + f32(go(dv_theirs, over_c)))
-        bias_in_grad = jnp.stack([jnp.sum(f32(dq), axis=0), jnp.sum(f32(dv), axis=0)])
+        branch = bf(middle_grad)
+        return middle_grad, branch, bf(nt(branch, w["proj"])), gain, shift, jnp.sum(f32(branch), axis=0)
+
+    def heads_back(layer, attended_grad):
+        hidden, normed, query, key, key_other, value, value_other, attended, lse = saved[layer][:9]
+        return attention_back(place, slot, query, key, key_other, value, value_other, attended_grad, attended, lse)
+
+    def input_back(layer, middle_grad, dq, dk, dv):
+        hidden, w = saved[layer][0], saved[layer][-1]
         normed_grad = nt(dq, w["q"]) + nt(dk, w["k"]) + nt(dv, w["v"])
-        part, gain_one, shift_one = norm_back(normed_grad, hidden, w["gain"][0])
-        grad = middle_grad + part
-
-        mixed = jnp.concatenate([dq, dk, dv], axis=1)
-        keep_cols = core_columns(normed, core), core_columns(attended, core)
-        send_cols = core_columns(normed, 1 - core), core_columns(attended, 1 - core)
-
-        def column(cols, near_y, near_x):
-            index = 2 * (row if near_y else 1 - row) + (col if near_x else 1 - col)
-            first = lax.dynamic_slice_in_dim(mixed, index * third, third, axis=1)
-            second = lax.dynamic_slice_in_dim(branch_grad, index * fourth, fourth, axis=1)
-            return bf(jnp.concatenate([tn(cols[0], first), tn(cols[1], second)], axis=1))
-
-        def chip_sum(near_y, near_x):
-            return add_pair(column(keep_cols, near_y, near_x), go(column(send_cols, near_y, near_x), over_c))
-
-        def row_sum(near_x):
-            return add_pair(chip_sum(True, near_x), go(chip_sum(False, near_x), over_y))
-
-        far_side = go(row_sum(False), over_x)
-        attn_part = sum_z(add_pair(row_sum(True), far_side))
-
-        def units_sum(value):
-            quarters = value.reshape(planes, 2, -1, width)
-            kept = lax.dynamic_index_in_dim(quarters, col, 1, keepdims=False)
-            sent = lax.dynamic_index_in_dim(quarters, 1 - col, 1, keepdims=False)
-            part = add_pair(kept, go(sent, over_x)).reshape(-1, width)
-            return turn_xc(sum_z(part))
-
-        fc2_part = units_sum(fc2_grad)
-        fc_part = units_sum(fc_grad)
-        sums = jnp.concatenate(
-            [
-                jnp.stack([gain_one, gain_two, shift_one, shift_two]),
-                bias_in_grad,
-                jnp.stack([attn_out_grad, mlp_bias_grad]),
-            ],
-            axis=0,
-        )
-        results[layer] = (attn_part, fc_part, fc2_part, sums, units_grad)
-
-    input_grad = spread_out(bf(grad))
-    sums = jnp.stack([entry[3] for entry in results])
-    sums = sums + go(sums, over_x)
-    sums = sums + go(sums, over_y)
-    units = turn_xc(jnp.stack([entry[4] for entry in results]))
-    sums = jnp.concatenate([sums, units[:, None, :]], axis=1)
-    sums = lax.psum_scatter(sums, "dp", scatter_dimension=2, tiled=True) * factor
-    attn_part = jnp.stack([f32(entry[0]) for entry in results]) * factor
+        part, gain, shift = norm_back(normed_grad, hidden, small[layer, 0])
+        return middle_grad + part, gain, shift
+
+    def mixed_of(dq, dkm, dkt, dvm, dvt):
+        dk = bf(dkm + f32(go(dkt, over_c)))
+        dv = bf(dvm + f32(go(dvt, over_c)))
+        return dq, dk, dv
+
+    def last_sum(parts, away, side):
+        return bf(f32(parts[3]) + f32(away) + f32(side))
+
+    turn_far = pairs_of(planes, lambda z, c, y, x: (z, y, c, 1 - x))
+
+    def regroup(value):
+        return go(value[:local], swap_yc), go(value[local:], turn_far)
+
+    def settle(value, mine, theirs):
+        mine = jnp.where(row == core, value[:local], mine)
+        return f32(jnp.stack([jnp.where(col == 0, mine, theirs), jnp.where(col == 0, theirs, mine)]))
+
+    def bias_sums(gains, shifts, dq, dv, branch_sum, out_grad):
+        return jnp.stack(
+            [*gains, *shifts, jnp.sum(f32(dq), axis=0), jnp.sum(f32(dv), axis=0), branch_sum, jnp.sum(f32(out_grad), axis=0)]
+        )
+
+    def row_parts(left):
+        columns = jnp.transpose(left).reshape(planes, 2, -1, left.shape[0])
+        keep = lax.dynamic_index_in_dim(columns, core, 1, keepdims=False)
+        send = lax.dynamic_index_in_dim(columns, 1 - core, 1, keepdims=False)
+        return keep.reshape(-1, left.shape[0]), send.reshape(-1, left.shape[0])
+
+    grad = f32(cot_rows.reshape(-1, width))
+    out_grad = cot_rows.reshape(-1, width)
+    final, out_grad = fence(final, out_grad)
+    da2, rows_grad, inner_grad, units_sum = mlp_back(1, out_grad)
+    final, da2, rows_grad, inner_grad, units_sum = fence(final, da2, rows_grad, inner_grad, units_sum)
+    fc2_grad = bf(tn(rows_grad, saved[1][11]))
+    fc2_grad, rows_in = fence(fc2_grad, saved[1][10])
+    fc2_sum = sum_z(fc2_grad)
+    fc_grad = bf(tn(rows_in, inner_grad))
+    middle_grad, branch, attended_grad, gain_two, shift_two, attn_out_grad = middle_back(1, grad, da2)
+    proj_parts = chip_sums(saved[1][7], branch)
+    fc_grad, middle_grad, branch, attended_grad, *proj_parts = fence(
+        fc_grad, middle_grad, branch, attended_grad, *proj_parts
+    )
+    fc_sum = sum_z(fc_grad)
+    proj_far = go(proj_parts[0], over_y)
+    proj_near = go(proj_parts[1], over_y)
+    final_moved = regroup(final)
+    back = fence(*heads_back(1, attended_grad), fc2_sum, proj_far, proj_near, *final_moved)
+    fc2_sum, proj_far, proj_near, *final_moved = back[5:]
+    dq, dk, dv = mixed_of(*back[:5])
+    dq, dk, dv = fence(dq, dk, dv)
+    below, gain_one, shift_one = input_back(1, middle_grad, dq, dk, dv)
+    out_grad_low = bf(below)
+    sums_one = bias_sums((gain_one, gain_two), (shift_one, shift_two), dq, dv, attn_out_grad, out_grad)
+    out_grad_low, below, dq, dk, dv, sums_one = fence(out_grad_low, below, dq, dk, dv, sums_one)
+    parts = chip_sums(saved[1][1], jnp.concatenate([dq, dk, dv], axis=1))
+    out_grad_low, *parts = fence(out_grad_low, *parts)
+    side_far = go(parts[0], over_x)
+    side_near = go(parts[2], over_x)
+    proj_side = go(add_pair(proj_parts[2], proj_far), over_x)
+    fc2_kept, fc2_sent = units_split(fc2_sum)
+    fc2_away = go(fc2_sent, over_x)
+    da2, rows_grad, inner_grad, units_low = mlp_back(0, out_grad_low)
+    da2, rows_grad, inner_grad, units_low, side_far, side_near, fc_sum, proj_side, fc2_away = fence(
+        da2, rows_grad, inner_grad, units_low, side_far, side_near, fc_sum, proj_side, fc2_away
+    )
+    proj_sum = sum_z(last_sum(proj_parts, proj_near, proj_side))
+    fc2_high = add_pair(fc2_kept, fc2_away)
+    fc_kept, fc_sent = units_split(fc_sum)
+    side_far = add_pair(parts[1], side_far)
+    fc2_grad = bf(tn(rows_grad, saved[0][11]))
+    fc2_grad, rows_in = fence(fc2_grad, saved[0][10])
+    fc2_sum = sum_z(fc2_grad)
+    fc_grad = bf(tn(rows_in, inner_grad))
+    middle_grad, branch, attended_grad, gain_two, shift_two, attn_out_grad = middle_back(0, below, da2)
+    low_parts = chip_sums(saved[0][7], branch)
+    fc_sent, fc_grad, middle_grad, branch, attended_grad, side_far, *low_parts = fence(
+        fc_sent, fc_grad, middle_grad, branch, attended_grad, side_far, *low_parts
+    )
+    away = go(side_far, over_y)
+    fc_away = go(fc_sent, over_x)
+    fc_sum = sum_z(fc_grad)
+    low_far = go(low_parts[0], over_y)
+    low_near = go(low_parts[1], over_y)
+    back = fence(*heads_back(0, attended_grad), fc_away, low_far, low_near, away, proj_sum, fc2_sum)
+    fc_away, low_far, low_near, away, proj_sum, fc2_sum = back[5:]
+    results_one = [add_pair(fc_kept, fc_away), fc2_high, proj_sum]
+    dq, dk, dv = mixed_of(*back[:5])
+    qkv_joined = bf(f32(parts[3]) + f32(side_near) + f32(away))
+    dq, dk, dv, qkv_joined = fence(dq, dk, dv, qkv_joined)
+    qkv_sum = sum_z(qkv_joined)
+    lowest, gain_one, shift_one = input_back(0, middle_grad, dq, dk, dv)
+    sums_zero = bias_sums((gain_one, gain_two), (shift_one, shift_two), dq, dv, attn_out_grad, out_grad_low)
+    low = bf(lowest)
+    third = 3 * width // 4
+    mixed = jnp.concatenate([dq, dk, dv], axis=1)
+    pieces = jnp.stack([mixed[:, i * third:(i + 1) * third] for i in range(4)])
+    keep, send = row_parts(saved[0][1])
+    spread = (jnp.arange(4) == 2 * row + core).astype(jnp.float32)
+    sums = jnp.concatenate(
+        [
+            sums_zero,
+            sums_one,
+            (spread[None, :, None] * jnp.concatenate([units_low, units_sum], axis=0)[:, None, :]).reshape(2 * 4, width),
+        ]
+    )
+    fc2_kept, fc2_sent = units_split(fc2_sum)
+    low, sums, pieces, keep, send, fc2_sent, results_one = fence(low, sums, pieces, keep, send, fc2_sent, results_one)
+    results_one[0] = turn_xc(results_one[0])
+    results_one[1] = turn_xc(results_one[1])
+    low_moved = regroup(low)
+    fc2_away = go(fc2_sent, over_x)
+    low_side = go(add_pair(low_parts[2], low_far), over_x)
+    sums = lax.psum(sums, AXES)
+    qkv_low = settle_columns(planes, keep, send, pieces)
+    qkv_low, fc2_away, low_side, sums, fc_sum, qkv_sum, results_one, *low_moved = fence(
+        qkv_low, fc2_away, low_side, sums, fc_sum, qkv_sum, results_one, *low_moved
+    )
+    proj_low = sum_z(last_sum(low_parts, low_near, low_side))
+    fc_kept, fc_sent = units_split(fc_sum)
+    results_zero = [
+        turn_xc(add_pair(fc_kept, go(fc_sent, over_x))),
+        turn_xc(add_pair(fc2_kept, fc2_away)),
+        proj_low,
+    ]
+    outputs = settle(final, *final_moved)
+    input_grad = settle(low, *low_moved)
+    held = width // (2 * planes)
+    sums = lax.dynamic_slice_in_dim(sums, dp_rank * held, held, axis=1) * factor
+    unit_rows = lax.dynamic_index_in_dim(sums[16:].reshape(2, 4, held), mp_rank, 1, keepdims=False)
+    sums = sums[:16].reshape(2, 8, held)
+    qkv_high = f32(qkv_sum) * factor
+    results = [results_zero, results_one]
     return (
         outputs,
         input_grad,
-        attn_part[:, :, :third],
-        attn_part[:, :, third:],
-        jnp.stack([f32(entry[1]) for entry in results]) * factor,
-        jnp.stack([f32(entry[2]).T for entry in results]) * factor,
-        sums[:, 8],
+        jnp.stack([qkv_low, qkv_high]),
+        jnp.stack([f32(entry[2]) for entry in results]) * factor,
+        jnp.stack([f32(entry[0]) for entry in results]) * factor,
+        jnp.stack([f32(entry[1]).T for entry in results]) * factor,
+        unit_rows,
         sums[:, 0:2],
         sums[:, 2:4],
         sums[:, 4:6],

time: 1830 us -> 1640 us (0.90)
  Pallas kernels: 176 us -> 833 us
  waiting for transfers between devices: 655 us -> 126 us
  matrix products: 435 us -> 252 us
  starting transfers between devices: 138 us -> 63.7 us
  other arithmetic: 173 us -> 142 us
    pallas_call x0 -> x6, Pallas kernels: none -> 633 us  [the longest x4 342 us: units(): pl.pallas_call(functools.partial(units_kernel, back), in_specs=[anywhere,...]
    ppermute x74 -> x50, waiting for transfers between devices: 366 us -> 66.8 us  [go(): return lax.ppermute(value, AXES, pairs)]
    all_gather x12 -> x6, waiting for transfers between devices: 286 us -> 23.1 us  [gather_dp(): return lax.all_gather(piece, 'dp', axis=0, tiled=True)]
    dot_general x12 -> x8, matrix products: 160 us -> 49.7 us  [nn(): return jnp.dot(a, b, preferred_element_type=jnp.float32)]
    ppermute x74 -> x50, starting transfers between devices: 137 us -> 63.2 us  [go(): return lax.ppermute(value, AXES, pairs)]
    dot_general x16 -> x8, matrix products: 114 us -> 56.8 us  [nt(): lax.dot_general(a, b, (((1,), (1,)), ((), ())), preferred_element_type=jn...]
    optimization_barrier x0 -> x16, local copies, waits for them, and re-layouts: none -> 42.7 us  [fence(): return lax.optimization_barrier(values)]
    select_n x2 -> x7, other arithmetic: 1.34 us -> 36.3 us  [the longest x4 24.9 us: turned_weight(): return jnp.where(col == core, slice_, moved)]
  transfers between devices with their start and end apart: 93 -> 64, of which waited for: 29 -> 10; matrix products, arithmetic and copies ran while one was open for 39% -> 30% of each run, Pallas kernels for 10% -> 41%
where the time goes in v2:
time: 1640 us; the launch traced here: 1630 us
  Pallas kernels  833 us (51%)
  matrix products  252 us (15%)
  local copies, waits for them, and re-layouts  198 us (12%)
  other arithmetic  142 us (9%)
  waiting for transfers between devices  126 us (8%)
  starting transfers between devices  63.7 us (4%)
    pallas_call x4, Pallas kernels, units(): pl.pallas_call(functools.partial(units_kernel, back), in_specs=[anywhere,...  342 us
    pallas_call x1, Pallas kernels, gather_four(): pl.pallas_call(functools.partial(gather_kernel, planes), in_specs=[anywhe...  168 us
    dot_general x28, matrix products, tn(): lax.dot_general(a, b, (((0,), (0,)), ((), ())), preferred_element_type=jn...  146 us
    pallas_call x1, Pallas kernels, settle_columns(): pl.pallas_call(functools.partial(settle_kernel, planes), in_specs=[inside...  123 us
    pallas_call x2, Pallas kernels, attention_back(): pl.pallas_call(functools.partial(attend_back_kernel, width, blocks, place...  110 us
    pallas_call x2, Pallas kernels, attention(): pl.pallas_call(functools.partial(attend_kernel, width, blocks, place.shap...  90 us
    ppermute x50, waiting for transfers between devices, go(): return lax.ppermute(value, AXES, pairs)  66.8 us
    ppermute x50, starting transfers between devices, go(): return lax.ppermute(value, AXES, pairs)  63.2 us
  transfers between devices with their start and end apart: 64, of which 10 were waited for; matrix products, arithmetic and copies ran while one was open for 30% of the time, Pallas kernels for 41%

profile of v2, /device:TPU:1, one launch (start us, length us, event | category | flops | bytes accessed | tf_op | source)
XLA Modules:
  0.0 1630.6 jit_solution(11242700729521445058)
XLA Ops:
  18.1 3.9 slice_bitcast_fusion
  24.5 167.6 %gather_four.1 = (bf16[4,8,200,1600]{3,2,1,0:T(8,128)(2,1)}, f32[8,24,200]{2,1,0:T(8,128)}, bf16[2,256,1600]{2,1,0:T(8,128)(2,1)}, bf16[2,256,1600]{2,1,0:T(8,128)(2,1)}) custom-call(bf16[200,1600]{1,0:T(8,128)(2,1)} %fusion.49.piece_ref, f32[24,200]{1,0:T(8,128)} %pad_convert_fusion.small_ref, bf16[2,256,1600]{2,1,0:T(8,128)(2,1)} %copy.137.token_ref, ...), custom_call_target="tpu_custom_call" | custom-call | bytes 314572800 | tf_op jit(solution)/shard_map/gather_four/pallas_call | solution.py:731
  206.0 13.6 fusion.130
  227.8 6.5 add_convert_fusion.16.vo_ref
  240.6 7.1 add_convert_fusion.17.q_ref
  247.8 23.0 %all-gather.10.cloned.1.call-done = bf16[1600,1600]{1,0:T(8,128)(2,1)} async-done(((bf16[200,1600]{1,0:T(8,128)(2,1)}), bf16[1600,1600]{1,0:T(8,128)(2,1)}) %all-gather.10.cloned.1.call-update) | async-done | bytes 5120016 | tf_op jit(solution)/shard_map/all_gather | solution.py:1177
  292.9 45.0 %attention.2 = (bf16[512,1600]{1,0:T(8,128)(2,1)S(1)}, f32[13,2,512]{2,1,0:T(2,128)S(1)}) custom-call(s32[4]{0:T(128)S(1)} %reshape.515.place_ref, s32[8]{0:T(128)S(1)} %select_reduce_fusion.slot_ref, bf16[512,1600]{1,0:T(8,128)(2,1)S(1)} %copy-done.26, bf16[512,1600]{1,0:T(8,128)(2,1)S(1)} %convolution_convert_fusion.11.ko_ref, ...), custom_call_target="tpu_custom_call" | custom-call | flops 6979321856 | bytes 9830400 | tf_op jit(solution)/shard_map/attention/pallas_call | solution.py:543
  339.1 7.0 broadcast_select_fusion.7.refs_1_.refs_2_
  346.1 7.2 fusion.135
  355.7 5.6 broadcast_select_fusion.6.refs_2_.refs_1_
  364.8 88.5 %units.2 = (f32[512,1600]{1,0:T(8,128)}, bf16[2048,1600]{1,0:T(8,128)(2,1)}, bf16[2048,1600]{1,0:T(8,128)(2,1)}, bf16[2048,1600]{1,0:T(8,128)(2,1)}) custom-call(bf16[512,1600]{1,0:T(8,128)(2,1)} %add_convert_fusion.15.refs_0_, bf16[1600,1600]{1,0:T(8,128)(2,1)} %broadcast_select_fusion.7.refs_1_.refs_2_, ...), custom_call_target="tpu_custom_call" | custom-call | flops 60000002048 | bytes 62914560 | tf_op jit(solution)/shard_map/units/pallas_call | solution.py:921
  453.6 5.4 broadcast_select_fusion.11
  459.7 3.9 collective-permute-start.11
  482.9 6.1 add_convert_fusion.12.vo_ref
  491.7 9.3 add_convert_fusion.13.q_ref
  501.0 20.9 %collective-permute-done.11 = bf16[1600,1600]{1,0:T(8,128)(2,1)} collective-permute-done((bf16[1600,1600]{1,0:T(8,128)(2,1)}, bf16[1600,1600]{1,0:T(8,128)(2,1)}, u32[]{:S(2)}, u32[]{:S(2)}) %collective-permute-start.11) | collective-permute-done | bytes 5120032 | tf_op jit(solution)/shard_map/ppermute | solution.py:1135
  525.3 3.8 copy.154.ks_ref
  537.0 45.0 %attention.3 = (bf16[512,1600]{1,0:T(8,128)(2,1)S(1)}, f32[13,2,512]{2,1,0:T(2,128)S(1)}) custom-call(s32[4]{0:T(128)S(1)} %reshape.515.place_ref, s32[8]{0:T(128)S(1)} %select_reduce_fusion.slot_ref, bf16[512,1600]{1,0:T(8,128)(2,1)S(1)} %copy-done.24, bf16[512,1600]{1,0:T(8,128)(2,1)S(1)} %convolution_convert_fusion.10.ko_ref, ...), custom_call_target="tpu_custom_call" | custom-call | flops 6979321856 | bytes 9830400 | tf_op jit(solution)/shard_map/attention/pallas_call | solution.py:543
  582.1 6.0 broadcast_select_fusion.5.refs_1_.refs_2_
  588.1 6.4 fusion.136
  595.1 6.2 broadcast_select_fusion.4.refs_2_.refs_1_
  605.4 86.7 %units.3 = (f32[512,1600]{1,0:T(8,128)}, bf16[2048,1600]{1,0:T(8,128)(2,1)}, bf16[2048,1600]{1,0:T(8,128)(2,1)}, bf16[2048,1600]{1,0:T(8,128)(2,1)}) custom-call(bf16[512,1600]{1,0:T(8,128)(2,1)} %add_convert_fusion.11.refs_0_, bf16[1600,1600]{1,0:T(8,128)(2,1)} %broadcast_select_fusion.5.refs_1_.refs_2_, ...), custom_call_target="tpu_custom_call" | custom-call | flops 60000002048 | bytes 62914560 | tf_op jit(solution)/shard_map/units/pallas_call | solution.py:921
  692.1 4.0 multiply_reduce_fusion.7
  696.2 84.4 %units_back.2 = (f32[512,1600]{1,0:T(8,128)}, bf16[2048,1600]{1,0:T(8,128)(2,1)}, bf16[2048,1600]{1,0:T(8,128)(2,1)}, f32[1,1600]{1,0:T(1,128)}) custom-call(bf16[512,1600]{1,0:T(8,128)(2,1)} %bitcast.240, bf16[1600,1600]{1,0:T(8,128)(2,1)} %broadcast_select_fusion.4.refs_2_.refs_1_, bf16[1600,1600]{1,0:T(8,128)(2,1)} %broadcast_select_fusion.5.refs_1_.refs_2_, ...), custom_call_target="tpu_custom_call" | custom-call | flops 60000002048 | bytes 62914560 | tf_op jit(solution)/shard_map/units_back/pallas_call | solution.py:921
  780.6 19.3 %convolution_convert_fusion.3 = bf16[1600,1600]{1,0:T(8,128)(2,1)} fusion(bf16[2048,1600]{1,0:T(8,128)(2,1)} %get-tuple-element.245, bf16[2048,1600]{1,0:T(8,128)(2,1)} %get-tuple-element.246), kind=kOutput, calls=%fused_computation.5 | convolution fusion | flops 10488320000 | bytes 18227200 | tf_op jit(solution)/shard_map/dot_general | solution.py:407
  805.5 4.5 multiply_reduce_fusion.3
  810.5 4.0 convert_reduce_fusion.6
  824.4 7.9 convolution_convert_fusion.9.do_ref
  832.3 19.6 %convolution_convert_fusion.2 = bf16[1600,1600]{1,0:T(8,128)(2,1)} fusion(bf16[2048,1600]{1,0:T(8,128)(2,1)} %get-tuple-element.248, bf16[2048,1600]{1,0:T(8,128)(2,1)} %get-tuple-element.249), kind=kOutput, calls=%fused_computation.4 | convolution fusion | flops 10488320000 | bytes 18227200 | tf_op jit(solution)/shard_map/dot_general | solution.py:407
  875.4 55.1 %attention_back.2 = (bf16[512,1600]{1,0:T(8,128)(2,1)S(1)}, f32[512,1600]{1,0:T(8,128)}, bf16[512,1600]{1,0:T(8,128)(2,1)S(1)}, f32[512,1600]{1,0:T(8,128)}, bf16[512,1600]{1,0:T(8,128)(2,1)S(1)}) custom-call(s32[4]{0:T(128)S(1)} %reshape.515.place_ref, s32[8]{0:T(128)S(1)} %select_reduce_fusion.slot_ref, bf16[512,1600]{1,0:T(8,128)(2,1)S(1)} %copy-done.25, ...), custom_call_target="tpu_custom_call" | custom-call | flops 17448304640 | bytes 24576000 | tf_op jit(solution)/shard_map/attention_back/pallas_call | solution.py:574
  933.0 3.7 copy.166
  960.3 8.2 fusion.90
  968.9 5.5 fusion.91
  974.8 12.5 multiply_reduce_fusion.4
  989.3 6.3 fusion.128
  995.5 8.3 concatenate.70
  1003.8 4.3 convolution_convert_fusion.7
  1008.2 4.0 convolution_convert_fusion.6
  1012.6 4.0 convolution_convert_fusion.5
  1016.8 4.2 convolution_convert_fusion.4
  1025.9 4.7 add_convert_fusion.5
  1030.7 4.3 add_convert_fusion.4
  1034.9 4.3 add_convert_fusion.3
  1039.2 4.3 add_convert_fusion.2
  1044.9 82.9 %units_back.3 = (f32[512,1600]{1,0:T(8,128)}, bf16[2048,1600]{1,0:T(8,128)(2,1)}, bf16[2048,1600]{1,0:T(8,128)(2,1)}, f32[1,1600]{1,0:T(1,128)}) custom-call(bf16[512,1600]{1,0:T(8,128)(2,1)} %get-tuple-element.277.refs_0_, bf16[1600,1600]{1,0:T(8,128)(2,1)} %broadcast_select_fusion.6.refs_2_.refs_1_, ...), custom_call_target="tpu_custom_call" | custom-call | flops 60000002048 | bytes 62914560 | tf_op jit(solution)/shard_map/units_back/pallas_call | solution.py:921
  1128.0 15.3 collective-permute-done.28
  1146.2 19.3 %convolution_convert_fusion.1 = bf16[1600,1600]{1,0:T(8,128)(2,1)} fusion(bf16[2048,1600]{1,0:T(8,128)(2,1)} %get-tuple-element.290, bf16[2048,1600]{1,0:T(8,128)(2,1)} %get-tuple-element.291), kind=kOutput, calls=%fused_computation.3 | convolution fusion | flops 10488320000 | bytes 18227200 | tf_op jit(solution)/shard_map/dot_general | solution.py:407
  1192.2 4.9 convolution_convert_fusion.8.do_ref
  1197.1 15.3 convolution_convert_fusion
  1212.5 4.2 add_convert_fusion.1
  1239.7 55.1 %attention_back.3 = (bf16[512,1600]{1,0:T(8,128)(2,1)S(1)}, f32[512,1600]{1,0:T(8,128)}, bf16[512,1600]{1,0:T(8,128)(2,1)S(1)}, f32[512,1600]{1,0:T(8,128)}, bf16[512,1600]{1,0:T(8,128)(2,1)S(1)}) custom-call(s32[4]{0:T(128)S(1)} %reshape.515.place_ref, s32[8]{0:T(128)S(1)} %select_reduce_fusion.slot_ref, bf16[512,1600]{1,0:T(8,128)(2,1)S(1)} %copy-done.27, ...), custom_call_target="tpu_custom_call" | custom-call | flops 17448304640 | bytes 24576000 | tf_op jit(solution)/shard_map/attention_back/pallas_call | solution.py:574
  1299.1 7.8 collective-permute-done.37
  1319.6 4.2 add_convert_fusion
  1326.6 3.9 copy.181
  1334.5 7.2 fusion.137
  1345.5 6.8 fusion.18
  1359.7 4.1 slice_bitcast_fusion.3
  1392.1 123.0 %settle_columns.1 = f32[200,1200]{1,0:T(8,128)} custom-call(bf16[800,512]{1,0:T(8,128)(2,1)} %bitcast.282, bf16[800,512]{1,0:T(8,128)(2,1)} %bitcast.281, bf16[4,512,1200]{2,1,0:T(8,128)(2,1)} %pad_maximum_fusion.2.piece_ref), custom_call_target="tpu_custom_call" | custom-call | flops 16000000000 | bytes 62914560 | tf_op jit(solution)/shard_map/settle_columns/pallas_call | solution.py:1059
  1516.4 11.0 collective-permute-start.46
  1531.6 7.8 collective-permute-done.46
  1539.5 34.9 %reduce-scatter.20.cloned.1.call-done = bf16[200,1200]{1,0:T(8,128)(2,1)} async-done(((bf16[800,1200]{1,0:T(8,128)(2,1)}), bf16[200,1200]{1,0:T(8,128)(2,1)}) %reduce-scatter.20.cloned.1.call-update) | async-done | bytes 480016 | tf_op jit(solution)/shard_map/reduce_scatter | solution.py:1144
  1597.6 6.2 collective-permute-done.47
  1605.2 6.1 collective-permute-start.48
  1613.7 6.0 collective-permute-done.48
  (617 shorter events, 335.9 us)
Async XLA Ops:
  7.2 194.8 %all-gather.18.cloned.1.call-start = ((), (), s32[]{:S(2)}) async-start(), calls=%async_computation.18 | async-start | bytes 5990400 | tf_op jit(solution)/shard_map/all_gather | solution.py:1177
  9.9 237.9 %all-gather.8.cloned.1.call-start = ((), (), s32[]{:S(2)}) async-start(), calls=%async_computation.7 | async-start | bytes 5990400 | tf_op jit(solution)/shard_map/all_gather | solution.py:1177
  12.6 258.2 %all-gather.10.cloned.1.call-start = ((), (), s32[]{:S(2)}) async-start(), calls=%async_computation.8 | async-start | bytes 5990400 | tf_op jit(solution)/shard_map/all_gather | solution.py:1177
  196.3 165.0 %all-gather.12.cloned.1.call-start = ((), (), s32[]{:S(2)}) async-start(), calls=%async_computation.9 | async-start | bytes 5990400 | tf_op jit(solution)/shard_map/all_gather | solution.py:1177
  196.9 262.1 %all-gather.14.cloned.1.call-start = ((), (), s32[]{:S(2)}) async-start(), calls=%async_computation.10 | async-start | bytes 5990400 | tf_op jit(solution)/shard_map/all_gather | solution.py:1177
  197.0 5.0 collective-permute-start.2
  202.0 68.8 %collective-permute-start.3 = (bf16[1600,1600]{1,0:T(8,128)(2,1)}, bf16[1600,1600]{1,0:T(8,128)(2,1)}, u32[]{:S(2)}, u32[]{:S(2)}) collective-permute-start(bf16[1600,1600]{1,0:T(8,128)(2,1)} %bitcast.246), channel_id=1, source_target_pairs={{1,4},{3,6},{4,1},{6,3},{9,12},{11,14},{12,9},{14,11},{17,20},{19,... | collective-permute-start | bytes 15360008 | tf_op jit(solution)/shard_map/ppermute | solution.py:1135
  227.8 20.0 %collective-permute-start = (bf16[512,1600]{0,1:T(8,128)(2,1)}, bf16[512,1600]{0,1:T(8,128)(2,1)}, u32[]{:S(2)}, u32[]{:S(2)}) collective-permute-start(bf16[512,1600]{0,1:T(8,128)(2,1)} %copy.143), channel_id=1, source_target_pairs={{0,4},{1,5},{2,6},{3,7},{4,0},{5,1},{6,2},{7,3},{8,12},{9,13},{10,... | collective-permute-start | bytes 4915208 | tf_op jit(solution)/shard_map/ppermute | solution.py:1135
  236.7 11.1 collective-permute-start.1
  270.9 230.1 %all-gather.16.cloned.1.call-start = ((), (), s32[]{:S(2)}) async-start(), calls=%async_computation.11 | async-start | bytes 5990400 | tf_op jit(solution)/shard_map/all_gather | solution.py:1177
  270.9 75.2 %collective-permute-start.4 = (bf16[1600,1600]{1,0:T(8,128)(2,1)}, bf16[1600,1600]{1,0:T(8,128)(2,1)}, u32[]{:S(2)}, u32[]{:S(2)}) collective-permute-start(bf16[1600,1600]{1,0:T(8,128)(2,1)} %all-gather.8.cloned.1.call-done), channel_id=1, source_target_pairs={{1,4},{3,6},{4,1},{6,3},{9,12},{11,14},{12,9},{14,11},{17,20},{19,... | collective-permute-start | bytes 15360008 | tf_op jit(solution)/shard_map/ppermute | solution.py:1135
  279.5 66.7 %collective-permute-start.5 = (bf16[800,1600]{1,0:T(8,128)(2,1)}, bf16[800,1600]{1,0:T(8,128)(2,1)}, u32[]{:S(2)}, u32[]{:S(2)}) collective-permute-start(bf16[800,1600]{1,0:T(8,128)(2,1)} %constant_dynamic-slice_fusion.10), channel_id=1, source_target_pairs={{0,2},{1,3},{2,0},{3,1},{4,6},{5,7},{6,4},{7,5},{8,10},{9,11},{10,... | collective-permute-start | bytes 7680008 | tf_op jit(solution)/shard_map/ppermute | solution.py:1135
  346.1 15.2 collective-permute-start.6
  353.4 579.6 %reduce-scatter.12.cloned.1.call-start = ((), (), s32[]{:S(2)}) async-start(), calls=%async_computation.12 | async-start | bytes 6656000 | tf_op jit(solution)/shard_map/reduce_scatter | solution.py:1144
  364.8 94.2 %collective-permute-start.7 = (bf16[800,1600]{1,0:T(8,128)(2,1)}, bf16[800,1600]{1,0:T(8,128)(2,1)}, u32[]{:S(2)}, u32[]{:S(2)}) collective-permute-start(bf16[800,1600]{1,0:T(8,128)(2,1)} %constant_dynamic-slice_fusion.9), channel_id=1, source_target_pairs={{0,1},{1,0},{2,3},{3,2},{4,5},{5,4},{6,7},{7,6},{8,9},{9,8},{10,11... | collective-permute-start | bytes 7680008 | tf_op jit(solution)/shard_map/ppermute | solution.py:1135
  459.0 18.4 %collective-permute-start.9 = (bf16[800,1600]{1,0:T(8,128)(2,1)}, bf16[800,1600]{1,0:T(8,128)(2,1)}, u32[]{:S(2)}, u32[]{:S(2)}) collective-permute-start(bf16[800,1600]{1,0:T(8,128)(2,1)} %collective-permute-done.7), channel_id=1, source_target_pairs={{0,4},{1,5},{2,6},{3,7},{4,0},{5,1},{6,2},{7,3},{8,12},{9,13},{10,... | collective-permute-start | bytes 7680008 | tf_op jit(solution)/shard_map/ppermute | solution.py:1135
  459.7 62.2 %collective-permute-start.11 = (bf16[1600,1600]{1,0:T(8,128)(2,1)}, bf16[1600,1600]{1,0:T(8,128)(2,1)}, u32[]{:S(2)}, u32[]{:S(2)}) collective-permute-start(bf16[1600,1600]{1,0:T(8,128)(2,1)} %all-gather.14.cloned.1.call-done), channel_id=1, source_target_pairs={{1,4},{3,6},{4,1},{6,3},{9,12},{11,14},{12,9},{14,11},{17,20},{19,... | collective-permute-start | bytes 15360008 | tf_op jit(solution)/shard_map/ppermute | solution.py:1135
  477.4 23.6 %collective-permute-start.8 = (bf16[512,1600]{0,1:T(8,128)(2,1)}, bf16[512,1600]{0,1:T(8,128)(2,1)}, u32[]{:S(2)}, u32[]{:S(2)}) collective-permute-start(bf16[512,1600]{0,1:T(8,128)(2,1)} %copy.151), channel_id=1, source_target_pairs={{0,4},{1,5},{2,6},{3,7},{4,0},{5,1},{6,2},{7,3},{8,12},{9,13},{10,... | collective-permute-start | bytes 4915208 | tf_op jit(solution)/shard_map/ppermute | solution.py:1135
  491.3 9.7 collective-permute-start.10
  521.9 66.2 %collective-permute-start.12 = (bf16[1600,1600]{1,0:T(8,128)(2,1)}, bf16[1600,1600]{1,0:T(8,128)(2,1)}, u32[]{:S(2)}, u32[]{:S(2)}) collective-permute-start(bf16[1600,1600]{1,0:T(8,128)(2,1)} %all-gather.16.cloned.1.call-done), channel_id=1, source_target_pairs={{1,4},{3,6},{4,1},{6,3},{9,12},{11,14},{12,9},{14,11},{17,20},{19,... | collective-permute-start | bytes 15360008 | tf_op jit(solution)/shard_map/ppermute | solution.py:1135
  799.9 328.0 %reduce-scatter.14.cloned.1.call-start = ((), (), s32[]{:S(2)}) async-start(), calls=%async_computation.13 | async-start | bytes 6656000 | tf_op jit(solution)/shard_map/reduce_scatter | solution.py:1144
  817.6 46.1 %collective-permute-start.13 = (bf16[800,400]{0,1:T(8,128)(2,1)}, bf16[800,400]{0,1:T(8,128)(2,1)}, u32[]{:S(2)}, u32[]{:S(2)}) collective-permute-start(bf16[800,400]{0,1:T(8,128)(2,1)} %convolution_convert_fusion.19), channel_id=1, source_target_pairs={{0,4},{1,5},{2,6},{3,7},{4,0},{5,1},{6,2},{7,3},{8,12},{9,13},{10,... | collective-permute-start | bytes 1920008 | tf_op jit(solution)/shard_map/ppermute | solution.py:1135
  821.5 111.4 %collective-permute-start.19 = (bf16[256,1600]{0,1:T(8,128)(2,1)}, bf16[256,1600]{0,1:T(8,128)(2,1)}, u32[]{:S(2)}, u32[]{:S(2)}) collective-permute-start(bf16[256,1600]{0,1:T(8,128)(2,1)} %copy.161), channel_id=1, source_target_pairs={{2,4},{3,5},{4,2},{5,3},{10,12},{11,13},{12,10},{13,11},{18,20},{1... | collective-permute-start | bytes 2457608 | tf_op jit(solution)/shard_map/ppermute | solution.py:1135
  854.8 11.8 collective-permute-start.14
  857.7 11.4 collective-permute-start.15
  861.1 11.0 collective-permute-start.16
  863.7 69.3 %collective-permute-start.20 = (bf16[256,1600]{0,1:T(8,128)(2,1)}, bf16[256,1600]{0,1:T(8,128)(2,1)}, u32[]{:S(2)}, u32[]{:S(2)}) collective-permute-start(bf16[256,1600]{0,1:T(8,128)(2,1)} %copy.162), channel_id=1, source_target_pairs={{0,1},{1,0},{2,5},{3,4},{4,3},{5,2},{6,7},{7,6},{8,9},{9,8},{10,13... | collective-permute-start | bytes 2457608 | tf_op jit(solution)/shard_map/ppermute | solution.py:1135
  873.9 59.0 %collective-permute-start.17 = (bf16[800,400]{0,1:T(8,128)(2,1)S(1)}, bf16[800,400]{0,1:T(8,128)(2,1)}, u32[]{:S(2)}, u32[]{:S(2)}) collective-permute-start(bf16[800,400]{0,1:T(8,128)(2,1)S(1)} %add_convert_fusion.29), channel_id=1, source_target_pairs={{0,2},{1,3},{2,0},{3,1},{4,6},{5,7},{6,4},{7,5},{8,10},{9,11},{10,... | collective-permute-start | bytes 1920008 | tf_op jit(solution)/shard_map/ppermute | solution.py:1135
  874.5 58.5 %collective-permute-start.18 = (bf16[800,400]{0,1:T(8,128)(2,1)S(1)}, bf16[800,400]{0,1:T(8,128)(2,1)}, u32[]{:S(2)}, u32[]{:S(2)}) collective-permute-start(bf16[800,400]{0,1:T(8,128)(2,1)S(1)} %add_convert_fusion.28), channel_id=1, source_target_pairs={{0,2},{1,3},{2,0},{3,1},{4,6},{5,7},{6,4},{7,5},{8,10},{9,11},{10,... | collective-permute-start | bytes 1920008 | tf_op jit(solution)/shard_map/ppermute | solution.py:1135
  936.7 9.5 collective-permute-start.21
  938.9 13.6 collective-permute-start.22
  946.1 351.0 %reduce-scatter.22.cloned.1.call-start = ((), (), s32[]{:S(2)}) async-start(), calls=%async_computation.19 | async-start | bytes 1024000
  1008.1 16.4 %collective-permute-start.23 = (bf16[800,1200]{1,0:T(8,128)(2,1)}, bf16[800,1200]{1,0:T(8,128)(2,1)}, u32[]{:S(2)}, u32[]{:S(2)}) collective-permute-start(bf16[800,1200]{1,0:T(8,128)(2,1)} %convolution_convert_fusion.7), channel_id=1, source_target_pairs={{0,4},{1,5},{2,6},{3,7},{4,0},{5,1},{6,2},{7,3},{8,12},{9,13},{10,... | collective-permute-start | bytes 5760008 | tf_op jit(solution)/shard_map/ppermute | solution.py:1135
  1012.2 18.4 %collective-permute-start.24 = (bf16[800,1200]{1,0:T(8,128)(2,1)}, bf16[800,1200]{1,0:T(8,128)(2,1)}, u32[]{:S(2)}, u32[]{:S(2)}) collective-permute-start(bf16[800,1200]{1,0:T(8,128)(2,1)} %convolution_convert_fusion.6), channel_id=1, source_target_pairs={{0,4},{1,5},{2,6},{3,7},{4,0},{5,1},{6,2},{7,3},{8,12},{9,13},{10,... | collective-permute-start | bytes 5760008 | tf_op jit(solution)/shard_map/ppermute | solution.py:1135
  1016.6 18.3 %collective-permute-start.25 = (bf16[800,1200]{1,0:T(8,128)(2,1)}, bf16[800,1200]{1,0:T(8,128)(2,1)}, u32[]{:S(2)}, u32[]{:S(2)}) collective-permute-start(bf16[800,1200]{1,0:T(8,128)(2,1)} %convolution_convert_fusion.5), channel_id=1, source_target_pairs={{0,4},{1,5},{2,6},{3,7},{4,0},{5,1},{6,2},{7,3},{8,12},{9,13},{10,... | collective-permute-start | bytes 5760008 | tf_op jit(solution)/shard_map/ppermute | solution.py:1135
  1020.9 18.3 %collective-permute-start.26 = (bf16[800,1200]{1,0:T(8,128)(2,1)}, bf16[800,1200]{1,0:T(8,128)(2,1)}, u32[]{:S(2)}, u32[]{:S(2)}) collective-permute-start(bf16[800,1200]{1,0:T(8,128)(2,1)} %convolution_convert_fusion.4), channel_id=1, source_target_pairs={{0,4},{1,5},{2,6},{3,7},{4,0},{5,1},{6,2},{7,3},{8,12},{9,13},{10,... | collective-permute-start | bytes 5760008 | tf_op jit(solution)/shard_map/ppermute | solution.py:1135
  1023.5 104.4 %collective-permute-start.29 = (bf16[800,400]{0,1:T(8,128)(2,1)}, bf16[800,400]{0,1:T(8,128)(2,1)S(1)}, u32[]{:S(2)}, u32[]{:S(2)}) collective-permute-start(bf16[800,400]{0,1:T(8,128)(2,1)} %add_convert_fusion.25), channel_id=1, source_target_pairs={{0,1},{1,0},{2,3},{3,2},{4,5},{5,4},{6,7},{7,6},{8,9},{9,8},{10,11... | collective-permute-start | bytes 1920008 | tf_op jit(solution)/shard_map/ppermute | solution.py:1135
  1024.5 103.5 %collective-permute-start.30 = (bf16[200,1600]{1,0:T(8,128)(2,1)}, bf16[200,1600]{1,0:T(8,128)(2,1)}, u32[]{:S(2)}, u32[]{:S(2)}) collective-permute-start(bf16[200,1600]{1,0:T(8,128)(2,1)} %dynamic-slice_bitcast_fusion.3), channel_id=1, source_target_pairs={{0,1},{1,0},{2,3},{3,2},{4,5},{5,4},{6,7},{7,6},{8,9},{9,8},{10,11... | collective-permute-start | bytes 1920008 | tf_op jit(solution)/shard_map/ppermute | solution.py:1135
  1043.5 84.5 %collective-permute-start.27 = (bf16[800,1200]{1,0:T(8,128)(2,1)}, bf16[800,1200]{1,0:T(8,128)(2,1)S(1)}, u32[]{:S(2)}, u32[]{:S(2)}) collective-permute-start(bf16[800,1200]{1,0:T(8,128)(2,1)} %add_convert_fusion.5), channel_id=1, source_target_pairs={{0,1},{1,0},{2,3},{3,2},{4,5},{5,4},{6,7},{7,6},{8,9},{9,8},{10,11... | collective-permute-start | bytes 5760008 | tf_op jit(solution)/shard_map/ppermute | solution.py:1135
  1044.1 99.2 %collective-permute-start.28 = (bf16[800,1200]{1,0:T(8,128)(2,1)}, bf16[800,1200]{1,0:T(8,128)(2,1)}, u32[]{:S(2)}, u32[]{:S(2)}) collective-permute-start(bf16[800,1200]{1,0:T(8,128)(2,1)} %add_convert_fusion.3), channel_id=1, source_target_pairs={{0,1},{1,0},{2,3},{3,2},{4,5},{5,4},{6,7},{7,6},{8,9},{9,8},{10,11... | collective-permute-start | bytes 5760008 | tf_op jit(solution)/shard_map/ppermute | solution.py:1135
  1146.2 160.7 %reduce-scatter.16.cloned.1.call-start = ((), (), s32[]{:S(2)}) async-start(), calls=%async_computation.14 | async-start | bytes 6656000 | tf_op jit(solution)/shard_map/reduce_scatter | solution.py:1144
  1165.5 366.1 %reduce-scatter.18.cloned.1.call-start = ((), (), s32[]{:S(2)}) async-start(), calls=%async_computation.16 | async-start | bytes 6656000 | tf_op jit(solution)/shard_map/reduce_scatter | solution.py:1144
  1185.9 32.4 %collective-permute-start.31 = (bf16[800,400]{0,1:T(8,128)(2,1)}, bf16[800,400]{0,1:T(8,128)(2,1)}, u32[]{:S(2)}, u32[]{:S(2)}) collective-permute-start(bf16[800,400]{0,1:T(8,128)(2,1)} %convolution_convert_fusion.15), channel_id=1, source_target_pairs={{0,4},{1,5},{2,6},{3,7},{4,0},{5,1},{6,2},{7,3},{8,12},{9,13},{10,... | collective-permute-start | bytes 1920008 | tf_op jit(solution)/shard_map/ppermute | solution.py:1135
  1188.8 32.5 %collective-permute-start.32 = (bf16[800,400]{0,1:T(8,128)(2,1)}, bf16[800,400]{0,1:T(8,128)(2,1)}, u32[]{:S(2)}, u32[]{:S(2)}) collective-permute-start(bf16[800,400]{0,1:T(8,128)(2,1)} %convolution_convert_fusion.14), channel_id=1, source_target_pairs={{0,4},{1,5},{2,6},{3,7},{4,0},{5,1},{6,2},{7,3},{8,12},{9,13},{10,... | collective-permute-start | bytes 1920008 | tf_op jit(solution)/shard_map/ppermute | solution.py:1135
  1190.6 33.6 %collective-permute-start.33 = (bf16[800,400]{0,1:T(8,128)(2,1)}, bf16[800,400]{0,1:T(8,128)(2,1)}, u32[]{:S(2)}, u32[]{:S(2)}) collective-permute-start(bf16[800,400]{0,1:T(8,128)(2,1)} %convolution_convert_fusion.13), channel_id=1, source_target_pairs={{0,4},{1,5},{2,6},{3,7},{4,0},{5,1},{6,2},{7,3},{8,12},{9,13},{10,... | collective-permute-start | bytes 1920008 | tf_op jit(solution)/shard_map/ppermute | solution.py:1135
  1192.1 35.1 %collective-permute-start.34 = (bf16[800,400]{0,1:T(8,128)(2,1)S(1)}, bf16[800,400]{0,1:T(8,128)(2,1)}, u32[]{:S(2)}, u32[]{:S(2)}) collective-permute-start(bf16[800,400]{0,1:T(8,128)(2,1)S(1)} %convolution_convert_fusion.12), channel_id=1, source_target_pairs={{0,4},{1,5},{2,6},{3,7},{4,0},{5,1},{6,2},{7,3},{8,12},{9,13},{10,... | collective-permute-start | bytes 1920008 | tf_op jit(solution)/shard_map/ppermute | solution.py:1135
  1230.1 76.7 %collective-permute-start.38 = (bf16[800,1200]{1,0:T(8,128)(2,1)}, bf16[800,1200]{1,0:T(8,128)(2,1)}, u32[]{:S(2)}, u32[]{:S(2)}) collective-permute-start(bf16[800,1200]{1,0:T(8,128)(2,1)} %add_convert_fusion.1), channel_id=1, source_target_pairs={{0,2},{1,3},{2,0},{3,1},{4,6},{5,7},{6,4},{7,5},{8,10},{9,11},{10,... | collective-permute-start | bytes 5760008 | tf_op jit(solution)/shard_map/ppermute | solution.py:1135
  1232.4 66.7 %collective-permute-start.35 = (bf16[200,1600]{1,0:T(8,128)(2,1)}, bf16[200,1600]{1,0:T(8,128)(2,1)}, u32[]{:S(2)}, u32[]{:S(2)}) collective-permute-start(bf16[200,1600]{1,0:T(8,128)(2,1)} %dynamic-slice_bitcast_fusion.2), channel_id=1, source_target_pairs={{0,1},{1,0},{2,3},{3,2},{4,5},{5,4},{6,7},{7,6},{8,9},{9,8},{10,11... | collective-permute-start | bytes 1920008 | tf_op jit(solution)/shard_map/ppermute | solution.py:1135
  1232.4 66.7 %collective-permute-start.36 = (bf16[800,400]{0,1:T(8,128)(2,1)}, bf16[800,400]{0,1:T(8,128)(2,1)}, u32[]{:S(2)}, u32[]{:S(2)}) collective-permute-start(bf16[800,400]{0,1:T(8,128)(2,1)} %add_convert_fusion.24), channel_id=1, source_target_pairs={{0,2},{1,3},{2,0},{3,1},{4,6},{5,7},{6,4},{7,5},{8,10},{9,11},{10,... | collective-permute-start | bytes 1920008 | tf_op jit(solution)/shard_map/ppermute | solution.py:1135
  1233.7 73.2 %collective-permute-start.37 = (bf16[800,400]{0,1:T(8,128)(2,1)}, bf16[800,400]{0,1:T(8,128)(2,1)}, u32[]{:S(2)}, u32[]{:S(2)}) collective-permute-start(bf16[800,400]{0,1:T(8,128)(2,1)} %add_convert_fusion.23), channel_id=1, source_target_pairs={{0,2},{1,3},{2,0},{3,1},{4,6},{5,7},{6,4},{7,5},{8,10},{9,11},{10,... | collective-permute-start | bytes 1920008 | tf_op jit(solution)/shard_map/ppermute | solution.py:1135
  1233.9 297.8 %all-reduce.3.cloned.1.call-start = ((), (), s32[]{:S(2)}) async-start(), calls=%async_computation.15 | async-start | bytes 319488 | tf_op jit(solution)/shard_map/psum | solution.py:1419
  1310.5 13.4 collective-permute-start.39
  1314.0 12.6 collective-permute-start.40
  1371.2 203.1 %reduce-scatter.20.cloned.1.call-start = ((), (), s32[]{:S(2)}) async-start(), calls=%async_computation.17 | async-start | bytes 2560000 | tf_op jit(solution)/shard_map/reduce_scatter | solution.py:1144
  1374.5 247.0 %reduce-scatter.24.cloned.1.call-start = ((), (), s32[]{:S(2)}) async-start(), calls=%async_computation.20 | async-start | bytes 1024000
  1380.2 151.4 %collective-permute-start.42 = (bf16[800,400]{0,1:T(8,128)(2,1)}, bf16[800,400]{0,1:T(8,128)(2,1)}, u32[]{:S(2)}, u32[]{:S(2)}) collective-permute-start(bf16[800,400]{0,1:T(8,128)(2,1)} %add_convert_fusion.19), channel_id=1, source_target_pairs={{0,1},{1,0},{2,3},{3,2},{4,5},{5,4},{6,7},{7,6},{8,9},{9,8},{10,11... | collective-permute-start | bytes 1920008 | tf_op jit(solution)/shard_map/ppermute | solution.py:1135
  1380.2 151.4 %collective-permute-start.41 = (bf16[200,1600]{1,0:T(8,128)(2,1)}, bf16[200,1600]{1,0:T(8,128)(2,1)}, u32[]{:S(2)}, u32[]{:S(2)}) collective-permute-start(bf16[200,1600]{1,0:T(8,128)(2,1)} %dynamic-slice_bitcast_fusion.1), channel_id=1, source_target_pairs={{0,1},{1,0},{2,3},{3,2},{4,5},{5,4},{6,7},{7,6},{8,9},{9,8},{10,11... | collective-permute-start | bytes 1920008 | tf_op jit(solution)/shard_map/ppermute | solution.py:1135
  1381.7 134.7 %collective-permute-start.43 = (bf16[200,1600]{1,0:T(8,128)(2,1)}, bf16[200,1600]{1,0:T(8,128)(2,1)}, u32[]{:S(2)}, u32[]{:S(2)}) collective-permute-start(bf16[200,1600]{1,0:T(8,128)(2,1)} %fusion.23), channel_id=1, source_target_pairs={{1,4},{3,6},{4,1},{6,3},{9,12},{11,14},{12,9},{14,11},{17,20},{19,... | collective-permute-start | bytes 1920008 | tf_op jit(solution)/shard_map/ppermute | solution.py:1135
  1384.5 145.0 %collective-permute-start.44 = (bf16[200,1600]{1,0:T(8,128)(2,1)}, bf16[200,1600]{1,0:T(8,128)(2,1)}, u32[]{:S(2)}, u32[]{:S(2)}) collective-permute-start(bf16[200,1600]{1,0:T(8,128)(2,1)} %fusion.22), channel_id=1, source_target_pairs={{1,4},{3,6},{4,1},{6,3},{9,12},{11,14},{12,9},{14,11},{17,20},{19,... | collective-permute-start | bytes 1920008 | tf_op jit(solution)/shard_map/ppermute | solution.py:1135
  1390.0 141.6 %collective-permute-start.45 = (bf16[256,1600]{0,1:T(8,128)(2,1)}, bf16[256,1600]{0,1:T(8,128)(2,1)}, u32[]{:S(2)}, u32[]{:S(2)}) collective-permute-start(bf16[256,1600]{0,1:T(8,128)(2,1)} %copy.186), channel_id=1, source_target_pairs={{2,4},{3,5},{4,2},{5,3},{10,12},{11,13},{12,10},{13,11},{18,20},{1... | collective-permute-start | bytes 2457608 | tf_op jit(solution)/shard_map/ppermute | solution.py:1135
  1516.4 23.1 %collective-permute-start.46 = (bf16[256,1600]{0,1:T(8,128)(2,1)}, bf16[256,1600]{0,1:T(8,128)(2,1)}, u32[]{:S(2)}, u32[]{:S(2)}) collective-permute-start(bf16[256,1600]{0,1:T(8,128)(2,1)} %copy.187), channel_id=1, source_target_pairs={{0,1},{1,0},{2,5},{3,4},{4,3},{5,2},{6,7},{7,6},{8,9},{9,8},{10,13... | collective-permute-start | bytes 2457608 | tf_op jit(solution)/shard_map/ppermute | solution.py:1135
  1587.9 15.9 collective-permute-start.47
  1590.3 21.6 %collective-permute-start.49 = (bf16[200,1600]{1,0:T(8,128)(2,1)S(1)}, bf16[200,1600]{1,0:T(8,128)(2,1)S(1)}, u32[]{:S(2)}, u32[]{:S(2)}) collective-permute-start(bf16[200,1600]{1,0:T(8,128)(2,1)S(1)} %fusion.20), channel_id=1, source_target_pairs={{1,4},{3,6},{4,1},{6,3},{9,12},{11,14},{12,9},{14,11},{17,20},{19,... | collective-permute-start | bytes 1920008 | tf_op jit(solution)/shard_map/ppermute | solution.py:1135
  1605.2 14.5 collective-permute-start.48
  (143 other events, 2133.8 us)
Sparse Core Ops, SparseCore 0:
  10.3 106.5 all-gather.17
  118.6 55.5 all-gather.7
  196.5 74.3 all-gather.9
  272.9 55.5 all-gather.11
  330.6 55.4 all-gather.13
  387.6 55.4 all-gather.15
  800.0 104.8 reduce-scatter.11
  946.3 105.9 reduce-scatter.13
  1146.3 34.2 reduce-scatter.21
  1182.7 95.1 reduce-scatter.15
  1280.2 95.7 reduce-scatter.17
  1381.5 135.4 all-reduce.2
  1519.9 54.3 reduce-scatter.19
  1586.0 22.5 reduce-scatter.23

commit v3 on v2

--- a/solution.py
+++ b/solution.py
@@ -569,8 +569,9 @@
     blocks, keys = slot.shape[0], slot.shape[0] * LANES
     tall, stat = attention_specs(rows)
     elems = rows * keys * steps * 2
-    wide = jax.ShapeDtypeStruct((rows, width), jnp.float32)
-    thin = jax.ShapeDtypeStruct((rows, width), jnp.bfloat16)
+    wide = jax.ShapeDtypeStruct((rows, steps * LANES), jnp.float32)
+    thin = jax.ShapeDtypeStruct((rows, steps * LANES), jnp.bfloat16)
+    narrow = jax.ShapeDtypeStruct((rows, width), jnp.bfloat16)
     return pl.pallas_call(
         functools.partial(attend_back_kernel, width, blocks, place.shape[0]),
         grid_spec=pltpu.PrefetchScalarGridSpec(
@@ -588,14 +589,14 @@
                 pltpu.VMEM((keys, LANES), jnp.float32),
             ],
         ),
-        out_shape=[thin, wide, thin, wide, thin],
+        out_shape=[narrow, wide, thin, wide, thin],
         cost_estimate=pl.CostEstimate(flops=elems * HD * 20, bytes_accessed=rows * width * 30, transcendentals=elems),
         compiler_params=pltpu.CompilerParams(vmem_limit_bytes=40 * 2 ** 20),
         name="attention_back",
     )(place, slot, q, ko, ks, vo, vs, do, o, lse)
 
 
-def gather_kernel(planes, piece_ref, small_ref, token_ref, cot_ref, out_ref, small_out, token_out, cot_out,
+def gather_kernel(planes, piece_ref, small_ref, token_ref, out_ref, small_out, token_out,
                   send_sem, recv_sem, small_send, small_recv, swap_send, swap_recv, own_sem):
     dp, mp = lax.axis_index("dp"), lax.axis_index("mp")
     z, c = dp // 2, dp % 2
@@ -710,7 +711,6 @@
         if k % 2 == 1:
             send(block, across, rows[k], to_x)
         send(block, across, rows[k], to_c)
-    finishes.append(swap(cot_ref, cot_out, 1))
     send(arrived(corner, rows[-1]), corner, rows[-1], to_c)
     for k in range(planes):
         beside = rows[k] + 1 - 2 * c
@@ -725,18 +725,17 @@
         copy.wait()
 
 
-def gather_four(planes, piece, small, tokens, cotangent):
+def gather_four(planes, piece, small, tokens):
     count = (planes - 1) + 3 * planes + planes + 3 * planes
     anywhere = pl.BlockSpec(memory_space=pl.ANY)
     return pl.pallas_call(
         functools.partial(gather_kernel, planes),
-        in_specs=[anywhere] * 4,
-        out_specs=[anywhere] * 4,
+        in_specs=[anywhere] * 3,
+        out_specs=[anywhere] * 3,
         out_shape=[
             jax.ShapeDtypeStruct((4, 2 * planes) + piece.shape, piece.dtype),
             jax.ShapeDtypeStruct((2 * planes,) + small.shape, small.dtype),
             jax.ShapeDtypeStruct(tokens.shape, tokens.dtype),
-            jax.ShapeDtypeStruct(cotangent.shape, cotangent.dtype),
         ],
         scratch_shapes=[
             pltpu.SemaphoreType.DMA((count,)),
@@ -750,7 +749,7 @@
         cost_estimate=pl.CostEstimate(flops=0, bytes_accessed=300 * 2 ** 20, transcendentals=0),
         compiler_params=pltpu.CompilerParams(collective_id=0, has_side_effects=True),
         name="gather_four",
-    )(piece, small, tokens, cotangent)
+    )(piece, small, tokens)
 
 
 GROUPS, PARTS = 4, 2
@@ -768,11 +767,14 @@
         body(whole * 256, width % 256)
 
 
-def units_kernel(back, *refs):
+def units_kernel(back, counts, *refs):
+    x_ref, wa_own, wb_own, *refs = refs
+    (*wa_moved,), refs = refs[:counts[0]], refs[counts[0]:]
+    (*wb_moved,), refs = refs[:counts[1]], refs[counts[1]:]
     if back:
-        (x_ref, wa_ref, wb_ref, slope_ref, out_ref, rows_ref, left_ref, sums_ref, *scratch) = refs
+        (slope_ref, act_ref, out_ref, rows_ref, left_ref, sums_ref, grad_ref, act, grad, *scratch) = refs
     else:
-        (x_ref, wa_ref, wb_ref, bias_ref, out_ref, rows_ref, left_ref, slope_ref, *scratch) = refs
+        (bias_ref, out_ref, rows_ref, left_ref, slope_ref, *scratch) = refs
     (wa, wb, rows, own, far, beside, corner, got_c, got_f, give, got_y, left, slope,
      in_sem, send_sem, recv_sem, out_sem) = scratch
     width = wa.shape[1]
@@ -783,9 +785,27 @@
     loads = [
         pltpu.make_async_copy(x_ref.at[pl.ds(h * part, part)], rows.at[0, h], in_sem.at[h]) for h in range(PARTS)
     ]
-    loads += [pltpu.make_async_copy(wa_ref, wa, in_sem.at[2]), pltpu.make_async_copy(wb_ref, wb, in_sem.at[3])]
-    for load in loads:
+    moved = []
+    for slot, (own_ref, moved_refs, target) in enumerate(((wa_own, wa_moved, wa), (wb_own, wb_moved, wb))):
+        tall = wa.shape[0] // len(moved_refs)
+        for side, part_ref in enumerate(moved_refs):
+            span = pl.ds(side * tall, tall)
+            sem = in_sem.at[6 + 2 * slot + side]
+            loads.append(pltpu.make_async_copy(own_ref.at[span], target.at[span], sem))
+            moved.append(pltpu.make_async_copy(part_ref, target.at[span], sem))
+    for load in loads[:PARTS]:
         load.start()
+
+    @pl.when(mp % 2 == dp % 2)
+    def _():
+        for load in loads[PARTS:]:
+            load.start()
+
+    @pl.when(mp % 2 != dp % 2)
+    def _():
+        for load in moved:
+            load.start()
+
     barrier = pltpu.get_barrier_semaphore()
     for peer in (to_c, to_y):
         pl.semaphore_signal(barrier, inc=1, device_id=peer, device_id_type=pl.DeviceIdType.MESH)
@@ -837,8 +857,10 @@
     if back:
         sums_ref[...] = jnp.zeros_like(sums_ref)
         fetched[0] = fetch(0)
-    loads[2].wait()
-    loads[3].wait()
+        act_load = pltpu.make_async_copy(act_ref, act, in_sem.at[10])
+        act_load.start()
+    for load in loads[PARTS:]:
+        load.wait()
 
     def work(index, target):
         group, h = order[index]
@@ -900,6 +922,31 @@
         work(5 + 2 * h, corner.at[h])
         arrivals["corner", h] = send(corner.at[h], got_f.at[h], slot_of("corner", h), to_c)
         combine(h)
+    if back:
+        act_load.wait()
+        leaving = {}
+        for j in range(-(-width // 256)):
+            at, size, side = j * 256, min(256, width - j * 256), j % 2
+            if j >= 2:
+                leaving[j - 2].wait()
+
+            def column(first, length, at=at, size=size, side=side):
+                span = pl.ds(first, length)
+                value = None
+                for group in range(GROUPS):
+                    for h in range(PARTS):
+                        here = pl.ds((group * PARTS + h) * part, part)
+                        term = tn(rows[group, h, :, at:at + size], act[here, span])
+                        value = term if value is None else value + term
+                grad[side, :size, span] = bf(value)
+
+            tiles(width, column)
+            leaving[j] = pltpu.make_async_copy(
+                grad.at[side, pl.ds(0, size)], grad_ref.at[pl.ds(at, size)], in_sem.at[11 + side]
+            )
+            leaving[j].start()
+        for j in list(leaving)[-2:]:
+            leaving[j].wait()
     for h in range(PARTS):
         arrivals["beside", h].wait_recv()
         arrivals["give", h].wait_recv()
@@ -910,7 +957,7 @@
         copy.wait()
 
 
-def units(back, x, wa, wb, extra):
+def units(back, x, wa, wb, *extra):
     rows, width = x.shape
     part = rows // PARTS
     half = jax.ShapeDtypeStruct((GROUPS * rows, width), jnp.bfloat16)
@@ -918,22 +965,24 @@
     inside = pl.BlockSpec(memory_space=pltpu.VMEM)
     thin, wide = pltpu.VMEM((PARTS, part, width), jnp.bfloat16), pltpu.VMEM((PARTS, part, width), jnp.float32)
     count = 6 * PARTS
+    moved = (*wa[1:], *wb[1:])
+    square = wa[0].shape
+    work = []
+    if back:
+        work = [pltpu.VMEM((GROUPS * rows, width), jnp.bfloat16), pltpu.VMEM((2, 256, width), jnp.bfloat16)]
     return pl.pallas_call(
-        functools.partial(units_kernel, back),
-        in_specs=[anywhere, anywhere, anywhere, anywhere if back else inside],
-        out_specs=[inside, anywhere, anywhere, inside if back else anywhere],
-        out_shape=[
-            jax.ShapeDtypeStruct((rows, width), jnp.float32),
-            half,
-            half,
-            jax.ShapeDtypeStruct((1, width), jnp.float32) if back else half,
-        ],
+        functools.partial(units_kernel, back, (len(wa) - 1, len(wb) - 1)),
+        in_specs=[anywhere] * (3 + len(moved)) + ([anywhere] * 2 if back else [inside]),
+        out_specs=[inside, anywhere, anywhere] + ([inside, anywhere] if back else [anywhere]),
+        out_shape=[jax.ShapeDtypeStruct((rows, width), jnp.float32), half, half]
+        + ([jax.ShapeDtypeStruct((1, width), jnp.float32), jax.ShapeDtypeStruct(square, jnp.bfloat16)] if back else [half]),
         scratch_shapes=[
-            pltpu.VMEM(wa.shape, jnp.bfloat16),
-            pltpu.VMEM(wb.shape, jnp.bfloat16),
+            *work,
+            pltpu.VMEM(square, jnp.bfloat16),
+            pltpu.VMEM(square, jnp.bfloat16),
             pltpu.VMEM((GROUPS, PARTS, part, width), jnp.bfloat16),
             wide, wide, thin, thin, thin, thin, thin, thin, thin, thin,
-            pltpu.SemaphoreType.DMA((6,)),
+            pltpu.SemaphoreType.DMA((13,)),
             pltpu.SemaphoreType.DMA((count,)),
             pltpu.SemaphoreType.DMA((count,)),
             pltpu.SemaphoreType.DMA((3, GROUPS * PARTS)),
@@ -942,14 +991,15 @@
             flops=60 * 10 ** 9, bytes_accessed=60 * 2 ** 20, transcendentals=0
         ),
         compiler_params=pltpu.CompilerParams(
-            collective_id=2 if back else 1, has_side_effects=True, vmem_limit_bytes=56 * 2 ** 20
+            collective_id=2 if back else 1, has_side_effects=True, vmem_limit_bytes=58 * 2 ** 20
         ),
         name="units_back" if back else "units",
-    )(x, wa, wb, extra)
-
-
-def settle_kernel(planes, keep_ref, send_ref, piece_ref, out_ref, pieces, outgo, income, total, from_y, from_x, to_give,
-                  final, from_z, load_sem, c_send, c_recv, xy_send, xy_recv, z_send, z_recv):
+    )(x, wa[0], wb[0], *moved, *extra)
+
+
+def settle_kernel(planes, keep_ref, send_ref, piece_ref, sum_ref, out_ref, sum_out, pieces, outgo, income, total, from_y, from_x, to_give,
+                  final, from_z, sum_at, sum_from, load_sem, c_send, c_recv, xy_send, xy_recv, z_send, z_recv,
+                  sum_send, sum_recv):
     dp, mp = lax.axis_index("dp"), lax.axis_index("mp")
     z, c = dp // 2, dp % 2
     y, x = mp // 2, mp % 2
@@ -990,6 +1040,14 @@
 
         tiles(width, body)
 
+    adding = [remote(sum_ref, sum_from.at[0], (sum_send, sum_recv), 0, to_c)]
+
+    def sum_step(k, source, peer):
+        adding[k].wait_recv()
+        sum_at[k] = source[...] + sum_from[k]
+        if peer is not None:
+            adding.append(remote(sum_at.at[k], sum_from.at[k + 1], (sum_send, sum_recv), k + 1, peer))
+
     crossing = []
     for k in range(4):
         loads[k].wait()
@@ -1018,14 +1076,19 @@
             target[block] = value.astype(target.dtype)
 
     sems = (xy_send, xy_recv)
+    sum_step(0, sum_ref, to_x)
     chip(0)
     y0 = remote(total.at[0, first], from_y.at[0], sems, 0, to_y)
     x0 = remote(total.at[0, second], from_x.at[0], sems, 1, to_x)
     chip(1)
     y1 = remote(total.at[1, first], from_y.at[1], sems, 2, to_y)
+    sum_step(1, sum_at.at[0], to_y)
     chip(2)
     x1 = remote(total.at[2, second], from_x.at[1], sems, 3, to_x)
     chip(3)
+    sum_step(2, sum_at.at[1], None)
+    for k, other in enumerate(others):
+        adding.append(remote(sum_at.at[2], sum_from.at[3 + k], (sum_send, sum_recv), 3 + k, (other * 2 + c, mp)))
     y0.wait_recv()
     add(to_give.at[0], total.at[2, first], [from_y.at[0]])
     x2 = remote(to_give.at[0], from_x.at[2], sems, 4, to_x)
@@ -1046,11 +1109,16 @@
         leaving[k].wait_recv()
         value = value + f32(from_z[k])
     out_ref[...] = value * (1.0 / (2 * planes))
-    for copy in (*crossing, y0, x0, y1, x1, x2, y2, *leaving):
+    value = sum_at[2]
+    for k in range(len(others)):
+        adding[3 + k].wait_recv()
+        value = value + sum_from[3 + k]
+    sum_out[...] = value
+    for copy in (*crossing, y0, x0, y1, x1, x2, y2, *leaving, *adding):
         copy.wait_send()
 
 
-def settle_columns(planes, keep, send, pieces):
+def settle_columns(planes, keep, send, pieces, sums):
     rows, width = keep.shape[0], pieces.shape[2]
     tall = rows // planes
     half = planes // 2
@@ -1058,24 +1126,30 @@
     inside = pl.BlockSpec(memory_space=pltpu.VMEM)
     return pl.pallas_call(
         functools.partial(settle_kernel, planes),
-        in_specs=[inside, inside, pl.BlockSpec(memory_space=pl.ANY)],
-        out_specs=inside,
-        out_shape=jax.ShapeDtypeStruct((tall, width), jnp.float32),
+        in_specs=[inside, inside, pl.BlockSpec(memory_space=pl.ANY), inside],
+        out_specs=[inside, inside],
+        out_shape=[
+            jax.ShapeDtypeStruct((tall, width), jnp.float32),
+            jax.ShapeDtypeStruct(sums.shape, jnp.float32),
+        ],
         scratch_shapes=[
             pltpu.VMEM(pieces.shape, jnp.bfloat16),
             low(4, planes), low(4, planes), low(4, planes),
             low(3, half), low(3, half), low(2, half), low(planes), low(planes - 1),
+            pltpu.VMEM((3, *sums.shape), jnp.float32),
+            pltpu.VMEM((2 + planes, *sums.shape), jnp.float32),
             pltpu.SemaphoreType.DMA((4,)),
             pltpu.SemaphoreType.DMA((4,)), pltpu.SemaphoreType.DMA((4,)),
             pltpu.SemaphoreType.DMA((6,)), pltpu.SemaphoreType.DMA((6,)),
             pltpu.SemaphoreType.DMA((planes - 1,)), pltpu.SemaphoreType.DMA((planes - 1,)),
+            pltpu.SemaphoreType.DMA((2 + planes,)), pltpu.SemaphoreType.DMA((2 + planes,)),
         ],
         cost_estimate=pl.CostEstimate(flops=16 * 10 ** 9, bytes_accessed=60 * 2 ** 20, transcendentals=0),
         compiler_params=pltpu.CompilerParams(
             collective_id=3, has_side_effects=True, vmem_limit_bytes=58 * 2 ** 20
         ),
         name="settle_columns",
-    )(keep, send, pieces)
+    )(keep, send, pieces, sums)
 
 
 def bf(value):
@@ -1123,6 +1197,7 @@
     core, row, col = dp_rank % 2, mp_rank // 2, mp_rank % 2
     over_x = pairs_of(planes, lambda z, c, y, x: (z, c, y, 1 - x))
     over_y = pairs_of(planes, lambda z, c, y, x: (z, c, 1 - y, x))
+    over_xy = pairs_of(planes, lambda z, c, y, x: (z, c, 1 - y, 1 - x))
     over_c = pairs_of(planes, lambda z, c, y, x: (z, 1 - c, y, x))
     swap_yc = pairs_of(planes, lambda z, c, y, x: (z, y, c, x))
     swap_xc = pairs_of(planes, lambda z, c, y, x: (z, x, y, c))
@@ -1130,6 +1205,8 @@
     along_z = [
         [flat(z, c, y, x) for z in range(planes)] for c in range(2) for y in range(2) for x in range(2)
     ]
+
+    along_dp = [[flat(z, c, y, x) for z in range(planes) for c in range(2)] for y in range(2) for x in range(2)]
 
     def go(value, pairs):
         return lax.ppermute(value, AXES, pairs)
@@ -1190,7 +1267,7 @@
     count = small.shape[0] * small.shape[1]
     small = jnp.pad(small.reshape(count, -1), ((0, -count % 8), (0, 0)))
     piece = lax.dynamic_index_in_dim(stacked(0), mp_rank, 0, keepdims=False)
-    full, small, token_rows, cot_rows = gather_four(planes, piece, small, tokens, cotangent)
+    full, small, token_rows = gather_four(planes, piece, small, tokens)
     first_four = full.reshape(4, width, width)
     small = jnp.transpose(small[:, :count].reshape(-1, LAYERS, 9, width // (2 * planes)), (1, 2, 0, 3))
     small = small.reshape(LAYERS, 9, width)
@@ -1201,19 +1278,21 @@
     fc_slice[0] = gather_dp(fc_weight[0])
     fc2_slice[0] = gather_dp(fc2_weight[0].T)
     qkv1 = qkv_weight[1]
-    pair_one = gather_dp(after(jnp.where(row == 0, qkv1[:, :width], qkv1[:, width:2 * width]), small))
-    pair_two = gather_dp(after(jnp.where(col == 0, qkv1[:, 2 * width:], proj_weight[1]), small))
-
-    def pair_send(whole, over):
-        tall = whole.shape[0] // 2
-        return go(lax.dynamic_slice_in_dim(whole, core * tall, tall, axis=0), over)
-
-    def pair_join(whole, got, beside, bit):
+    pair = gather_dp(jnp.where(row == 0, qkv1[:, :width], qkv1[:, width:2 * width]))
+    tall = width // 2
+
+    def pair_join(whole, got, bit):
+        got = jnp.concatenate(got, axis=0)
+        beside = go(got, over_c)
         other = jnp.concatenate([jnp.where(core == 0, got, beside), jnp.where(core == 0, beside, got)], axis=0)
         return jnp.where(bit == 0, whole, other), jnp.where(bit == 0, other, whole)
 
-    def turned_weight(slice_, moved):
-        return jnp.where(col == core, slice_, moved)
+    def halves(value):
+        middle = value.shape[0] // 2
+        return value[:middle], value[middle:]
+
+    def padded(value):
+        return jnp.pad(value, ((0, 0), (0, -width % LANES)))
 
     def normal(value, layer, which):
         centred, rate = norm_parts(value)
@@ -1221,9 +1300,9 @@
 
     def attend(layer, hidden, w):
         normed = normal(hidden, layer, 0)
-        key = bf(nn(normed, w["k"]))
+        key = padded(bf(nn(normed, w["k"])))
         key_other = go(key, over_c)
-        value = bf(nn(normed, w["v"]) + small[layer, 5])
+        value = padded(bf(nn(normed, w["v"]) + small[layer, 5]))
         value_other = go(value, over_c)
         query = bf(nn(normed, w["q"]) + small[layer, 4])
         return normed, query, key, key_other, value, value_other
@@ -1232,45 +1311,56 @@
         middle = hidden + nn(attended, w["proj"]) + small[layer, 6]
         return middle, normal(middle, layer, 1)
 
+    turn_far = pairs_of(planes, lambda z, c, y, x: (z, y, c, 1 - x))
+
+    def cot_regroup():
+        mine = lax.dynamic_index_in_dim(cotangent, col, 0, keepdims=False)
+        theirs = lax.dynamic_index_in_dim(cotangent, 1 - col, 0, keepdims=False)
+        return mine, go(mine, swap_yc), go(theirs, turn_far)
+
     saved = []
     hidden = f32(token_rows.reshape(-1, width))
     w = dict(q=first_four[0], k=first_four[1], v=first_four[2], proj=first_four[3])
+    first_fc = after(fc_slice[0], units_bias)
+    fc_moved = go(first_fc, swap_xc)
+    fc_slice[1] = gather_dp(after(fc_weight[1], small))
     parts = attend(0, hidden, w)
-    moved_fc = go(after(fc_slice[0], units_bias), swap_xc)
-    *parts, moved_fc, fc2_now, pair_one = fence(*parts, moved_fc, fc2_slice[0], pair_one)
+    *parts, fc_moved, fc2_now, pair = fence(*parts, fc_moved, fc2_slice[0], pair)
     normed, query, key, key_other, value, value_other = parts
-    fc_slice[1] = gather_dp(after(fc_weight[1], normed))
-    moved_fc2 = go(fc2_now, swap_xc)
-    got_one = pair_send(pair_one, over_y)
+    v1 = gather_dp(after(qkv1[:, 2 * width:], normed))
+    fc2_parts = halves(fc2_now)
+    pair_parts = halves(lax.dynamic_slice_in_dim(pair, core * tall, tall, axis=0))
+    fc2_top = go(fc2_parts[0], swap_xc)
+    got = [go(pair_parts[0], over_y)]
     attended, lse = attention(place, slot, query, key, key_other, value, value_other)
-    attended, lse, moved_fc2, got_one = fence(attended, lse, moved_fc2, got_one)
-    fc2_slice[1] = gather_dp(after(fc2_weight[1].T, attended))
+    attended, lse, fc2_top, got[0] = fence(attended, lse, fc2_top, got[0])
+    proj1 = gather_dp(after(proj_weight[1], attended))
+    fc2_end = go(fc2_parts[1], swap_xc)
+    got.append(go(pair_parts[1], over_y))
     middle, normed_two = project(0, hidden, attended, w)
-    w["fc"] = turned_weight(fc_slice[0], moved_fc)
-    w["fc2"] = turned_weight(fc2_now, moved_fc2)
-    beside_one = go(got_one, over_c)
-    middle, normed_two, w["fc"], w["fc2"], beside_one, pair_two = fence(
-        middle, normed_two, w["fc"], w["fc2"], beside_one, pair_two
-    )
-    got_two = pair_send(pair_two, over_x)
+    middle, normed_two, fc2_end, got[1], fc_now = fence(middle, normed_two, fc2_end, got[1], fc_slice[1])
+    w["fc"] = (first_fc, fc_moved)
+    w["fc2"] = (fc2_now, fc2_top, fc2_end)
+    fc2_slice[1] = gather_dp(after(fc2_weight[1].T, middle))
+    fc_moved = go(fc_now, swap_xc)
     ff_out, rows_in, active, slope = units(False, normed_two, w["fc"], w["fc2"], units_bias[0:1])
-    ff_out, rows_in, active, slope, got_two, fc_now = fence(ff_out, rows_in, active, slope, got_two, fc_slice[1])
+    ff_out, rows_in, active, slope, fc_moved, v1 = fence(ff_out, rows_in, active, slope, fc_moved, v1)
     saved.append((hidden, *parts, attended, lse, middle, rows_in, active, slope, w))
-    moved_fc = go(fc_now, swap_xc)
-    beside_two = go(got_two, over_c)
-    w = dict()
-    w["q"], w["k"] = pair_join(pair_one, got_one, beside_one, row)
-    w["v"], w["proj"] = pair_join(pair_two, got_two, beside_two, col)
+    w = dict(v=v1, proj=proj1, fc=(fc_now, fc_moved))
+    w["q"], w["k"] = pair_join(pair, got, row)
     hidden = middle + ff_out + small[0, 7]
-    *parts, moved_fc, fc2_now = fence(*attend(1, hidden, w), moved_fc, fc2_slice[1])
+    cot_moved = cot_regroup()
+    *parts, cot_moved, fc2_now = fence(*attend(1, hidden, w), cot_moved, fc2_slice[1])
     normed, query, key, key_other, value, value_other = parts
-    moved_fc2 = go(fc2_now, swap_xc)
+    fc2_parts = halves(fc2_now)
+    fc2_top = go(fc2_parts[0], swap_xc)
     attended, lse = attention(place, slot, query, key, key_other, value, value_other)
-    attended, lse, moved_fc2 = fence(attended, lse, moved_fc2)
+    attended, lse, fc2_top = fence(attended, lse, fc2_top)
+    fc2_end = go(fc2_parts[1], swap_xc)
     middle, normed_two = project(1, hidden, attended, w)
-    w["fc"] = turned_weight(fc_now, moved_fc)
-    w["fc2"] = turned_weight(fc2_now, moved_fc2)
-    middle, normed_two, w["fc"], w["fc2"] = fence(middle, normed_two, w["fc"], w["fc2"])
+    w["fc2"] = (fc2_now, fc2_top, fc2_end)
+    middle, normed_two, fc2_end = fence(middle, normed_two, fc2_end)
+    w["fc2"] = (fc2_now, fc2_top, fc2_end)
     ff_out, rows_in, active, slope = units(False, normed_two, w["fc"], w["fc2"], units_bias[1:2])
     saved.append((hidden, *parts, attended, lse, middle, rows_in, active, slope, w))
     final = bf(middle + ff_out + small[1, 7])
@@ -1279,13 +1369,39 @@
     results = [None] * LAYERS
 
     def units_split(value):
+        quarters = value.reshape(planes, 2, -1, width)
+        kept = lax.dynamic_index_in_dim(quarters, col, 1, keepdims=False)
+        return kept, lax.dynamic_index_in_dim(quarters, 1 - col, 1, keepdims=False)
+
+    def halves_of(value):
         halves = value.reshape(2, -1, width)
         kept = lax.dynamic_index_in_dim(halves, col, 0, keepdims=False)
         return kept, lax.dynamic_index_in_dim(halves, 1 - col, 0, keepdims=False)
 
+    def sum_dp(value):
+        return lax.psum_scatter(value, AXES, axis_index_groups=along_dp, scatter_dimension=0, tiled=True)
+
+    def mp_pieces(*values):
+        def piece(y, x):
+            parts = []
+            for value in values:
+                size = value.shape[1] // 4
+                parts.append(lax.dynamic_slice_in_dim(value, (2 * y + x) * size, size, axis=1))
+            return jnp.concatenate(parts, axis=1)
+
+        return [
+            piece(row, col),
+            go(piece(row, 1 - col), over_x),
+            go(piece(1 - row, col), over_y),
+            go(piece(1 - row, 1 - col), over_xy),
+        ]
+
+    def total_of(pieces):
+        return sum(f32(piece) for piece in pieces[1:]) + f32(pieces[0])
+
     def mlp_back(layer, out_grad, *held):
         (*_, active, slope, w) = saved[layer]
-        return units(True, out_grad, w["fc2"], w["fc"], slope)
+        return units(True, out_grad, w["fc2"], w["fc"], slope, active)
 
     def middle_back(layer, grad, da2):
         middle, w = saved[layer][9], saved[layer][-1]
@@ -1305,19 +1421,19 @@
         return middle_grad + part, gain, shift
 
     def mixed_of(dq, dkm, dkt, dvm, dvt):
-        dk = bf(dkm + f32(go(dkt, over_c)))
-        dv = bf(dvm + f32(go(dvt, over_c)))
+        dk = bf(dkm + f32(go(dkt, over_c)))[:, :width]
+        dv = bf(dvm + f32(go(dvt, over_c)))[:, :width]
         return dq, dk, dv
 
     def last_sum(parts, away, side):
         return bf(f32(parts[3]) + f32(away) + f32(side))
 
-    turn_far = pairs_of(planes, lambda z, c, y, x: (z, y, c, 1 - x))
-
     def regroup(value):
+        value = padded(value)
         return go(value[:local], swap_yc), go(value[local:], turn_far)
 
     def settle(value, mine, theirs):
+        mine, theirs = mine[:, :width], theirs[:, :width]
         mine = jnp.where(row == core, value[:local], mine)
         return f32(jnp.stack([jnp.where(col == 0, mine, theirs), jnp.where(col == 0, theirs, mine)]))
 
@@ -1332,68 +1448,65 @@
         send = lax.dynamic_index_in_dim(columns, 1 - core, 1, keepdims=False)
         return keep.reshape(-1, left.shape[0]), send.reshape(-1, left.shape[0])
 
-    grad = f32(cot_rows.reshape(-1, width))
-    out_grad = cot_rows.reshape(-1, width)
+    out_grad = jnp.concatenate([jnp.where(row == core, cot_moved[0], cot_moved[1]), cot_moved[2]], axis=0)
+    grad = f32(out_grad)
     final, out_grad = fence(final, out_grad)
-    da2, rows_grad, inner_grad, units_sum = mlp_back(1, out_grad)
-    final, da2, rows_grad, inner_grad, units_sum = fence(final, da2, rows_grad, inner_grad, units_sum)
-    fc2_grad = bf(tn(rows_grad, saved[1][11]))
-    fc2_grad, rows_in = fence(fc2_grad, saved[1][10])
+    da2, rows_grad, inner_grad, units_sum, fc2_grad = mlp_back(1, out_grad)
+    final, da2, inner_grad, units_sum, fc2_grad = fence(final, da2, inner_grad, units_sum, fc2_grad)
     fc2_sum = sum_z(fc2_grad)
-    fc_grad = bf(tn(rows_in, inner_grad))
+    fc_kept, fc_sent = units_split(bf(tn(saved[1][10], inner_grad)))
+    fc_kept, fc_top, fc_end, da2 = fence(fc_kept, fc_sent[:planes // 2], fc_sent[planes // 2:], da2)
+    fc_away = [go(fc_top, over_x)]
     middle_grad, branch, attended_grad, gain_two, shift_two, attn_out_grad = middle_back(1, grad, da2)
-    proj_parts = chip_sums(saved[1][7], branch)
-    fc_grad, middle_grad, branch, attended_grad, *proj_parts = fence(
-        fc_grad, middle_grad, branch, attended_grad, *proj_parts
+    proj_grad = bf(tn(saved[1][7], branch))
+    fc_away[0], fc_end, middle_grad, branch, attended_grad, proj_grad = fence(
+        fc_away[0], fc_end, middle_grad, branch, attended_grad, proj_grad
     )
-    fc_sum = sum_z(fc_grad)
-    proj_far = go(proj_parts[0], over_y)
-    proj_near = go(proj_parts[1], over_y)
+    proj_sum = sum_dp(proj_grad)
+    fc_away.append(go(fc_end, over_x))
     final_moved = regroup(final)
-    back = fence(*heads_back(1, attended_grad), fc2_sum, proj_far, proj_near, *final_moved)
-    fc2_sum, proj_far, proj_near, *final_moved = back[5:]
+    back = fence(*heads_back(1, attended_grad), fc2_sum, fc_away[1], *final_moved)
+    fc2_sum, fc_away[1], *final_moved = back[5:]
     dq, dk, dv = mixed_of(*back[:5])
-    dq, dk, dv = fence(dq, dk, dv)
+    dq_grad = bf(tn(saved[1][1], back[0]))
+    dq, dk, dv, dq_grad = fence(dq, dk, dv, dq_grad)
+    dq_sum = sum_dp(dq_grad)
     below, gain_one, shift_one = input_back(1, middle_grad, dq, dk, dv)
     out_grad_low = bf(below)
     sums_one = bias_sums((gain_one, gain_two), (shift_one, shift_two), dq, dv, attn_out_grad, out_grad)
     out_grad_low, below, dq, dk, dv, sums_one = fence(out_grad_low, below, dq, dk, dv, sums_one)
-    parts = chip_sums(saved[1][1], jnp.concatenate([dq, dk, dv], axis=1))
-    out_grad_low, *parts = fence(out_grad_low, *parts)
-    side_far = go(parts[0], over_x)
-    side_near = go(parts[2], over_x)
-    proj_side = go(add_pair(proj_parts[2], proj_far), over_x)
-    fc2_kept, fc2_sent = units_split(fc2_sum)
+    dkv_grad = bf(tn(saved[1][1], jnp.concatenate([dk, dv], axis=1)))
+    fc_joined = add_pair(fc_kept, jnp.concatenate(fc_away, axis=0))
+    fc2_kept, fc2_sent = halves_of(fc2_sum)
+    out_grad_low, dkv_grad, fc_joined, fc2_sent = fence(out_grad_low, dkv_grad, fc_joined, fc2_sent)
+    dkv_sum = sum_dp(dkv_grad)
+    fc_sum = sum_z(fc_joined.reshape(-1, width))
     fc2_away = go(fc2_sent, over_x)
-    da2, rows_grad, inner_grad, units_low = mlp_back(0, out_grad_low)
-    da2, rows_grad, inner_grad, units_low, side_far, side_near, fc_sum, proj_side, fc2_away = fence(
-        da2, rows_grad, inner_grad, units_low, side_far, side_near, fc_sum, proj_side, fc2_away
+    da2, rows_grad, inner_grad, units_low, fc2_grad = mlp_back(0, out_grad_low)
+    da2, inner_grad, units_low, fc2_grad, fc2_away, proj_sum, dq_sum = fence(
+        da2, inner_grad, units_low, fc2_grad, fc2_away, proj_sum, dq_sum
     )
-    proj_sum = sum_z(last_sum(proj_parts, proj_near, proj_side))
     fc2_high = add_pair(fc2_kept, fc2_away)
-    fc_kept, fc_sent = units_split(fc_sum)
-    side_far = add_pair(parts[1], side_far)
-    fc2_grad = bf(tn(rows_grad, saved[0][11]))
-    fc2_grad, rows_in = fence(fc2_grad, saved[0][10])
-    fc2_sum = sum_z(fc2_grad)
-    fc_grad = bf(tn(rows_in, inner_grad))
+    fc2_kept, fc2_sent = units_split(fc2_grad)
+    top = planes // 2
+    fc2_kept, fc2_top, fc2_end, da2, fc2_high = fence(fc2_kept, fc2_sent[:top], fc2_sent[top:], da2, fc2_high)
+    fc2_away = [go(fc2_top, over_x)]
+    fc_kept, fc_sent = units_split(bf(tn(saved[0][10], inner_grad)))
+    fc2_away[0], fc2_end, fc_kept, fc_sent, da2 = fence(fc2_away[0], fc2_end, fc_kept, fc_sent, da2)
+    fc2_away.append(go(fc2_end, over_x))
     middle_grad, branch, attended_grad, gain_two, shift_two, attn_out_grad = middle_back(0, below, da2)
-    low_parts = chip_sums(saved[0][7], branch)
-    fc_sent, fc_grad, middle_grad, branch, attended_grad, side_far, *low_parts = fence(
-        fc_sent, fc_grad, middle_grad, branch, attended_grad, side_far, *low_parts
+    proj_grad = bf(tn(saved[0][7], branch))
+    fc2_away[1], fc_sent, middle_grad, branch, attended_grad, proj_grad = fence(
+        fc2_away[1], fc_sent, middle_grad, branch, attended_grad, proj_grad
     )
-    away = go(side_far, over_y)
     fc_away = go(fc_sent, over_x)
-    fc_sum = sum_z(fc_grad)
-    low_far = go(low_parts[0], over_y)
-    low_near = go(low_parts[1], over_y)
-    back = fence(*heads_back(0, attended_grad), fc_away, low_far, low_near, away, proj_sum, fc2_sum)
-    fc_away, low_far, low_near, away, proj_sum, fc2_sum = back[5:]
-    results_one = [add_pair(fc_kept, fc_away), fc2_high, proj_sum]
+    fc2_low = sum_z(add_pair(fc2_kept, jnp.concatenate(fc2_away, axis=0)).reshape(-1, width))
+    back = fence(*heads_back(0, attended_grad), fc_away, dkv_sum)
+    fc_away, dkv_sum = back[5:]
     dq, dk, dv = mixed_of(*back[:5])
-    qkv_joined = bf(f32(parts[3]) + f32(side_near) + f32(away))
-    dq, dk, dv, qkv_joined = fence(dq, dk, dv, qkv_joined)
-    qkv_sum = sum_z(qkv_joined)
+    dq, dk, dv, proj_grad = fence(dq, dk, dv, proj_grad)
+    proj_low = sum_dp(proj_grad)
+    fc_low = sum_z(add_pair(fc_kept, fc_away).reshape(-1, width))
     lowest, gain_one, shift_one = input_back(0, middle_grad, dq, dk, dv)
     sums_zero = bias_sums((gain_one, gain_two), (shift_one, shift_two), dq, dv, attn_out_grad, out_grad_low)
     low = bf(lowest)
@@ -1409,32 +1522,29 @@
             (spread[None, :, None] * jnp.concatenate([units_low, units_sum], axis=0)[:, None, :]).reshape(2 * 4, width),
         ]
     )
-    fc2_kept, fc2_sent = units_split(fc2_sum)
-    low, sums, pieces, keep, send, fc2_sent, results_one = fence(low, sums, pieces, keep, send, fc2_sent, results_one)
-    results_one[0] = turn_xc(results_one[0])
-    results_one[1] = turn_xc(results_one[1])
+    low, sums, pieces, keep, send, dq_sum, dkv_sum, proj_sum, fc_sum, fc2_low = fence(
+        low, sums, pieces, keep, send, dq_sum, dkv_sum, proj_sum, fc_sum, fc2_low
+    )
+    held_rows = proj_sum.shape[0]
+    turned = turn_xc(jnp.concatenate([fc_sum, fc2_high, fc2_low], axis=0))
     low_moved = regroup(low)
-    fc2_away = go(fc2_sent, over_x)
-    low_side = go(add_pair(low_parts[2], low_far), over_x)
-    sums = lax.psum(sums, AXES)
-    qkv_low = settle_columns(planes, keep, send, pieces)
-    qkv_low, fc2_away, low_side, sums, fc_sum, qkv_sum, results_one, *low_moved = fence(
-        qkv_low, fc2_away, low_side, sums, fc_sum, qkv_sum, results_one, *low_moved
+    columns = mp_pieces(jnp.concatenate([dq_sum, dkv_sum], axis=1), proj_sum)
+    qkv_low, sums = settle_columns(planes, keep, send, pieces, sums)
+    qkv_low, sums, fc_low, proj_low, turned, columns, low_moved = fence(
+        qkv_low, sums, fc_low, proj_low, turned, columns, low_moved
     )
-    proj_low = sum_z(last_sum(low_parts, low_near, low_side))
-    fc_kept, fc_sent = units_split(fc_sum)
-    results_zero = [
-        turn_xc(add_pair(fc_kept, go(fc_sent, over_x))),
-        turn_xc(add_pair(fc2_kept, fc2_away)),
-        proj_low,
-    ]
+    columns = total_of(columns)
+    turned = turned.reshape(3, held_rows, width)
+    qkv_high = columns[:, :third]
+    results_zero = [turn_xc(fc_low), turned[2], total_of(mp_pieces(proj_low))]
+    results_one = [turned[0], turned[1], columns[:, third:]]
     outputs = settle(final, *final_moved)
     input_grad = settle(low, *low_moved)
     held = width // (2 * planes)
     sums = lax.dynamic_slice_in_dim(sums, dp_rank * held, held, axis=1) * factor
     unit_rows = lax.dynamic_index_in_dim(sums[16:].reshape(2, 4, held), mp_rank, 1, keepdims=False)
     sums = sums[:16].reshape(2, 8, held)
-    qkv_high = f32(qkv_sum) * factor
+    qkv_high = qkv_high * factor
     results = [results_zero, results_one]
     return (
         outputs,

time: 1640 us -> 1440 us (0.88)
  matrix products: 252 us -> 167 us
  local copies, waits for them, and re-layouts: 198 us -> 143 us
  waiting for transfers between devices: 126 us -> 72.2 us
  other arithmetic: 142 us -> 120 us
    dot_general x28 -> x6, matrix products: 146 us -> 63.1 us  [tn(): lax.dot_general(a, b, (((0,), (0,)), ((), ())), preferred_element_type=jn...]
    optimization_barrier x16 -> x2, local copies, waits for them, and re-layouts: 42.7 us -> 4.37 us  [fence(): return lax.optimization_barrier(values)]
    reduce_scatter x5 -> x1, waiting for transfers between devices: 34.9 us -> 0.02 us  [sum_z(): lax.psum_scatter(value, AXES, axis_index_groups=along_z, scatter_dimensio...]
    select_n x5 -> x1, other arithmetic: 27.8 us -> 0.99 us  [quick_body(): jnp.where(row == core, cot_moved[0], cot_moved[1])]
    pallas_call x1, Pallas kernels: 168 us -> 149 us  [gather_four(): pl.pallas_call(functools.partial(gather_kernel, planes), in_specs=[anywhe...]
    ppermute x50 -> x38, starting transfers between devices: 63.2 us -> 76.8 us  [go(): return lax.ppermute(value, AXES, pairs)]
    ppermute x50 -> x38, waiting for transfers between devices: 66.8 us -> 56.2 us  [go(): return lax.ppermute(value, AXES, pairs)]
    convert_element_type x21 -> x15, other arithmetic: 50.3 us -> 40.8 us  [bf(): return value.astype(jnp.bfloat16)]
  transfers between devices with their start and end apart: 64 -> 53, of which waited for: 10 -> 8; matrix products, arithmetic and copies ran while one was open for 30% -> 27% of each run, Pallas kernels for 41% -> 46%
where the time goes in v3:
time: 1440 us; the launch traced here: 1420 us
  Pallas kernels  823 us (57%)
  matrix products  167 us (12%)
  local copies, waits for them, and re-layouts  143 us (10%)
  other arithmetic  120 us (8%)
  starting transfers between devices  78.1 us (5%)
  waiting for transfers between devices  72.2 us (5%)
  between operations  16.3 us (1%)
    pallas_call x4, Pallas kernels, units(): pl.pallas_call(functools.partial(units_kernel, back, (len(wa) - 1, len(wb...  344 us
    pallas_call x1, Pallas kernels, gather_four(): pl.pallas_call(functools.partial(gather_kernel, planes), in_specs=[anywhe...  149 us
    pallas_call x1, Pallas kernels, settle_columns(): pl.pallas_call(functools.partial(settle_kernel, planes), in_specs=[inside...  136 us
    pallas_call x2, Pallas kernels, attention_back(): pl.pallas_call(functools.partial(attend_back_kernel, width, blocks, place...  105 us
    pallas_call x2, Pallas kernels, attention(): pl.pallas_call(functools.partial(attend_kernel, width, blocks, place.shap...  88.4 us
    ppermute x38, starting transfers between devices, go(): return lax.ppermute(value, AXES, pairs)  76.8 us
    dot_general x6, matrix products, tn(): lax.dot_general(a, b, (((0,), (0,)), ((), ())), preferred_element_type=jn...  63.1 us
    dot_general x8, matrix products, nt(): lax.dot_general(a, b, (((1,), (1,)), ((), ())), preferred_element_type=jn...  57.3 us
  transfers between devices with their start and end apart: 53, of which 8 were waited for; matrix products, arithmetic and copies ran while one was open for 27% of the time, Pallas kernels for 46%

profile of v3, /device:TPU:1, one launch (start us, length us, event | category | flops | bytes accessed | tf_op | source)
XLA Modules:
  0.0 1420.1 jit_solution(9913854781012279048)
XLA Ops:
  15.1 3.6 copy.135.token_ref
  21.9 149.2 %gather_four.1 = (bf16[4,8,200,1600]{3,2,1,0:T(8,128)(2,1)}, f32[8,24,200]{2,1,0:T(8,128)}, bf16[2,256,1600]{2,1,0:T(8,128)(2,1)}) custom-call(bf16[200,1600]{1,0:T(8,128)(2,1)} %fusion.34.piece_ref, f32[24,200]{1,0:T(8,128)} %pad_convert_fusion.small_ref, bf16[2,256,1600]{2,1,0:T(8,128)(2,1)} %copy.135.token_ref), custom_call_target="tpu_custom_call" | custom-call | bytes 314572800 | tf_op jit(solution)/shard_map/gather_four/pallas_call | solution.py:731
  172.5 3.5 collective-permute-start.2
  182.3 13.6 fusion.52
  195.9 3.5 add_convert_fusion.9
  199.9 3.2 convolution_convert_fusion.9
  209.5 7.2 add_convert_fusion.10.q_ref
  218.0 15.5 %all-gather.11.cloned.1.call-done = bf16[1600,1600]{1,0:T(8,128)(2,1)} async-done(((bf16[200,1600]{1,0:T(8,128)(2,1)}), bf16[1600,1600]{1,0:T(8,128)(2,1)}) %all-gather.11.cloned.1.call-update) | async-done | bytes 5120016 | tf_op jit(solution)/shard_map/all_gather | solution.py:1254
  233.5 8.2 collective-permute-done.3.refs_3_.refs_5_
  241.7 5.8 fusion.54
  249.6 3.5 constant_dynamic-slice_fusion.12
  253.1 3.5 collective-permute-start.5
  263.9 44.1 %attention.2 = (bf16[512,1600]{1,0:T(8,128)(2,1)S(1)}, f32[13,2,512]{2,1,0:T(2,128)S(1)}) custom-call(s32[4]{0:T(128)S(1)} %reshape.492.place_ref, s32[8]{0:T(128)S(1)} %select_reduce_fusion.slot_ref, bf16[512,1600]{1,0:T(8,128)(2,1)S(1)} %copy-done.20, bf16[512,1664]{1,0:T(8,128)(2,1)S(1)} %pad.27.ko_ref, bf16[512,1664]{1,0:T(8,128)(2,1)S(1)} %copy-done.7, ...), custom_call_target="tpu_custom_call" | custom-call | flops 6979321856 | bytes 9830400 | tf_op jit(solution)/shard_map/attention/pallas_call | solution.py:543
  308.1 6.7 fusion.58
  325.3 89.7 %units.2 = (f32[512,1600]{1,0:T(8,128)}, bf16[2048,1600]{1,0:T(8,128)(2,1)}, bf16[2048,1600]{1,0:T(8,128)(2,1)}, bf16[2048,1600]{1,0:T(8,128)(2,1)}) custom-call(bf16[512,1600]{1,0:T(8,128)(2,1)} %add_convert_fusion.8.refs_0_, bf16[1600,1600]{1,0:T(8,128)(2,1)} %bitcast.249, bf16[1600,1600]{1,0:T(8,128)(2,1)} %all-gather.9.cloned.1.call-done.refs_2_.refs_1_, ...), custom_call_target="tpu_custom_call" | custom-call | flops 60000002048 | bytes 62914560 | tf_op jit(solution)/shard_map/units/pallas_call | solution.py:973
  415.3 5.5 broadcast_select_fusion.3
  420.8 3.5 fusion.51
  428.8 3.3 convolution_convert_fusion.8
  435.0 6.1 add_convert_fusion.5
  444.5 4.6 collective-permute-start.12
  451.4 9.3 add_convert_fusion.6.q_ref
  460.7 6.7 collective-permute-done.12
  468.9 5.3 fusion.53
  478.4 3.6 collective-permute-start.15
  483.5 44.3 %attention.3 = (bf16[512,1600]{1,0:T(8,128)(2,1)S(1)}, f32[13,2,512]{2,1,0:T(2,128)S(1)}) custom-call(s32[4]{0:T(128)S(1)} %reshape.492.place_ref, s32[8]{0:T(128)S(1)} %select_reduce_fusion.slot_ref, bf16[512,1600]{1,0:T(8,128)(2,1)S(1)} %copy-done.18, bf16[512,1664]{1,0:T(8,128)(2,1)S(1)} %pad.29.ko_ref, bf16[512,1664]{1,0:T(8,128)(2,1)} %collective-permute-done.10.ks_ref, ...), custom_call_target="tpu_custom_call" | custom-call | flops 6979321856 | bytes 9830400 | tf_op jit(solution)/shard_map/attention/pallas_call | solution.py:543
  534.9 7.6 fusion.59
  547.3 84.5 %units.3 = (f32[512,1600]{1,0:T(8,128)}, bf16[2048,1600]{1,0:T(8,128)(2,1)}, bf16[2048,1600]{1,0:T(8,128)(2,1)}, bf16[2048,1600]{1,0:T(8,128)(2,1)}) custom-call(bf16[512,1600]{1,0:T(8,128)(2,1)} %add_convert_fusion.4.refs_0_, bf16[1600,1600]{1,0:T(8,128)(2,1)} %all-gather.13.cloned.1.call-done.refs_1_.refs_2_, ...), custom_call_target="tpu_custom_call" | custom-call | flops 60000002048 | bytes 62914560 | tf_op jit(solution)/shard_map/units/pallas_call | solution.py:973
  631.9 4.9 multiply_reduce_fusion.7
  636.7 85.9 %units_back.2 = (f32[512,1600]{1,0:T(8,128)}, bf16[2048,1600]{1,0:T(8,128)(2,1)}, bf16[2048,1600]{1,0:T(8,128)(2,1)}, f32[1,1600]{1,0:T(1,128)}, bf16[1600,1600]{1,0:T(8,128)(2,1)}) custom-call(bf16[512,1600]{1,0:T(8,128)(2,1)} %pad_maximum_fusion.3.refs_0_, bf16[1600,1600]{1,0:T(8,128)(2,1)} %all-gather.17.cloned.1.call-done.refs_2_.refs_1_, ...), custom_call_target="tpu_custom_call" | custom-call | flops 60000002048 | bytes 62914560 | tf_op jit(solution)/shard_map/units_back/pallas_call | solution.py:973
  722.7 18.3 %convolution_convert_fusion.5 = bf16[1600,1600]{1,0:T(8,128)(2,1)S(1)} fusion(bf16[2048,1600]{1,0:T(8,128)(2,1)} %get-tuple-element.243, bf16[2048,1600]{1,0:T(8,128)(2,1)} %get-tuple-element.244), kind=kOutput, calls=%fused_computation.7 | convolution fusion | flops 10488320000 | bytes 18227200 | tf_op jit(solution)/shard_map/dot_general | solution.py:407
  748.9 4.8 convert_reduce_fusion.6
  754.8 5.5 convolution_convert_fusion.3
  760.3 7.7 convolution_convert_fusion.7.do_ref
  768.0 8.2 collective-permute-done.16
  783.0 52.7 %attention_back.2 = (bf16[512,1600]{1,0:T(8,128)(2,1)S(1)}, f32[512,1664]{1,0:T(8,128)}, bf16[512,1664]{1,0:T(8,128)(2,1)S(1)}, f32[512,1664]{1,0:T(8,128)}, bf16[512,1664]{1,0:T(8,128)(2,1)S(1)}) custom-call(s32[4]{0:T(128)S(1)} %reshape.492.place_ref, s32[8]{0:T(128)S(1)} %select_reduce_fusion.slot_ref, bf16[512,1600]{1,0:T(8,128)(2,1)S(1)} %copy-done.19, ...), custom_call_target="tpu_custom_call" | custom-call | flops 17448304640 | bytes 24576000 | tf_op jit(solution)/shard_map/attention_back/pallas_call | solution.py:575
  839.9 7.7 convolution_convert_fusion.2
  847.7 3.2 fusion.3
  858.1 4.1 add_convert_fusion.2
  863.9 8.1 fusion.39
  872.1 5.3 fusion.40
  877.5 9.1 multiply_reduce_fusion.4
  888.0 5.4 fusion.50
  894.1 9.3 convolution_convert_fusion
  905.0 84.3 %units_back.3 = (f32[512,1600]{1,0:T(8,128)}, bf16[2048,1600]{1,0:T(8,128)(2,1)}, bf16[2048,1600]{1,0:T(8,128)(2,1)}, f32[1,1600]{1,0:T(1,128)}, bf16[1600,1600]{1,0:T(8,128)(2,1)}) custom-call(bf16[512,1600]{1,0:T(8,128)(2,1)} %get-tuple-element.277.refs_0_, bf16[1600,1600]{1,0:T(8,128)(2,1)} %all-gather.9.cloned.1.call-done.refs_2_.refs_1_, ...), custom_call_target="tpu_custom_call" | custom-call | flops 60000002048 | bytes 62914560 | tf_op jit(solution)/shard_map/units_back/pallas_call | solution.py:973
  992.1 4.6 dynamic-slice_bitcast_fusion.2
  998.9 16.8 %convolution_convert_fusion.4 = bf16[1600,1600]{1,0:T(8,128)(2,1)S(1)} fusion(bf16[2048,1600]{1,0:T(8,128)(2,1)} %get-tuple-element.292, bf16[2048,1600]{1,0:T(8,128)(2,1)S(1)} %bitcast.254), kind=kOutput, calls=%fused_computation.6 | convolution fusion | flops 10488320000 | bytes 18227200 | tf_op jit(solution)/shard_map/dot_general | solution.py:407
  1015.7 3.3 dynamic-slice_bitcast_fusion
  1019.0 9.5 collective-permute-done.23
  1034.0 5.5 convolution_convert_fusion.1
  1039.5 7.3 convolution_convert_fusion.6.do_ref
  1046.8 11.6 collective-permute-done.24
  1059.5 3.7 add_convert_fusion.1
  1068.5 52.7 %attention_back.3 = (bf16[512,1600]{1,0:T(8,128)(2,1)S(1)}, f32[512,1664]{1,0:T(8,128)}, bf16[512,1664]{1,0:T(8,128)(2,1)S(1)}, f32[512,1664]{1,0:T(8,128)}, bf16[512,1664]{1,0:T(8,128)(2,1)S(1)}) custom-call(s32[4]{0:T(128)S(1)} %reshape.492.place_ref, s32[8]{0:T(128)S(1)} %select_reduce_fusion.slot_ref, bf16[512,1600]{1,0:T(8,128)(2,1)S(1)} %copy-done.21, ...), custom_call_target="tpu_custom_call" | custom-call | flops 17448304640 | bytes 24576000 | tf_op jit(solution)/shard_map/attention_back/pallas_call | solution.py:575
  1123.6 4.8 add_convert_fusion
  1138.2 4.9 copy.163
  1146.9 4.1 fusion.1
  1154.0 6.3 fusion.60
  1160.4 6.2 fusion.61
  1166.7 7.1 fusion.22
  1181.0 4.1 slice_bitcast_fusion.5
  1207.2 136.0 %settle_columns.1 = (f32[200,1200]{1,0:T(8,128)}, f32[24,1600]{1,0:T(8,128)}) custom-call(bf16[800,512]{1,0:T(8,128)(2,1)} %bitcast.237, bf16[800,512]{1,0:T(8,128)(2,1)} %bitcast.236, bf16[4,512,1200]{2,1,0:T(8,128)(2,1)} %pad_maximum_fusion.1.piece_ref, f32[24,1600]{1,0:T(8,128)} %concatenate.101.sum_ref), custom_call_target="tpu_custom_call" | custom-call | flops 16000000000 | bytes 62914560 | tf_op jit(solution)/shard_map/settle_columns/pallas_call | solution.py:1127
  1343.2 24.1 %collective-permute-start.31 = (bf16[200,1600]{1,0:T(8,128)(2,1)}, bf16[200,1600]{1,0:T(8,128)(2,1)S(1)}, u32[]{:S(2)}, u32[]{:S(2)}) collective-permute-start(bf16[200,1600]{1,0:T(8,128)(2,1)} %pad_maximum_fusion.9), channel_id=1, source_target_pairs={{0,3},{1,2},{2,1},{3,0},{4,7},{5,6},{6,5},{7,4},{8,11},{9,10},{10,... | collective-permute-start | bytes 1920008 | tf_op jit(solution)/shard_map/ppermute | solution.py:1212
  1370.5 10.6 collective-permute-done.31
  1392.5 3.6 collective-permute-start.37
  (529 shorter events, 207.3 us)
Async XLA Ops:
  7.2 172.2 %all-gather.21.cloned.1.call-start = ((), (), s32[]{:S(2)}) async-start(), calls=%async_computation.15 | async-start | bytes 5990400 | tf_op jit(solution)/shard_map/all_gather | solution.py:1254
  9.8 208.2 %all-gather.9.cloned.1.call-start = ((), (), s32[]{:S(2)}) async-start(), calls=%async_computation.8 | async-start | bytes 5990400 | tf_op jit(solution)/shard_map/all_gather | solution.py:1254
  11.0 222.4 %all-gather.11.cloned.1.call-start = ((), (), s32[]{:S(2)}) async-start(), calls=%async_computation.9 | async-start | bytes 5990400 | tf_op jit(solution)/shard_map/all_gather | solution.py:1254
  14.9 302.3 %all-gather.13.cloned.1.call-start = ((), (), s32[]{:S(2)}) async-start(), calls=%async_computation.10 | async-start | bytes 5990400 | tf_op jit(solution)/shard_map/all_gather | solution.py:1254
  172.4 248.4 %all-gather.15.cloned.1.call-start = ((), (), s32[]{:S(2)}) async-start(), calls=%async_computation.11 | async-start | bytes 5990400 | tf_op jit(solution)/shard_map/all_gather | solution.py:1254
  172.5 6.8 collective-permute-start.2
  179.3 28.2 %copy-start.86 = (f32[1600]{0:T(1024)}, f32[1600]{0:T(1024)S(1)}, u32[]{:S(2)}) copy-start(f32[1600]{0:T(1024)S(1)} %get-tuple-element.441) | copy-start | bytes 19204
  179.3 136.0 %copy-start.88 = (f32[1600]{0:T(1024)}, f32[1600]{0:T(1024)S(1)}, u32[]{:S(2)}) copy-start(f32[1600]{0:T(1024)S(1)} %get-tuple-element.436) | copy-start | bytes 19204
  179.3 245.6 %copy-start.91 = (f32[1600]{0:T(1024)}, f32[1600]{0:T(1024)S(1)}, u32[]{:S(2)}) copy-start(f32[1600]{0:T(1024)S(1)} %get-tuple-element.433) | copy-start | bytes 19204
  179.4 62.3 %collective-permute-start.3 = (bf16[1600,1600]{1,0:T(8,128)(2,1)}, bf16[1600,1600]{1,0:T(8,128)(2,1)}, u32[]{:S(2)}, u32[]{:S(2)}) collective-permute-start(bf16[1600,1600]{1,0:T(8,128)(2,1)} %bitcast.248), channel_id=1, source_target_pairs={{1,4},{3,6},{4,1},{6,3},{9,12},{11,14},{12,9},{14,11},{17,20},{19,... | collective-permute-start | bytes 15360008 | tf_op jit(solution)/shard_map/ppermute | solution.py:1212
  199.5 61.4 %copy-start = (bf16[512,1664]{1,0:T(8,128)(2,1)}, bf16[512,1664]{1,0:T(8,128)(2,1)S(1)}, u32[]{:S(2)}) copy-start(bf16[512,1664]{1,0:T(8,128)(2,1)S(1)} %pad.28.vo_ref) | copy-start | bytes 5111812
  199.5 17.1 %collective-permute-start.1 = (bf16[512,1664]{1,0:T(8,128)(2,1)S(1)}, bf16[512,1664]{1,0:T(8,128)(2,1)}, u32[]{:S(2)}, u32[]{:S(2)}) collective-permute-start(bf16[512,1664]{1,0:T(8,128)(2,1)S(1)} %pad.28.vo_ref), channel_id=1, source_target_pairs={{0,4},{1,5},{2,6},{3,7},{4,0},{5,1},{6,2},{7,3},{8,12},{9,13},{10,... | collective-permute-start | bytes 5111816 | tf_op jit(solution)/shard_map/ppermute | solution.py:1212
  207.2 53.7 %copy-start.2 = (bf16[512,1664]{1,0:T(8,128)(2,1)}, bf16[512,1664]{1,0:T(8,128)(2,1)S(1)}, u32[]{:S(2)}) copy-start(bf16[512,1664]{1,0:T(8,128)(2,1)S(1)} %pad.27.ko_ref) | copy-start | bytes 5111812
  207.2 9.5 collective-permute-start
  241.6 227.3 %all-gather.17.cloned.1.call-start = ((), (), s32[]{:S(2)}) async-start(), calls=%async_computation.12 | async-start | bytes 5990400 | tf_op jit(solution)/shard_map/all_gather | solution.py:1254
  247.4 60.6 %collective-permute-start.4 = (bf16[800,1600]{1,0:T(8,128)(2,1)}, bf16[800,1600]{1,0:T(8,128)(2,1)}, u32[]{:S(2)}, u32[]{:S(2)}) collective-permute-start(bf16[800,1600]{1,0:T(8,128)(2,1)} %get-tuple-element.469), channel_id=1, source_target_pairs={{1,4},{3,6},{4,1},{6,3},{9,12},{11,14},{12,9},{14,11},{17,20},{19,... | collective-permute-start | bytes 7680008 | tf_op jit(solution)/shard_map/ppermute | solution.py:1212
  253.1 54.9 %collective-permute-start.5 = (bf16[400,1600]{1,0:T(8,128)(2,1)}, bf16[400,1600]{1,0:T(8,128)(2,1)}, u32[]{:S(2)}, u32[]{:S(2)}) collective-permute-start(bf16[400,1600]{1,0:T(8,128)(2,1)} %get-tuple-element.467), channel_id=1, source_target_pairs={{0,2},{1,3},{2,0},{3,1},{4,6},{5,7},{6,4},{7,5},{8,10},{9,11},{10,... | collective-permute-start | bytes 3840008 | tf_op jit(solution)/shard_map/ppermute | solution.py:1212
  258.3 58.9 %collective-permute-start.7 = (bf16[400,1600]{1,0:T(8,128)(2,1)}, bf16[400,1600]{1,0:T(8,128)(2,1)}, u32[]{:S(2)}, u32[]{:S(2)}) collective-permute-start(bf16[400,1600]{1,0:T(8,128)(2,1)} %get-tuple-element.466), channel_id=1, source_target_pairs={{0,2},{1,3},{2,0},{3,1},{4,6},{5,7},{6,4},{7,5},{8,10},{9,11},{10,... | collective-permute-start | bytes 3840008 | tf_op jit(solution)/shard_map/ppermute | solution.py:1212
  258.4 58.8 %collective-permute-start.6 = (bf16[800,1600]{1,0:T(8,128)(2,1)}, bf16[800,1600]{1,0:T(8,128)(2,1)}, u32[]{:S(2)}, u32[]{:S(2)}) collective-permute-start(bf16[800,1600]{1,0:T(8,128)(2,1)} %get-tuple-element.468), channel_id=1, source_target_pairs={{1,4},{3,6},{4,1},{6,3},{9,12},{11,14},{12,9},{14,11},{17,20},{19,... | collective-permute-start | bytes 7680008 | tf_op jit(solution)/shard_map/ppermute | solution.py:1212
  263.9 44.2 %copy-start.30 = (bf16[2,256,1600]{2,1,0:T(8,128)(2,1)S(1)}, bf16[2,256,1600]{2,1,0:T(8,128)(2,1)}, u32[]{:S(2)}) copy-start(bf16[2,256,1600]{2,1,0:T(8,128)(2,1)} %get-tuple-element.183) | copy-start | bytes 4915204
  263.9 44.2 %copy-start.114 = (f32[1600]{0:T(1024)S(1)}, f32[1600]{0:T(1024)}, u32[]{:S(2)}) copy-start(f32[1600]{0:T(1024)} %get-tuple-element.437) | copy-start | bytes 19204
  314.8 106.0 %copy-start.22 = (f32[512,1600]{1,0:T(8,128)}, f32[512,1600]{1,0:T(8,128)S(1)}, u32[]{:S(2)}) copy-start(f32[512,1600]{1,0:T(8,128)S(1)} %get-tuple-element.198) | copy-start | bytes 9830404
  317.2 217.7 %all-gather.19.cloned.1.call-start = ((), (), s32[]{:S(2)}) async-start(), calls=%async_computation.13 | async-start | bytes 5990400 | tf_op jit(solution)/shard_map/all_gather | solution.py:1254
  322.9 92.4 %collective-permute-start.9 = (bf16[800,1600]{1,0:T(8,128)(2,1)}, bf16[800,1600]{1,0:T(8,128)(2,1)}, u32[]{:S(2)}, u32[]{:S(2)}) collective-permute-start(bf16[800,1600]{1,0:T(8,128)(2,1)} %constant_dynamic-update-slice_fusion), channel_id=1, source_target_pairs={{0,4},{1,5},{2,6},{3,7},{4,0},{5,1},{6,2},{7,3},{8,12},{9,13},{10,... | collective-permute-start | bytes 7680008 | tf_op jit(solution)/shard_map/ppermute | solution.py:1212
  322.9 98.0 %collective-permute-start.8 = (bf16[1600,1600]{1,0:T(8,128)(2,1)}, bf16[1600,1600]{1,0:T(8,128)(2,1)}, u32[]{:S(2)}, u32[]{:S(2)}) collective-permute-start(bf16[1600,1600]{1,0:T(8,128)(2,1)} %all-gather.13.cloned.1.call-done.refs_1_.refs_2_), channel_id=1, source_target_pairs={{1,4},{3,6},{4,1},{6,3},{9,12},{11,14},{12,9},{14,11},{17,20},{19,... | collective-permute-start | bytes 15360008 | tf_op jit(solution)/shard_map/ppermute | solution.py:1212
  324.8 514.5 %reduce-scatter.23.cloned.1.call-start = ((), (), s32[]{:S(2)}) async-start(), calls=%async_computation.14 | async-start | bytes 6656000 | tf_op jit(solution)/shard_map/reduce_scatter | solution.py:1221
  441.2 27.7 %collective-permute-start.11 = (bf16[512,1664]{1,0:T(8,128)(2,1)S(1)}, bf16[512,1664]{1,0:T(8,128)(2,1)}, u32[]{:S(2)}, u32[]{:S(2)}) collective-permute-start(bf16[512,1664]{1,0:T(8,128)(2,1)S(1)} %pad.30.vo_ref), channel_id=1, source_target_pairs={{0,4},{1,5},{2,6},{3,7},{4,0},{5,1},{6,2},{7,3},{8,12},{9,13},{10,... | collective-permute-start | bytes 5111816 | tf_op jit(solution)/shard_map/ppermute | solution.py:1212
  441.3 27.6 %collective-permute-start.10 = (bf16[512,1664]{1,0:T(8,128)(2,1)S(1)}, bf16[512,1664]{1,0:T(8,128)(2,1)}, u32[]{:S(2)}, u32[]{:S(2)}) collective-permute-start(bf16[512,1664]{1,0:T(8,128)(2,1)S(1)} %pad.29.ko_ref), channel_id=1, source_target_pairs={{0,4},{1,5},{2,6},{3,7},{4,0},{5,1},{6,2},{7,3},{8,12},{9,13},{10,... | collective-permute-start | bytes 5111816 | tf_op jit(solution)/shard_map/ppermute | solution.py:1212
  444.5 23.0 %collective-permute-start.12 = (bf16[256,1600]{0,1:T(8,128)(2,1)}, bf16[256,1600]{0,1:T(8,128)(2,1)}, u32[]{:S(2)}, u32[]{:S(2)}) collective-permute-start(bf16[256,1600]{0,1:T(8,128)(2,1)} %bitcast.27), channel_id=1, source_target_pairs={{2,4},{3,5},{4,2},{5,3},{10,12},{11,13},{12,10},{13,11},{18,20},{1... | collective-permute-start | bytes 2457608 | tf_op jit(solution)/shard_map/ppermute | solution.py:1212
  449.1 19.8 %collective-permute-start.13 = (bf16[256,1600]{0,1:T(8,128)(2,1)}, bf16[256,1600]{0,1:T(8,128)(2,1)}, u32[]{:S(2)}, u32[]{:S(2)}) collective-permute-start(bf16[256,1600]{0,1:T(8,128)(2,1)} %get-tuple-element.501), channel_id=1, source_target_pairs={{0,1},{1,0},{2,5},{3,4},{4,3},{5,2},{6,7},{7,6},{8,9},{9,8},{10,13... | collective-permute-start | bytes 2457608 | tf_op jit(solution)/shard_map/ppermute | solution.py:1212
  474.2 60.7 %collective-permute-start.14 = (bf16[800,1600]{1,0:T(8,128)(2,1)}, bf16[800,1600]{1,0:T(8,128)(2,1)}, u32[]{:S(2)}, u32[]{:S(2)}) collective-permute-start(bf16[800,1600]{1,0:T(8,128)(2,1)} %get-tuple-element.463), channel_id=1, source_target_pairs={{1,4},{3,6},{4,1},{6,3},{9,12},{11,14},{12,9},{14,11},{17,20},{19,... | collective-permute-start | bytes 7680008 | tf_op jit(solution)/shard_map/ppermute | solution.py:1212
  478.4 66.8 %collective-permute-start.15 = (bf16[800,1600]{1,0:T(8,128)(2,1)}, bf16[800,1600]{1,0:T(8,128)(2,1)}, u32[]{:S(2)}, u32[]{:S(2)}) collective-permute-start(bf16[800,1600]{1,0:T(8,128)(2,1)} %get-tuple-element.462), channel_id=1, source_target_pairs={{1,4},{3,6},{4,1},{6,3},{9,12},{11,14},{12,9},{14,11},{17,20},{19,... | collective-permute-start | bytes 7680008 | tf_op jit(solution)/shard_map/ppermute | solution.py:1212
  483.4 45.6 %copy-start.48 = (bf16[1,256,1600]{2,1,0:T(8,128)(2,1)S(1)}, bf16[1,256,1600]{2,1,0:T(8,128)(2,1)}, u32[]{:S(2)}) copy-start(bf16[1,256,1600]{2,1,0:T(8,128)(2,1)} %copy.147) | copy-start | bytes 2457604
  483.5 45.6 %copy-start.49 = (bf16[256,1600]{1,0:T(8,128)(2,1)S(1)}, bf16[256,1600]{1,0:T(8,128)(2,1)}, u32[]{:S(2)}) copy-start(bf16[256,1600]{1,0:T(8,128)(2,1)} %copy.150) | copy-start | bytes 2457604
  547.3 84.5 %copy-start.96 = (f32[1600]{0:T(1024)S(1)}, f32[1600]{0:T(1024)}, u32[]{:S(2)}) copy-start(f32[1600]{0:T(1024)} %get-tuple-element.426) | copy-start | bytes 19204
  722.7 266.6 %reduce-scatter.25.cloned.1.call-start = ((), (), s32[]{:S(2)}) async-start(), calls=%async_computation.16 | async-start | bytes 5990400
  745.5 30.7 %collective-permute-start.16 = (bf16[2,200,1600]{2,1,0:T(8,128)(2,1)}, bf16[2,200,1600]{2,1,0:T(8,128)(2,1)}, u32[]{:S(2)}, u32[]{:S(2)}) collective-permute-start(bf16[2,200,1600]{2,1,0:T(8,128)(2,1)} %slice_bitcast_fusion.3), channel_id=1, source_target_pairs={{0,1},{1,0},{2,3},{3,2},{4,5},{5,4},{6,7},{7,6},{8,9},{9,8},{10,11... | collective-permute-start | bytes 3840008 | tf_op jit(solution)/shard_map/ppermute | solution.py:1212
  776.3 213.1 %reduce-scatter.27.cloned.1.call-start = ((), (), s32[]{:S(2)}) async-start(), calls=%async_computation.17 | async-start | bytes 5990400
  778.0 61.3 %collective-permute-start.19 = (bf16[256,1664]{1,0:T(8,128)(2,1)S(1)}, bf16[256,1664]{1,0:T(8,128)(2,1)}, u32[]{:S(2)}, u32[]{:S(2)}) collective-permute-start(bf16[256,1664]{1,0:T(8,128)(2,1)S(1)} %get-tuple-element.497), channel_id=1, source_target_pairs={{0,1},{1,0},{2,5},{3,4},{4,3},{5,2},{6,7},{7,6},{8,9},{9,8},{10,13... | collective-permute-start | bytes 2555912 | tf_op jit(solution)/shard_map/ppermute | solution.py:1212
  779.0 60.3 %collective-permute-start.18 = (bf16[256,1664]{1,0:T(8,128)(2,1)S(1)}, bf16[256,1664]{1,0:T(8,128)(2,1)}, u32[]{:S(2)}, u32[]{:S(2)}) collective-permute-start(bf16[256,1664]{1,0:T(8,128)(2,1)S(1)} %get-tuple-element.498), channel_id=1, source_target_pairs={{2,4},{3,5},{4,2},{5,3},{10,12},{11,13},{12,10},{13,11},{18,20},{1... | collective-permute-start | bytes 2555912 | tf_op jit(solution)/shard_map/ppermute | solution.py:1212
  781.8 57.5 %collective-permute-start.17 = (bf16[2,200,1600]{2,1,0:T(8,128)(2,1)S(1)}, bf16[2,200,1600]{2,1,0:T(8,128)(2,1)}, u32[]{:S(2)}, u32[]{:S(2)}) collective-permute-start(bf16[2,200,1600]{2,1,0:T(8,128)(2,1)S(1)} %copy-done.70), channel_id=1, source_target_pairs={{0,1},{1,0},{2,3},{3,2},{4,5},{5,4},{6,7},{7,6},{8,9},{9,8},{10,11... | collective-permute-start | bytes 3840008 | tf_op jit(solution)/shard_map/ppermute | solution.py:1212
  839.3 8.3 collective-permute-start.20
  839.4 11.4 collective-permute-start.21
  853.8 269.8 %reduce-scatter.29.cloned.1.call-start = ((), (), s32[]{:S(2)}) async-start(), calls=%async_computation.18 | async-start | bytes 11520000
  903.3 288.8 %reduce-scatter.31.cloned.1.call-start = ((), (), s32[]{:S(2)}) async-start(), calls=%async_computation.19 | async-start | bytes 3328000
  904.4 84.9 %collective-permute-start.22 = (bf16[200,1600]{1,0:T(8,128)(2,1)S(1)}, bf16[200,1600]{1,0:T(8,128)(2,1)S(1)}, u32[]{:S(2)}, u32[]{:S(2)}) collective-permute-start(bf16[200,1600]{1,0:T(8,128)(2,1)S(1)} %copy-done.81), channel_id=1, source_target_pairs={{0,1},{1,0},{2,3},{3,2},{4,5},{5,4},{6,7},{7,6},{8,9},{9,8},{10,11... | collective-permute-start | bytes 1920008 | tf_op jit(solution)/shard_map/ppermute | solution.py:1212
  905.0 287.2 %reduce-scatter.33.cloned.1.call-start = ((), (), s32[]{:S(2)}) async-start(), calls=%async_computation.20 | async-start | bytes 3328000
  997.9 30.6 %collective-permute-start.23 = (bf16[2,200,1600]{2,1,0:T(8,128)(2,1)S(1)}, bf16[2,200,1600]{2,1,0:T(8,128)(2,1)S(1)}, u32[]{:S(2)}, u32[]{:S(2)}) collective-permute-start(bf16[2,200,1600]{2,1,0:T(8,128)(2,1)S(1)} %slice_bitcast_fusion.2), channel_id=1, source_target_pairs={{0,1},{1,0},{2,3},{3,2},{4,5},{5,4},{6,7},{7,6},{8,9},{9,8},{10,11... | collective-permute-start | bytes 3840008 | tf_op jit(solution)/shard_map/ppermute | solution.py:1212
  1028.5 29.9 %collective-permute-start.24 = (bf16[2,200,1600]{2,1,0:T(8,128)(2,1)}, bf16[2,200,1600]{2,1,0:T(8,128)(2,1)S(1)}, u32[]{:S(2)}, u32[]{:S(2)}) collective-permute-start(bf16[2,200,1600]{2,1,0:T(8,128)(2,1)} %dynamic-slice_bitcast_fusion.6), channel_id=1, source_target_pairs={{0,1},{1,0},{2,3},{3,2},{4,5},{5,4},{6,7},{7,6},{8,9},{9,8},{10,11... | collective-permute-start | bytes 3840008 | tf_op jit(solution)/shard_map/ppermute | solution.py:1212
  1063.2 318.7 %reduce-scatter.35.cloned.1.call-start = ((), (), s32[]{:S(2)}) async-start(), calls=%async_computation.21 | async-start | bytes 3328000
  1063.3 60.3 %collective-permute-start.25 = (bf16[4,200,1600]{2,1,0:T(8,128)(2,1)}, bf16[4,200,1600]{2,1,0:T(8,128)(2,1)}, u32[]{:S(2)}, u32[]{:S(2)}) collective-permute-start(bf16[4,200,1600]{2,1,0:T(8,128)(2,1)} %get-tuple-element.307), channel_id=1, source_target_pairs={{0,1},{1,0},{2,3},{3,2},{4,5},{5,4},{6,7},{7,6},{8,9},{9,8},{10,11... | collective-permute-start | bytes 7680008 | tf_op jit(solution)/shard_map/ppermute | solution.py:1212
  1128.5 253.5 %reduce-scatter.37.cloned.1.call-start = ((), (), s32[]{:S(2)}) async-start(), calls=%async_computation.22 | async-start | bytes 5990400
  1133.7 13.2 collective-permute-start.26
  1135.9 15.1 %collective-permute-start.27 = (bf16[512,1664]{1,0:T(8,128)(2,1)S(1)}, bf16[512,1664]{1,0:T(8,128)(2,1)}, u32[]{:S(2)}, u32[]{:S(2)}) collective-permute-start(bf16[512,1664]{1,0:T(8,128)(2,1)S(1)} %copy-done.10), channel_id=1, source_target_pairs={{0,4},{1,5},{2,6},{3,7},{4,0},{5,1},{6,2},{7,3},{8,12},{9,13},{10,... | collective-permute-start | bytes 5111816 | tf_op jit(solution)/shard_map/ppermute | solution.py:1212
  1193.5 187.6 %collective-permute-start.33 = (bf16[256,1664]{1,0:T(8,128)(2,1)}, bf16[256,1664]{1,0:T(8,128)(2,1)S(1)}, u32[]{:S(2)}, u32[]{:S(2)}) collective-permute-start(bf16[256,1664]{1,0:T(8,128)(2,1)} %get-tuple-element.491), channel_id=1, source_target_pairs={{0,1},{1,0},{2,5},{3,4},{4,3},{5,2},{6,7},{7,6},{8,9},{9,8},{10,13... | collective-permute-start | bytes 2555912 | tf_op jit(solution)/shard_map/ppermute | solution.py:1212
  1195.0 186.9 %collective-permute-start.32 = (bf16[256,1664]{1,0:T(8,128)(2,1)}, bf16[256,1664]{1,0:T(8,128)(2,1)}, u32[]{:S(2)}, u32[]{:S(2)}) collective-permute-start(bf16[256,1664]{1,0:T(8,128)(2,1)} %get-tuple-element.492), channel_id=1, source_target_pairs={{2,4},{3,5},{4,2},{5,3},{10,12},{11,13},{12,10},{13,11},{18,20},{1... | collective-permute-start | bytes 2555912 | tf_op jit(solution)/shard_map/ppermute | solution.py:1212
  1198.0 145.2 %collective-permute-start.28 = (bf16[600,1600]{1,0:T(8,128)(2,1)S(1)}, bf16[600,1600]{1,0:T(8,128)(2,1)}, u32[]{:S(2)}, u32[]{:S(2)}) collective-permute-start(bf16[600,1600]{1,0:T(8,128)(2,1)S(1)} %constant_dynamic-update-slice_fusion.2), channel_id=1, source_target_pairs={{1,4},{3,6},{4,1},{6,3},{9,12},{11,14},{12,9},{14,11},{17,20},{19,... | collective-permute-start | bytes 5760008 | tf_op jit(solution)/shard_map/ppermute | solution.py:1212
  1203.6 166.9 %collective-permute-start.30 = (bf16[200,1600]{1,0:T(8,128)(2,1)}, bf16[200,1600]{1,0:T(8,128)(2,1)}, u32[]{:S(2)}, u32[]{:S(2)}) collective-permute-start(bf16[200,1600]{1,0:T(8,128)(2,1)} %pad_maximum_fusion.8), channel_id=1, source_target_pairs={{0,2},{1,3},{2,0},{3,1},{4,6},{5,7},{6,4},{7,5},{8,10},{9,11},{10,... | collective-permute-start | bytes 1920008 | tf_op jit(solution)/shard_map/ppermute | solution.py:1212
  1206.2 164.3 %collective-permute-start.29 = (bf16[200,1600]{1,0:T(8,128)(2,1)}, bf16[200,1600]{1,0:T(8,128)(2,1)}, u32[]{:S(2)}, u32[]{:S(2)}) collective-permute-start(bf16[200,1600]{1,0:T(8,128)(2,1)} %pad_maximum_fusion.7), channel_id=1, source_target_pairs={{0,1},{1,0},{2,3},{3,2},{4,5},{5,4},{6,7},{7,6},{8,9},{9,8},{10,11... | collective-permute-start | bytes 1920008 | tf_op jit(solution)/shard_map/ppermute | solution.py:1212
  1343.2 37.9 %collective-permute-start.31 = (bf16[200,1600]{1,0:T(8,128)(2,1)}, bf16[200,1600]{1,0:T(8,128)(2,1)S(1)}, u32[]{:S(2)}, u32[]{:S(2)}) collective-permute-start(bf16[200,1600]{1,0:T(8,128)(2,1)} %pad_maximum_fusion.9), channel_id=1, source_target_pairs={{0,3},{1,2},{2,1},{3,0},{4,7},{5,6},{6,5},{7,4},{8,11},{9,10},{10,... | collective-permute-start | bytes 1920008 | tf_op jit(solution)/shard_map/ppermute | solution.py:1212
  1387.5 19.5 %collective-permute-start.34 = (bf16[200,400]{1,0:T(8,128)(2,1)}, bf16[200,400]{1,0:T(8,128)(2,1)}, u32[]{:S(2)}, u32[]{:S(2)}) collective-permute-start(bf16[200,400]{1,0:T(8,128)(2,1)} %get-tuple-element.509), channel_id=1, source_target_pairs={{0,1},{1,0},{2,3},{3,2},{4,5},{5,4},{6,7},{7,6},{8,9},{9,8},{10,11... | collective-permute-start | bytes 480008 | tf_op jit(solution)/shard_map/ppermute | solution.py:1212
  1389.8 17.1 %collective-permute-start.36 = (bf16[200,400]{1,0:T(8,128)(2,1)}, bf16[200,400]{1,0:T(8,128)(2,1)}, u32[]{:S(2)}, u32[]{:S(2)}) collective-permute-start(bf16[200,400]{1,0:T(8,128)(2,1)} %get-tuple-element.510), channel_id=1, source_target_pairs={{0,3},{1,2},{2,1},{3,0},{4,7},{5,6},{6,5},{7,4},{8,11},{9,10},{10,... | collective-permute-start | bytes 480008 | tf_op jit(solution)/shard_map/ppermute | solution.py:1212
  1392.5 14.4 %collective-permute-start.35 = (bf16[200,400]{1,0:T(8,128)(2,1)}, bf16[200,400]{1,0:T(8,128)(2,1)}, u32[]{:S(2)}, u32[]{:S(2)}) collective-permute-start(bf16[200,400]{1,0:T(8,128)(2,1)} %get-tuple-element.511), channel_id=1, source_target_pairs={{0,2},{1,3},{2,0},{3,1},{4,6},{5,7},{6,4},{7,5},{8,10},{9,11},{10,... | collective-permute-start | bytes 480008 | tf_op jit(solution)/shard_map/ppermute | solution.py:1212
  1392.5 17.8 %collective-permute-start.37 = (bf16[200,1600]{1,0:T(8,128)(2,1)}, bf16[200,1600]{1,0:T(8,128)(2,1)}, u32[]{:S(2)}, u32[]{:S(2)}) collective-permute-start(bf16[200,1600]{1,0:T(8,128)(2,1)} %reduce-scatter.35.cloned.1.call-done), channel_id=1, source_target_pairs={{1,4},{3,6},{4,1},{6,3},{9,12},{11,14},{12,9},{14,11},{17,20},{19,... | collective-permute-start | bytes 1920008 | tf_op jit(solution)/shard_map/ppermute | solution.py:1212
  (119 other events, 585.3 us)
Sparse Core Ops, SparseCore 0:
  10.2 107.6 all-gather.20
  120.1 55.5 all-gather.8
  177.9 55.4 all-gather.10
  235.0 55.5 all-gather.12
  292.0 55.5 all-gather.14
  349.2 56.3 all-gather.16
  407.2 56.1 all-gather.18
  722.8 111.9 reduce-scatter.22
  837.1 59.4 reduce-scatter.24
  898.8 60.1 reduce-scatter.26
  961.3 106.8 reduce-scatter.28
  1070.9 52.9 reduce-scatter.30
  1126.8 52.6 reduce-scatter.32
  1182.2 52.6 reduce-scatter.34
  1237.0 70.0 reduce-scatter.36

commit v4 on v3

--- a/solution.py
+++ b/solution.py
@@ -426,7 +426,7 @@
 
 
 def attend_kernel(width, blocks, qblocks, place_ref, slot_ref, q_ref, ko_ref, ks_ref, vo_ref, vs_ref,
-                  o_ref, lse_ref, cat, ksort, vturn):
+                  o_ref, lse_ref, cat, ksort, vsort):
     lane = lax.broadcasted_iota(jnp.int32, (1, LANES), 1)
     ok = lane + pl.program_id(0) * LANES < width
     first = lane < HD
@@ -435,7 +435,7 @@
         ksort[j * LANES:(j + 1) * LANES, :] = rows
 
     def put_v(j, rows):
-        vturn[:, j * LANES:(j + 1) * LANES] = rows.astype(jnp.float32).T.astype(jnp.bfloat16)
+        vsort[j * LANES:(j + 1) * LANES, :] = rows
 
     sort_keys(slot_ref, blocks, ok, ko_ref, ks_ref, cat, put_k)
     sort_keys(slot_ref, blocks, ok, vo_ref, vs_ref, cat, put_v)
@@ -457,7 +457,7 @@
                 top = jnp.max(s, axis=0, keepdims=True)
                 e = jnp.exp(s - top)
                 total = jnp.sum(e, axis=0, keepdims=True)
-                turned = nn(vturn[:, :keys], e.astype(jnp.bfloat16)) / total
+                turned = tn(vsort[:keys, :], e.astype(jnp.bfloat16)) / total
                 joined = jnp.concatenate([turned[:HD, :LANES], turned[HD:, LANES:]], axis=0)
                 o_ref[here, :] = joined.T.astype(jnp.bfloat16)
                 lse = top + jnp.log(total)
@@ -550,7 +550,7 @@
             scratch_shapes=[
                 pltpu.VMEM((keys, LANES), jnp.bfloat16),
                 pltpu.VMEM((keys, LANES), jnp.bfloat16),
-                pltpu.VMEM((LANES, keys), jnp.bfloat16),
+                pltpu.VMEM((keys, LANES), jnp.bfloat16),
             ],
         ),
         out_shape=[
@@ -1395,6 +1395,13 @@
             go(piece(1 - row, col), over_y),
             go(piece(1 - row, 1 - col), over_xy),
         ]
+
+    def columns_of(values, parts, index):
+        cut = []
+        for value in values:
+            size = value.shape[1] // parts
+            cut.append(lax.dynamic_slice_in_dim(value, index * size, size, axis=1))
+        return jnp.concatenate(cut, axis=1)
 
     def total_of(pieces):
         return sum(f32(piece) for piece in pieces[1:]) + f32(pieces[0])
@@ -1501,13 +1508,23 @@
     )
     fc_away = go(fc_sent, over_x)
     fc2_low = sum_z(add_pair(fc2_kept, jnp.concatenate(fc2_away, axis=0)).reshape(-1, width))
-    back = fence(*heads_back(0, attended_grad), fc_away, dkv_sum)
-    fc_away, dkv_sum = back[5:]
+    back = fence(*heads_back(0, attended_grad), fc_away, dkv_sum, fc_sum, fc2_high, dq_sum, proj_sum)
+    fc_away, dkv_sum, fc_sum, fc2_high, dq_sum, proj_sum = back[5:]
+    turned = turn_xc(jnp.concatenate([fc_sum, fc2_high], axis=0))
+    qkv_sum = jnp.concatenate([dq_sum, dkv_sum], axis=1)
+    near_columns, far_columns = [columns_of((qkv_sum, proj_sum), 2, side) for side in (row, 1 - row)]
+    far_top, far_end = halves(far_columns)
+    far_top = go(far_top, over_y)
     dq, dk, dv = mixed_of(*back[:5])
-    dq, dk, dv, proj_grad = fence(dq, dk, dv, proj_grad)
+    dq, dk, dv, proj_grad, turned, near_columns, far_top, far_end = fence(
+        dq, dk, dv, proj_grad, turned, near_columns, far_top, far_end
+    )
+    far_end = go(far_end, over_y)
     proj_low = sum_dp(proj_grad)
     fc_low = sum_z(add_pair(fc_kept, fc_away).reshape(-1, width))
     lowest, gain_one, shift_one = input_back(0, middle_grad, dq, dk, dv)
+    lowest, far_end = fence(lowest, far_end)
+    far_columns = jnp.concatenate([far_top, far_end], axis=0)
     sums_zero = bias_sums((gain_one, gain_two), (shift_one, shift_two), dq, dv, attn_out_grad, out_grad_low)
     low = bf(lowest)
     third = 3 * width // 4
@@ -1522,22 +1539,25 @@
             (spread[None, :, None] * jnp.concatenate([units_low, units_sum], axis=0)[:, None, :]).reshape(2 * 4, width),
         ]
     )
-    low, sums, pieces, keep, send, dq_sum, dkv_sum, proj_sum, fc_sum, fc2_low = fence(
-        low, sums, pieces, keep, send, dq_sum, dkv_sum, proj_sum, fc_sum, fc2_low
+    held_rows = proj_sum.shape[0]
+    split = 3 * width // 2
+    columns = add_pair(near_columns, far_columns)
+    halves_x = columns[:, :split], columns[:, split:]
+    near_columns, far_columns = [columns_of(halves_x, 2, side) for side in (col, 1 - col)]
+    low, sums, pieces, keep, send, fc2_low, near_columns, far_columns = fence(
+        low, sums, pieces, keep, send, fc2_low, near_columns, far_columns
     )
-    held_rows = proj_sum.shape[0]
-    turned = turn_xc(jnp.concatenate([fc_sum, fc2_high, fc2_low], axis=0))
+    fc2_low = turn_xc(fc2_low)
     low_moved = regroup(low)
-    columns = mp_pieces(jnp.concatenate([dq_sum, dkv_sum], axis=1), proj_sum)
+    far_columns = go(far_columns, over_x)
     qkv_low, sums = settle_columns(planes, keep, send, pieces, sums)
-    qkv_low, sums, fc_low, proj_low, turned, columns, low_moved = fence(
-        qkv_low, sums, fc_low, proj_low, turned, columns, low_moved
+    qkv_low, sums, fc_low, proj_low, fc2_low, far_columns, low_moved = fence(
+        qkv_low, sums, fc_low, proj_low, fc2_low, far_columns, low_moved
     )
-    columns = total_of(columns)
-    turned = turned.reshape(3, held_rows, width)
+    columns = f32(near_columns) + f32(far_columns)
     qkv_high = columns[:, :third]
-    results_zero = [turn_xc(fc_low), turned[2], total_of(mp_pieces(proj_low))]
-    results_one = [turned[0], turned[1], columns[:, third:]]
+    results_zero = [turn_xc(fc_low), fc2_low, total_of(mp_pieces(proj_low))]
+    results_one = [turned[:held_rows], turned[held_rows:], columns[:, third:]]
     outputs = settle(final, *final_moved)
     input_grad = settle(low, *low_moved)
     held = width // (2 * planes)

time: 1440 us -> 1420 us (0.986)
    ppermute x38 -> x39, starting transfers between devices: 76.8 us -> 74.6 us  [go(): return lax.ppermute(value, AXES, pairs)]
    ppermute x38 -> x39, waiting for transfers between devices: 56.2 us -> 54.2 us  [go(): return lax.ppermute(value, AXES, pairs)]
    unnamed x269 -> x264, local copies, waits for them, and re-layouts: 47.3 us -> 46.3 us
  transfers between devices with their start and end apart: 53 -> 54, of which waited for: 8 -> 10; matrix products, arithmetic and copies ran while one was open for 27% -> 27% of each run, Pallas kernels for 46% -> 46%
where the time goes in v4:
time: 1420 us; the launch traced here: 1410 us
  Pallas kernels  818 us (58%)
  matrix products  167 us (12%)
  local copies, waits for them, and re-layouts  143 us (10%)
  other arithmetic  118 us (8%)
  starting transfers between devices  75.9 us (5%)
  waiting for transfers between devices  70.5 us (5%)
  between operations  16 us (1%)
    pallas_call x4, Pallas kernels, units(): pl.pallas_call(functools.partial(units_kernel, back, (len(wa) - 1, len(wb...  348 us
    pallas_call x1, Pallas kernels, gather_four(): pl.pallas_call(functools.partial(gather_kernel, planes), in_specs=[anywhe...  149 us
    pallas_call x1, Pallas kernels, settle_columns(): pl.pallas_call(functools.partial(settle_kernel, planes), in_specs=[inside...  137 us
    pallas_call x2, Pallas kernels, attention_back(): pl.pallas_call(functools.partial(attend_back_kernel, width, blocks, place...  101 us
    pallas_call x2, Pallas kernels, attention(): pl.pallas_call(functools.partial(attend_kernel, width, blocks, place.shap...  82.2 us
    ppermute x39, starting transfers between devices, go(): return lax.ppermute(value, AXES, pairs)  74.6 us
    dot_general x6, matrix products, tn(): lax.dot_general(a, b, (((0,), (0,)), ((), ())), preferred_element_type=jn...  62.7 us
    dot_general x8, matrix products, nt(): lax.dot_general(a, b, (((1,), (1,)), ((), ())), preferred_element_type=jn...  57.2 us
  transfers between devices with their start and end apart: 54, of which 10 were waited for; matrix products, arithmetic and copies ran while one was open for 27% of the time, Pallas kernels for 46%

profile of v4, /device:TPU:1, one launch (start us, length us, event | category | flops | bytes accessed | tf_op | source)
XLA Modules:
  0.0 1407.3 jit_solution(18132318207968113060)
XLA Ops:
  15.1 3.6 copy.135.token_ref
  21.9 149.2 %gather_four.1 = (bf16[4,8,200,1600]{3,2,1,0:T(8,128)(2,1)}, f32[8,24,200]{2,1,0:T(8,128)}, bf16[2,256,1600]{2,1,0:T(8,128)(2,1)}) custom-call(bf16[200,1600]{1,0:T(8,128)(2,1)} %fusion.36.piece_ref, f32[24,200]{1,0:T(8,128)} %pad_convert_fusion.small_ref, bf16[2,256,1600]{2,1,0:T(8,128)(2,1)} %copy.135.token_ref), custom_call_target="tpu_custom_call" | custom-call | bytes 314572800 | tf_op jit(solution)/shard_map/gather_four/pallas_call | solution.py:731
  172.5 3.6 collective-permute-start.2
  182.6 13.5 fusion.50
  196.1 3.5 add_convert_fusion.9
  200.1 3.2 convolution_convert_fusion.9
  209.7 7.2 add_convert_fusion.10.q_ref
  218.0 15.4 %all-gather.11.cloned.1.call-done = bf16[1600,1600]{1,0:T(8,128)(2,1)} async-done(((bf16[200,1600]{1,0:T(8,128)(2,1)}), bf16[1600,1600]{1,0:T(8,128)(2,1)}) %all-gather.11.cloned.1.call-update) | async-done | bytes 5120016 | tf_op jit(solution)/shard_map/all_gather | solution.py:1254
  233.5 8.1 collective-permute-done.3.refs_3_.refs_5_
  241.6 5.8 fusion.52
  249.6 3.5 constant_dynamic-slice_fusion.14
  253.0 3.6 collective-permute-start.5
  263.8 41.2 %attention.2 = (bf16[512,1600]{1,0:T(8,128)(2,1)S(1)}, f32[13,2,512]{2,1,0:T(2,128)S(1)}) custom-call(s32[4]{0:T(128)S(1)} %reshape.482.place_ref, s32[8]{0:T(128)S(1)} %select_reduce_fusion.slot_ref, bf16[512,1600]{1,0:T(8,128)(2,1)S(1)} %copy-done.20, bf16[512,1664]{1,0:T(8,128)(2,1)S(1)} %pad.27.ko_ref, bf16[512,1664]{1,0:T(8,128)(2,1)S(1)} %copy-done.7, ...), custom_call_target="tpu_custom_call" | custom-call | flops 6979321856 | bytes 9830400 | tf_op jit(solution)/shard_map/attention/pallas_call | solution.py:543
  305.1 6.7 fusion.56
  319.9 3.7 collective-permute-start.8
  323.8 88.7 %units.2 = (f32[512,1600]{1,0:T(8,128)}, bf16[2048,1600]{1,0:T(8,128)(2,1)}, bf16[2048,1600]{1,0:T(8,128)(2,1)}, bf16[2048,1600]{1,0:T(8,128)(2,1)}) custom-call(bf16[512,1600]{1,0:T(8,128)(2,1)} %add_convert_fusion.8.refs_0_, bf16[1600,1600]{1,0:T(8,128)(2,1)} %bitcast.247, bf16[1600,1600]{1,0:T(8,128)(2,1)} %all-gather.9.cloned.1.call-done.refs_2_.refs_1_, ...), custom_call_target="tpu_custom_call" | custom-call | flops 60000002048 | bytes 62914560 | tf_op jit(solution)/shard_map/units/pallas_call | solution.py:973
  412.8 6.0 broadcast_select_fusion.3
  418.8 3.5 fusion.49
  426.8 3.3 convolution_convert_fusion.8
  433.0 6.0 add_convert_fusion.5
  442.8 4.3 collective-permute-start.12
  449.6 9.3 add_convert_fusion.6.q_ref
  458.9 6.7 collective-permute-done.12
  466.6 5.3 fusion.51
  476.0 3.6 collective-permute-start.15
  481.1 41.0 %attention.3 = (bf16[512,1600]{1,0:T(8,128)(2,1)S(1)}, f32[13,2,512]{2,1,0:T(2,128)S(1)}) custom-call(s32[4]{0:T(128)S(1)} %reshape.482.place_ref, s32[8]{0:T(128)S(1)} %select_reduce_fusion.slot_ref, bf16[512,1600]{1,0:T(8,128)(2,1)S(1)} %copy-done.18, bf16[512,1664]{1,0:T(8,128)(2,1)S(1)} %pad.29.ko_ref, bf16[512,1664]{1,0:T(8,128)(2,1)} %collective-permute-done.10.ks_ref, ...), custom_call_target="tpu_custom_call" | custom-call | flops 6979321856 | bytes 9830400 | tf_op jit(solution)/shard_map/attention/pallas_call | solution.py:543
  529.4 7.6 fusion.57
  541.8 88.4 %units.3 = (f32[512,1600]{1,0:T(8,128)}, bf16[2048,1600]{1,0:T(8,128)(2,1)}, bf16[2048,1600]{1,0:T(8,128)(2,1)}, bf16[2048,1600]{1,0:T(8,128)(2,1)}) custom-call(bf16[512,1600]{1,0:T(8,128)(2,1)} %add_convert_fusion.4.refs_0_, bf16[1600,1600]{1,0:T(8,128)(2,1)} %all-gather.13.cloned.1.call-done.refs_1_.refs_2_, ...), custom_call_target="tpu_custom_call" | custom-call | flops 60000002048 | bytes 62914560 | tf_op jit(solution)/shard_map/units/pallas_call | solution.py:973
  630.2 4.8 multiply_reduce_fusion.7
  635.0 83.9 %units_back.2 = (f32[512,1600]{1,0:T(8,128)}, bf16[2048,1600]{1,0:T(8,128)(2,1)}, bf16[2048,1600]{1,0:T(8,128)(2,1)}, f32[1,1600]{1,0:T(1,128)}, bf16[1600,1600]{1,0:T(8,128)(2,1)}) custom-call(bf16[512,1600]{1,0:T(8,128)(2,1)} %pad_maximum_fusion.3.refs_0_, bf16[1600,1600]{1,0:T(8,128)(2,1)} %all-gather.17.cloned.1.call-done.refs_2_.refs_1_, ...), custom_call_target="tpu_custom_call" | custom-call | flops 60000002048 | bytes 62914560 | tf_op jit(solution)/shard_map/units_back/pallas_call | solution.py:973
  719.0 18.1 %convolution_convert_fusion.5 = bf16[1600,1600]{1,0:T(8,128)(2,1)S(1)} fusion(bf16[2048,1600]{1,0:T(8,128)(2,1)} %get-tuple-element.248, bf16[2048,1600]{1,0:T(8,128)(2,1)} %get-tuple-element.249), kind=kOutput, calls=%fused_computation.7 | convolution fusion | flops 10488320000 | bytes 18227200 | tf_op jit(solution)/shard_map/dot_general | solution.py:407
  744.9 4.8 convert_reduce_fusion.6
  750.9 5.5 convolution_convert_fusion.3
  756.4 7.7 convolution_convert_fusion.7.do_ref
  764.2 7.9 collective-permute-done.16
  779.7 50.7 %attention_back.2 = (bf16[512,1600]{1,0:T(8,128)(2,1)S(1)}, f32[512,1664]{1,0:T(8,128)}, bf16[512,1664]{1,0:T(8,128)(2,1)S(1)}, f32[512,1664]{1,0:T(8,128)}, bf16[512,1664]{1,0:T(8,128)(2,1)S(1)}) custom-call(s32[4]{0:T(128)S(1)} %reshape.482.place_ref, s32[8]{0:T(128)S(1)} %select_reduce_fusion.slot_ref, bf16[512,1600]{1,0:T(8,128)(2,1)S(1)} %copy-done.19, ...), custom_call_target="tpu_custom_call" | custom-call | flops 17448304640 | bytes 24576000 | tf_op jit(solution)/shard_map/attention_back/pallas_call | solution.py:575
  834.6 7.8 convolution_convert_fusion.2
  853.3 4.1 add_convert_fusion.2
  859.1 8.1 fusion.37
  867.3 5.4 fusion.38
  872.7 8.7 multiply_reduce_fusion.4
  882.8 5.4 fusion.48
  888.8 9.3 convolution_convert_fusion
  899.5 86.7 %units_back.3 = (f32[512,1600]{1,0:T(8,128)}, bf16[2048,1600]{1,0:T(8,128)(2,1)}, bf16[2048,1600]{1,0:T(8,128)(2,1)}, f32[1,1600]{1,0:T(1,128)}, bf16[1600,1600]{1,0:T(8,128)(2,1)}) custom-call(bf16[512,1600]{1,0:T(8,128)(2,1)} %get-tuple-element.282.refs_0_, bf16[1600,1600]{1,0:T(8,128)(2,1)} %all-gather.9.cloned.1.call-done.refs_2_.refs_1_, ...), custom_call_target="tpu_custom_call" | custom-call | flops 60000002048 | bytes 62914560 | tf_op jit(solution)/shard_map/units_back/pallas_call | solution.py:973
  994.7 16.5 %convolution_convert_fusion.4 = bf16[1600,1600]{1,0:T(8,128)(2,1)S(1)} fusion(bf16[2048,1600]{1,0:T(8,128)(2,1)} %get-tuple-element.297, bf16[2048,1600]{1,0:T(8,128)(2,1)S(1)} %bitcast.252), kind=kOutput, calls=%fused_computation.6 | convolution fusion | flops 10488320000 | bytes 18227200 | tf_op jit(solution)/shard_map/dot_general | solution.py:407
  1011.2 3.3 dynamic-slice_bitcast_fusion
  1014.5 9.8 collective-permute-done.23
  1031.5 5.5 convolution_convert_fusion.1
  1037.1 7.8 convolution_convert_fusion.6.do_ref
  1044.9 9.9 collective-permute-done.24
  1054.9 3.7 add_convert_fusion.1
  1070.0 50.7 %attention_back.3 = (bf16[512,1600]{1,0:T(8,128)(2,1)S(1)}, f32[512,1664]{1,0:T(8,128)}, bf16[512,1664]{1,0:T(8,128)(2,1)S(1)}, f32[512,1664]{1,0:T(8,128)}, bf16[512,1664]{1,0:T(8,128)(2,1)S(1)}) custom-call(s32[4]{0:T(128)S(1)} %reshape.482.place_ref, s32[8]{0:T(128)S(1)} %select_reduce_fusion.slot_ref, bf16[512,1600]{1,0:T(8,128)(2,1)S(1)} %copy-done.21, ...), custom_call_target="tpu_custom_call" | custom-call | flops 17448304640 | bytes 24576000 | tf_op jit(solution)/shard_map/attention_back/pallas_call | solution.py:575
  1123.2 4.8 add_convert_fusion
  1131.9 4.7 copy.163
  1142.9 5.2 collective-permute-start.28
  1154.0 9.6 collective-permute-done.28
  1169.5 6.2 fusion.58
  1175.7 6.2 fusion.59
  1182.0 7.1 fusion.21
  1199.0 3.7 slice_bitcast_fusion.5
  1211.9 5.3 collective-permute-start.31
  1219.6 137.3 %settle_columns.1 = (f32[200,1200]{1,0:T(8,128)}, f32[24,1600]{1,0:T(8,128)}) custom-call(bf16[800,512]{1,0:T(8,128)(2,1)} %bitcast.235, bf16[800,512]{1,0:T(8,128)(2,1)} %bitcast.234, bf16[4,512,1200]{2,1,0:T(8,128)(2,1)} %pad_maximum_fusion.1.piece_ref, f32[24,1600]{1,0:T(8,128)} %concatenate.108.sum_ref), custom_call_target="tpu_custom_call" | custom-call | flops 16000000000 | bytes 62914560 | tf_op jit(solution)/shard_map/settle_columns/pallas_call | solution.py:1127
  1364.9 11.8 collective-permute-start.35
  1379.9 5.9 collective-permute-start.38
  (532 shorter events, 211.5 us)
Async XLA Ops:
  7.2 172.1 %all-gather.21.cloned.1.call-start = ((), (), s32[]{:S(2)}) async-start(), calls=%async_computation.15 | async-start | bytes 5990400 | tf_op jit(solution)/shard_map/all_gather | solution.py:1254
  9.8 208.2 %all-gather.9.cloned.1.call-start = ((), (), s32[]{:S(2)}) async-start(), calls=%async_computation.8 | async-start | bytes 5990400 | tf_op jit(solution)/shard_map/all_gather | solution.py:1254
  11.0 222.4 %all-gather.11.cloned.1.call-start = ((), (), s32[]{:S(2)}) async-start(), calls=%async_computation.9 | async-start | bytes 5990400 | tf_op jit(solution)/shard_map/all_gather | solution.py:1254
  14.9 299.3 %all-gather.13.cloned.1.call-start = ((), (), s32[]{:S(2)}) async-start(), calls=%async_computation.10 | async-start | bytes 5990400 | tf_op jit(solution)/shard_map/all_gather | solution.py:1254
  172.4 246.4 %all-gather.15.cloned.1.call-start = ((), (), s32[]{:S(2)}) async-start(), calls=%async_computation.11 | async-start | bytes 5990400 | tf_op jit(solution)/shard_map/all_gather | solution.py:1254
  172.5 6.8 collective-permute-start.2
  179.3 133.1 %copy-start.85 = (f32[1600]{0:T(1024)}, f32[1600]{0:T(1024)S(1)}, u32[]{:S(2)}) copy-start(f32[1600]{0:T(1024)S(1)} %get-tuple-element.446) | copy-start | bytes 19204
  179.3 243.6 %copy-start.88 = (f32[1600]{0:T(1024)}, f32[1600]{0:T(1024)S(1)}, u32[]{:S(2)}) copy-start(f32[1600]{0:T(1024)S(1)} %get-tuple-element.443) | copy-start | bytes 19204
  179.3 62.3 %collective-permute-start.3 = (bf16[1600,1600]{1,0:T(8,128)(2,1)}, bf16[1600,1600]{1,0:T(8,128)(2,1)}, u32[]{:S(2)}, u32[]{:S(2)}) collective-permute-start(bf16[1600,1600]{1,0:T(8,128)(2,1)} %bitcast.246), channel_id=1, source_target_pairs={{1,4},{3,6},{4,1},{6,3},{9,12},{11,14},{12,9},{14,11},{17,20},{19,... | collective-permute-start | bytes 15360008 | tf_op jit(solution)/shard_map/ppermute | solution.py:1212
  199.8 61.1 %copy-start = (bf16[512,1664]{1,0:T(8,128)(2,1)}, bf16[512,1664]{1,0:T(8,128)(2,1)S(1)}, u32[]{:S(2)}) copy-start(bf16[512,1664]{1,0:T(8,128)(2,1)S(1)} %pad.28.vo_ref) | copy-start | bytes 5111812
  199.8 17.1 %collective-permute-start.1 = (bf16[512,1664]{1,0:T(8,128)(2,1)S(1)}, bf16[512,1664]{1,0:T(8,128)(2,1)}, u32[]{:S(2)}, u32[]{:S(2)}) collective-permute-start(bf16[512,1664]{1,0:T(8,128)(2,1)S(1)} %pad.28.vo_ref), channel_id=1, source_target_pairs={{0,4},{1,5},{2,6},{3,7},{4,0},{5,1},{6,2},{7,3},{8,12},{9,13},{10,... | collective-permute-start | bytes 5111816 | tf_op jit(solution)/shard_map/ppermute | solution.py:1212
  207.4 53.5 %copy-start.2 = (bf16[512,1664]{1,0:T(8,128)(2,1)}, bf16[512,1664]{1,0:T(8,128)(2,1)S(1)}, u32[]{:S(2)}) copy-start(bf16[512,1664]{1,0:T(8,128)(2,1)S(1)} %pad.27.ko_ref) | copy-start | bytes 5111812
  207.4 9.5 collective-permute-start
  241.6 225.0 %all-gather.17.cloned.1.call-start = ((), (), s32[]{:S(2)}) async-start(), calls=%async_computation.12 | async-start | bytes 5990400 | tf_op jit(solution)/shard_map/all_gather | solution.py:1254
  247.4 57.7 %collective-permute-start.4 = (bf16[800,1600]{1,0:T(8,128)(2,1)}, bf16[800,1600]{1,0:T(8,128)(2,1)}, u32[]{:S(2)}, u32[]{:S(2)}) collective-permute-start(bf16[800,1600]{1,0:T(8,128)(2,1)} %get-tuple-element.480), channel_id=1, source_target_pairs={{1,4},{3,6},{4,1},{6,3},{9,12},{11,14},{12,9},{14,11},{17,20},{19,... | collective-permute-start | bytes 7680008 | tf_op jit(solution)/shard_map/ppermute | solution.py:1212
  253.0 52.0 %collective-permute-start.5 = (bf16[400,1600]{1,0:T(8,128)(2,1)}, bf16[400,1600]{1,0:T(8,128)(2,1)}, u32[]{:S(2)}, u32[]{:S(2)}) collective-permute-start(bf16[400,1600]{1,0:T(8,128)(2,1)} %get-tuple-element.478), channel_id=1, source_target_pairs={{0,2},{1,3},{2,0},{3,1},{4,6},{5,7},{6,4},{7,5},{8,10},{9,11},{10,... | collective-permute-start | bytes 3840008 | tf_op jit(solution)/shard_map/ppermute | solution.py:1212
  258.4 55.8 %collective-permute-start.7 = (bf16[400,1600]{1,0:T(8,128)(2,1)}, bf16[400,1600]{1,0:T(8,128)(2,1)}, u32[]{:S(2)}, u32[]{:S(2)}) collective-permute-start(bf16[400,1600]{1,0:T(8,128)(2,1)} %get-tuple-element.477), channel_id=1, source_target_pairs={{0,2},{1,3},{2,0},{3,1},{4,6},{5,7},{6,4},{7,5},{8,10},{9,11},{10,... | collective-permute-start | bytes 3840008 | tf_op jit(solution)/shard_map/ppermute | solution.py:1212
  258.4 55.8 %collective-permute-start.6 = (bf16[800,1600]{1,0:T(8,128)(2,1)}, bf16[800,1600]{1,0:T(8,128)(2,1)}, u32[]{:S(2)}, u32[]{:S(2)}) collective-permute-start(bf16[800,1600]{1,0:T(8,128)(2,1)} %get-tuple-element.479), channel_id=1, source_target_pairs={{1,4},{3,6},{4,1},{6,3},{9,12},{11,14},{12,9},{14,11},{17,20},{19,... | collective-permute-start | bytes 7680008 | tf_op jit(solution)/shard_map/ppermute | solution.py:1212
  263.8 41.2 %copy-start.30 = (bf16[2,256,1600]{2,1,0:T(8,128)(2,1)S(1)}, bf16[2,256,1600]{2,1,0:T(8,128)(2,1)}, u32[]{:S(2)}) copy-start(bf16[2,256,1600]{2,1,0:T(8,128)(2,1)} %get-tuple-element.188) | copy-start | bytes 4915204
  263.8 41.2 %copy-start.111 = (f32[1600]{0:T(1024)S(1)}, f32[1600]{0:T(1024)}, u32[]{:S(2)}) copy-start(f32[1600]{0:T(1024)} %get-tuple-element.447) | copy-start | bytes 19204
  311.8 107.0 %copy-start.22 = (f32[512,1600]{1,0:T(8,128)}, f32[512,1600]{1,0:T(8,128)S(1)}, u32[]{:S(2)}) copy-start(f32[512,1600]{1,0:T(8,128)S(1)} %get-tuple-element.203) | copy-start | bytes 9830404
  314.2 215.1 %all-gather.19.cloned.1.call-start = ((), (), s32[]{:S(2)}) async-start(), calls=%async_computation.13 | async-start | bytes 5990400 | tf_op jit(solution)/shard_map/all_gather | solution.py:1254
  319.9 92.9 %collective-permute-start.9 = (bf16[800,1600]{1,0:T(8,128)(2,1)}, bf16[800,1600]{1,0:T(8,128)(2,1)}, u32[]{:S(2)}, u32[]{:S(2)}) collective-permute-start(bf16[800,1600]{1,0:T(8,128)(2,1)} %constant_dynamic-update-slice_fusion), channel_id=1, source_target_pairs={{0,4},{1,5},{2,6},{3,7},{4,0},{5,1},{6,2},{7,3},{8,12},{9,13},{10,... | collective-permute-start | bytes 7680008 | tf_op jit(solution)/shard_map/ppermute | solution.py:1212
  319.9 98.9 %collective-permute-start.8 = (bf16[1600,1600]{1,0:T(8,128)(2,1)}, bf16[1600,1600]{1,0:T(8,128)(2,1)}, u32[]{:S(2)}, u32[]{:S(2)}) collective-permute-start(bf16[1600,1600]{1,0:T(8,128)(2,1)} %all-gather.13.cloned.1.call-done.refs_1_.refs_2_), channel_id=1, source_target_pairs={{1,4},{3,6},{4,1},{6,3},{9,12},{11,14},{12,9},{14,11},{17,20},{19,... | collective-permute-start | bytes 15360008 | tf_op jit(solution)/shard_map/ppermute | solution.py:1212
  323.6 510.4 %reduce-scatter.23.cloned.1.call-start = ((), (), s32[]{:S(2)}) async-start(), calls=%async_computation.14 | async-start | bytes 6656000 | tf_op jit(solution)/shard_map/reduce_scatter | solution.py:1221
  439.2 27.4 %collective-permute-start.11 = (bf16[512,1664]{1,0:T(8,128)(2,1)S(1)}, bf16[512,1664]{1,0:T(8,128)(2,1)}, u32[]{:S(2)}, u32[]{:S(2)}) collective-permute-start(bf16[512,1664]{1,0:T(8,128)(2,1)S(1)} %pad.30.vo_ref), channel_id=1, source_target_pairs={{0,4},{1,5},{2,6},{3,7},{4,0},{5,1},{6,2},{7,3},{8,12},{9,13},{10,... | collective-permute-start | bytes 5111816 | tf_op jit(solution)/shard_map/ppermute | solution.py:1212
  440.1 26.5 %collective-permute-start.10 = (bf16[512,1664]{1,0:T(8,128)(2,1)S(1)}, bf16[512,1664]{1,0:T(8,128)(2,1)}, u32[]{:S(2)}, u32[]{:S(2)}) collective-permute-start(bf16[512,1664]{1,0:T(8,128)(2,1)S(1)} %pad.29.ko_ref), channel_id=1, source_target_pairs={{0,4},{1,5},{2,6},{3,7},{4,0},{5,1},{6,2},{7,3},{8,12},{9,13},{10,... | collective-permute-start | bytes 5111816 | tf_op jit(solution)/shard_map/ppermute | solution.py:1212
  442.8 22.7 %collective-permute-start.12 = (bf16[256,1600]{0,1:T(8,128)(2,1)}, bf16[256,1600]{0,1:T(8,128)(2,1)}, u32[]{:S(2)}, u32[]{:S(2)}) collective-permute-start(bf16[256,1600]{0,1:T(8,128)(2,1)} %bitcast.27), channel_id=1, source_target_pairs={{2,4},{3,5},{4,2},{5,3},{10,12},{11,13},{12,10},{13,11},{18,20},{1... | collective-permute-start | bytes 2457608 | tf_op jit(solution)/shard_map/ppermute | solution.py:1212
  447.2 19.4 %collective-permute-start.13 = (bf16[256,1600]{0,1:T(8,128)(2,1)}, bf16[256,1600]{0,1:T(8,128)(2,1)}, u32[]{:S(2)}, u32[]{:S(2)}) collective-permute-start(bf16[256,1600]{0,1:T(8,128)(2,1)} %get-tuple-element.507), channel_id=1, source_target_pairs={{0,1},{1,0},{2,5},{3,4},{4,3},{5,2},{6,7},{7,6},{8,9},{9,8},{10,13... | collective-permute-start | bytes 2457608 | tf_op jit(solution)/shard_map/ppermute | solution.py:1212
  471.9 57.5 %collective-permute-start.14 = (bf16[800,1600]{1,0:T(8,128)(2,1)}, bf16[800,1600]{1,0:T(8,128)(2,1)}, u32[]{:S(2)}, u32[]{:S(2)}) collective-permute-start(bf16[800,1600]{1,0:T(8,128)(2,1)} %get-tuple-element.474), channel_id=1, source_target_pairs={{1,4},{3,6},{4,1},{6,3},{9,12},{11,14},{12,9},{14,11},{17,20},{19,... | collective-permute-start | bytes 7680008 | tf_op jit(solution)/shard_map/ppermute | solution.py:1212
  476.0 63.5 %collective-permute-start.15 = (bf16[800,1600]{1,0:T(8,128)(2,1)}, bf16[800,1600]{1,0:T(8,128)(2,1)}, u32[]{:S(2)}, u32[]{:S(2)}) collective-permute-start(bf16[800,1600]{1,0:T(8,128)(2,1)} %get-tuple-element.473), channel_id=1, source_target_pairs={{1,4},{3,6},{4,1},{6,3},{9,12},{11,14},{12,9},{14,11},{17,20},{19,... | collective-permute-start | bytes 7680008 | tf_op jit(solution)/shard_map/ppermute | solution.py:1212
  481.1 42.3 %copy-start.50 = (bf16[1,256,1600]{2,1,0:T(8,128)(2,1)S(1)}, bf16[1,256,1600]{2,1,0:T(8,128)(2,1)}, u32[]{:S(2)}) copy-start(bf16[1,256,1600]{2,1,0:T(8,128)(2,1)} %copy.147) | copy-start | bytes 2457604
  481.1 42.3 %copy-start.51 = (bf16[256,1600]{1,0:T(8,128)(2,1)S(1)}, bf16[256,1600]{1,0:T(8,128)(2,1)}, u32[]{:S(2)}) copy-start(bf16[256,1600]{1,0:T(8,128)(2,1)} %copy.150) | copy-start | bytes 2457604
  541.8 88.4 %copy-start.93 = (f32[1600]{0:T(1024)S(1)}, f32[1600]{0:T(1024)}, u32[]{:S(2)}) copy-start(f32[1600]{0:T(1024)} %get-tuple-element.436) | copy-start | bytes 19204
  719.0 267.3 %reduce-scatter.25.cloned.1.call-start = ((), (), s32[]{:S(2)}) async-start(), calls=%async_computation.16 | async-start | bytes 5990400
  741.5 30.6 %collective-permute-start.16 = (bf16[2,200,1600]{2,1,0:T(8,128)(2,1)}, bf16[2,200,1600]{2,1,0:T(8,128)(2,1)}, u32[]{:S(2)}, u32[]{:S(2)}) collective-permute-start(bf16[2,200,1600]{2,1,0:T(8,128)(2,1)} %slice_bitcast_fusion.3), channel_id=1, source_target_pairs={{0,1},{1,0},{2,3},{3,2},{4,5},{5,4},{6,7},{7,6},{8,9},{9,8},{10,11... | collective-permute-start | bytes 3840008 | tf_op jit(solution)/shard_map/ppermute | solution.py:1212
  772.1 214.1 %reduce-scatter.27.cloned.1.call-start = ((), (), s32[]{:S(2)}) async-start(), calls=%async_computation.17 | async-start | bytes 5990400
  773.9 60.0 %collective-permute-start.19 = (bf16[256,1664]{1,0:T(8,128)(2,1)S(1)}, bf16[256,1664]{1,0:T(8,128)(2,1)}, u32[]{:S(2)}, u32[]{:S(2)}) collective-permute-start(bf16[256,1664]{1,0:T(8,128)(2,1)S(1)} %get-tuple-element.503), channel_id=1, source_target_pairs={{0,1},{1,0},{2,5},{3,4},{4,3},{5,2},{6,7},{7,6},{8,9},{9,8},{10,13... | collective-permute-start | bytes 2555912 | tf_op jit(solution)/shard_map/ppermute | solution.py:1212
  776.2 57.8 %collective-permute-start.18 = (bf16[256,1664]{1,0:T(8,128)(2,1)S(1)}, bf16[256,1664]{1,0:T(8,128)(2,1)}, u32[]{:S(2)}, u32[]{:S(2)}) collective-permute-start(bf16[256,1664]{1,0:T(8,128)(2,1)S(1)} %get-tuple-element.504), channel_id=1, source_target_pairs={{2,4},{3,5},{4,2},{5,3},{10,12},{11,13},{12,10},{13,11},{18,20},{1... | collective-permute-start | bytes 2555912 | tf_op jit(solution)/shard_map/ppermute | solution.py:1212
  778.4 55.5 %collective-permute-start.17 = (bf16[2,200,1600]{2,1,0:T(8,128)(2,1)S(1)}, bf16[2,200,1600]{2,1,0:T(8,128)(2,1)}, u32[]{:S(2)}, u32[]{:S(2)}) collective-permute-start(bf16[2,200,1600]{2,1,0:T(8,128)(2,1)S(1)} %copy-done.73), channel_id=1, source_target_pairs={{0,1},{1,0},{2,3},{3,2},{4,5},{5,4},{6,7},{7,6},{8,9},{9,8},{10,11... | collective-permute-start | bytes 3840008 | tf_op jit(solution)/shard_map/ppermute | solution.py:1212
  834.0 8.4 collective-permute-start.20
  834.4 11.1 collective-permute-start.21
  848.6 274.6 %reduce-scatter.31.cloned.1.call-start = ((), (), s32[]{:S(2)}) async-start(), calls=%async_computation.19 | async-start | bytes 3328000
  898.1 225.0 %reduce-scatter.29.cloned.1.call-start = ((), (), s32[]{:S(2)}) async-start(), calls=%async_computation.18 | async-start | bytes 11520000
  898.7 313.1 %reduce-scatter.33.cloned.1.call-start = ((), (), s32[]{:S(2)}) async-start(), calls=%async_computation.20 | async-start | bytes 3328000
  899.2 87.0 %collective-permute-start.22 = (bf16[200,1600]{1,0:T(8,128)(2,1)S(1)}, bf16[200,1600]{1,0:T(8,128)(2,1)S(1)}, u32[]{:S(2)}, u32[]{:S(2)}) collective-permute-start(bf16[200,1600]{1,0:T(8,128)(2,1)S(1)} %copy-done.80), channel_id=1, source_target_pairs={{0,1},{1,0},{2,3},{3,2},{4,5},{5,4},{6,7},{7,6},{8,9},{9,8},{10,11... | collective-permute-start | bytes 1920008 | tf_op jit(solution)/shard_map/ppermute | solution.py:1212
  993.2 31.1 %collective-permute-start.23 = (bf16[2,200,1600]{2,1,0:T(8,128)(2,1)S(1)}, bf16[2,200,1600]{2,1,0:T(8,128)(2,1)S(1)}, u32[]{:S(2)}, u32[]{:S(2)}) collective-permute-start(bf16[2,200,1600]{2,1,0:T(8,128)(2,1)S(1)} %slice_bitcast_fusion.2), channel_id=1, source_target_pairs={{0,1},{1,0},{2,3},{3,2},{4,5},{5,4},{6,7},{7,6},{8,9},{9,8},{10,11... | collective-permute-start | bytes 3840008 | tf_op jit(solution)/shard_map/ppermute | solution.py:1212
  1024.4 30.5 %collective-permute-start.24 = (bf16[2,200,1600]{2,1,0:T(8,128)(2,1)}, bf16[2,200,1600]{2,1,0:T(8,128)(2,1)}, u32[]{:S(2)}, u32[]{:S(2)}) collective-permute-start(bf16[2,200,1600]{2,1,0:T(8,128)(2,1)} %dynamic-slice_bitcast_fusion.6), channel_id=1, source_target_pairs={{0,1},{1,0},{2,3},{3,2},{4,5},{5,4},{6,7},{7,6},{8,9},{9,8},{10,11... | collective-permute-start | bytes 3840008 | tf_op jit(solution)/shard_map/ppermute | solution.py:1212
  1058.6 300.3 %reduce-scatter.35.cloned.1.call-start = ((), (), s32[]{:S(2)}) async-start(), calls=%async_computation.21 | async-start | bytes 3328000
  1058.6 64.5 %collective-permute-start.25 = (bf16[4,200,1600]{2,1,0:T(8,128)(2,1)}, bf16[4,200,1600]{2,1,0:T(8,128)(2,1)}, u32[]{:S(2)}, u32[]{:S(2)}) collective-permute-start(bf16[4,200,1600]{2,1,0:T(8,128)(2,1)} %get-tuple-element.312), channel_id=1, source_target_pairs={{0,1},{1,0},{2,3},{3,2},{4,5},{5,4},{6,7},{7,6},{8,9},{9,8},{10,11... | collective-permute-start | bytes 7680008 | tf_op jit(solution)/shard_map/ppermute | solution.py:1212
  1128.0 230.9 %reduce-scatter.37.cloned.1.call-start = ((), (), s32[]{:S(2)}) async-start(), calls=%async_computation.22 | async-start | bytes 5990400
  1142.9 20.7 %collective-permute-start.28 = (bf16[400,1600]{1,0:T(8,128)(2,1)S(1)}, bf16[400,1600]{1,0:T(8,128)(2,1)S(1)}, u32[]{:S(2)}, u32[]{:S(2)}) collective-permute-start(bf16[400,1600]{1,0:T(8,128)(2,1)S(1)} %constant_dynamic-update-slice_fusion.2), channel_id=1, source_target_pairs={{1,4},{3,6},{4,1},{6,3},{9,12},{11,14},{12,9},{14,11},{17,20},{19,... | collective-permute-start | bytes 3840008 | tf_op jit(solution)/shard_map/ppermute | solution.py:1212
  1148.1 16.8 %collective-permute-start.26 = (bf16[512,1664]{1,0:T(8,128)(2,1)}, bf16[512,1664]{1,0:T(8,128)(2,1)S(1)}, u32[]{:S(2)}, u32[]{:S(2)}) collective-permute-start(bf16[512,1664]{1,0:T(8,128)(2,1)} %copy-done.11), channel_id=1, source_target_pairs={{0,4},{1,5},{2,6},{3,7},{4,0},{5,1},{6,2},{7,3},{8,12},{9,13},{10,... | collective-permute-start | bytes 5111816 | tf_op jit(solution)/shard_map/ppermute | solution.py:1212
  1148.2 18.2 %collective-permute-start.27 = (bf16[512,1664]{1,0:T(8,128)(2,1)S(1)}, bf16[512,1664]{1,0:T(8,128)(2,1)S(1)}, u32[]{:S(2)}, u32[]{:S(2)}) collective-permute-start(bf16[512,1664]{1,0:T(8,128)(2,1)S(1)} %copy-done.10), channel_id=1, source_target_pairs={{0,4},{1,5},{2,6},{3,7},{4,0},{5,1},{6,2},{7,3},{8,12},{9,13},{10,... | collective-permute-start | bytes 5111816 | tf_op jit(solution)/shard_map/ppermute | solution.py:1212
  1152.8 16.6 %collective-permute-start.29 = (bf16[100,3200]{1,0:T(8,128)(2,1)S(1)}, bf16[100,3200]{1,0:T(8,128)(2,1)}, u32[]{:S(2)}, u32[]{:S(2)}) collective-permute-start(bf16[100,3200]{1,0:T(8,128)(2,1)S(1)} %get-tuple-element.512), channel_id=1, source_target_pairs={{0,2},{1,3},{2,0},{3,1},{4,6},{5,7},{6,4},{7,5},{8,10},{9,11},{10,... | collective-permute-start | bytes 1920008 | tf_op jit(solution)/shard_map/ppermute | solution.py:1212
  1192.2 15.9 %collective-permute-start.30 = (bf16[100,3200]{1,0:T(8,128)(2,1)}, bf16[100,3200]{1,0:T(8,128)(2,1)}, u32[]{:S(2)}, u32[]{:S(2)}) collective-permute-start(bf16[100,3200]{1,0:T(8,128)(2,1)} %get-tuple-element.332), channel_id=1, source_target_pairs={{0,2},{1,3},{2,0},{3,1},{4,6},{5,7},{6,4},{7,5},{8,10},{9,11},{10,... | collective-permute-start | bytes 1920008 | tf_op jit(solution)/shard_map/ppermute | solution.py:1212
  1211.8 146.2 %collective-permute-start.32 = (bf16[200,1600]{1,0:T(8,128)(2,1)}, bf16[200,1600]{1,0:T(8,128)(2,1)S(1)}, u32[]{:S(2)}, u32[]{:S(2)}) collective-permute-start(bf16[200,1600]{1,0:T(8,128)(2,1)} %pad_maximum_fusion.9), channel_id=1, source_target_pairs={{0,1},{1,0},{2,3},{3,2},{4,5},{5,4},{6,7},{7,6},{8,9},{9,8},{10,11... | collective-permute-start | bytes 1920008 | tf_op jit(solution)/shard_map/ppermute | solution.py:1212
  1211.9 144.9 %collective-permute-start.31 = (bf16[200,1600]{1,0:T(8,128)(2,1)}, bf16[200,1600]{1,0:T(8,128)(2,1)}, u32[]{:S(2)}, u32[]{:S(2)}) collective-permute-start(bf16[200,1600]{1,0:T(8,128)(2,1)} %reduce-scatter.33.cloned.1.call-done), channel_id=1, source_target_pairs={{1,4},{3,6},{4,1},{6,3},{9,12},{11,14},{12,9},{14,11},{17,20},{19,... | collective-permute-start | bytes 1920008 | tf_op jit(solution)/shard_map/ppermute | solution.py:1212
  1217.3 140.7 %collective-permute-start.34 = (bf16[256,1664]{1,0:T(8,128)(2,1)S(1)}, bf16[256,1664]{1,0:T(8,128)(2,1)}, u32[]{:S(2)}, u32[]{:S(2)}) collective-permute-start(bf16[256,1664]{1,0:T(8,128)(2,1)S(1)} %get-tuple-element.497), channel_id=1, source_target_pairs={{0,1},{1,0},{2,5},{3,4},{4,3},{5,2},{6,7},{7,6},{8,9},{9,8},{10,13... | collective-permute-start | bytes 2555912 | tf_op jit(solution)/shard_map/ppermute | solution.py:1212
  1217.4 141.5 %collective-permute-start.33 = (bf16[256,1664]{1,0:T(8,128)(2,1)S(1)}, bf16[256,1664]{1,0:T(8,128)(2,1)}, u32[]{:S(2)}, u32[]{:S(2)}) collective-permute-start(bf16[256,1664]{1,0:T(8,128)(2,1)S(1)} %get-tuple-element.498), channel_id=1, source_target_pairs={{2,4},{3,5},{4,2},{5,3},{10,12},{11,13},{12,10},{13,11},{18,20},{1... | collective-permute-start | bytes 2555912 | tf_op jit(solution)/shard_map/ppermute | solution.py:1212
  1364.9 29.4 %collective-permute-start.35 = (bf16[200,400]{1,0:T(8,128)(2,1)}, bf16[200,400]{1,0:T(8,128)(2,1)}, u32[]{:S(2)}, u32[]{:S(2)}) collective-permute-start(bf16[200,400]{1,0:T(8,128)(2,1)} %get-tuple-element.521), channel_id=1, source_target_pairs={{0,1},{1,0},{2,3},{3,2},{4,5},{5,4},{6,7},{7,6},{8,9},{9,8},{10,11... | collective-permute-start | bytes 480008 | tf_op jit(solution)/shard_map/ppermute | solution.py:1212
  1376.7 17.5 %collective-permute-start.37 = (bf16[200,400]{1,0:T(8,128)(2,1)}, bf16[200,400]{1,0:T(8,128)(2,1)}, u32[]{:S(2)}, u32[]{:S(2)}) collective-permute-start(bf16[200,400]{1,0:T(8,128)(2,1)} %get-tuple-element.522), channel_id=1, source_target_pairs={{0,3},{1,2},{2,1},{3,0},{4,7},{5,6},{6,5},{7,4},{8,11},{9,10},{10,... | collective-permute-start | bytes 480008 | tf_op jit(solution)/shard_map/ppermute | solution.py:1212
  1379.8 14.4 %collective-permute-start.36 = (bf16[200,400]{1,0:T(8,128)(2,1)}, bf16[200,400]{1,0:T(8,128)(2,1)}, u32[]{:S(2)}, u32[]{:S(2)}) collective-permute-start(bf16[200,400]{1,0:T(8,128)(2,1)} %get-tuple-element.523), channel_id=1, source_target_pairs={{0,2},{1,3},{2,0},{3,1},{4,6},{5,7},{6,4},{7,5},{8,10},{9,11},{10,... | collective-permute-start | bytes 480008 | tf_op jit(solution)/shard_map/ppermute | solution.py:1212
  1379.9 17.8 %collective-permute-start.38 = (bf16[200,1600]{1,0:T(8,128)(2,1)}, bf16[200,1600]{1,0:T(8,128)(2,1)}, u32[]{:S(2)}, u32[]{:S(2)}) collective-permute-start(bf16[200,1600]{1,0:T(8,128)(2,1)} %reduce-scatter.35.cloned.1.call-done), channel_id=1, source_target_pairs={{1,4},{3,6},{4,1},{6,3},{9,12},{11,14},{12,9},{14,11},{17,20},{19,... | collective-permute-start | bytes 1920008 | tf_op jit(solution)/shard_map/ppermute | solution.py:1212
  (118 other events, 621.8 us)
Sparse Core Ops, SparseCore 0:
  10.2 107.6 all-gather.20
  120.1 55.5 all-gather.8
  177.9 55.4 all-gather.10
  235.0 55.4 all-gather.12
  292.0 55.6 all-gather.14
  349.1 55.4 all-gather.16
  406.3 56.1 all-gather.18
  719.1 111.7 reduce-scatter.22
  833.2 59.4 reduce-scatter.24
  894.9 60.0 reduce-scatter.26
  957.9 53.5 reduce-scatter.30
  1013.7 105.9 reduce-scatter.28
  1122.0 52.9 reduce-scatter.32
  1177.7 52.6 reduce-scatter.34
  1232.6 59.1 reduce-scatter.36

commit v5 on v4

--- a/solution.py
+++ b/solution.py
@@ -1325,10 +1325,11 @@
     fc_moved = go(first_fc, swap_xc)
     fc_slice[1] = gather_dp(after(fc_weight[1], small))
     parts = attend(0, hidden, w)
-    *parts, fc_moved, fc2_now, pair = fence(*parts, fc_moved, fc2_slice[0], pair)
+    fc2_now = fc2_slice[0]
+    *parts, fc_moved, fc2_top, fc2_end, pair = fence(*parts, fc_moved, *halves(fc2_now), pair)
     normed, query, key, key_other, value, value_other = parts
     v1 = gather_dp(after(qkv1[:, 2 * width:], normed))
-    fc2_parts = halves(fc2_now)
+    fc2_parts = fc2_top, fc2_end
     pair_parts = halves(lax.dynamic_slice_in_dim(pair, core * tall, tall, axis=0))
     fc2_top = go(fc2_parts[0], swap_xc)
     got = [go(pair_parts[0], over_y)]
@@ -1462,21 +1463,22 @@
     final, da2, inner_grad, units_sum, fc2_grad = fence(final, da2, inner_grad, units_sum, fc2_grad)
     fc2_sum = sum_z(fc2_grad)
     fc_kept, fc_sent = units_split(bf(tn(saved[1][10], inner_grad)))
-    fc_kept, fc_top, fc_end, da2 = fence(fc_kept, fc_sent[:planes // 2], fc_sent[planes // 2:], da2)
-    fc_away = [go(fc_top, over_x)]
+    fc_kept, fc_one, fc_two, fc_three, da2 = fence(fc_kept, fc_sent[:1], fc_sent[1:3], fc_sent[3:], da2)
+    fc_away = [go(fc_one, over_x)]
     middle_grad, branch, attended_grad, gain_two, shift_two, attn_out_grad = middle_back(1, grad, da2)
     proj_grad = bf(tn(saved[1][7], branch))
-    fc_away[0], fc_end, middle_grad, branch, attended_grad, proj_grad = fence(
-        fc_away[0], fc_end, middle_grad, branch, attended_grad, proj_grad
+    fc_away[0], fc_two, fc_three, middle_grad, branch, attended_grad, proj_grad = fence(
+        fc_away[0], fc_two, fc_three, middle_grad, branch, attended_grad, proj_grad
     )
     proj_sum = sum_dp(proj_grad)
-    fc_away.append(go(fc_end, over_x))
+    fc_away.append(go(fc_two, over_x))
     final_moved = regroup(final)
-    back = fence(*heads_back(1, attended_grad), fc2_sum, fc_away[1], *final_moved)
-    fc2_sum, fc_away[1], *final_moved = back[5:]
+    back = fence(*heads_back(1, attended_grad), fc2_sum, fc_away[1], fc_three, *final_moved)
+    fc2_sum, fc_away[1], fc_three, *final_moved = back[5:]
+    fc_away.append(go(fc_three, over_x))
     dq, dk, dv = mixed_of(*back[:5])
     dq_grad = bf(tn(saved[1][1], back[0]))
-    dq, dk, dv, dq_grad = fence(dq, dk, dv, dq_grad)
+    dq, dk, dv, dq_grad, fc_away[2] = fence(dq, dk, dv, dq_grad, fc_away[2])
     dq_sum = sum_dp(dq_grad)
     below, gain_one, shift_one = input_back(1, middle_grad, dq, dk, dv)
     out_grad_low = bf(below)
@@ -1495,35 +1497,45 @@
     )
     fc2_high = add_pair(fc2_kept, fc2_away)
     fc2_kept, fc2_sent = units_split(fc2_grad)
-    top = planes // 2
-    fc2_kept, fc2_top, fc2_end, da2, fc2_high = fence(fc2_kept, fc2_sent[:top], fc2_sent[top:], da2, fc2_high)
-    fc2_away = [go(fc2_top, over_x)]
+    fc2_kept, fc2_one, fc2_two, fc2_three, da2, fc2_high = fence(
+        fc2_kept, fc2_sent[:1], fc2_sent[1:2], fc2_sent[2:], da2, fc2_high
+    )
+    fc2_away = [go(fc2_one, over_x)]
     fc_kept, fc_sent = units_split(bf(tn(saved[0][10], inner_grad)))
-    fc2_away[0], fc2_end, fc_kept, fc_sent, da2 = fence(fc2_away[0], fc2_end, fc_kept, fc_sent, da2)
-    fc2_away.append(go(fc2_end, over_x))
+    fc2_away[0], fc2_two, fc2_three, fc_kept, fc_sent, da2 = fence(
+        fc2_away[0], fc2_two, fc2_three, fc_kept, fc_sent, da2
+    )
+    fc2_away.append(go(fc2_two, over_x))
     middle_grad, branch, attended_grad, gain_two, shift_two, attn_out_grad = middle_back(0, below, da2)
     proj_grad = bf(tn(saved[0][7], branch))
-    fc2_away[1], fc_sent, middle_grad, branch, attended_grad, proj_grad = fence(
-        fc2_away[1], fc_sent, middle_grad, branch, attended_grad, proj_grad
+    fc2_away[1], fc2_three, fc_sent, middle_grad, branch, attended_grad, proj_grad = fence(
+        fc2_away[1], fc2_three, fc_sent, middle_grad, branch, attended_grad, proj_grad
     )
-    fc_away = go(fc_sent, over_x)
+    fc2_away.append(go(fc2_three, over_x))
+    fc_away = [go(fc_sent[:1], over_x)]
+    fc_one, fc_two, fc_three = fc_sent[1:2], fc_sent[2:3], fc_sent[3:]
+    back = fence(
+        *heads_back(0, attended_grad), fc2_away[2], fc_away[0], fc_one, fc_two, fc_three,
+        dkv_sum, fc_sum, fc2_high, dq_sum, proj_sum
+    )
+    fc2_away[2], fc_away[0], fc_one, fc_two, fc_three, dkv_sum, fc_sum, fc2_high, dq_sum, proj_sum = back[5:]
     fc2_low = sum_z(add_pair(fc2_kept, jnp.concatenate(fc2_away, axis=0)).reshape(-1, width))
-    back = fence(*heads_back(0, attended_grad), fc_away, dkv_sum, fc_sum, fc2_high, dq_sum, proj_sum)
-    fc_away, dkv_sum, fc_sum, fc2_high, dq_sum, proj_sum = back[5:]
+    fc_away.append(go(fc_one, over_x))
     turned = turn_xc(jnp.concatenate([fc_sum, fc2_high], axis=0))
     qkv_sum = jnp.concatenate([dq_sum, dkv_sum], axis=1)
     near_columns, far_columns = [columns_of((qkv_sum, proj_sum), 2, side) for side in (row, 1 - row)]
     far_top, far_end = halves(far_columns)
     far_top = go(far_top, over_y)
     dq, dk, dv = mixed_of(*back[:5])
-    dq, dk, dv, proj_grad, turned, near_columns, far_top, far_end = fence(
-        dq, dk, dv, proj_grad, turned, near_columns, far_top, far_end
+    dq, dk, dv, proj_grad, turned, near_columns, far_top, far_end, fc_away[1], fc_two, fc_three = fence(
+        dq, dk, dv, proj_grad, turned, near_columns, far_top, far_end, fc_away[1], fc_two, fc_three
     )
     far_end = go(far_end, over_y)
+    fc_away.append(go(fc_two, over_x))
     proj_low = sum_dp(proj_grad)
-    fc_low = sum_z(add_pair(fc_kept, fc_away).reshape(-1, width))
     lowest, gain_one, shift_one = input_back(0, middle_grad, dq, dk, dv)
-    lowest, far_end = fence(lowest, far_end)
+    lowest, far_end, fc_away[2], fc_three = fence(lowest, far_end, fc_away[2], fc_three)
+    fc_away.append(go(fc_three, over_x))
     far_columns = jnp.concatenate([far_top, far_end], axis=0)
     sums_zero = bias_sums((gain_one, gain_two), (shift_one, shift_two), dq, dv, attn_out_grad, out_grad_low)
     low = bf(lowest)
@@ -1544,9 +1556,10 @@
     columns = add_pair(near_columns, far_columns)
     halves_x = columns[:, :split], columns[:, split:]
     near_columns, far_columns = [columns_of(halves_x, 2, side) for side in (col, 1 - col)]
-    low, sums, pieces, keep, send, fc2_low, near_columns, far_columns = fence(
-        low, sums, pieces, keep, send, fc2_low, near_columns, far_columns
+    low, sums, pieces, keep, send, fc2_low, near_columns, far_columns, fc_away[3] = fence(
+        low, sums, pieces, keep, send, fc2_low, near_columns, far_columns, fc_away[3]
     )
+    fc_low = sum_z(add_pair(fc_kept, jnp.concatenate(fc_away, axis=0)).reshape(-1, width))
     fc2_low = turn_xc(fc2_low)
     low_moved = regroup(low)
     far_columns = go(far_columns, over_x)
@@ -1583,7 +1596,7 @@
 
 def solution(mesh):
     planes = mesh.shape["dp"] // 2
-    if mesh.shape["mp"] == 4:
+    if mesh.shape["mp"] == 4 and planes == 4:
         body = functools.partial(quick_body, planes)
     else:
         body = general_body

time: 1420 us -> 1430 us (level)
  waiting for transfers between devices: 70.5 us -> 97.5 us
    optimization_barrier x7, waiting for transfers between devices: 0.07 us -> 24.6 us  [fence(): return lax.optimization_barrier(values)]
    unnamed x264 -> x274, local copies, waits for them, and re-layouts: 46.3 us -> 38 us
    ppermute x39 -> x44, waiting for transfers between devices: 54.2 us -> 48.1 us  [go(): return lax.ppermute(value, AXES, pairs)]
    ppermute x39 -> x44, starting transfers between devices: 74.6 us -> 74.4 us  [go(): return lax.ppermute(value, AXES, pairs)]
  transfers between devices with their start and end apart: 54 -> 59, of which waited for: 10 -> 11; matrix products, arithmetic and copies ran while one was open for 27% -> 25% of each run, Pallas kernels for 46% -> 45%
where the time goes in v5:
time: 1430 us; the launch traced here: 1410 us
  Pallas kernels  814 us (57%)
  matrix products  159 us (11%)
  local copies, waits for them, and re-layouts  135 us (9%)
  other arithmetic  115 us (8%)
  waiting for transfers between devices  97.5 us (7%)
  starting transfers between devices  75.9 us (5%)
  between operations  16.5 us (1%)
    pallas_call x4, Pallas kernels, units(): pl.pallas_call(functools.partial(units_kernel, back, (len(wa) - 1, len(wb...  344 us
    pallas_call x1, Pallas kernels, gather_four(): pl.pallas_call(functools.partial(gather_kernel, planes), in_specs=[anywhe...  149 us
    pallas_call x1, Pallas kernels, settle_columns(): pl.pallas_call(functools.partial(settle_kernel, planes), in_specs=[inside...  143 us
    pallas_call x2, Pallas kernels, attention_back(): pl.pallas_call(functools.partial(attend_back_kernel, width, blocks, place...  98.8 us
    pallas_call x2, Pallas kernels, attention(): pl.pallas_call(functools.partial(attend_kernel, width, blocks, place.shap...  79.9 us
    ppermute x44, starting transfers between devices, go(): return lax.ppermute(value, AXES, pairs)  74.4 us
    dot_general x6, matrix products, tn(): lax.dot_general(a, b, (((0,), (0,)), ((), ())), preferred_element_type=jn...  64.5 us
    ppermute x44, waiting for transfers between devices, go(): return lax.ppermute(value, AXES, pairs)  48.1 us
  transfers between devices with their start and end apart: 59, of which 11 were waited for; matrix products, arithmetic and copies ran while one was open for 25% of the time, Pallas kernels for 45%

profile of v5, /device:TPU:1, one launch (start us, length us, event | category | flops | bytes accessed | tf_op | source)
XLA Modules:
  0.0 1412.7 jit_solution(4342634645970818636)
XLA Ops:
  15.1 3.6 copy.127.token_ref
  21.9 149.2 %gather_four.1 = (bf16[4,8,200,1600]{3,2,1,0:T(8,128)(2,1)}, f32[8,24,200]{2,1,0:T(8,128)}, bf16[2,256,1600]{2,1,0:T(8,128)(2,1)}) custom-call(bf16[200,1600]{1,0:T(8,128)(2,1)} %fusion.36.piece_ref, f32[24,200]{1,0:T(8,128)} %pad_convert_fusion.small_ref, bf16[2,256,1600]{2,1,0:T(8,128)(2,1)} %copy.127.token_ref), custom_call_target="tpu_custom_call" | custom-call | bytes 314572800 | tf_op jit(solution)/shard_map/gather_four/pallas_call | solution.py:731
  172.5 3.5 collective-permute-start.2
  182.3 13.6 fusion.50
  195.8 3.5 add_convert_fusion.9
  209.4 7.2 add_convert_fusion.10.q_ref
  216.6 5.4 fusion.52
  222.0 11.5 all-gather.11.cloned.1.call-done
  233.5 8.1 collective-permute-done.3.refs_3_.refs_5_
  243.7 3.4 constant_dynamic-slice_fusion.14
  247.1 4.1 collective-permute-start.5
  257.2 39.7 %attention.2 = (bf16[512,1600]{1,0:T(8,128)(2,1)S(1)}, f32[13,2,512]{2,1,0:T(2,128)S(1)}) custom-call(s32[4]{0:T(128)S(1)} %reshape.484.place_ref, s32[8]{0:T(128)S(1)} %select_reduce_fusion.slot_ref, bf16[512,1600]{1,0:T(8,128)(2,1)S(1)} %copy-done.17, bf16[512,1664]{1,0:T(8,128)(2,1)S(1)} %pad.27.ko_ref, bf16[512,1664]{1,0:T(8,128)(2,1)} %collective-permute-done.ks_ref, ...), custom_call_target="tpu_custom_call" | custom-call | flops 6979321856 | bytes 9830400 | tf_op jit(solution)/shard_map/attention/pallas_call | solution.py:543
  296.9 7.3 fusion.57
  312.3 5.3 collective-permute-start.8
  318.1 86.9 %units.2 = (f32[512,1600]{1,0:T(8,128)}, bf16[2048,1600]{1,0:T(8,128)(2,1)}, bf16[2048,1600]{1,0:T(8,128)(2,1)}, bf16[2048,1600]{1,0:T(8,128)(2,1)}) custom-call(bf16[512,1600]{1,0:T(8,128)(2,1)} %add_convert_fusion.8.refs_0_, bf16[1600,1600]{1,0:T(8,128)(2,1)} %bitcast.257, bf16[1600,1600]{1,0:T(8,128)(2,1)} %all-gather.9.cloned.1.call-done.refs_2_.refs_1_, ...), custom_call_target="tpu_custom_call" | custom-call | flops 60000002048 | bytes 62914560 | tf_op jit(solution)/shard_map/units/pallas_call | solution.py:973
  405.3 5.4 broadcast_select_fusion.3
  410.7 3.8 fusion.49
  418.9 3.3 convolution_convert_fusion.8
  425.1 6.1 add_convert_fusion.5
  435.2 4.3 collective-permute-start.12
  443.5 9.4 add_convert_fusion.6.q_ref
  452.8 5.0 collective-permute-done.12
  459.7 5.4 fusion.51
  469.2 3.6 collective-permute-start.15
  474.3 40.1 %attention.3 = (bf16[512,1600]{1,0:T(8,128)(2,1)S(1)}, f32[13,2,512]{2,1,0:T(2,128)S(1)}) custom-call(s32[4]{0:T(128)S(1)} %reshape.484.place_ref, s32[8]{0:T(128)S(1)} %select_reduce_fusion.slot_ref, bf16[512,1600]{1,0:T(8,128)(2,1)S(1)} %copy-done.15, bf16[512,1664]{1,0:T(8,128)(2,1)S(1)} %pad.29.ko_ref, bf16[512,1664]{1,0:T(8,128)(2,1)} %collective-permute-done.10.ks_ref, ...), custom_call_target="tpu_custom_call" | custom-call | flops 6979321856 | bytes 9830400 | tf_op jit(solution)/shard_map/attention/pallas_call | solution.py:543
  521.6 7.6 fusion.58
  534.1 89.0 %units.3 = (f32[512,1600]{1,0:T(8,128)}, bf16[2048,1600]{1,0:T(8,128)(2,1)}, bf16[2048,1600]{1,0:T(8,128)(2,1)}, bf16[2048,1600]{1,0:T(8,128)(2,1)}) custom-call(bf16[512,1600]{1,0:T(8,128)(2,1)} %add_convert_fusion.4.refs_0_, bf16[1600,1600]{1,0:T(8,128)(2,1)} %all-gather.13.cloned.1.call-done.refs_1_.refs_2_, ...), custom_call_target="tpu_custom_call" | custom-call | flops 60000002048 | bytes 62914560 | tf_op jit(solution)/shard_map/units/pallas_call | solution.py:973
  623.0 4.9 multiply_reduce_fusion.7
  627.9 83.7 %units_back.2 = (f32[512,1600]{1,0:T(8,128)}, bf16[2048,1600]{1,0:T(8,128)(2,1)}, bf16[2048,1600]{1,0:T(8,128)(2,1)}, f32[1,1600]{1,0:T(1,128)}, bf16[1600,1600]{1,0:T(8,128)(2,1)}) custom-call(bf16[512,1600]{1,0:T(8,128)(2,1)} %pad_maximum_fusion.3.refs_0_, bf16[1600,1600]{1,0:T(8,128)(2,1)} %all-gather.17.cloned.1.call-done.refs_2_.refs_1_, ...), custom_call_target="tpu_custom_call" | custom-call | flops 60000002048 | bytes 62914560 | tf_op jit(solution)/shard_map/units_back/pallas_call | solution.py:973
  711.7 18.3 %convolution_convert_fusion.5 = bf16[1600,1600]{1,0:T(8,128)(2,1)S(1)} fusion(bf16[2048,1600]{1,0:T(8,128)(2,1)} %get-tuple-element.267, bf16[2048,1600]{1,0:T(8,128)(2,1)} %get-tuple-element.268), kind=kOutput, calls=%fused_computation.7 | convolution fusion | flops 10488320000 | bytes 18227200 | tf_op jit(solution)/shard_map/dot_general | solution.py:407
  738.1 4.4 convert_reduce_fusion.6
  742.5 5.1 convolution_convert_fusion.7.do_ref
  747.6 5.5 convolution_convert_fusion.3
  760.1 49.4 %attention_back.2 = (bf16[512,1600]{1,0:T(8,128)(2,1)S(1)}, f32[512,1664]{1,0:T(8,128)}, bf16[512,1664]{1,0:T(8,128)(2,1)S(1)}, f32[512,1664]{1,0:T(8,128)}, bf16[512,1664]{1,0:T(8,128)(2,1)S(1)}) custom-call(s32[4]{0:T(128)S(1)} %reshape.484.place_ref, s32[8]{0:T(128)S(1)} %select_reduce_fusion.slot_ref, bf16[512,1600]{1,0:T(8,128)(2,1)S(1)} %copy-done.16, ...), custom_call_target="tpu_custom_call" | custom-call | flops 17448304640 | bytes 24576000 | tf_op jit(solution)/shard_map/attention_back/pallas_call | solution.py:575
  813.1 12.0 reduce-scatter.23.cloned.1.call-done
  826.9 7.5 convolution_convert_fusion.2
  834.4 3.3 fusion.3
  846.0 9.0 fusion.37
  855.1 5.4 fusion.38
  860.5 8.4 multiply_reduce_fusion.4
  870.3 5.5 fusion.48
  875.9 4.1 add_convert_fusion.2
  880.0 9.3 convolution_convert_fusion
  894.8 84.2 %units_back.3 = (f32[512,1600]{1,0:T(8,128)}, bf16[2048,1600]{1,0:T(8,128)(2,1)}, bf16[2048,1600]{1,0:T(8,128)(2,1)}, f32[1,1600]{1,0:T(1,128)}, bf16[1600,1600]{1,0:T(8,128)(2,1)}) custom-call(bf16[512,1600]{1,0:T(8,128)(2,1)} %get-tuple-element.305.refs_0_, bf16[1600,1600]{1,0:T(8,128)(2,1)} %all-gather.9.cloned.1.call-done.refs_2_.refs_1_, ...), custom_call_target="tpu_custom_call" | custom-call | flops 60000002048 | bytes 62914560 | tf_op jit(solution)/shard_map/units_back/pallas_call | solution.py:973
  988.0 18.4 %convolution_convert_fusion.4 = bf16[1600,1600]{1,0:T(8,128)(2,1)S(1)} fusion(bf16[2048,1600]{1,0:T(8,128)(2,1)} %get-tuple-element.321, bf16[2048,1600]{1,0:T(8,128)(2,1)} %get-tuple-element.322), kind=kOutput, calls=%fused_computation.6 | convolution fusion | flops 10488320000 | bytes 18227200 | tf_op jit(solution)/shard_map/dot_general | solution.py:407
  1012.0 3.8 multiply_reduce_fusion
  1018.8 4.9 convolution_convert_fusion.6.do_ref
  1024.4 5.5 convolution_convert_fusion.1
  1030.3 3.3 fusion.53
  1037.6 49.4 %attention_back.3 = (bf16[512,1600]{1,0:T(8,128)(2,1)S(1)}, f32[512,1664]{1,0:T(8,128)}, bf16[512,1664]{1,0:T(8,128)(2,1)S(1)}, f32[512,1664]{1,0:T(8,128)}, bf16[512,1664]{1,0:T(8,128)(2,1)S(1)}) custom-call(s32[4]{0:T(128)S(1)} %reshape.484.place_ref, s32[8]{0:T(128)S(1)} %select_reduce_fusion.slot_ref, bf16[512,1600]{1,0:T(8,128)(2,1)S(1)} %copy-done.18, ...), custom_call_target="tpu_custom_call" | custom-call | flops 17448304640 | bytes 24576000 | tf_op jit(solution)/shard_map/attention_back/pallas_call | solution.py:575
  1089.3 24.6 %reduce-scatter.29.cloned.1.call-done = bf16[200,3200]{1,0:T(8,128)(2,1)} async-done(((bf16[1600,3200]{1,0:T(8,128)(2,1)}), bf16[200,3200]{1,0:T(8,128)(2,1)}) %reduce-scatter.29.cloned.1.call-update) | async-done | bytes 1280016 | tf_op jit(solution)/shard_map/optimization_barrier | solution.py:1260
  1113.9 4.6 add_convert_fusion.1
  1122.2 5.7 collective-permute-start.30
  1135.0 15.2 %collective-permute-done.30 = bf16[400,1600]{1,0:T(8,128)(2,1)S(1)} collective-permute-done((bf16[400,1600]{1,0:T(8,128)(2,1)S(1)}, bf16[400,1600]{1,0:T(8,128)(2,1)S(1)}, u32[]{:S(2)}, u32[]{:S(2)}) %collective-permute-start.30) | collective-permute-done | bytes 1280032 | tf_op jit(solution)/shard_map/ppermute | solution.py:1212
  1155.4 3.6 fusion.59
  1159.1 3.6 fusion.60
  1162.8 7.2 fusion.21
  1178.4 4.3 slice_bitcast_fusion.3
  1195.7 13.0 collective-permute-done.35
  1208.7 3.7 add_convert_fusion
  1221.1 5.1 collective-permute-start.36
  1228.9 142.5 %settle_columns.1 = (f32[200,1200]{1,0:T(8,128)}, f32[24,1600]{1,0:T(8,128)}) custom-call(bf16[800,512]{1,0:T(8,128)(2,1)} %bitcast.245, bf16[800,512]{1,0:T(8,128)(2,1)} %bitcast.244, bf16[4,512,1200]{2,1,0:T(8,128)(2,1)} %pad_maximum_fusion.1.piece_ref, f32[24,1600]{1,0:T(8,128)} %concatenate.111.sum_ref), custom_call_target="tpu_custom_call" | custom-call | flops 16000000000 | bytes 62914560 | tf_op jit(solution)/shard_map/settle_columns/pallas_call | solution.py:1127
  1380.3 5.3 collective-permute-start.40
  1386.8 3.9 collective-permute-start.43
  (557 shorter events, 213.5 us)
Async XLA Ops:
  7.2 172.1 %all-gather.21.cloned.1.call-start = ((), (), s32[]{:S(2)}) async-start(), calls=%async_computation.15 | async-start | bytes 5990400 | tf_op jit(solution)/shard_map/all_gather | solution.py:1254
  9.8 206.8 %all-gather.9.cloned.1.call-start = ((), (), s32[]{:S(2)}) async-start(), calls=%async_computation.8 | async-start | bytes 5990400 | tf_op jit(solution)/shard_map/all_gather | solution.py:1254
  11.0 222.4 %all-gather.11.cloned.1.call-start = ((), (), s32[]{:S(2)}) async-start(), calls=%async_computation.9 | async-start | bytes 5990400 | tf_op jit(solution)/shard_map/all_gather | solution.py:1254
  14.9 291.7 %all-gather.13.cloned.1.call-start = ((), (), s32[]{:S(2)}) async-start(), calls=%async_computation.10 | async-start | bytes 5990400 | tf_op jit(solution)/shard_map/all_gather | solution.py:1254
  172.4 238.3 %all-gather.15.cloned.1.call-start = ((), (), s32[]{:S(2)}) async-start(), calls=%async_computation.11 | async-start | bytes 5990400 | tf_op jit(solution)/shard_map/all_gather | solution.py:1254
  172.5 6.8 collective-permute-start.2
  179.3 125.5 %copy-start.87 = (f32[1600]{0:T(1024)}, f32[1600]{0:T(1024)S(1)}, u32[]{:S(2)}) copy-start(f32[1600]{0:T(1024)S(1)} %get-tuple-element.482) | copy-start | bytes 19204
  179.3 235.8 %copy-start.90 = (f32[1600]{0:T(1024)}, f32[1600]{0:T(1024)S(1)}, u32[]{:S(2)}) copy-start(f32[1600]{0:T(1024)S(1)} %get-tuple-element.479) | copy-start | bytes 19204
  179.3 62.3 %collective-permute-start.3 = (bf16[1600,1600]{1,0:T(8,128)(2,1)}, bf16[1600,1600]{1,0:T(8,128)(2,1)}, u32[]{:S(2)}, u32[]{:S(2)}) collective-permute-start(bf16[1600,1600]{1,0:T(8,128)(2,1)} %bitcast.256), channel_id=1, source_target_pairs={{1,4},{3,6},{4,1},{6,3},{9,12},{11,14},{12,9},{14,11},{17,20},{19,... | collective-permute-start | bytes 15360008 | tf_op jit(solution)/shard_map/ppermute | solution.py:1212
  199.5 22.5 %collective-permute-start.1 = (bf16[512,1664]{1,0:T(8,128)(2,1)S(1)}, bf16[512,1664]{1,0:T(8,128)(2,1)}, u32[]{:S(2)}, u32[]{:S(2)}) collective-permute-start(bf16[512,1664]{1,0:T(8,128)(2,1)S(1)} %pad.28.vo_ref), channel_id=1, source_target_pairs={{0,4},{1,5},{2,6},{3,7},{4,0},{5,1},{6,2},{7,3},{8,12},{9,13},{10,... | collective-permute-start | bytes 5111816 | tf_op jit(solution)/shard_map/ppermute | solution.py:1212
  207.2 14.8 %collective-permute-start = (bf16[512,1664]{1,0:T(8,128)(2,1)S(1)}, bf16[512,1664]{1,0:T(8,128)(2,1)}, u32[]{:S(2)}, u32[]{:S(2)}) collective-permute-start(bf16[512,1664]{1,0:T(8,128)(2,1)S(1)} %pad.27.ko_ref), channel_id=1, source_target_pairs={{0,4},{1,5},{2,6},{3,7},{4,0},{5,1},{6,2},{7,3},{8,12},{9,13},{10,... | collective-permute-start | bytes 5111816 | tf_op jit(solution)/shard_map/ppermute | solution.py:1212
  241.6 218.1 %all-gather.17.cloned.1.call-start = ((), (), s32[]{:S(2)}) async-start(), calls=%async_computation.12 | async-start | bytes 5990400 | tf_op jit(solution)/shard_map/all_gather | solution.py:1254
  241.6 55.3 %collective-permute-start.4 = (bf16[800,1600]{1,0:T(8,128)(2,1)}, bf16[800,1600]{1,0:T(8,128)(2,1)}, u32[]{:S(2)}, u32[]{:S(2)}) collective-permute-start(bf16[800,1600]{1,0:T(8,128)(2,1)} %get-tuple-element.217), channel_id=1, source_target_pairs={{1,4},{3,6},{4,1},{6,3},{9,12},{11,14},{12,9},{14,11},{17,20},{19,... | collective-permute-start | bytes 7680008 | tf_op jit(solution)/shard_map/ppermute | solution.py:1212
  247.1 49.8 %collective-permute-start.5 = (bf16[400,1600]{1,0:T(8,128)(2,1)}, bf16[400,1600]{1,0:T(8,128)(2,1)}, u32[]{:S(2)}, u32[]{:S(2)}) collective-permute-start(bf16[400,1600]{1,0:T(8,128)(2,1)} %get-tuple-element.515), channel_id=1, source_target_pairs={{0,2},{1,3},{2,0},{3,1},{4,6},{5,7},{6,4},{7,5},{8,10},{9,11},{10,... | collective-permute-start | bytes 3840008 | tf_op jit(solution)/shard_map/ppermute | solution.py:1212
  252.9 53.7 %collective-permute-start.7 = (bf16[400,1600]{1,0:T(8,128)(2,1)}, bf16[400,1600]{1,0:T(8,128)(2,1)}, u32[]{:S(2)}, u32[]{:S(2)}) collective-permute-start(bf16[400,1600]{1,0:T(8,128)(2,1)} %get-tuple-element.514), channel_id=1, source_target_pairs={{0,2},{1,3},{2,0},{3,1},{4,6},{5,7},{6,4},{7,5},{8,10},{9,11},{10,... | collective-permute-start | bytes 3840008 | tf_op jit(solution)/shard_map/ppermute | solution.py:1212
  253.0 53.6 %collective-permute-start.6 = (bf16[800,1600]{1,0:T(8,128)(2,1)}, bf16[800,1600]{1,0:T(8,128)(2,1)}, u32[]{:S(2)}, u32[]{:S(2)}) collective-permute-start(bf16[800,1600]{1,0:T(8,128)(2,1)} %get-tuple-element.220), channel_id=1, source_target_pairs={{1,4},{3,6},{4,1},{6,3},{9,12},{11,14},{12,9},{14,11},{17,20},{19,... | collective-permute-start | bytes 7680008 | tf_op jit(solution)/shard_map/ppermute | solution.py:1212
  304.2 106.5 %copy-start.19 = (f32[512,1600]{1,0:T(8,128)}, f32[512,1600]{1,0:T(8,128)S(1)}, u32[]{:S(2)}) copy-start(f32[512,1600]{1,0:T(8,128)S(1)} %get-tuple-element.222) | copy-start | bytes 9830404
  306.6 215.0 %all-gather.19.cloned.1.call-start = ((), (), s32[]{:S(2)}) async-start(), calls=%async_computation.13 | async-start | bytes 5990400 | tf_op jit(solution)/shard_map/all_gather | solution.py:1254
  312.3 93.0 %collective-permute-start.9 = (bf16[800,1600]{1,0:T(8,128)(2,1)}, bf16[800,1600]{1,0:T(8,128)(2,1)}, u32[]{:S(2)}, u32[]{:S(2)}) collective-permute-start(bf16[800,1600]{1,0:T(8,128)(2,1)} %constant_dynamic-update-slice_fusion), channel_id=1, source_target_pairs={{0,4},{1,5},{2,6},{3,7},{4,0},{5,1},{6,2},{7,3},{8,12},{9,13},{10,... | collective-permute-start | bytes 7680008 | tf_op jit(solution)/shard_map/ppermute | solution.py:1212
  312.3 98.4 %collective-permute-start.8 = (bf16[1600,1600]{1,0:T(8,128)(2,1)}, bf16[1600,1600]{1,0:T(8,128)(2,1)}, u32[]{:S(2)}, u32[]{:S(2)}) collective-permute-start(bf16[1600,1600]{1,0:T(8,128)(2,1)} %all-gather.13.cloned.1.call-done.refs_1_.refs_2_), channel_id=1, source_target_pairs={{1,4},{3,6},{4,1},{6,3},{9,12},{11,14},{12,9},{14,11},{17,20},{19,... | collective-permute-start | bytes 15360008 | tf_op jit(solution)/shard_map/ppermute | solution.py:1212
  317.6 507.5 %reduce-scatter.23.cloned.1.call-start = ((), (), s32[]{:S(2)}) async-start(), calls=%async_computation.14 | async-start | bytes 6656000 | tf_op jit(solution)/shard_map/reduce_scatter | solution.py:1221
  431.3 28.4 %collective-permute-start.11 = (bf16[512,1664]{1,0:T(8,128)(2,1)S(1)}, bf16[512,1664]{1,0:T(8,128)(2,1)}, u32[]{:S(2)}, u32[]{:S(2)}) collective-permute-start(bf16[512,1664]{1,0:T(8,128)(2,1)S(1)} %pad.30.vo_ref), channel_id=1, source_target_pairs={{0,4},{1,5},{2,6},{3,7},{4,0},{5,1},{6,2},{7,3},{8,12},{9,13},{10,... | collective-permute-start | bytes 5111816 | tf_op jit(solution)/shard_map/ppermute | solution.py:1212
  432.4 27.3 %collective-permute-start.10 = (bf16[512,1664]{1,0:T(8,128)(2,1)S(1)}, bf16[512,1664]{1,0:T(8,128)(2,1)}, u32[]{:S(2)}, u32[]{:S(2)}) collective-permute-start(bf16[512,1664]{1,0:T(8,128)(2,1)S(1)} %pad.29.ko_ref), channel_id=1, source_target_pairs={{0,4},{1,5},{2,6},{3,7},{4,0},{5,1},{6,2},{7,3},{8,12},{9,13},{10,... | collective-permute-start | bytes 5111816 | tf_op jit(solution)/shard_map/ppermute | solution.py:1212
  435.2 22.7 %collective-permute-start.12 = (bf16[256,1600]{0,1:T(8,128)(2,1)}, bf16[256,1600]{0,1:T(8,128)(2,1)}, u32[]{:S(2)}, u32[]{:S(2)}) collective-permute-start(bf16[256,1600]{0,1:T(8,128)(2,1)} %bitcast.27), channel_id=1, source_target_pairs={{2,4},{3,5},{4,2},{5,3},{10,12},{11,13},{12,10},{13,11},{18,20},{1... | collective-permute-start | bytes 2457608 | tf_op jit(solution)/shard_map/ppermute | solution.py:1212
  439.5 20.2 %collective-permute-start.13 = (bf16[256,1600]{0,1:T(8,128)(2,1)}, bf16[256,1600]{0,1:T(8,128)(2,1)}, u32[]{:S(2)}, u32[]{:S(2)}) collective-permute-start(bf16[256,1600]{0,1:T(8,128)(2,1)} %get-tuple-element.548), channel_id=1, source_target_pairs={{0,1},{1,0},{2,5},{3,4},{4,3},{5,2},{6,7},{7,6},{8,9},{9,8},{10,13... | collective-permute-start | bytes 2457608 | tf_op jit(solution)/shard_map/ppermute | solution.py:1212
  465.1 56.6 %collective-permute-start.14 = (bf16[800,1600]{1,0:T(8,128)(2,1)}, bf16[800,1600]{1,0:T(8,128)(2,1)}, u32[]{:S(2)}, u32[]{:S(2)}) collective-permute-start(bf16[800,1600]{1,0:T(8,128)(2,1)} %get-tuple-element.511), channel_id=1, source_target_pairs={{1,4},{3,6},{4,1},{6,3},{9,12},{11,14},{12,9},{14,11},{17,20},{19,... | collective-permute-start | bytes 7680008 | tf_op jit(solution)/shard_map/ppermute | solution.py:1212
  469.2 62.6 %collective-permute-start.15 = (bf16[800,1600]{1,0:T(8,128)(2,1)}, bf16[800,1600]{1,0:T(8,128)(2,1)}, u32[]{:S(2)}, u32[]{:S(2)}) collective-permute-start(bf16[800,1600]{1,0:T(8,128)(2,1)} %get-tuple-element.510), channel_id=1, source_target_pairs={{1,4},{3,6},{4,1},{6,3},{9,12},{11,14},{12,9},{14,11},{17,20},{19,... | collective-permute-start | bytes 7680008 | tf_op jit(solution)/shard_map/ppermute | solution.py:1212
  534.0 89.0 %copy-start.95 = (f32[1600]{0:T(1024)S(1)}, f32[1600]{0:T(1024)}, u32[]{:S(2)}) copy-start(f32[1600]{0:T(1024)} %get-tuple-element.472) | copy-start | bytes 19204
  711.6 267.7 %reduce-scatter.25.cloned.1.call-start = ((), (), s32[]{:S(2)}) async-start(), calls=%async_computation.16 | async-start | bytes 5990400
  734.1 19.1 %collective-permute-start.16 = (bf16[1,200,1600]{2,1,0:T(8,128)(2,1)}, bf16[1,200,1600]{2,1,0:T(8,128)(2,1)}, u32[]{:S(2)}, u32[]{:S(2)}) collective-permute-start(bf16[1,200,1600]{2,1,0:T(8,128)(2,1)} %get-tuple-element.270), channel_id=1, source_target_pairs={{0,1},{1,0},{2,3},{3,2},{4,5},{5,4},{6,7},{7,6},{8,9},{9,8},{10,11... | collective-permute-start | bytes 1920008 | tf_op jit(solution)/shard_map/ppermute | solution.py:1212
  753.2 226.2 %reduce-scatter.27.cloned.1.call-start = ((), (), s32[]{:S(2)}) async-start(), calls=%async_computation.17 | async-start | bytes 5990400
  755.0 58.1 %collective-permute-start.19 = (bf16[256,1664]{1,0:T(8,128)(2,1)S(1)}, bf16[256,1664]{1,0:T(8,128)(2,1)}, u32[]{:S(2)}, u32[]{:S(2)}) collective-permute-start(bf16[256,1664]{1,0:T(8,128)(2,1)S(1)} %get-tuple-element.544), channel_id=1, source_target_pairs={{0,1},{1,0},{2,5},{3,4},{4,3},{5,2},{6,7},{7,6},{8,9},{9,8},{10,13... | collective-permute-start | bytes 2555912 | tf_op jit(solution)/shard_map/ppermute | solution.py:1212
  757.8 55.2 %collective-permute-start.18 = (bf16[256,1664]{1,0:T(8,128)(2,1)S(1)}, bf16[256,1664]{1,0:T(8,128)(2,1)}, u32[]{:S(2)}, u32[]{:S(2)}) collective-permute-start(bf16[256,1664]{1,0:T(8,128)(2,1)S(1)} %get-tuple-element.545), channel_id=1, source_target_pairs={{2,4},{3,5},{4,2},{5,3},{10,12},{11,13},{12,10},{13,11},{18,20},{1... | collective-permute-start | bytes 2555912 | tf_op jit(solution)/shard_map/ppermute | solution.py:1212
  760.0 53.0 %collective-permute-start.17 = (bf16[2,200,1600]{2,1,0:T(8,128)(2,1)S(1)}, bf16[2,200,1600]{2,1,0:T(8,128)(2,1)}, u32[]{:S(2)}, u32[]{:S(2)}) collective-permute-start(bf16[2,200,1600]{2,1,0:T(8,128)(2,1)S(1)} %copy-done.71), channel_id=1, source_target_pairs={{0,1},{1,0},{2,3},{3,2},{4,5},{5,4},{6,7},{7,6},{8,9},{9,8},{10,11... | collective-permute-start | bytes 3840008 | tf_op jit(solution)/shard_map/ppermute | solution.py:1212
  825.1 9.3 collective-permute-start.20
  825.7 12.0 collective-permute-start.21
  825.7 16.3 %collective-permute-start.22 = (bf16[1,200,1600]{2,1,0:T(8,128)(2,1)}, bf16[1,200,1600]{2,1,0:T(8,128)(2,1)}, u32[]{:S(2)}, u32[]{:S(2)}) collective-permute-start(bf16[1,200,1600]{2,1,0:T(8,128)(2,1)} %get-tuple-element.293), channel_id=1, source_target_pairs={{0,1},{1,0},{2,3},{3,2},{4,5},{5,4},{6,7},{7,6},{8,9},{9,8},{10,11... | collective-permute-start | bytes 1920008 | tf_op jit(solution)/shard_map/ppermute | solution.py:1212
  842.0 247.3 %reduce-scatter.31.cloned.1.call-start = ((), (), s32[]{:S(2)}) async-start(), calls=%async_computation.19 | async-start | bytes 3328000
  889.3 224.6 %reduce-scatter.29.cloned.1.call-start = ((), (), s32[]{:S(2)}) async-start(), calls=%async_computation.18 | async-start | bytes 11520000
  889.9 318.8 %reduce-scatter.33.cloned.1.call-start = ((), (), s32[]{:S(2)}) async-start(), calls=%async_computation.20 | async-start | bytes 3328000
  893.5 85.9 %collective-permute-start.23 = (bf16[200,1600]{1,0:T(8,128)(2,1)}, bf16[200,1600]{1,0:T(8,128)(2,1)S(1)}, u32[]{:S(2)}, u32[]{:S(2)}) collective-permute-start(bf16[200,1600]{1,0:T(8,128)(2,1)} %dynamic-slice_bitcast_fusion.11), channel_id=1, source_target_pairs={{0,1},{1,0},{2,3},{3,2},{4,5},{5,4},{6,7},{7,6},{8,9},{9,8},{10,11... | collective-permute-start | bytes 1920008 | tf_op jit(solution)/shard_map/ppermute | solution.py:1212
  987.4 23.5 %collective-permute-start.24 = (bf16[1,200,1600]{2,1,0:T(8,128)(2,1)}, bf16[1,200,1600]{2,1,0:T(8,128)(2,1)}, u32[]{:S(2)}, u32[]{:S(2)}) collective-permute-start(bf16[1,200,1600]{2,1,0:T(8,128)(2,1)} %get-tuple-element.318), channel_id=1, source_target_pairs={{0,1},{1,0},{2,3},{3,2},{4,5},{5,4},{6,7},{7,6},{8,9},{9,8},{10,11... | collective-permute-start | bytes 1920008 | tf_op jit(solution)/shard_map/ppermute | solution.py:1212
  1011.0 18.9 %collective-permute-start.25 = (bf16[1,200,1600]{2,1,0:T(8,128)(2,1)}, bf16[1,200,1600]{2,1,0:T(8,128)(2,1)}, u32[]{:S(2)}, u32[]{:S(2)}) collective-permute-start(bf16[1,200,1600]{2,1,0:T(8,128)(2,1)} %get-tuple-element.324), channel_id=1, source_target_pairs={{0,1},{1,0},{2,3},{3,2},{4,5},{5,4},{6,7},{7,6},{8,9},{9,8},{10,11... | collective-permute-start | bytes 1920008 | tf_op jit(solution)/shard_map/ppermute | solution.py:1212
  1029.9 59.5 %collective-permute-start.26 = (bf16[2,200,1600]{2,1,0:T(8,128)(2,1)}, bf16[2,200,1600]{2,1,0:T(8,128)(2,1)}, u32[]{:S(2)}, u32[]{:S(2)}) collective-permute-start(bf16[2,200,1600]{2,1,0:T(8,128)(2,1)} %dynamic-slice_bitcast_fusion.4), channel_id=1, source_target_pairs={{0,1},{1,0},{2,3},{3,2},{4,5},{5,4},{6,7},{7,6},{8,9},{9,8},{10,11... | collective-permute-start | bytes 3840008 | tf_op jit(solution)/shard_map/ppermute | solution.py:1212
  1033.6 55.7 %collective-permute-start.27 = (bf16[1,200,1600]{2,1,0:T(8,128)(2,1)}, bf16[1,200,1600]{2,1,0:T(8,128)(2,1)}, u32[]{:S(2)}, u32[]{:S(2)}) collective-permute-start(bf16[1,200,1600]{2,1,0:T(8,128)(2,1)} %get-tuple-element.530), channel_id=1, source_target_pairs={{0,1},{1,0},{2,3},{3,2},{4,5},{5,4},{6,7},{7,6},{8,9},{9,8},{10,11... | collective-permute-start | bytes 1920008 | tf_op jit(solution)/shard_map/ppermute | solution.py:1212
  1118.6 255.7 %reduce-scatter.35.cloned.1.call-start = ((), (), s32[]{:S(2)}) async-start(), calls=%async_computation.21 | async-start | bytes 3328000
  1118.6 35.8 %collective-permute-start.32 = (bf16[1,200,1600]{2,1,0:T(8,128)(2,1)}, bf16[1,200,1600]{2,1,0:T(8,128)(2,1)S(1)}, u32[]{:S(2)}, u32[]{:S(2)}) collective-permute-start(bf16[1,200,1600]{2,1,0:T(8,128)(2,1)} %get-tuple-element.355), channel_id=1, source_target_pairs={{0,1},{1,0},{2,3},{3,2},{4,5},{5,4},{6,7},{7,6},{8,9},{9,8},{10,11... | collective-permute-start | bytes 1920008 | tf_op jit(solution)/shard_map/ppermute | solution.py:1212
  1122.2 28.1 %collective-permute-start.30 = (bf16[400,1600]{1,0:T(8,128)(2,1)S(1)}, bf16[400,1600]{1,0:T(8,128)(2,1)S(1)}, u32[]{:S(2)}, u32[]{:S(2)}) collective-permute-start(bf16[400,1600]{1,0:T(8,128)(2,1)S(1)} %constant_dynamic-update-slice_fusion.2), channel_id=1, source_target_pairs={{1,4},{3,6},{4,1},{6,3},{9,12},{11,14},{12,9},{14,11},{17,20},{19,... | collective-permute-start | bytes 3840008 | tf_op jit(solution)/shard_map/ppermute | solution.py:1212
  1127.9 23.6 %collective-permute-start.28 = (bf16[512,1664]{1,0:T(8,128)(2,1)}, bf16[512,1664]{1,0:T(8,128)(2,1)S(1)}, u32[]{:S(2)}, u32[]{:S(2)}) collective-permute-start(bf16[512,1664]{1,0:T(8,128)(2,1)} %copy-done.8), channel_id=1, source_target_pairs={{0,4},{1,5},{2,6},{3,7},{4,0},{5,1},{6,2},{7,3},{8,12},{9,13},{10,... | collective-permute-start | bytes 5111816 | tf_op jit(solution)/shard_map/ppermute | solution.py:1212
  1128.0 23.8 %collective-permute-start.29 = (bf16[512,1664]{1,0:T(8,128)(2,1)S(1)}, bf16[512,1664]{1,0:T(8,128)(2,1)S(1)}, u32[]{:S(2)}, u32[]{:S(2)}) collective-permute-start(bf16[512,1664]{1,0:T(8,128)(2,1)S(1)} %copy-done.7), channel_id=1, source_target_pairs={{0,4},{1,5},{2,6},{3,7},{4,0},{5,1},{6,2},{7,3},{8,12},{9,13},{10,... | collective-permute-start | bytes 5111816 | tf_op jit(solution)/shard_map/ppermute | solution.py:1212
  1132.6 21.9 %collective-permute-start.31 = (bf16[100,3200]{1,0:T(8,128)(2,1)S(1)}, bf16[100,3200]{1,0:T(8,128)(2,1)S(1)}, u32[]{:S(2)}, u32[]{:S(2)}) collective-permute-start(bf16[100,3200]{1,0:T(8,128)(2,1)S(1)} %get-tuple-element.553), channel_id=1, source_target_pairs={{0,2},{1,3},{2,0},{3,1},{4,6},{5,7},{6,4},{7,5},{8,10},{9,11},{10,... | collective-permute-start | bytes 1920008 | tf_op jit(solution)/shard_map/ppermute | solution.py:1212
  1173.1 15.0 %collective-permute-start.33 = (bf16[100,3200]{1,0:T(8,128)(2,1)}, bf16[100,3200]{1,0:T(8,128)(2,1)}, u32[]{:S(2)}, u32[]{:S(2)}) collective-permute-start(bf16[100,3200]{1,0:T(8,128)(2,1)} %get-tuple-element.361), channel_id=1, source_target_pairs={{0,2},{1,3},{2,0},{3,1},{4,6},{5,7},{6,4},{7,5},{8,10},{9,11},{10,... | collective-permute-start | bytes 1920008 | tf_op jit(solution)/shard_map/ppermute | solution.py:1212
  1174.3 16.9 %collective-permute-start.34 = (bf16[1,200,1600]{2,1,0:T(8,128)(2,1)}, bf16[1,200,1600]{2,1,0:T(8,128)(2,1)}, u32[]{:S(2)}, u32[]{:S(2)}) collective-permute-start(bf16[1,200,1600]{2,1,0:T(8,128)(2,1)} %get-tuple-element.362), channel_id=1, source_target_pairs={{0,1},{1,0},{2,3},{3,2},{4,5},{5,4},{6,7},{7,6},{8,9},{9,8},{10,11... | collective-permute-start | bytes 1920008 | tf_op jit(solution)/shard_map/ppermute | solution.py:1212
  1192.8 15.9 %collective-permute-start.35 = (bf16[1,200,1600]{2,1,0:T(8,128)(2,1)S(1)}, bf16[1,200,1600]{2,1,0:T(8,128)(2,1)}, u32[]{:S(2)}, u32[]{:S(2)}) collective-permute-start(bf16[1,200,1600]{2,1,0:T(8,128)(2,1)S(1)} %copy-done.81), channel_id=1, source_target_pairs={{0,1},{1,0},{2,3},{3,2},{4,5},{5,4},{6,7},{7,6},{8,9},{9,8},{10,11... | collective-permute-start | bytes 1920008 | tf_op jit(solution)/shard_map/ppermute | solution.py:1212
  1212.4 161.9 %reduce-scatter.37.cloned.1.call-start = ((), (), s32[]{:S(2)}) async-start(), calls=%async_computation.22 | async-start | bytes 5990400
  1221.1 152.3 %collective-permute-start.37 = (bf16[200,1600]{1,0:T(8,128)(2,1)}, bf16[200,1600]{1,0:T(8,128)(2,1)S(1)}, u32[]{:S(2)}, u32[]{:S(2)}) collective-permute-start(bf16[200,1600]{1,0:T(8,128)(2,1)} %pad_maximum_fusion.9), channel_id=1, source_target_pairs={{0,1},{1,0},{2,3},{3,2},{4,5},{5,4},{6,7},{7,6},{8,9},{9,8},{10,11... | collective-permute-start | bytes 1920008 | tf_op jit(solution)/shard_map/ppermute | solution.py:1212
  1221.1 150.3 %collective-permute-start.36 = (bf16[200,1600]{1,0:T(8,128)(2,1)}, bf16[200,1600]{1,0:T(8,128)(2,1)}, u32[]{:S(2)}, u32[]{:S(2)}) collective-permute-start(bf16[200,1600]{1,0:T(8,128)(2,1)} %reduce-scatter.33.cloned.1.call-done), channel_id=1, source_target_pairs={{1,4},{3,6},{4,1},{6,3},{9,12},{11,14},{12,9},{14,11},{17,20},{19,... | collective-permute-start | bytes 1920008 | tf_op jit(solution)/shard_map/ppermute | solution.py:1212
  1226.4 147.1 %collective-permute-start.39 = (bf16[256,1664]{1,0:T(8,128)(2,1)S(1)}, bf16[256,1664]{1,0:T(8,128)(2,1)}, u32[]{:S(2)}, u32[]{:S(2)}) collective-permute-start(bf16[256,1664]{1,0:T(8,128)(2,1)S(1)} %get-tuple-element.538), channel_id=1, source_target_pairs={{0,1},{1,0},{2,5},{3,4},{4,3},{5,2},{6,7},{7,6},{8,9},{9,8},{10,13... | collective-permute-start | bytes 2555912 | tf_op jit(solution)/shard_map/ppermute | solution.py:1212
  1226.6 148.6 %copy-start.63 = (bf16[200,1600]{1,0:T(8,128)(2,1)S(1)}, bf16[200,1600]{1,0:T(8,128)(2,1)}, u32[]{:S(2)}) copy-start(bf16[200,1600]{1,0:T(8,128)(2,1)} %pad_maximum_fusion.8) | copy-start | bytes 1920004
  1226.6 147.7 %collective-permute-start.38 = (bf16[256,1664]{1,0:T(8,128)(2,1)S(1)}, bf16[256,1664]{1,0:T(8,128)(2,1)}, u32[]{:S(2)}, u32[]{:S(2)}) collective-permute-start(bf16[256,1664]{1,0:T(8,128)(2,1)S(1)} %get-tuple-element.539), channel_id=1, source_target_pairs={{2,4},{3,5},{4,2},{5,3},{10,12},{11,13},{12,10},{13,11},{18,20},{1... | collective-permute-start | bytes 2555912 | tf_op jit(solution)/shard_map/ppermute | solution.py:1212
  1380.3 18.9 %collective-permute-start.40 = (bf16[200,400]{1,0:T(8,128)(2,1)}, bf16[200,400]{1,0:T(8,128)(2,1)}, u32[]{:S(2)}, u32[]{:S(2)}) collective-permute-start(bf16[200,400]{1,0:T(8,128)(2,1)} %get-tuple-element.562), channel_id=1, source_target_pairs={{0,1},{1,0},{2,3},{3,2},{4,5},{5,4},{6,7},{7,6},{8,9},{9,8},{10,11... | collective-permute-start | bytes 480008 | tf_op jit(solution)/shard_map/ppermute | solution.py:1212
  1385.6 13.6 collective-permute-start.42
  1385.6 13.6 collective-permute-start.41
  1386.8 16.0 %collective-permute-start.43 = (bf16[200,1600]{1,0:T(8,128)(2,1)}, bf16[200,1600]{1,0:T(8,128)(2,1)}, u32[]{:S(2)}, u32[]{:S(2)}) collective-permute-start(bf16[200,1600]{1,0:T(8,128)(2,1)} %reduce-scatter.35.cloned.1.call-done), channel_id=1, source_target_pairs={{1,4},{3,6},{4,1},{6,3},{9,12},{11,14},{12,9},{14,11},{17,20},{19,... | collective-permute-start | bytes 1920008 | tf_op jit(solution)/shard_map/ppermute | solution.py:1212
  (128 other events, 1025.8 us)
Sparse Core Ops, SparseCore 0:
  10.2 107.6 all-gather.20
  120.1 55.5 all-gather.8
  177.9 55.4 all-gather.10
  235.0 55.4 all-gather.12
  292.0 55.5 all-gather.14
  349.1 55.5 all-gather.16
  406.3 55.4 all-gather.18
  711.7 113.2 reduce-scatter.22
  827.4 59.4 reduce-scatter.24
  889.1 60.1 reduce-scatter.26
  952.1 53.5 reduce-scatter.30
  1007.9 105.9 reduce-scatter.28
  1118.7 52.9 reduce-scatter.32
  1212.5 52.1 reduce-scatter.34
  1266.8 91.2 reduce-scatter.36
